TPU v7x, 32 devices: a whole 2x2x4 slice. The times are simulated.
32 devices in a mesh: groups: 2 (over x), sub: 16 (over z, y, core).
Axes of the slice: x: 2, y: 2, z: 4, core: 2. Of those that a mesh axis runs over, the one named last changes fastest.
Arguments:
- rhs: float32 [2, 2048, 512], P(None, ('groups', 'sub')), parts along dimension 1, may hold values from -6 to 6
- viscosity: float32 [2048, 512], P(('groups', 'sub')), parts along dimension 0, may hold values from 0.3 to 3
- coupling: float32 [2, 2048, 512], P(None, ('groups', 'sub')), parts along dimension 1, may hold values from -0.3 to 0.3
- margin_rows: int32 [32], P('groups'), parts along dimension 0, may hold values from 1 to 20, as said below
- coarse_basis: bfloat16 [48, 2, 2048, 512], P(None, None, ('groups', 'sub')), parts along dimension 2, may hold values from -0.0078125 to 0.0078125
- coarse_inverse: float32 [1536, 768], P(('groups', 'sub')), parts along dimension 0, as said below
Outputs:
- solution: float32 [2, 2048, 512], P(None, ('groups', 'sub')), parts along dimension 1
- hessenberg: float32 [6, 2], P('groups'), parts along dimension 0
There are 2 independent parts, one for each index of `groups`. A program takes and returns all parts, laid end to end along the dimension named above; each array names one. Nothing has to cross between parts.
Inputs may be any that keep to these rules, and one draw needn't show every extreme that they name: `margin_rows`: the last entry is not read; some entry before it equals 20. `coarse_inverse`: A dense matrix.
All inputs are finite; a program needn't handle non-finite values.
Results may differ from a plain program's by a relative error of at most 0.003.
Values sent between devices are 32-bit elements; how exact they have to be, the bound alone decides.
No kernel may reach another device: no remote copies, remote signals or barrier semaphores. Data moves between devices by JAX's collectives and lax.ppermute only.
A program may use at most 64 MiB of HBM per device.

v0:
```python
import jax
import jax.numpy as jnp
from jax import lax
from jax.sharding import PartitionSpec as P

ROWS = 64
CELLS = 512
MARGIN = 20
SWEEPS = 4
ITERS = 2


relax_factor = 0.7


def with_halo(cells, sides, width):
    for axis, dim in sides:
        count = lax.axis_size(axis)
        ends = count - 1
        head = lax.slice_in_dim(cells, 0, width, axis=dim)
        tail = lax.slice_in_dim(cells, cells.shape[dim] - width, cells.shape[dim], axis=dim)
        cells = jnp.concatenate(
            [
                lax.ppermute(tail, axis, [(i, (i + 1) % count) for i in range(ends)]),
                cells,
                lax.ppermute(head, axis, [((i + 1) % count, i) for i in range(ends)]),
            ],
            axis=dim,
        )
    return cells


def apply_operator(padded, viscosity, coupling):
    middle = padded[:, 1:-1]
    row_sum = padded[:, :-2] + padded[:, 2:]
    bordered = jnp.pad(middle, ((0, 0), (0, 0), (1, 1)))
    col_sum = bordered[:, :, :-2] + bordered[:, :, 2:]
    row_factor = jnp.array([1.0, 4.0], jnp.float32)[:, None, None]
    col_factor = jnp.array([4.0, 1.0], jnp.float32)[:, None, None]
    diagonal = 10.0 * viscosity + jnp.abs(coupling) + 0.05
    return (
        diagonal * middle
        - viscosity * (row_factor * row_sum + col_factor * col_sum)
        + coupling * middle[::-1]
    )


def pad_rows(field):
    return jnp.pad(field, ((0, 0), (1, 1), (0, 0)))


def local_solve(residual, viscosity, coupling, live):
    live_grid = live[None, :, None]
    diagonal = 10.0 * viscosity + jnp.abs(coupling) + 0.05
    solved = jnp.zeros_like(residual)
    for sweep in range(SWEEPS):
        image = apply_operator(pad_rows(solved), viscosity, coupling)
        solved = live_grid * (solved + relax_factor * (residual - image) / diagonal)
    return solved


def window_weights(lower, upper, length):
    places = jnp.arange(length, dtype=jnp.int32) - MARGIN
    place_f = places.astype(jnp.float32)
    lower_f = lower.astype(jnp.float32)
    upper_f = upper.astype(jnp.float32)
    live = ((places >= -lower) & (places < ROWS + upper)).astype(jnp.float32)
    weight = jnp.ones((length,), jnp.float32)
    weight = jnp.where(
        places < lower, (place_f + lower_f + 0.5) / (2.0 * jnp.maximum(lower_f, 1.0)), weight
    )
    weight = jnp.where(
        places >= ROWS - upper,
        (ROWS + upper_f - place_f - 0.5) / (2.0 * jnp.maximum(upper_f, 1.0)),
        weight,
    )
    return (live, weight * live)


def least_squares(hessenberg, beta):
    normal = jnp.dot(hessenberg.T, hessenberg, precision=lax.Precision.HIGHEST)
    target = beta * hessenberg[0]
    factor = jnp.linalg.cholesky(normal)
    forward = []
    for row in range(ITERS):
        acc = target[row]
        for col in range(row):
            acc = acc - factor[row, col] * forward[col]
        forward.append(acc / factor[row, row])
    backward = [None] * ITERS
    for row in reversed(range(ITERS)):
        acc = forward[row]
        for col in range(row + 1, ITERS):
            acc = acc - factor[col, row] * backward[col]
        backward[row] = acc / factor[row, row]
    return backward


def global_sums(values):
    return lax.psum(values, "sub")


def on_device(rhs, viscosity, coupling, margin_rows, coarse_basis, coarse_inverse):
    length = ROWS + 2 * MARGIN
    count = lax.axis_size("sub")
    rank = lax.axis_index("sub")
    lower = jnp.where(rank > 0, margin_rows[jnp.maximum(rank - 1, 0)], 0)
    upper = jnp.where(rank < count - 1, margin_rows[rank], 0)
    live, weight = window_weights(lower, upper, length)
    coefficients = with_halo(jnp.concatenate([viscosity[None], coupling], 0), (("sub", 1),), MARGIN)
    flat_basis = coarse_basis.reshape(coarse_basis.shape[0], -1)
    depth = MARGIN
    beta = jnp.sqrt(global_sums((jnp.sum(rhs * rhs),))[0])
    krylov = [rhs / beta]
    directions = []
    hessenberg = jnp.zeros((ITERS + 1, ITERS), jnp.float32)
    for turn in range(ITERS):
        vector = krylov[turn]
        extended = with_halo(vector, (("sub", 1),), MARGIN)
        coarse_res = jnp.dot(
            flat_basis, vector.astype(jnp.bfloat16).reshape(-1), preferred_element_type=jnp.float32
        )
        gathered = lax.all_gather(coarse_res, "sub", axis=0, tiled=True)
        lifted = jnp.dot(coarse_inverse, gathered, precision=lax.Precision.HIGHEST).astype(
            jnp.bfloat16
        )
        coarse = jnp.dot(lifted, flat_basis, preferred_element_type=jnp.float32).reshape(
            2, ROWS, CELLS
        )
        solved = local_solve(extended, coefficients[0], coefficients[1:], live)
        shares = solved * weight[None, :, None]
        shares = shares.at[:, MARGIN : MARGIN + ROWS].add(coarse)
        outgoing = jnp.concatenate([shares[:, :depth], shares[:, length - depth :]], 1)
        received = with_halo(outgoing, (("sub", 1),), depth)
        result = shares[:, MARGIN : MARGIN + ROWS]
        result = result.at[:, :MARGIN].add(received[:, depth - MARGIN : depth])
        result = result.at[:, ROWS - MARGIN :].add(received[:, 3 * depth : 3 * depth + MARGIN])
        padded = with_halo(result, (("sub", 1),), 1)
        direction, padded = (result, padded)
        directions.append(direction)
        image = apply_operator(padded, viscosity, coupling)
        totals = global_sums(
            tuple((jnp.sum(earlier * image) for earlier in krylov)) + (jnp.sum(image * image),)
        )
        heights = list(totals[:-1])
        squares = totals[-1]
        for earlier, height in zip(krylov, heights):
            image = image - height * earlier
            squares = squares - height * height
        length_new = jnp.sqrt(squares)
        for slot, height in enumerate(heights):
            hessenberg = hessenberg.at[slot, turn].set(height)
        hessenberg = hessenberg.at[turn + 1, turn].set(length_new)
        krylov.append(image / length_new)
    coeffs = least_squares(hessenberg, beta)
    solution = coeffs[0] * directions[0]
    turn = 1
    solution = solution + coeffs[turn] * directions[turn]
    return (solution, hessenberg)


def solution(mesh):
    in_specs = (
        P(None, ("groups", "sub"), None),
        P(("groups", "sub"), None),
        P(None, ("groups", "sub"), None),
        P("groups"),
        P(None, None, ("groups", "sub"), None),
        P(("groups", "sub"), None),
    )
    out_specs = (P(None, ("groups", "sub"), None), P("groups", None))
    return jax.shard_map(
        on_device, mesh=mesh, in_specs=in_specs, out_specs=out_specs, check_vma=False
    )
```

profile of v0, /device:TPU:0, one launch (start us, length us, event | category | flops | bytes accessed | tf_op | source)
XLA Modules:
  0.0 261.1 jit_solution(7641065931824454767)
XLA Ops:
  0.7 1.0 pad_maximum_fusion.11
  1.7 2.4 collective-permute-start.2
  4.0 1.6 multiply_reduce_fusion.5
  5.7 1.3 collective-permute-start.3
  7.0 36.4 %psum.42 = f32[]{:T(128)} all-reduce(f32[]{:T(128)} %multiply_reduce_fusion.5), channel_id=1, replica_groups=mesh['groups'=2,'sub'=16] {'sub'}, use_global_device_ids=true, to_apply=%region_1.2 | all-reduce | flops 1 | bytes 8 | tf_op jit(solution)/shard_map/psum | solution.py:100
  44.1 1.0 convert_bitcast_fusion.1
  45.1 1.3 collective-permute-start
  46.4 1.3 collective-permute-start.1
  47.7 1.3 fusion.131
  49.8 10.1 %fusion.8 = f32[48]{0:T(128)S(1)} fusion(bf16[48,2,64,512]{3,2,1,0:T(8,128)(2,1)} %param.52, bf16[2,64,512,1]{2,1,0,3:T(8,128)(2,1)S(1)} %get-tuple-element.147), kind=kOutput, calls=%fused_computation.8 | convolution fusion | flops 6291456 | bytes 6422720 | tf_op jit(solution)/shard_map/dot_general | solution.py:120
  61.4 30.8 %all-reduce.17 = f32[768]{0:T(1024)S(1)} all-reduce(f32[768]{0:T(1024)S(1)} %dynamic-update-slice.31), channel_id=1, replica_groups=mesh['groups'=2,'sub'=16] {'sub'}, use_global_device_ids=true, to_apply=%add.17 | all-reduce | flops 768 | bytes 6144
  93.1 6.4 %fusion.2 = f32[1,2,64,512]{3,0,2,1:T(1,128)S(1)} fusion(bf16[48,1,1,1]{0,1,3,2:T(2,128)(2,1)S(1)} %fusion.15, bf16[2,64,512,48]{2,1,0,3:T(8,128)(2,1)} %bitcast.78), kind=kOutput, calls=%fused_computation.2 | convolution fusion | flops 6291456 | bytes 6553696 | tf_op jit(solution)/shard_map/dot_general | solution.py:127
  101.6 1.3 collective-permute-start.4
  103.0 1.3 collective-permute-start.5
  104.9 1.3 collective-permute-done.5
  106.6 1.3 collective-permute-start.7
  107.9 4.6 %collective-permute-start.6 = (f32[2,1,512]{2,1,0:T(1,128)S(1)}, f32[2,1,512]{2,1,0:T(1,128)S(1)}, u32[]{:S(2)}, u32[]{:S(2)}) collective-permute-start(f32[2,1,512]{2,1,0:T(1,128)S(1)} %slice.522), channel_id=1, source_target_pairs={{0,1},{1,2},{2,3},{3,4},{4,5},{5,6},{6,7},{7,8},{8,9},{9,10},{10,1... | collective-permute-start | bytes 12296 | tf_op jit(solution)/shard_map/ppermute | solution.py:24
  113.3 0.9 multiply_reduce_fusion.4
  114.2 31.8 %all-reduce.20 = (f32[]{:T(128)}, f32[]{:T(128)}) all-reduce(f32[]{:T(128)} %get-tuple-element.138, f32[]{:T(128)} %get-tuple-element.137), channel_id=1, replica_groups=mesh['groups'=2,'sub'=16] {'sub'}, use_global_device_ids=true, to_apply=%region_5.6 | all-reduce | flops 2 | bytes 16 | tf_op jit(solution)/shard_map/psum | solution.py:100
  148.6 1.3 collective-permute-start.8
  149.9 1.5 collective-permute-start.9
  151.4 10.0 %fusion.11 = f32[48]{0:T(128)S(1)} fusion(bf16[48,2,64,512]{3,2,1,0:T(8,128)(2,1)} %param.52, bf16[2,64,512,1]{2,1,0,3:T(8,128)(2,1)S(1)} %get-tuple-element.144), kind=kOutput, calls=%fused_computation.9 | convolution fusion | flops 6291456 | bytes 6422720 | tf_op jit(solution)/shard_map/dot_general | solution.py:120
  161.6 30.9 %all-reduce.18 = f32[768]{0:T(1024)S(1)} all-reduce(f32[768]{0:T(1024)S(1)} %dynamic-update-slice.32), channel_id=1, replica_groups=mesh['groups'=2,'sub'=16] {'sub'}, use_global_device_ids=true, to_apply=%add.18 | all-reduce | flops 768 | bytes 6144
  192.7 6.4 %fusion = f32[1,2,64,512]{3,0,2,1:T(1,128)S(1)} fusion(bf16[48,1,1,1]{0,1,3,2:T(2,128)(2,1)S(1)} %fusion.17, bf16[2,64,512,48]{2,1,0,3:T(8,128)(2,1)} %bitcast.79), kind=kOutput, calls=%fused_computation | convolution fusion | flops 6291456 | bytes 6553696 | tf_op jit(solution)/shard_map/dot_general | solution.py:127
  201.1 1.3 collective-permute-start.10
  202.4 1.3 collective-permute-start.11
  204.3 1.3 collective-permute-done.11
  206.0 1.3 collective-permute-start.13
  207.3 4.6 %collective-permute-start.12 = (f32[2,1,512]{2,1,0:T(1,128)S(1)}, f32[2,1,512]{2,1,0:T(1,128)S(1)}, u32[]{:S(2)}, u32[]{:S(2)}) collective-permute-start(f32[2,1,512]{2,1,0:T(1,128)S(1)} %slice.531), channel_id=1, source_target_pairs={{0,1},{1,2},{2,3},{3,4},{4,5},{5,6},{6,7},{7,8},{8,9},{9,10},{10,1... | collective-permute-start | bytes 12296 | tf_op jit(solution)/shard_map/ppermute | solution.py:24
  213.4 0.9 multiply_reduce_fusion
  214.3 31.9 %all-reduce.19 = (f32[]{:T(128)}, f32[]{:T(128)}, f32[]{:T(128)}) all-reduce(f32[]{:T(128)} %get-tuple-element.136, f32[]{:T(128)} %get-tuple-element.135, f32[]{:T(128)} %get-tuple-element.134), channel_id=1, replica_groups=mesh['groups'=2,'sub'=16] {'sub'}, use_global_device_ids=true, to_apply=%region_7.8 | all-reduce | flops 3 | bytes 24 | tf_op jit(solution)/shard_map/psum | solution.py:100
  249.4 1.9 scatter.20
  (86 shorter events, 15.0 us)
Async XLA Ops:
  0.6 92.2 %copy-start = (f32[48,768]{1,0:T(8,128)S(1)}, f32[48,768]{1,0:T(8,128)}, u32[]{:S(2)}) copy-start(f32[48,768]{1,0:T(8,128)} %param.53) | copy-start | bytes 442372
  0.6 59.2 %copy-start.6 = (u32[32]{0:T(128)S(1)}, u32[32]{0:T(128)}, u32[]{:S(2)}) copy-start(u32[32]{0:T(128)} %constant.396) | copy-start | bytes 388
  1.7 97.8 %collective-permute-start.2 = (f32[3,20,512]{2,1,0:T(8,128)S(1)}, f32[3,20,512]{2,1,0:T(8,128)S(1)}, u32[]{:S(2)}, u32[]{:S(2)}) collective-permute-start(f32[3,20,512]{2,1,0:T(8,128)S(1)} %get-tuple-element.157), channel_id=1, source_target_pairs={{0,1},{1,2},{2,3},{3,4},{4,5},{5,6},{6,7},{7,8},{8,9},{9,10},{10,1... | collective-permute-start | bytes 368648 | tf_op jit(solution)/shard_map/ppermute | solution.py:24
  5.7 93.8 %collective-permute-start.3 = (f32[3,20,512]{2,1,0:T(8,128)S(1)}, f32[3,20,512]{2,1,0:T(8,128)S(1)}, u32[]{:S(2)}, u32[]{:S(2)}) collective-permute-start(f32[3,20,512]{2,1,0:T(8,128)S(1)} %get-tuple-element.158), channel_id=1, source_target_pairs={{1,0},{2,1},{3,2},{4,3},{5,4},{6,5},{7,6},{8,7},{9,8},{10,9},{11,1... | collective-permute-start | bytes 368648 | tf_op jit(solution)/shard_map/ppermute | solution.py:26
  45.1 54.4 %collective-permute-start = (f32[2,20,512]{2,1,0:T(8,128)S(1)}, f32[2,20,512]{2,1,0:T(8,128)S(1)}, u32[]{:S(2)}, u32[]{:S(2)}) collective-permute-start(f32[2,20,512]{2,1,0:T(8,128)S(1)} %get-tuple-element.161), channel_id=1, source_target_pairs={{0,1},{1,2},{2,3},{3,4},{4,5},{5,6},{6,7},{7,8},{8,9},{9,10},{10,1... | collective-permute-start | bytes 245768 | tf_op jit(solution)/shard_map/ppermute | solution.py:24
  46.4 53.2 %collective-permute-start.1 = (f32[2,20,512]{2,1,0:T(8,128)S(1)}, f32[2,20,512]{2,1,0:T(8,128)S(1)}, u32[]{:S(2)}, u32[]{:S(2)}) collective-permute-start(f32[2,20,512]{2,1,0:T(8,128)S(1)} %get-tuple-element.162), channel_id=1, source_target_pairs={{1,0},{2,1},{3,2},{4,3},{5,4},{6,5},{7,6},{8,7},{9,8},{10,9},{11,1... | collective-permute-start | bytes 245768 | tf_op jit(solution)/shard_map/ppermute | solution.py:26
  49.8 49.7 %copy-start.1 = (f32[2,64,512]{2,1,0:T(8,128)S(1)}, f32[2,64,512]{2,1,0:T(8,128)}, u32[]{:S(2)}) copy-start(f32[2,64,512]{2,1,0:T(8,128)} %param.50) | copy-start | bytes 786436
  49.8 49.7 %copy-start.2 = (f32[64,512]{1,0:T(8,128)S(1)}, f32[64,512]{1,0:T(8,128)}, u32[]{:S(2)}) copy-start(f32[64,512]{1,0:T(8,128)} %param.49) | copy-start | bytes 393220
  49.8 49.8 %copy-start.3 = (f32[2]{0:T(128)S(1)}, f32[2]{0:T(128)}, u32[]{:S(2)}) copy-start(f32[2]{0:T(128)} %constant.357.clone) | copy-start | bytes 28
  49.8 49.8 %copy-start.4 = (f32[2]{0:T(128)S(1)}, f32[2]{0:T(128)}, u32[]{:S(2)}) copy-start(f32[2]{0:T(128)} %constant.358.clone) | copy-start | bytes 28
  101.6 2.7 %collective-permute-start.4 = (f32[2,20,512]{2,1,0:T(8,128)S(1)}, f32[2,20,512]{2,1,0:T(8,128)S(1)}, u32[]{:S(2)}, u32[]{:S(2)}) collective-permute-start(f32[2,20,512]{2,1,0:T(8,128)S(1)} %get-tuple-element.156), channel_id=1, source_target_pairs={{0,1},{1,2},{2,3},{3,4},{4,5},{5,6},{6,7},{7,8},{8,9},{9,10},{10,1... | collective-permute-start | bytes 245768 | tf_op jit(solution)/shard_map/ppermute | solution.py:24
  103.0 3.2 %collective-permute-start.5 = (f32[2,20,512]{2,1,0:T(8,128)S(1)}, f32[2,20,512]{2,1,0:T(8,128)S(1)}, u32[]{:S(2)}, u32[]{:S(2)}) collective-permute-start(f32[2,20,512]{2,1,0:T(8,128)S(1)} %get-tuple-element.155), channel_id=1, source_target_pairs={{1,0},{2,1},{3,2},{4,3},{5,4},{6,5},{7,6},{8,7},{9,8},{10,9},{11,1... | collective-permute-start | bytes 245768 | tf_op jit(solution)/shard_map/ppermute | solution.py:26
  106.6 5.9 %collective-permute-start.7 = (f32[2,1,512]{2,1,0:T(1,128)S(1)}, f32[2,1,512]{2,1,0:T(1,128)S(1)}, u32[]{:S(2)}, u32[]{:S(2)}) collective-permute-start(f32[2,1,512]{2,1,0:T(1,128)S(1)} %slice.523), channel_id=1, source_target_pairs={{1,0},{2,1},{3,2},{4,3},{5,4},{6,5},{7,6},{8,7},{9,8},{10,9},{11,1... | collective-permute-start | bytes 12296 | tf_op jit(solution)/shard_map/ppermute | solution.py:26
  107.9 5.4 %collective-permute-start.6 = (f32[2,1,512]{2,1,0:T(1,128)S(1)}, f32[2,1,512]{2,1,0:T(1,128)S(1)}, u32[]{:S(2)}, u32[]{:S(2)}) collective-permute-start(f32[2,1,512]{2,1,0:T(1,128)S(1)} %slice.522), channel_id=1, source_target_pairs={{0,1},{1,2},{2,3},{3,4},{4,5},{5,6},{6,7},{7,8},{8,9},{9,10},{10,1... | collective-permute-start | bytes 12296 | tf_op jit(solution)/shard_map/ppermute | solution.py:24
  148.6 50.5 %collective-permute-start.8 = (f32[2,20,512]{2,1,0:T(8,128)S(1)}, f32[2,20,512]{2,1,0:T(8,128)S(1)}, u32[]{:S(2)}, u32[]{:S(2)}) collective-permute-start(f32[2,20,512]{2,1,0:T(8,128)S(1)} %get-tuple-element.159), channel_id=1, source_target_pairs={{0,1},{1,2},{2,3},{3,4},{4,5},{5,6},{6,7},{7,8},{8,9},{9,10},{10,1... | collective-permute-start | bytes 245768 | tf_op jit(solution)/shard_map/ppermute | solution.py:24
  149.9 49.2 %collective-permute-start.9 = (f32[2,20,512]{2,1,0:T(8,128)S(1)}, f32[2,20,512]{2,1,0:T(8,128)S(1)}, u32[]{:S(2)}, u32[]{:S(2)}) collective-permute-start(f32[2,20,512]{2,1,0:T(8,128)S(1)} %get-tuple-element.160), channel_id=1, source_target_pairs={{1,0},{2,1},{3,2},{4,3},{5,4},{6,5},{7,6},{8,7},{9,8},{10,9},{11,1... | collective-permute-start | bytes 245768 | tf_op jit(solution)/shard_map/ppermute | solution.py:26
  201.1 2.7 %collective-permute-start.10 = (f32[2,20,512]{2,1,0:T(8,128)S(1)}, f32[2,20,512]{2,1,0:T(8,128)S(1)}, u32[]{:S(2)}, u32[]{:S(2)}) collective-permute-start(f32[2,20,512]{2,1,0:T(8,128)S(1)} %get-tuple-element.154), channel_id=1, source_target_pairs={{0,1},{1,2},{2,3},{3,4},{4,5},{5,6},{6,7},{7,8},{8,9},{9,10},{10,1... | collective-permute-start | bytes 245768 | tf_op jit(solution)/shard_map/ppermute | solution.py:24
  202.4 3.2 %collective-permute-start.11 = (f32[2,20,512]{2,1,0:T(8,128)S(1)}, f32[2,20,512]{2,1,0:T(8,128)S(1)}, u32[]{:S(2)}, u32[]{:S(2)}) collective-permute-start(f32[2,20,512]{2,1,0:T(8,128)S(1)} %get-tuple-element.153), channel_id=1, source_target_pairs={{1,0},{2,1},{3,2},{4,3},{5,4},{6,5},{7,6},{8,7},{9,8},{10,9},{11,1... | collective-permute-start | bytes 245768 | tf_op jit(solution)/shard_map/ppermute | solution.py:26
  206.0 7.3 %collective-permute-start.13 = (f32[2,1,512]{2,1,0:T(1,128)S(1)}, f32[2,1,512]{2,1,0:T(1,128)S(1)}, u32[]{:S(2)}, u32[]{:S(2)}) collective-permute-start(f32[2,1,512]{2,1,0:T(1,128)S(1)} %slice.532), channel_id=1, source_target_pairs={{1,0},{2,1},{3,2},{4,3},{5,4},{6,5},{7,6},{8,7},{9,8},{10,9},{11,1... | collective-permute-start | bytes 12296 | tf_op jit(solution)/shard_map/ppermute | solution.py:26
  207.3 6.1 %collective-permute-start.12 = (f32[2,1,512]{2,1,0:T(1,128)S(1)}, f32[2,1,512]{2,1,0:T(1,128)S(1)}, u32[]{:S(2)}, u32[]{:S(2)}) collective-permute-start(f32[2,1,512]{2,1,0:T(1,128)S(1)} %slice.531), channel_id=1, source_target_pairs={{0,1},{1,2},{2,3},{3,4},{4,5},{5,6},{6,7},{7,8},{8,9},{9,10},{10,1... | collective-permute-start | bytes 12296 | tf_op jit(solution)/shard_map/ppermute | solution.py:24
  252.3 8.9 %copy-start.5 = (f32[3,2]{0,1:T(2,128)}, f32[3,2]{0,1:T(2,128)S(1)}, u32[]{:S(2)}) copy-start(f32[3,2]{0,1:T(2,128)S(1)} %scatter.24) | copy-start | bytes 76
where the time goes:
time: 262 us; the launch traced here: 261 us
  blocking collectives  162 us (62%)
  matrix products  33.3 us (13%)
  starting transfers between devices  25.9 us (10%)
  between operations  14.2 us (5%)
  other arithmetic  12.6 us (5%)
  local copies, waits for them, and re-layouts  9.89 us (4%)
  waiting for transfers between devices  3.39 us (1%)
    psum x3, blocking collectives, global_sums(): return lax.psum(values, 'sub')  100 us
    unnamed x2, blocking collectives  61.8 us
    dot_general x2, matrix products, on_device(): jnp.dot(flat_basis, vector.astype(jnp.bfloat16).reshape(-1), preferred_el...  20.1 us
    ppermute x7, starting transfers between devices, with_halo(): lax.ppermute(tail, axis, [(i, (i + 1) % count) for i in range(ends)])  16.7 us
    dot_general x2, matrix products, on_device(): jnp.dot(lifted, flat_basis, preferred_element_type=jnp.float32)  12.7 us
    ppermute x7, starting transfers between devices, with_halo(): lax.ppermute(head, axis, [((i + 1) % count, i) for i in range(ends)])  9.25 us
  transfers between devices with their start and end apart: 14, of which 3 were waited for; matrix products, arithmetic and copies ran while one was open for 16% of the time, Pallas kernels for 0%

commit v1 on v0

v1 whole, which is shorter than its diff:
```python
import jax
import jax.numpy as jnp
from jax import lax
from jax.sharding import PartitionSpec as P

ROWS = 64
CELLS = 512
MARGIN = 20
SWEEPS = 4
ITERS = 2


relax_factor = 0.7


def with_halo(cells, sides, width):
    for axis, dim in sides:
        count = lax.axis_size(axis)
        ends = count - 1
        head = lax.slice_in_dim(cells, 0, width, axis=dim)
        tail = lax.slice_in_dim(cells, cells.shape[dim] - width, cells.shape[dim], axis=dim)
        cells = jnp.concatenate(
            [
                lax.ppermute(tail, axis, [(i, (i + 1) % count) for i in range(ends)]),
                cells,
                lax.ppermute(head, axis, [((i + 1) % count, i) for i in range(ends)]),
            ],
            axis=dim,
        )
    return cells


def apply_operator(padded, viscosity, coupling):
    middle = padded[:, 1:-1]
    row_sum = padded[:, :-2] + padded[:, 2:]
    bordered = jnp.pad(middle, ((0, 0), (0, 0), (1, 1)))
    col_sum = bordered[:, :, :-2] + bordered[:, :, 2:]
    row_factor = jnp.array([1.0, 4.0], jnp.float32)[:, None, None]
    col_factor = jnp.array([4.0, 1.0], jnp.float32)[:, None, None]
    diagonal = 10.0 * viscosity + jnp.abs(coupling) + 0.05
    return (
        diagonal * middle
        - viscosity * (row_factor * row_sum + col_factor * col_sum)
        + coupling * middle[::-1]
    )


def pad_rows(field):
    return jnp.pad(field, ((0, 0), (1, 1), (0, 0)))


def local_solve(residual, viscosity, coupling, live):
    live_grid = live[None, :, None]
    diagonal = 10.0 * viscosity + jnp.abs(coupling) + 0.05
    solved = jnp.zeros_like(residual)
    for sweep in range(SWEEPS):
        image = apply_operator(pad_rows(solved), viscosity, coupling)
        solved = live_grid * (solved + relax_factor * (residual - image) / diagonal)
    return solved


def window_weights(lower, upper, length):
    places = jnp.arange(length, dtype=jnp.int32) - MARGIN
    place_f = places.astype(jnp.float32)
    lower_f = lower.astype(jnp.float32)
    upper_f = upper.astype(jnp.float32)
    live = ((places >= -lower) & (places < ROWS + upper)).astype(jnp.float32)
    weight = jnp.ones((length,), jnp.float32)
    weight = jnp.where(
        places < lower, (place_f + lower_f + 0.5) / (2.0 * jnp.maximum(lower_f, 1.0)), weight
    )
    weight = jnp.where(
        places >= ROWS - upper,
        (ROWS + upper_f - place_f - 0.5) / (2.0 * jnp.maximum(upper_f, 1.0)),
        weight,
    )
    return (live, weight * live)


def from_everyone(values):
    count = lax.axis_size("sub")
    copies = jnp.broadcast_to(values[None], (count,) + values.shape)
    return lax.all_to_all(copies, "sub", 0, 0, tiled=True)


def restrict(flat_basis, field):
    flat = field.reshape(-1)
    high = flat.astype(jnp.bfloat16)
    low = (flat - high.astype(jnp.float32)).astype(jnp.bfloat16)
    both = jnp.dot(flat_basis, jnp.stack([high, low], 1), preferred_element_type=jnp.float32)
    return both[:, 0] + both[:, 1]


def schwarz_part(field, coefficients, live, weight):
    length = live.shape[0]
    extended = with_halo(field, (("sub", 1),), MARGIN)
    solved = local_solve(extended, coefficients[0], coefficients[1:], live)
    shares = solved * weight[None, :, None]
    outgoing = jnp.concatenate([shares[:, :MARGIN], shares[:, length - MARGIN :]], 1)
    received = with_halo(outgoing, (("sub", 1),), MARGIN)
    middle = shares[:, MARGIN : MARGIN + ROWS]
    return jnp.concatenate(
        [
            middle[:, :MARGIN] + received[:, :MARGIN],
            middle[:, MARGIN : ROWS - MARGIN],
            middle[:, ROWS - MARGIN :] + received[:, 3 * MARGIN :],
        ],
        1,
    )


def on_device(rhs, viscosity, coupling, margin_rows, coarse_basis, coarse_inverse):
    length = ROWS + 2 * MARGIN
    count = lax.axis_size("sub")
    rank = lax.axis_index("sub")
    vectors = coarse_basis.shape[0]
    lower = jnp.where(rank > 0, margin_rows[jnp.maximum(rank - 1, 0)], 0)
    upper = jnp.where(rank < count - 1, margin_rows[rank], 0)
    live, weight = window_weights(lower, upper, length)
    coefficients = with_halo(jnp.concatenate([viscosity[None], coupling], 0), (("sub", 1),), MARGIN)
    flat_basis = coarse_basis.reshape(vectors, -1)

    def coarse_part(residuals):
        lifted = jnp.dot(coarse_inverse, residuals, precision=lax.Precision.HIGHEST)
        lifted = lifted.astype(jnp.bfloat16)
        return jnp.dot(lifted, flat_basis, preferred_element_type=jnp.float32).reshape(rhs.shape)

    def image_of(field):
        return apply_operator(with_halo(field, (("sub", 1),), 1), viscosity, coupling)

    first = from_everyone(
        jnp.concatenate([restrict(flat_basis, rhs), jnp.sum(rhs * rhs)[None]])
    )
    smooth_0 = schwarz_part(rhs, coefficients, live, weight)
    beta = jnp.sqrt(jnp.sum(first[:, vectors]))
    res_0 = first[:, :vectors].reshape(-1) / beta
    z_0 = smooth_0 / beta + coarse_part(res_0)
    w_0 = image_of(z_0)
    second = from_everyone(
        jnp.concatenate(
            [
                restrict(flat_basis, w_0),
                jnp.stack([jnp.sum(rhs * w_0), jnp.sum(w_0 * w_0)]),
            ]
        )
    )
    smooth_1 = schwarz_part(w_0, coefficients, live, weight)
    h_00 = jnp.sum(second[:, vectors]) / beta
    h_10 = jnp.sqrt(jnp.sum(second[:, vectors + 1]) - h_00 * h_00)
    res_1 = (second[:, :vectors].reshape(-1) - h_00 * res_0) / h_10
    z_1 = (smooth_1 - (h_00 / beta) * smooth_0) / h_10 + coarse_part(res_1)
    w_1 = image_of(z_1)
    third = from_everyone(
        jnp.stack([jnp.sum(rhs * w_1), jnp.sum(w_0 * w_1), jnp.sum(w_1 * w_1)])
    )
    sums = jnp.sum(third, 0)
    h_01 = sums[0] / beta
    h_11 = (sums[1] - h_00 * h_01) / h_10
    h_21 = jnp.sqrt(sums[2] - h_01 * h_01 - h_11 * h_11)
    zero = jnp.zeros_like(beta)
    hessenberg = jnp.stack([h_00, h_01, h_10, h_11, zero, h_21]).reshape(ITERS + 1, ITERS)
    n_00 = h_00 * h_00 + h_10 * h_10
    n_01 = h_00 * h_01 + h_10 * h_11
    n_11 = h_01 * h_01 + h_11 * h_11 + h_21 * h_21
    l_00 = jnp.sqrt(n_00)
    l_10 = n_01 / l_00
    l_11 = jnp.sqrt(n_11 - l_10 * l_10)
    f_0 = beta * h_00 / l_00
    f_1 = (beta * h_01 - l_10 * f_0) / l_11
    c_1 = f_1 / l_11
    c_0 = (f_0 - l_10 * c_1) / l_00
    return (c_0 * z_0 + c_1 * z_1, hessenberg)


def solution(mesh):
    in_specs = (
        P(None, ("groups", "sub"), None),
        P(("groups", "sub"), None),
        P(None, ("groups", "sub"), None),
        P("groups"),
        P(None, None, ("groups", "sub"), None),
        P(("groups", "sub"), None),
    )
    out_specs = (P(None, ("groups", "sub"), None), P("groups", None))
    return jax.shard_map(
        on_device, mesh=mesh, in_specs=in_specs, out_specs=out_specs, check_vma=False
    )
```

time: 262 us -> 153 us (0.58)
  blocking collectives: 162 us -> 0 us
  starting transfers between devices: 25.9 us -> 60.3 us
  matrix products: 33.3 us -> 14.5 us
  other arithmetic: 12.6 us -> 30.2 us
  waiting for transfers between devices: 3.39 us -> 18.8 us
  local copies, waits for them, and re-layouts: 9.89 us -> 20.5 us
  between operations: 14.2 us -> 7.7 us
    psum x3 -> x0, blocking collectives: 100 us -> none  [global_sums(): return lax.psum(values, 'sub')]
    unnamed x2 -> x0, blocking collectives: 61.8 us -> none
    all_to_all x0 -> x3, starting transfers between devices: none -> 25.2 us  [from_everyone(): return lax.all_to_all(copies, 'sub', 0, 0, tiled=True)]
    dot_general x7 -> x6, matrix products: 33.3 us -> 14.5 us  [the longest x2 7.72 us: coarse_part(): jnp.dot(lifted, flat_basis, preferred_element_type=jnp.float32)]
    all_to_all x0 -> x3, waiting for transfers between devices: none -> 11 us  [from_everyone(): return lax.all_to_all(copies, 'sub', 0, 0, tiled=True)]
    unnamed x21 -> x54, local copies, waits for them, and re-layouts: 1.07 us -> 12 us
    ppermute x7, starting transfers between devices: 16.7 us -> 25.6 us  [with_halo(): lax.ppermute(tail, axis, [(i, (i + 1) % count) for i in range(ends)])]
    mul x6, other arithmetic: 2.81 us -> 9.6 us  [local_solve(): solved = live_grid * (solved + relax_factor * (residual - image) / diagonal)]
  transfers between devices with their start and end apart: 14 -> 17, of which waited for: 3 -> 7; matrix products, arithmetic and copies ran while one was open for 16% -> 18% of each run, Pallas kernels for 0% -> 0%
where the time goes in v1:
time: 153 us; the launch traced here: 152 us
  starting transfers between devices  60.3 us (39%)
  other arithmetic  30.2 us (20%)
  local copies, waits for them, and re-layouts  20.5 us (13%)
  waiting for transfers between devices  18.8 us (12%)
  matrix products  14.5 us (9%)
  between operations  7.7 us (5%)
    ppermute x7, starting transfers between devices, with_halo(): lax.ppermute(tail, axis, [(i, (i + 1) % count) for i in range(ends)])  25.6 us
    all_to_all x3, starting transfers between devices, from_everyone(): return lax.all_to_all(copies, 'sub', 0, 0, tiled=True)  25.2 us
    unnamed x54, local copies, waits for them, and re-layouts  12 us
    all_to_all x3, waiting for transfers between devices, from_everyone(): return lax.all_to_all(copies, 'sub', 0, 0, tiled=True)  11 us
    mul x6, other arithmetic, local_solve(): solved = live_grid * (solved + relax_factor * (residual - image) / diagonal)  9.6 us
    ppermute x7, starting transfers between devices, with_halo(): lax.ppermute(head, axis, [((i + 1) % count, i) for i in range(ends)])  9.55 us
    dot_general x2, matrix products, coarse_part(): jnp.dot(lifted, flat_basis, preferred_element_type=jnp.float32)  7.72 us
    dot_general x2, matrix products, restrict(): jnp.dot(flat_basis, jnp.stack([high, low], 1), preferred_element_type=jnp...  6.41 us
  transfers between devices with their start and end apart: 17, of which 7 were waited for; matrix products, arithmetic and copies ran while one was open for 18% of the time, Pallas kernels for 0%

profile of v1, /device:TPU:0, one launch (start us, length us, event | category | flops | bytes accessed | tf_op | source)
XLA Modules:
  0.0 152.0 jit_solution(14740003642164739799)
XLA Ops:
  0.6 1.7 %fusion.125 = (f32[2,20,512]{2,1,0:T(8,128)}, f32[2,20,512]{2,1,0:T(8,128)}) fusion(f32[2,64,512]{2,1,0:T(8,128)} %param.26), kind=kLoop, calls=%fused_computation.210 | loop fusion | bytes 327680 | tf_op jit(solution)/shard_map/slice | solution.py:21
  2.3 2.4 %collective-permute-start = (f32[2,20,512]{2,1,0:T(8,128)}, f32[2,20,512]{2,1,0:T(8,128)S(1)}, u32[]{:S(2)}, u32[]{:S(2)}) collective-permute-start(f32[2,20,512]{2,1,0:T(8,128)} %get-tuple-element.42), channel_id=1, source_target_pairs={{0,1},{1,2},{2,3},{3,4},{4,5},{5,6},{6,7},{7,8},{8,9},{9,10},{10,1... | collective-permute-start | bytes 245768 | tf_op jit(solution)/shard_map/ppermute | solution.py:24
  6.0 1.7 %pad_maximum_fusion.12 = (f32[3,20,512]{2,1,0:T(8,128)}, f32[3,20,512]{2,1,0:T(8,128)}) fusion(f32[2,64,512]{2,1,0:T(8,128)} %param.28, f32[1,64,512]{2,1,0:T(8,128)} %bitcast.91), kind=kLoop, calls=%fused_computation.178 | loop fusion | flops 61440 | bytes 638976 | tf_op jit(solution)/shard_map/slice | solution.py:21
  7.7 5.2 %collective-permute-start.2 = (f32[3,20,512]{2,1,0:T(8,128)}, f32[3,20,512]{2,1,0:T(8,128)S(1)}, u32[]{:S(2)}, u32[]{:S(2)}) collective-permute-start(f32[3,20,512]{2,1,0:T(8,128)} %get-tuple-element.30), channel_id=1, source_target_pairs={{0,1},{1,2},{2,3},{3,4},{4,5},{5,6},{6,7},{7,8},{8,9},{9,10},{10,1... | collective-permute-start | bytes 368648 | tf_op jit(solution)/shard_map/ppermute | solution.py:24
  14.1 1.6 %multiply_reduce_fusion.5 = f32[]{:T(128)} fusion(f32[2,64,512]{2,1,0:T(8,128)} %param.26), kind=kLoop, calls=%fused_computation.173 | loop fusion | flops 131071 | bytes 262148 | tf_op jit(solution)/shard_map/reduce_sum | solution.py:132
  17.3 6.5 %copy.57 = bf16[6,8,128,512]{3,1,2,0:T(8,128)(2,1)S(1)} copy(bf16[6,8,128,512]{3,2,1,0:T(8,128)(2,1)} %bitcast.74) | data formatting | bytes 12582912
  23.9 2.5 %copy-done.1 = bf16[6,8,128,512]{3,1,2,0:T(8,128)(2,1)} copy-done((bf16[6,8,128,512]{3,1,2,0:T(8,128)(2,1)}, bf16[6,8,128,512]{3,1,2,0:T(8,128)(2,1)S(1)}, u32[]{:S(2)}) %copy-start.1) | copy-done | bytes 6291480
  26.5 1.7 %convolution_bitcast_fusion.1 = f32[48,2]{0,1:T(2,128)S(1)} fusion(bf16[48,65536]{1,0:T(8,128)(2,1)S(1)} %bitcast.81, bf16[65536,1]{0,1:T(2,128)(2,1)S(1)} %get-tuple-element.41, bf16[65536,1]{0,1:T(2,128)(2,1)S(1)} %get-tuple-element.40), kind=kOutput, calls=%fused_computation.5 | convolution fusion | flops 13107200 | bytes 6553984 | tf_op jit(solution)/shard_map/dot_general | solution.py:90
  29.5 9.2 %all-to-all-start = ((f32[16,1,49]{2,1,0:T(1,128)}), f32[16,1,49]{2,1,0:T(1,128)S(1)}, u32[]{:S(2)}, u32[]{:S(2)}) async-start(f32[16,1,49]{2,1,0:T(1,128)} %broadcast_in_dim.13), calls=%async_computation | async-start | bytes 16384 | tf_op jit(solution)/shard_map/all_to_all | solution.py:83
  40.9 4.3 %all-to-all-done = f32[16,1,49]{2,1,0:T(1,128)S(1)} async-done(((f32[16,1,49]{2,1,0:T(1,128)}), f32[16,1,49]{2,1,0:T(1,128)S(1)}, u32[]{:S(2)}, u32[]{:S(2)}) %all-to-all-start) | async-done | bytes 3168 | tf_op jit(solution)/shard_map/all_to_all | solution.py:83
  49.7 1.7 %divide_multiply_fusion.1 = (f32[2,104,512]{2,1,0:T(8,128)S(1)}, f32[2,104,512]{2,1,0:T(8,128)S(1)}) fusion(f32[2,104,512]{2,1,0:T(8,128)S(1)} %pad.57, f32[2]{0:T(128)S(1)} %copy-done.19, f32[104]{0:T(128)S(1)} %fusion.114, f32[2]{0:T(128)S(1)} %copy-done.20, f32[104,512]{1,0:T(8,128)S(1)} %bitcast.83, f32[104,512]{1,0:T(8,128)S(1)} %get-tuple-element.24, ...), kind=kLoop, calls=%fused_computation.124 | loop fusion | flops 2236416 | bytes 2769744 | tf_op jit(solution)/shard_map/mul | solution.py:58
  55.7 1.7 %collective-permute-start.4 = (f32[2,20,512]{2,1,0:T(8,128)S(1)}, f32[2,20,512]{2,1,0:T(8,128)S(1)}, u32[]{:S(2)}, u32[]{:S(2)}) collective-permute-start(f32[2,20,512]{2,1,0:T(8,128)S(1)} %slice.314), channel_id=1, source_target_pairs={{0,1},{1,2},{2,3},{3,4},{4,5},{5,6},{6,7},{7,8},{8,9},{9,10},{10,1... | collective-permute-start | bytes 245768 | tf_op jit(solution)/shard_map/ppermute | solution.py:24
  59.9 3.5 %fusion.2 = f32[1,2,64,512]{3,0,2,1:T(1,128)S(1)} fusion(bf16[48,1,1,1]{0,1,3,2:T(2,128)(2,1)S(1)} %fusion.5, bf16[2,64,512,48]{2,1,0,3:T(8,128)(2,1)S(1)} %bitcast.77), kind=kOutput, calls=%fused_computation.2 | convolution fusion | flops 6291456 | bytes 6553696 | tf_op jit(solution)/shard_map/dot_general | solution.py:126
  63.6 5.0 %collective-permute-start.6 = (f32[2,1,512]{2,1,0:T(1,128)S(1)}, f32[2,1,512]{2,1,0:T(1,128)S(1)}, u32[]{:S(2)}, u32[]{:S(2)}) collective-permute-start(f32[2,1,512]{2,1,0:T(1,128)S(1)} %get-tuple-element.38), channel_id=1, source_target_pairs={{0,1},{1,2},{2,3},{3,4},{4,5},{5,6},{6,7},{7,8},{8,9},{9,10},{10,1... | collective-permute-start | bytes 12296 | tf_op jit(solution)/shard_map/ppermute | solution.py:24
  70.0 2.6 %collective-permute-done.7 = f32[2,1,512]{2,1,0:T(1,128)S(1)} collective-permute-done((f32[2,1,512]{2,1,0:T(1,128)S(1)}, f32[2,1,512]{2,1,0:T(1,128)S(1)}, u32[]{:S(2)}, u32[]{:S(2)}) %collective-permute-start.7) | collective-permute-done | bytes 4128 | tf_op jit(solution)/shard_map/ppermute | solution.py:26
  72.6 1.8 %multiply_reduce_fusion.4 = (f32[]{:T(128)}, f32[]{:T(128)}, f32[2,64,512]{2,1,0:T(8,128)S(1)}) fusion(f32[2,64,512]{2,1,0:T(8,128)S(1)} %copy-done.2, f32[2,64,512]{2,1,0:T(8,128)} %param.28, f32[2,64,512]{2,1,0:T(8,128)S(1)} %bitcast_add_fusion, f32[2]{0:T(128)S(1)} %copy-done.19, f32[2,1,512]{2,1,0:T(1,128)S(1)} %collective-permute-done.7, ...), kind=kLoop, calls=%fused_computation.170 | loop fusion | flops 1245182 | bytes 1318936 | tf_op jit(solution)/shard_map/reduce_sum | solution.py:143
  75.2 4.7 %convolution_bitcast_fusion = f32[48,2]{0,1:T(2,128)S(1)} fusion(bf16[48,65536]{1,0:T(8,128)(2,1)} %bitcast.82, bf16[65536,1]{0,1:T(2,128)(2,1)S(1)} %get-tuple-element.35, bf16[65536,1]{0,1:T(2,128)(2,1)S(1)} %get-tuple-element.34), kind=kOutput, calls=%fused_computation.4 | convolution fusion | flops 13107200 | bytes 6553984 | tf_op jit(solution)/shard_map/dot_general | solution.py:90
  81.8 6.7 %all-to-all-start.1 = ((f32[16,1,50]{2,1,0:T(1,128)}), f32[16,1,50]{2,1,0:T(1,128)S(1)}, u32[]{:S(2)}, u32[]{:S(2)}) async-start(f32[16,1,50]{2,1,0:T(1,128)} %broadcast_in_dim.16), calls=%async_computation.1 | async-start | bytes 16384 | tf_op jit(solution)/shard_map/all_to_all | solution.py:83
  88.5 1.7 %fusion.122 = (f32[2,20,512]{2,1,0:T(8,128)}, f32[2,20,512]{2,1,0:T(8,128)}) fusion(f32[2,64,512]{2,1,0:T(8,128)} %copy-done.3), kind=kLoop, calls=%fused_computation.207 | loop fusion | bytes 327680 | tf_op jit(solution)/shard_map/slice | solution.py:21
  90.2 2.9 %collective-permute-start.8 = (f32[2,20,512]{2,1,0:T(8,128)}, f32[2,20,512]{2,1,0:T(8,128)}, u32[]{:S(2)}, u32[]{:S(2)}) collective-permute-start(f32[2,20,512]{2,1,0:T(8,128)} %get-tuple-element.36), channel_id=1, source_target_pairs={{0,1},{1,2},{2,3},{3,4},{4,5},{5,6},{6,7},{7,8},{8,9},{9,10},{10,1... | collective-permute-start | bytes 245768 | tf_op jit(solution)/shard_map/ppermute | solution.py:24
  97.2 2.0 %divide_multiply_fusion = f32[2,104,512]{2,1,0:T(8,128)S(1)} fusion(f32[2,104,512]{2,1,0:T(8,128)S(1)} %get-tuple-element.23, f32[2,104,512]{2,1,0:T(8,128)} %copy-done.7, f32[2]{0:T(128)S(1)} %copy-done.19, f32[104]{0:T(128)S(1)} %fusion.114, f32[2]{0:T(128)S(1)} %copy-done.20, f32[104,512]{1,0:T(8,128)S(1)} %bitcast.87, ...), kind=kLoop, calls=%fused_computation.122 | loop fusion | flops 1916928 | bytes 2130768 | tf_op jit(solution)/shard_map/mul | solution.py:58
  99.2 1.5 fusion.87
  100.7 1.5 fusion.86
  103.7 5.2 %collective-permute-start.10 = (f32[2,20,512]{2,1,0:T(8,128)S(1)}, f32[2,20,512]{2,1,0:T(8,128)S(1)}, u32[]{:S(2)}, u32[]{:S(2)}) collective-permute-start(f32[2,20,512]{2,1,0:T(8,128)S(1)} %slice.326), channel_id=1, source_target_pairs={{0,1},{1,2},{2,3},{3,4},{4,5},{5,6},{6,7},{7,8},{8,9},{9,10},{10,1... | collective-permute-start | bytes 245768 | tf_op jit(solution)/shard_map/ppermute | solution.py:24
  110.6 1.6 %collective-permute-start.11 = (f32[2,20,512]{2,1,0:T(8,128)}, f32[2,20,512]{2,1,0:T(8,128)}, u32[]{:S(2)}, u32[]{:S(2)}) collective-permute-start(f32[2,20,512]{2,1,0:T(8,128)} %get-tuple-element.27), channel_id=1, source_target_pairs={{1,0},{2,1},{3,2},{4,3},{5,4},{6,5},{7,6},{8,7},{9,8},{10,9},{11,1... | collective-permute-start | bytes 245768 | tf_op jit(solution)/shard_map/ppermute | solution.py:26
  112.2 4.2 %fusion = f32[1,2,64,512]{3,0,2,1:T(1,128)} fusion(bf16[48,1,1,1]{0,1,3,2:T(2,128)(2,1)S(1)} %fusion.7, bf16[2,64,512,48]{2,1,0,3:T(8,128)(2,1)S(1)} %bitcast.80), kind=kOutput, calls=%fused_computation | convolution fusion | flops 6291456 | bytes 6553696 | tf_op jit(solution)/shard_map/dot_general | solution.py:126
  119.3 3.2 %collective-permute-start.12 = (f32[2,1,512]{2,1,0:T(1,128)S(1)}, f32[2,1,512]{2,1,0:T(1,128)S(1)}, u32[]{:S(2)}, u32[]{:S(2)}) collective-permute-start(f32[2,1,512]{2,1,0:T(1,128)S(1)} %get-tuple-element.32), channel_id=1, source_target_pairs={{0,1},{1,2},{2,3},{3,4},{4,5},{5,6},{6,7},{7,8},{8,9},{9,10},{10,1... | collective-permute-start | bytes 12296 | tf_op jit(solution)/shard_map/ppermute | solution.py:24
  123.8 3.7 %collective-permute-done.13 = f32[2,1,512]{2,1,0:T(1,128)S(1)} collective-permute-done((f32[2,1,512]{2,1,0:T(1,128)S(1)}, f32[2,1,512]{2,1,0:T(1,128)S(1)}, u32[]{:S(2)}, u32[]{:S(2)}) %collective-permute-start.13) | collective-permute-done | bytes 4128 | tf_op jit(solution)/shard_map/ppermute | solution.py:26
  127.5 1.9 %multiply_reduce_fusion.2 = (f32[]{:T(128)}, f32[]{:T(128)}, f32[]{:T(128)}) fusion(f32[2,64,512]{2,1,0:T(8,128)S(1)} %copy-done.2, f32[2,64,512]{2,1,0:T(8,128)} %copy-done.3, f32[2,64,512]{2,1,0:T(8,128)} %param.28, f32[2,64,512]{2,1,0:T(8,128)S(1)} %fusion.113, f32[2]{0:T(128)S(1)} %copy-done.19, f32[2,1,512]{2,1,0:T(1,128)S(1)} %collective-permute-done.13, ...), kind=kLoop, calls=%fused_computation.168 | loop fusion | flops 1376253 | bytes 1318940 | tf_op jit(solution)/shard_map/reduce_sum | solution.py:154
  129.4 1.9 %pad_maximum_fusion.15 = f32[3]{0:T(128)S(1)} fusion(f32[1]{0:T(128)} %bitcast.25, f32[1]{0:T(128)} %bitcast.24, f32[1]{0:T(128)} %bitcast.23), kind=kLoop, calls=%fused_computation.197 | loop fusion | flops 6 | bytes 24 | tf_op jit(solution)/shard_map/stack | solution.py:154
  132.0 9.3 %all-to-all-start.2 = ((f32[16,1,3]{2,1,0:T(1,128)}), f32[16,1,3]{2,1,0:T(1,128)S(1)}, u32[]{:S(2)}, u32[]{:S(2)}) async-start(f32[16,1,3]{2,1,0:T(1,128)} %broadcast_in_dim.17), calls=%async_computation.2 | async-start | bytes 16384 | tf_op jit(solution)/shard_map/all_to_all | solution.py:83
  141.4 6.2 %all-to-all-done.2 = f32[16,1,3]{2,1,0:T(1,128)S(1)} async-done(((f32[16,1,3]{2,1,0:T(1,128)}), f32[16,1,3]{2,1,0:T(1,128)S(1)}, u32[]{:S(2)}, u32[]{:S(2)}) %all-to-all-start.2) | async-done | bytes 224 | tf_op jit(solution)/shard_map/all_to_all | solution.py:83
  (124 shorter events, 32.8 us)
Async XLA Ops:
  0.6 56.8 %copy-start = (f32[48,768]{1,0:T(8,128)S(1)}, f32[48,768]{1,0:T(8,128)}, u32[]{:S(2)}) copy-start(f32[48,768]{1,0:T(8,128)} %param.31) | copy-start | bytes 442372
  2.3 45.9 %collective-permute-start = (f32[2,20,512]{2,1,0:T(8,128)}, f32[2,20,512]{2,1,0:T(8,128)S(1)}, u32[]{:S(2)}, u32[]{:S(2)}) collective-permute-start(f32[2,20,512]{2,1,0:T(8,128)} %get-tuple-element.42), channel_id=1, source_target_pairs={{0,1},{1,2},{2,3},{3,4},{4,5},{5,6},{6,7},{7,8},{8,9},{9,10},{10,1... | collective-permute-start | bytes 245768 | tf_op jit(solution)/shard_map/ppermute | solution.py:24
  4.7 43.5 %collective-permute-start.1 = (f32[2,20,512]{2,1,0:T(8,128)}, f32[2,20,512]{2,1,0:T(8,128)}, u32[]{:S(2)}, u32[]{:S(2)}) collective-permute-start(f32[2,20,512]{2,1,0:T(8,128)} %get-tuple-element.43), channel_id=1, source_target_pairs={{1,0},{2,1},{3,2},{4,3},{5,4},{6,5},{7,6},{8,7},{9,8},{10,9},{11,1... | collective-permute-start | bytes 245768 | tf_op jit(solution)/shard_map/ppermute | solution.py:26
  7.7 39.0 %collective-permute-start.2 = (f32[3,20,512]{2,1,0:T(8,128)}, f32[3,20,512]{2,1,0:T(8,128)S(1)}, u32[]{:S(2)}, u32[]{:S(2)}) collective-permute-start(f32[3,20,512]{2,1,0:T(8,128)} %get-tuple-element.30), channel_id=1, source_target_pairs={{0,1},{1,2},{2,3},{3,4},{4,5},{5,6},{6,7},{7,8},{8,9},{9,10},{10,1... | collective-permute-start | bytes 368648 | tf_op jit(solution)/shard_map/ppermute | solution.py:24
  12.8 34.5 %collective-permute-start.3 = (f32[3,20,512]{2,1,0:T(8,128)}, f32[3,20,512]{2,1,0:T(8,128)}, u32[]{:S(2)}, u32[]{:S(2)}) collective-permute-start(f32[3,20,512]{2,1,0:T(8,128)} %get-tuple-element.31), channel_id=1, source_target_pairs={{1,0},{2,1},{3,2},{4,3},{5,4},{6,5},{7,6},{8,7},{9,8},{10,9},{11,1... | collective-permute-start | bytes 368648 | tf_op jit(solution)/shard_map/ppermute | solution.py:26
  23.9 14.9 %copy-start.21 = (s32[16]{0:T(128)S(1)}, s32[16]{0:T(128)}, u32[]{:S(2)}) copy-start(s32[16]{0:T(128)} %param.29) | copy-start | bytes 196
  23.9 23.5 %copy-start.5 = (f32[2,64,512]{2,1,0:T(8,128)S(1)}, f32[2,64,512]{2,1,0:T(8,128)}, u32[]{:S(2)}) copy-start(f32[2,64,512]{2,1,0:T(8,128)} %param.28) | copy-start | bytes 786436
  23.9 23.5 %copy-start.6 = (f32[64,512]{1,0:T(8,128)S(1)}, f32[64,512]{1,0:T(8,128)}, u32[]{:S(2)}) copy-start(f32[64,512]{1,0:T(8,128)} %param.27) | copy-start | bytes 393220
  23.9 25.8 %copy-start.2 = (f32[2,64,512]{2,1,0:T(8,128)S(1)}, f32[2,64,512]{2,1,0:T(8,128)}, u32[]{:S(2)}) copy-start(f32[2,64,512]{2,1,0:T(8,128)} %param.26) | copy-start | bytes 786436
  23.9 25.8 %copy-start.19 = (f32[2]{0:T(128)S(1)}, f32[2]{0:T(128)}, u32[]{:S(2)}) copy-start(f32[2]{0:T(128)} %constant.50.clone) | copy-start | bytes 28
  23.9 25.8 %copy-start.20 = (f32[2]{0:T(128)S(1)}, f32[2]{0:T(128)}, u32[]{:S(2)}) copy-start(f32[2]{0:T(128)} %constant.49.clone) | copy-start | bytes 28
  26.5 33.4 %slice-start = ((s8[6291456]{0:T(1024)(128)(4,1)}), s8[2097152]{0:T(1024)(128)(4,1)S(1)}, s32[]{:S(2)}) async-start(s8[6291456]{0:T(1024)(128)(4,1)} %bitcast.75), calls=%async_computation.3 | async-start | bytes 4194304
  29.5 15.7 %all-to-all-start = ((f32[16,1,49]{2,1,0:T(1,128)}), f32[16,1,49]{2,1,0:T(1,128)S(1)}, u32[]{:S(2)}, u32[]{:S(2)}) async-start(f32[16,1,49]{2,1,0:T(1,128)} %broadcast_in_dim.13), calls=%async_computation | async-start | bytes 16384 | tf_op jit(solution)/shard_map/all_to_all | solution.py:83
  49.7 10.2 %slice-start.1 = ((s8[6291456]{0:T(1024)(128)(4,1)}), s8[4194304]{0:T(1024)(128)(4,1)S(1)}, s32[]{:S(2)}) async-start(s8[6291456]{0:T(1024)(128)(4,1)} %bitcast.75), calls=%async_computation.4 | async-start | bytes 8388608
  55.7 2.6 %collective-permute-start.4 = (f32[2,20,512]{2,1,0:T(8,128)S(1)}, f32[2,20,512]{2,1,0:T(8,128)S(1)}, u32[]{:S(2)}, u32[]{:S(2)}) collective-permute-start(f32[2,20,512]{2,1,0:T(8,128)S(1)} %slice.314), channel_id=1, source_target_pairs={{0,1},{1,2},{2,3},{3,4},{4,5},{5,6},{6,7},{7,8},{8,9},{9,10},{10,1... | collective-permute-start | bytes 245768 | tf_op jit(solution)/shard_map/ppermute | solution.py:24
  58.4 11.5 %copy-start.17 = (f32[2,20,512]{2,1,0:T(8,128)}, f32[2,20,512]{2,1,0:T(8,128)S(1)}, u32[]{:S(2)}) copy-start(f32[2,20,512]{2,1,0:T(8,128)S(1)} %get-tuple-element.28) | copy-start | bytes 245764
  58.4 5.0 %collective-permute-start.5 = (f32[2,20,512]{2,1,0:T(8,128)S(1)}, f32[2,20,512]{2,1,0:T(8,128)S(1)}, u32[]{:S(2)}, u32[]{:S(2)}) collective-permute-start(f32[2,20,512]{2,1,0:T(8,128)S(1)} %get-tuple-element.29), channel_id=1, source_target_pairs={{1,0},{2,1},{3,2},{4,3},{5,4},{6,5},{7,6},{8,7},{9,8},{10,9},{11,1... | collective-permute-start | bytes 245768 | tf_op jit(solution)/shard_map/ppermute | solution.py:26
  63.5 11.5 %copy-start.8 = (f32[2,64,512]{2,1,0:T(8,128)}, f32[2,64,512]{2,1,0:T(8,128)S(1)}, u32[]{:S(2)}) copy-start(f32[2,64,512]{2,1,0:T(8,128)S(1)} %bitcast_add_fusion) | copy-start | bytes 786436
  63.6 6.4 %collective-permute-start.6 = (f32[2,1,512]{2,1,0:T(1,128)S(1)}, f32[2,1,512]{2,1,0:T(1,128)S(1)}, u32[]{:S(2)}, u32[]{:S(2)}) collective-permute-start(f32[2,1,512]{2,1,0:T(1,128)S(1)} %get-tuple-element.38), channel_id=1, source_target_pairs={{0,1},{1,2},{2,3},{3,4},{4,5},{5,6},{6,7},{7,8},{8,9},{9,10},{10,1... | collective-permute-start | bytes 12296 | tf_op jit(solution)/shard_map/ppermute | solution.py:24
  68.6 4.0 %collective-permute-start.7 = (f32[2,1,512]{2,1,0:T(1,128)S(1)}, f32[2,1,512]{2,1,0:T(1,128)S(1)}, u32[]{:S(2)}, u32[]{:S(2)}) collective-permute-start(f32[2,1,512]{2,1,0:T(1,128)S(1)} %get-tuple-element.39), channel_id=1, source_target_pairs={{1,0},{2,1},{3,2},{4,3},{5,4},{6,5},{7,6},{8,7},{9,8},{10,9},{11,1... | collective-permute-start | bytes 12296 | tf_op jit(solution)/shard_map/ppermute | solution.py:26
  75.2 37.0 %slice-start.2 = ((s8[6291456]{0:T(1024)(128)(4,1)}), s8[2097152]{0:T(1024)(128)(4,1)S(1)}, s32[]{:S(2)}) async-start(s8[6291456]{0:T(1024)(128)(4,1)} %bitcast.78), calls=%async_computation.5 | async-start | bytes 4194304
  81.8 13.1 %all-to-all-start.1 = ((f32[16,1,50]{2,1,0:T(1,128)}), f32[16,1,50]{2,1,0:T(1,128)S(1)}, u32[]{:S(2)}, u32[]{:S(2)}) async-start(f32[16,1,50]{2,1,0:T(1,128)} %broadcast_in_dim.16), calls=%async_computation.1 | async-start | bytes 16384 | tf_op jit(solution)/shard_map/all_to_all | solution.py:83
  90.2 7.0 %collective-permute-start.8 = (f32[2,20,512]{2,1,0:T(8,128)}, f32[2,20,512]{2,1,0:T(8,128)}, u32[]{:S(2)}, u32[]{:S(2)}) collective-permute-start(f32[2,20,512]{2,1,0:T(8,128)} %get-tuple-element.36), channel_id=1, source_target_pairs={{0,1},{1,2},{2,3},{3,4},{4,5},{5,6},{6,7},{7,8},{8,9},{9,10},{10,1... | collective-permute-start | bytes 245768 | tf_op jit(solution)/shard_map/ppermute | solution.py:24
  93.1 4.1 %collective-permute-start.9 = (f32[2,20,512]{2,1,0:T(8,128)}, f32[2,20,512]{2,1,0:T(8,128)}, u32[]{:S(2)}, u32[]{:S(2)}) collective-permute-start(f32[2,20,512]{2,1,0:T(8,128)} %get-tuple-element.37), channel_id=1, source_target_pairs={{1,0},{2,1},{3,2},{4,3},{5,4},{6,5},{7,6},{8,7},{9,8},{10,9},{11,1... | collective-permute-start | bytes 245768 | tf_op jit(solution)/shard_map/ppermute | solution.py:26
  97.2 15.1 %slice-start.3 = ((s8[6291456]{0:T(1024)(128)(4,1)}), s8[4194304]{0:T(1024)(128)(4,1)S(1)}, s32[]{:S(2)}) async-start(s8[6291456]{0:T(1024)(128)(4,1)} %bitcast.78), calls=%async_computation.6 | async-start | bytes 8388608
  103.7 46.8 %copy-start.9 = (f32[2,64,512]{2,1,0:T(8,128)S(1)}, f32[2,64,512]{2,1,0:T(8,128)}, u32[]{:S(2)}) copy-start(f32[2,64,512]{2,1,0:T(8,128)} %copy-done.8) | copy-start | bytes 786436
  103.7 6.1 %collective-permute-start.10 = (f32[2,20,512]{2,1,0:T(8,128)S(1)}, f32[2,20,512]{2,1,0:T(8,128)S(1)}, u32[]{:S(2)}, u32[]{:S(2)}) collective-permute-start(f32[2,20,512]{2,1,0:T(8,128)S(1)} %slice.326), channel_id=1, source_target_pairs={{0,1},{1,2},{2,3},{3,4},{4,5},{5,6},{6,7},{7,8},{8,9},{9,10},{10,1... | collective-permute-start | bytes 245768 | tf_op jit(solution)/shard_map/ppermute | solution.py:24
  110.6 7.5 %slice-start.4 = ((f32[2,104,512]{2,1,0:T(8,128)}), f32[2,24,512]{2,1,0:T(8,128)S(1)}, s32[]{:S(2)}) async-start(f32[2,104,512]{2,1,0:T(8,128)} %copy-done.10), calls=%async_computation.7 | async-start | bytes 196608 | tf_op jit(solution)/shard_map/slice | solution.py:105
  110.6 6.5 %collective-permute-start.11 = (f32[2,20,512]{2,1,0:T(8,128)}, f32[2,20,512]{2,1,0:T(8,128)}, u32[]{:S(2)}, u32[]{:S(2)}) collective-permute-start(f32[2,20,512]{2,1,0:T(8,128)} %get-tuple-element.27), channel_id=1, source_target_pairs={{1,0},{2,1},{3,2},{4,3},{5,4},{6,5},{7,6},{8,7},{9,8},{10,9},{11,1... | collective-permute-start | bytes 245768 | tf_op jit(solution)/shard_map/ppermute | solution.py:26
  119.3 4.6 %collective-permute-start.12 = (f32[2,1,512]{2,1,0:T(1,128)S(1)}, f32[2,1,512]{2,1,0:T(1,128)S(1)}, u32[]{:S(2)}, u32[]{:S(2)}) collective-permute-start(f32[2,1,512]{2,1,0:T(1,128)S(1)} %get-tuple-element.32), channel_id=1, source_target_pairs={{0,1},{1,2},{2,3},{3,4},{4,5},{5,6},{6,7},{7,8},{8,9},{9,10},{10,1... | collective-permute-start | bytes 12296 | tf_op jit(solution)/shard_map/ppermute | solution.py:24
  122.5 5.0 %collective-permute-start.13 = (f32[2,1,512]{2,1,0:T(1,128)S(1)}, f32[2,1,512]{2,1,0:T(1,128)S(1)}, u32[]{:S(2)}, u32[]{:S(2)}) collective-permute-start(f32[2,1,512]{2,1,0:T(1,128)S(1)} %get-tuple-element.33), channel_id=1, source_target_pairs={{1,0},{2,1},{3,2},{4,3},{5,4},{6,5},{7,6},{8,7},{9,8},{10,9},{11,1... | collective-permute-start | bytes 12296 | tf_op jit(solution)/shard_map/ppermute | solution.py:26
  132.0 15.7 %all-to-all-start.2 = ((f32[16,1,3]{2,1,0:T(1,128)}), f32[16,1,3]{2,1,0:T(1,128)S(1)}, u32[]{:S(2)}, u32[]{:S(2)}) async-start(f32[16,1,3]{2,1,0:T(1,128)} %broadcast_in_dim.17), calls=%async_computation.2 | async-start | bytes 16384 | tf_op jit(solution)/shard_map/all_to_all | solution.py:83
  (12 other events, 43.2 us)

commit v2 on v1

v2 whole, which is shorter than its diff:
```python
import functools

import jax
import jax.numpy as jnp
from jax import lax
from jax.experimental import pallas as pl
from jax.experimental.pallas import tpu as pltpu
from jax.sharding import PartitionSpec as P

ROWS = 64
CELLS = 512
VECTORS = 48
HALO = 8
EXT = ROWS + 2 * HALO
STRIP = 32
CHUNK = 16
CHUNKS = 2 * ROWS // CHUNK
LANES = 128
SLOTS = 56
EDGE_AT = 5 * HALO
INVERSE_AT = EDGE_AT + 2 * VECTORS
SWEEPS = 4
RELAX = 0.7
ROW_FACTOR = (1.0, 4.0)
CELL_FACTOR = (4.0, 1.0)

VMEM = pl.BlockSpec(memory_space=pltpu.VMEM)
SMEM = pl.BlockSpec(memory_space=pltpu.SMEM)
ANY = pl.BlockSpec(memory_space=pl.ANY)


def packed_rows(columns):
    return INVERSE_AT + VECTORS * (columns // 512) + (VECTORS // 2) * (columns % 512 // 256)


def cell_sum(field):
    column = lax.broadcasted_iota(jnp.int32, field.shape, 1)
    left = jnp.where(column == 0, 0.0, pltpu.roll(field, 1, 1))
    right = jnp.where(column == CELLS - 1, 0.0, pltpu.roll(field, CELLS - 1, 1))
    return left + right


def row_sum(field):
    count = field.shape[0]
    return pltpu.roll(field, 1, 0) + pltpu.roll(field, count - 1, 0)


def neighbours(field, component):
    rows, cells = row_sum(field), cell_sum(field)
    if component == 0:
        return rows + CELL_FACTOR[0] * cells
    return ROW_FACTOR[1] * rows + cells


def apply_operator(extended, viscosity, coupling):
    inner = slice(HALO, HALO + ROWS)
    images = []
    for a in range(2):
        around = neighbours(extended[a], a)[inner]
        diagonal = 10.0 * viscosity + jnp.abs(coupling[a]) + 0.05
        images.append(
            diagonal * extended[a][inner]
            - viscosity * around
            + coupling[a] * extended[1 - a][inner]
        )
    return images


def basis_copies(basis_ref, held, sems):
    return [
        pltpu.make_async_copy(
            basis_ref.at[:, i // 4, pl.ds(CHUNK * (i % 4), CHUNK), :], held.at[i], sems.at[i]
        )
        for i in range(CHUNKS)
    ]


def restrict_chunk(i, held, field, sums):
    a = i // 4
    start = pl.multiple_of((i % 4) * CHUNK, CHUNK)
    parts = [field[a, pl.ds(start, CHUNK), pl.ds(LANES * c, LANES)] for c in range(4)]
    for k in range(VECTORS):
        total = None
        for c in range(4):
            term = held[i, k, :, pl.ds(LANES * c, LANES)].astype(jnp.float32) * parts[c]
            total = term if total is None else total + term
        sums[8 * k : 8 * k + 8, :] += total[:8] + total[8:]


def fold(field):
    total = None
    for part in field:
        for r in range(0, part.shape[0], 8):
            for c in range(0, part.shape[1], LANES):
                term = part[r : r + 8, c : c + LANES]
                total = term if total is None else total + term
    return total


def send_sums(sums, out_ref):
    pick_row = lax.broadcasted_iota(jnp.int32, (LANES, 8 * SLOTS), 0)
    pick_col = lax.broadcasted_iota(jnp.int32, (LANES, 8 * SLOTS), 1)
    pick = (pick_col // 8 == pick_row).astype(jnp.float32)
    by_slot = jnp.dot(
        pick, sums[...], precision=lax.Precision.HIGHEST, preferred_element_type=jnp.float32
    )
    row = lax.dot_general(
        jnp.ones((8, LANES), jnp.float32),
        by_slot,
        (((1,), (1,)), ((), ())),
        precision=lax.Precision.HIGHEST,
        preferred_element_type=jnp.float32,
    )
    out_ref[...] = jnp.broadcast_to(row[:1], out_ref.shape)


def start_kernel(
    rhs_ref, visc_ref, coup_ref, inverse_ref, basis_ref,
    sums_ref, up_ref, down_ref,
    held, sums, sems,
):
    copies = basis_copies(basis_ref, held, sems)
    for copy in copies:
        copy.start()
    columns = inverse_ref.shape[1]
    for out_ref, rows in ((up_ref, slice(ROWS - HALO, ROWS)), (down_ref, slice(0, HALO))):
        out_ref[0:HALO] = visc_ref[rows]
        for a in range(2):
            out_ref[HALO * (1 + a) : HALO * (2 + a)] = coup_ref[a, rows]
            out_ref[HALO * (3 + a) : HALO * (4 + a)] = rhs_ref[a, rows]
        at = INVERSE_AT
        for c in range(0, columns - 511, 512):
            out_ref[at : at + VECTORS] = inverse_ref[:, c : c + 512]
            at += VECTORS
        if columns % 512:
            half = VECTORS // 2
            out_ref[at : at + half, :256] = inverse_ref[:half, columns - 256 :]
            out_ref[at : at + half, 256:] = inverse_ref[half:, columns - 256 :]
    sums[...] = jnp.zeros_like(sums)
    sums[8 * VECTORS : 8 * VECTORS + 8] = fold([rhs_ref[a] * rhs_ref[a] for a in range(2)])
    for copy in copies:
        copy.wait()

    def body(i, carry):
        restrict_chunk(i, held, rhs_ref, sums)
        return carry

    lax.fori_loop(0, CHUNKS, body, 0)
    picker = lax.broadcasted_iota(jnp.int32, (VECTORS, CHUNK * VECTORS), 0) * CHUNK
    place = lax.broadcasted_iota(jnp.int32, (VECTORS, CHUNK * VECTORS), 1)
    for out_ref, block, row in ((up_ref, 3, CHUNK - 1), (down_ref, 0, 0)):
        pick = (place == picker + row).astype(jnp.float32).astype(jnp.bfloat16)
        for a in range(2):
            rows = held[4 * a + block].reshape(CHUNK * VECTORS, CELLS)
            at = EDGE_AT + VECTORS * a
            out_ref[at : at + VECTORS] = jnp.dot(pick, rows, preferred_element_type=jnp.float32)
    send_sums(sums, sums_ref)


def solve_kernel(count, margin_ref, own_refs, below_refs, above_refs, out_ref):
    rank = lax.axis_index("sub")
    lower = jnp.where(rank > 0, margin_ref[jnp.maximum(rank - 1, 0)], 0)
    upper = jnp.where(rank < count - 1, margin_ref[rank], 0)
    lower_f, upper_f = lower.astype(jnp.float32), upper.astype(jnp.float32)
    low_scale = 2.0 * jnp.maximum(lower_f, 1.0)
    high_scale = 2.0 * jnp.maximum(upper_f, 1.0)

    def masks(first, rows, side):
        place = lax.broadcasted_iota(jnp.int32, (rows, LANES), 0) + first
        place_f = place.astype(jnp.float32)
        rising = lambda base, scale: (place_f - base + 0.5) / scale
        falling = lambda base, scale: (base - place_f - 0.5) / scale
        if side == 0:
            live = (place >= -lower) & (place < ROWS + upper)
            weight = jnp.where(place < lower, rising(-lower_f, low_scale), 1.0)
            weight = jnp.where(
                place >= ROWS - upper, falling(ROWS + upper_f, high_scale), weight
            )
        elif side < 0:
            live = place < lower
            weight = jnp.where(place >= -lower, falling(lower_f, low_scale), 1.0)
        else:
            live = place >= ROWS - upper
            weight = jnp.where(place < ROWS + upper, rising(ROWS - upper_f, high_scale), 1.0)
        wide = lambda x: jnp.concatenate([x] * (CELLS // LANES), 1)
        return wide(live.astype(jnp.float32)), wide(weight)

    def stack(below, own, above):
        return jnp.concatenate([below, own, above], 0)

    def triple(field):
        return jnp.concatenate([field, field[:STRIP], field[EXT - STRIP :]], 0)

    viscosity = stack(below_refs[0][...], own_refs[0][...], above_refs[0][...])
    blocks = [masks(-HALO, EXT, 0), masks(-HALO, STRIP, -1), masks(ROWS + HALO - STRIP, STRIP, 1)]
    live = jnp.concatenate([block[0] for block in blocks], 0)
    first, across, other = [], [], []
    for a in range(2):
        coupling = stack(below_refs[1][a], own_refs[1][a], above_refs[1][a])
        field = stack(below_refs[2][a], own_refs[2][a], above_refs[2][a])
        scale = RELAX / (10.0 * viscosity + jnp.abs(coupling) + 0.05)
        first.append(live * triple(scale * field))
        across.append(live * triple(scale * viscosity))
        other.append(live * triple(scale * coupling))
    solved = list(first)
    for _ in range(SWEEPS - 1):
        solved = [
            (1.0 - RELAX) * solved[a]
            + first[a]
            + across[a] * neighbours(solved[a], a)
            - other[a] * solved[1 - a]
            for a in range(2)
        ]
    for a in range(2):
        shares = solved[a] * jnp.concatenate([block[1] for block in blocks], 0)
        out_ref[a] = shares[:EXT]
        out_ref[a, :STRIP] += shares[EXT : EXT + STRIP]
        out_ref[a, EXT - STRIP :] += shares[EXT + STRIP :]


class Part:
    def __init__(self, ref, at, stacked):
        self.ref, self.at, self.stacked = ref, at, stacked

    def __getitem__(self, index):
        at = self.at + (HALO * index if self.stacked else 0)
        return self.ref[at : at + HALO, :]


def packed_fields(ref):
    return (Part(ref, 0, False), Part(ref, HALO, True), Part(ref, 3 * HALO, True))


def first_solve_kernel(count, margin_ref, visc_ref, coup_ref, rhs_ref, low_ref, high_ref, out_ref):
    solve_kernel(
        count,
        margin_ref,
        (visc_ref, coup_ref, rhs_ref),
        packed_fields(low_ref),
        packed_fields(high_ref),
        out_ref,
    )


def second_solve_kernel(
    count, margin_ref, visc_ref, coup_ref, image_ref, low_ref, high_ref,
    low_image_ref, high_image_ref, out_ref,
):
    solve_kernel(
        count,
        margin_ref,
        (visc_ref, coup_ref, image_ref),
        packed_fields(low_ref)[:2] + (low_image_ref,),
        packed_fields(high_ref)[:2] + (high_image_ref,),
        out_ref,
    )


def line_up(residuals):
    devices = residuals.shape[0]
    lane = lax.broadcasted_iota(jnp.int32, (1, LANES), 1)
    tiles = [jnp.zeros((1, LANES), jnp.float32) for _ in range(devices * VECTORS // LANES)]
    for t in range(devices):
        tile, offset = divmod(VECTORS * t, LANES)
        row = jnp.where(lane < VECTORS, residuals[t : t + 1], 0.0)
        if offset:
            row = pltpu.roll(row, offset, 1)
        if offset + VECTORS <= LANES:
            tiles[tile] = tiles[tile] + row
        else:
            tiles[tile] = tiles[tile] + jnp.where(lane >= offset, row, 0.0)
            tiles[tile + 1] = tiles[tile + 1] + jnp.where(lane < offset, row, 0.0)
    return jnp.concatenate(tiles, 1)


def rounded(column):
    return column.astype(jnp.bfloat16).astype(jnp.float32)


def lift(inverse_ref, residual):
    return rounded(jnp.sum(inverse_ref[...] * residual, 1, keepdims=True))


def lift_packed(ref, residual):
    columns = residual.shape[1]
    at, total = INVERSE_AT, None
    for c in range(0, columns - 511, 512):
        term = jnp.sum(ref[at : at + VECTORS] * residual[:, c : c + 512], 1, keepdims=True)
        total = term if total is None else total + term
        at += VECTORS
    if columns % 512:
        half = VECTORS // 2
        last = residual[:, columns - 256 :]
        term = jnp.concatenate(
            [
                jnp.sum(ref[at : at + half, :256] * last, 1, keepdims=True),
                jnp.sum(ref[at : at + half, 256:] * last, 1, keepdims=True),
            ],
            0,
        )
        total = term if total is None else total + term
    return rounded(total)


def edge_values(ref, lifted):
    return [
        jnp.sum(ref[EDGE_AT + VECTORS * a : EDGE_AT + VECTORS * (a + 1)] * lifted, 0, keepdims=True)
        for a in range(2)
    ]


def spread(lifted):
    shape = (VECTORS, CHUNK * VECTORS)
    owner = lax.broadcasted_iota(jnp.int32, shape, 1) // CHUNK
    row = lax.broadcasted_iota(jnp.int32, shape, 0)
    line = jnp.sum(jnp.where(owner == row, lifted, 0.0), 0, keepdims=True)
    shape = (CHUNK, CHUNK * VECTORS)
    place = lax.broadcasted_iota(jnp.int32, shape, 1) % CHUNK
    row = lax.broadcasted_iota(jnp.int32, shape, 0)
    return jnp.where(place == row, line, 0.0).astype(jnp.bfloat16)


def prolong(residual, inverse_ref, low_ref, high_ref, smooth, held, copies, extended):
    low_edge = edge_values(low_ref, lift_packed(low_ref, residual))
    high_edge = edge_values(high_ref, lift_packed(high_ref, residual))
    place = lax.broadcasted_iota(jnp.int32, (HALO, CELLS), 0)
    for a in range(2):
        rows = slice(0, HALO)
        extended[a, rows] = smooth(a, rows) + jnp.where(place == HALO - 1, low_edge[a], 0.0)
        rows = slice(EXT - HALO, EXT)
        extended[a, rows] = smooth(a, rows) + jnp.where(place == 0, high_edge[a], 0.0)
    matrix = spread(lift(inverse_ref, residual))
    for i in range(CHUNKS):
        a, start = i // 4, HALO + CHUNK * (i % 4)
        rows = slice(start, start + CHUNK)
        copies[i].wait()
        coarse = jnp.dot(
            matrix,
            held[i].reshape(CHUNK * VECTORS, CELLS),
            preferred_element_type=jnp.float32,
        )
        extended[a, rows] = smooth(a, rows) + coarse


def lane_total(received, lane):
    return jnp.sum(received[:, lane : lane + 1], 0, keepdims=True)


def first_turn_kernel(
    sums_ref, inverse_ref, low_ref, high_ref, basis_ref, smooth_ref, rhs_ref, visc_ref, coup_ref,
    direction_ref, image_ref, head_ref, tail_ref, next_ref,
    held, extended, sums, sems,
):
    copies = basis_copies(basis_ref, held, sems)
    for copy in copies:
        copy.start()
    received = sums_ref[...]
    over_beta = 1.0 / jnp.sqrt(lane_total(received, VECTORS))
    residual = line_up(received) * over_beta
    prolong(
        residual,
        inverse_ref,
        low_ref,
        high_ref,
        lambda a, rows: smooth_ref[a, rows] * over_beta,
        held,
        copies,
        extended,
    )
    images = apply_operator(
        [extended[a] for a in range(2)], visc_ref[...], [coup_ref[a] for a in range(2)]
    )
    for a in range(2):
        direction_ref[a] = extended[a, HALO : HALO + ROWS]
        image_ref[a] = images[a]
        head_ref[a] = images[a][:HALO]
        tail_ref[a] = images[a][ROWS - HALO :]
    sums[...] = jnp.zeros_like(sums)
    at = 8 * VECTORS
    sums[at : at + 8] = fold([rhs_ref[a] * images[a] for a in range(2)])
    sums[at + 8 : at + 16] = fold([images[a] * images[a] for a in range(2)])

    def body(i, carry):
        restrict_chunk(i, held, image_ref, sums)
        return carry

    lax.fori_loop(0, CHUNKS, body, 0)
    send_sums(sums, next_ref)


def first_column(first, second):
    beta = jnp.sqrt(lane_total(first, VECTORS))
    h_00 = lane_total(second, VECTORS) / beta
    h_10 = jnp.sqrt(lane_total(second, VECTORS + 1) - h_00 * h_00)
    return beta, h_00, h_10


def second_turn_kernel(
    first_ref, second_ref, inverse_ref, low_ref, high_ref, basis_ref, smooth_ref, image_smooth_ref,
    rhs_ref, image_ref, visc_ref, coup_ref,
    direction_ref, next_ref,
    held, extended, sums, sems,
):
    copies = basis_copies(basis_ref, held, sems)
    for copy in copies:
        copy.start()
    first, second = first_ref[...], second_ref[...]
    beta, h_00, h_10 = first_column(first, second)
    ratio = h_00 / beta
    over = 1.0 / h_10
    residual = (line_up(second) - ratio * line_up(first)) * over
    prolong(
        residual,
        inverse_ref,
        low_ref,
        high_ref,
        lambda a, rows: (image_smooth_ref[a, rows] - ratio * smooth_ref[a, rows]) * over,
        held,
        copies,
        extended,
    )
    images = apply_operator(
        [extended[a] for a in range(2)], visc_ref[...], [coup_ref[a] for a in range(2)]
    )
    sums[...] = jnp.zeros_like(sums)
    sums[0:8] = fold([rhs_ref[a] * images[a] for a in range(2)])
    sums[8:16] = fold([image_ref[a] * images[a] for a in range(2)])
    sums[16:24] = fold([images[a] * images[a] for a in range(2)])
    for a in range(2):
        direction_ref[a] = extended[a, HALO : HALO + ROWS]
    send_sums(sums, next_ref)


def finish_kernel(
    first_ref, second_ref, third_ref, first_direction_ref, second_direction_ref,
    solution_ref, hessenberg_ref,
):
    third = third_ref[...]
    beta, h_00, h_10 = first_column(first_ref[...], second_ref[...])
    h_01 = lane_total(third, 0) / beta
    h_11 = (lane_total(third, 1) - h_00 * h_01) / h_10
    h_21 = jnp.sqrt(lane_total(third, 2) - h_01 * h_01 - h_11 * h_11)
    n_00 = h_00 * h_00 + h_10 * h_10
    n_10 = h_00 * h_01 + h_10 * h_11
    n_11 = h_01 * h_01 + h_11 * h_11 + h_21 * h_21
    l_00 = jnp.sqrt(n_00)
    l_10 = n_10 / l_00
    l_11 = jnp.sqrt(n_11 - l_10 * l_10)
    f_0 = beta * h_00 / l_00
    f_1 = (beta * h_01 - l_10 * f_0) / l_11
    c_1 = f_1 / l_11
    c_0 = (f_0 - l_10 * c_1) / l_00
    for a in range(2):
        solution_ref[a] = c_0 * first_direction_ref[a] + c_1 * second_direction_ref[a]
    shape = hessenberg_ref.shape
    row = lax.broadcasted_iota(jnp.int32, shape, 0)
    column = lax.broadcasted_iota(jnp.int32, shape, 1)
    entries = jnp.zeros(shape, jnp.float32)
    for i, j, value in ((0, 0, h_00), (0, 1, h_01), (1, 0, h_10), (1, 1, h_11), (2, 1, h_21)):
        entries = jnp.where((row == i) & (column == j), value, entries)
    hessenberg_ref[...] = entries


def call(kernel, name, in_specs, out_shapes, flops, scratch=()):
    outs = [jax.ShapeDtypeStruct(shape, jnp.float32) for shape in out_shapes]
    return pl.pallas_call(
        kernel,
        name=name,
        in_specs=in_specs,
        out_specs=[VMEM] * len(outs),
        out_shape=outs,
        scratch_shapes=scratch,
        compiler_params=pltpu.CompilerParams(vmem_limit_bytes=40 * 1024 * 1024),
        cost_estimate=pl.CostEstimate(flops=flops, bytes_accessed=4_000_000, transcendentals=0),
    )


def from_everyone(rows):
    return lax.all_to_all(rows, "sub", 0, 0, tiled=True)


def shift(up, down):
    count = lax.axis_size("sub")
    ends = count - 1
    from_below = lax.ppermute(up, "sub", [(i, i + 1) for i in range(ends)])
    from_above = lax.ppermute(down, "sub", [(i + 1, i) for i in range(ends)])
    return from_below, from_above


def on_device(rhs, viscosity, coupling, margin_rows, coarse_basis, coarse_inverse):
    count = lax.axis_size("sub")
    columns = coarse_inverse.shape[1]
    held = pltpu.VMEM((CHUNKS, VECTORS, CHUNK, CELLS), jnp.bfloat16)
    extended = pltpu.VMEM((2, EXT, CELLS), jnp.float32)
    sums = pltpu.VMEM((8 * SLOTS, LANES), jnp.float32)
    sems = pltpu.SemaphoreType.DMA((CHUNKS,))
    row, whole, edge = (count, LANES), (2, ROWS, CELLS), (2, HALO, CELLS)
    packed = (packed_rows(columns), CELLS)
    first, up, down = call(
        start_kernel, "start", [VMEM] * 4 + [ANY], [row, packed, packed], 10_000_000,
        [held, sums, sems],
    )(rhs, viscosity, coupling, coarse_inverse, coarse_basis)
    low, high = shift(up, down)
    first = from_everyone(first)
    (smooth,) = call(
        functools.partial(first_solve_kernel, count), "first_solve", [SMEM] + [VMEM] * 5,
        [(2, EXT, CELLS)], 10_000_000,
    )(margin_rows, viscosity, coupling, rhs, low, high)
    direction, image, head, tail, second = call(
        first_turn_kernel, "first_turn", [VMEM] * 4 + [ANY] + [VMEM] * 4,
        [whole, whole, edge, edge, row], 20_000_000, [held, extended, sums, sems],
    )(first, coarse_inverse, low, high, coarse_basis, smooth, rhs, viscosity, coupling)
    low_image, high_image = shift(tail, head)
    second = from_everyone(second)
    (image_smooth,) = call(
        functools.partial(second_solve_kernel, count), "second_solve", [SMEM] + [VMEM] * 7,
        [(2, EXT, CELLS)], 10_000_000,
    )(margin_rows, viscosity, coupling, image, low, high, low_image, high_image)
    second_direction, third = call(
        second_turn_kernel, "second_turn", [VMEM] * 5 + [ANY] + [VMEM] * 6, [whole, row],
        20_000_000, [held, extended, sums, sems],
    )(
        first, second, coarse_inverse, low, high, coarse_basis, smooth, image_smooth, rhs, image,
        viscosity, coupling,
    )
    third = from_everyone(third)
    return tuple(
        call(finish_kernel, "finish", [VMEM] * 5, [whole, (3, 2)], 1_000_000)(
            first, second, third, direction, second_direction
        )
    )


def solution(mesh):
    in_specs = (
        P(None, ("groups", "sub"), None),
        P(("groups", "sub"), None),
        P(None, ("groups", "sub"), None),
        P("groups"),
        P(None, None, ("groups", "sub"), None),
        P(("groups", "sub"), None),
    )
    out_specs = (P(None, ("groups", "sub"), None), P("groups", None))
    return jax.shard_map(
        on_device, mesh=mesh, in_specs=in_specs, out_specs=out_specs, check_vma=False
    )
```

time: 153 us -> 72 us (0.47)
  starting transfers between devices: 60.3 us -> 21.8 us
  other arithmetic: 30.2 us -> 0 us
  Pallas kernels: 0 us -> 18.4 us
  matrix products: 14.5 us -> 0 us
  waiting for transfers between devices: 18.8 us -> 8.77 us
  blocking collectives: 0 us -> 8.98 us
  local copies, waits for them, and re-layouts: 20.5 us -> 12.7 us
  between operations: 7.7 us -> 0.81 us
    ppermute x14 -> x4, starting transfers between devices: 35.1 us -> 6.66 us  [the longest x2 4.07 us: shift(): from_below = lax.ppermute(up, 'sub', [(i, i + 1) for i in range(ends)])]
    pallas_call x0 -> x6, Pallas kernels: none -> 18.4 us  [the longest x1 5.45 us: on_device(): call(first_turn_kernel, 'first_turn', [VMEM] * 4 + [ANY] + [VMEM] * 4, [w...]
    dot_general x6 -> x0, matrix products: 14.5 us -> none  [the longest x2 7.72 us: coarse_part(): jnp.dot(lifted, flat_basis, preferred_element_type=jnp.float32)]
    mul x10 -> x0, other arithmetic: 12.5 us -> none  [the longest x6 9.6 us: local_solve(): solved = live_grid * (solved + relax_factor * (residual - image) / diagonal)]
    all_to_all x3 -> x2, starting transfers between devices: 25.2 us -> 15.2 us  [from_everyone(): return lax.all_to_all(rows, 'sub', 0, 0, tiled=True)]
    all_to_all x0 -> x1, blocking collectives: none -> 8.98 us  [from_everyone(): return lax.all_to_all(rows, 'sub', 0, 0, tiled=True)]
    ppermute x14 -> x4, waiting for transfers between devices: 7.78 us -> 0.01 us  [the longest x2 0.01 us: shift(): from_above = lax.ppermute(down, 'sub', [(i + 1, i) for i in range(ends)])]
    reduce_sum x6 -> x0, other arithmetic: 6.86 us -> none  [the longest x1 1.93 us: on_device(): jnp.sum(rhs * w_1)]
  transfers between devices with their start and end apart: 17 -> 6, of which waited for: 7 -> 2; matrix products, arithmetic and copies ran while one was open for 18% -> 0% of each run, Pallas kernels for 0% -> 5%
where the time goes in v2:
time: 72 us; the launch traced here: 71.5 us
  starting transfers between devices  21.8 us (30%)
  Pallas kernels  18.4 us (26%)
  local copies, waits for them, and re-layouts  12.7 us (18%)
  blocking collectives  8.98 us (12%)
  waiting for transfers between devices  8.77 us (12%)
  between operations  0.81 us (1%)
    all_to_all x2, starting transfers between devices, from_everyone(): return lax.all_to_all(rows, 'sub', 0, 0, tiled=True)  15.2 us
    unnamed x24, local copies, waits for them, and re-layouts  12.1 us
    all_to_all x1, blocking collectives, from_everyone(): return lax.all_to_all(rows, 'sub', 0, 0, tiled=True)  8.98 us
    all_to_all x2, waiting for transfers between devices, from_everyone(): return lax.all_to_all(rows, 'sub', 0, 0, tiled=True)  8.76 us
    pallas_call x1, Pallas kernels, on_device(): call(first_turn_kernel, 'first_turn', [VMEM] * 4 + [ANY] + [VMEM] * 4, [w...  5.45 us
    ppermute x2, starting transfers between devices, shift(): from_below = lax.ppermute(up, 'sub', [(i, i + 1) for i in range(ends)])  4.07 us
    pallas_call x1, Pallas kernels, on_device(): call(start_kernel, 'start', [VMEM] * 4 + [ANY], [row, packed, packed], 10...  3.91 us
    pallas_call x1, Pallas kernels, on_device(): call(second_turn_kernel, 'second_turn', [VMEM] * 5 + [ANY] + [VMEM] * 6,...  3.83 us
  transfers between devices with their start and end apart: 6, of which 2 were waited for; matrix products, arithmetic and copies ran while one was open for 0% of the time, Pallas kernels for 5%

profile of v2, /device:TPU:0, one launch (start us, length us, event | category | flops | bytes accessed | tf_op | source)
XLA Modules:
  0.0 71.5 jit_solution(1870147206882158217)
XLA Ops:
  0.6 0.0 copy-start
  0.6 2.8 %copy-done = bf16[48,2,64,512]{3,2,1,0:T(8,128)(2,1)S(1)} copy-done((bf16[48,2,64,512]{3,2,1,0:T(8,128)(2,1)S(1)}, bf16[48,2,64,512]{3,2,1,0:T(8,128)(2,1)}, u32[]{:S(2)}) %copy-start) | copy-done | bytes 6291480
  3.4 0.9 %copy-done.3 = f32[2,64,512]{2,1,0:T(8,128)S(1)} copy-done((f32[2,64,512]{2,1,0:T(8,128)S(1)}, f32[2,64,512]{2,1,0:T(8,128)}, u32[]{:S(2)}) %copy-start.3) | copy-done | bytes 262168
  4.4 0.9 %copy-done.5 = f32[2,64,512]{2,1,0:T(8,128)S(1)} copy-done((f32[2,64,512]{2,1,0:T(8,128)S(1)}, f32[2,64,512]{2,1,0:T(8,128)}, u32[]{:S(2)}) %copy-start.5) | copy-done | bytes 262168
  5.3 0.9 %copy-done.7 = f32[64,512]{1,0:T(8,128)S(1)} copy-done((f32[64,512]{1,0:T(8,128)S(1)}, f32[64,512]{1,0:T(8,128)}, u32[]{:S(2)}) %copy-start.7) | copy-done | bytes 131096
  6.2 0.9 %copy-done.9 = f32[48,768]{1,0:T(8,128)S(1)} copy-done((f32[48,768]{1,0:T(8,128)S(1)}, f32[48,768]{1,0:T(8,128)}, u32[]{:S(2)}) %copy-start.9) | copy-done | bytes 147480
  7.2 3.9 %start.1 = (f32[16,128]{1,0:T(8,128)}, f32[208,512]{1,0:T(8,128)S(1)}, f32[208,512]{1,0:T(8,128)S(1)}) custom-call(f32[2,64,512]{2,1,0:T(8,128)S(1)} %copy-done.5, f32[64,512]{1,0:T(8,128)S(1)} %copy-done.7, f32[2,64,512]{2,1,0:T(8,128)S(1)} %copy-done.3, f32[48,768]{1,0:T(8,128)S(1)} %copy-done.9, bf16[48,2,64,512]{3,2,1,0:T(8,128)(2,1)S(1)} %copy-done), custom_call_target="tpu_custom_call" | custom-call | flops 10000000 | bytes 4000000 | tf_op jit(solution)/shard_map/start/pallas_call | solution.py:499
  11.1 2.4 %collective-permute-start = (f32[208,512]{1,0:T(8,128)S(1)}, f32[208,512]{1,0:T(8,128)S(1)}, u32[]{:S(2)}, u32[]{:S(2)}) collective-permute-start(f32[208,512]{1,0:T(8,128)S(1)} %get-tuple-element.13), channel_id=1, source_target_pairs={{0,1},{1,2},{2,3},{3,4},{4,5},{5,6},{6,7},{7,8},{8,9},{9,10},{10,1... | collective-permute-start | bytes 1277960 | tf_op jit(solution)/shard_map/ppermute | solution.py:485
  13.5 1.3 %collective-permute-start.1 = (f32[208,512]{1,0:T(8,128)S(1)}, f32[208,512]{1,0:T(8,128)S(1)}, u32[]{:S(2)}, u32[]{:S(2)}) collective-permute-start(f32[208,512]{1,0:T(8,128)S(1)} %get-tuple-element.14), channel_id=1, source_target_pairs={{1,0},{2,1},{3,2},{4,3},{5,4},{6,5},{7,6},{8,7},{9,8},{10,9},{11,1... | collective-permute-start | bytes 1277960 | tf_op jit(solution)/shard_map/ppermute | solution.py:486
  14.8 9.3 %all-to-all-start = ((f32[16,1,128]{2,1,0:T(1,128)}), f32[16,1,128]{2,1,0:T(1,128)S(1)}, u32[]{:S(2)}, u32[]{:S(2)}) async-start(f32[16,1,128]{2,1,0:T(1,128)} %bitcast.1), calls=%async_computation | async-start | bytes 16384 | tf_op jit(solution)/shard_map/all_to_all | solution.py:479
  24.1 0.0 collective-permute-done.low_ref
  24.1 0.0 collective-permute-done.1.high_ref
  24.1 0.0 copy-done.4
  24.1 0.0 copy-done.6
  24.1 0.0 copy-done.8
  24.1 0.0 copy-done.11
  24.1 1.9 %first_solve.1.smooth_ref = f32[2,80,512]{2,1,0:T(8,128)S(1)} custom-call(s32[16]{0:T(128)S(1)} %copy-done.11, f32[64,512]{1,0:T(8,128)S(1)} %copy-done.8, f32[2,64,512]{2,1,0:T(8,128)S(1)} %copy-done.4, f32[2,64,512]{2,1,0:T(8,128)S(1)} %copy-done.6, f32[208,512]{1,0:T(8,128)S(1)} %collective-permute-done.low_ref, ...), custom_call_target="tpu_custom_call" | custom-call | flops 10000000 | bytes 4000000 | tf_op jit(solution)/shard_map/first_solve/pallas_call | solution.py:505
  26.0 4.4 %all-to-all-done = f32[16,1,128]{2,1,0:T(1,128)S(1)} async-done(((f32[16,1,128]{2,1,0:T(1,128)}), f32[16,1,128]{2,1,0:T(1,128)S(1)}, u32[]{:S(2)}, u32[]{:S(2)}) %all-to-all-start) | async-done | bytes 8224 | tf_op jit(solution)/shard_map/all_to_all | solution.py:479
  30.4 2.8 %copy-done.1 = bf16[48,2,64,512]{3,2,1,0:T(8,128)(2,1)S(1)} copy-done((bf16[48,2,64,512]{3,2,1,0:T(8,128)(2,1)S(1)}, bf16[48,2,64,512]{3,2,1,0:T(8,128)(2,1)}, u32[]{:S(2)}) %copy-start.1) | copy-done | bytes 6291480
  33.2 5.4 %first_turn.1 = (f32[2,64,512]{2,1,0:T(8,128)S(1)}, f32[2,64,512]{2,1,0:T(8,128)S(1)}, f32[2,8,512]{2,1,0:T(8,128)S(1)}, f32[2,8,512]{2,1,0:T(8,128)S(1)}, f32[16,128]{1,0:T(8,128)}) custom-call(f32[16,128]{1,0:T(8,128)S(1)} %bitcast.12, f32[48,768]{1,0:T(8,128)S(1)} %copy-done.10, f32[208,512]{1,0:T(8,128)S(1)} %collective-permute-done.low_ref, ...), custom_call_target="tpu_custom_call" | custom-call | flops 20000000 | bytes 4000000 | tf_op jit(solution)/shard_map/first_turn/pallas_call | solution.py:509
  38.6 1.7 %collective-permute-start.2 = (f32[2,8,512]{2,1,0:T(8,128)S(1)}, f32[2,8,512]{2,1,0:T(8,128)S(1)}, u32[]{:S(2)}, u32[]{:S(2)}) collective-permute-start(f32[2,8,512]{2,1,0:T(8,128)S(1)} %get-tuple-element.17), channel_id=1, source_target_pairs={{0,1},{1,2},{2,3},{3,4},{4,5},{5,6},{6,7},{7,8},{8,9},{9,10},{10,1... | collective-permute-start | bytes 98312 | tf_op jit(solution)/shard_map/ppermute | solution.py:485
  40.3 1.3 %collective-permute-start.3 = (f32[2,8,512]{2,1,0:T(8,128)S(1)}, f32[2,8,512]{2,1,0:T(8,128)S(1)}, u32[]{:S(2)}, u32[]{:S(2)}) collective-permute-start(f32[2,8,512]{2,1,0:T(8,128)S(1)} %get-tuple-element.18), channel_id=1, source_target_pairs={{1,0},{2,1},{3,2},{4,3},{5,4},{6,5},{7,6},{8,7},{9,8},{10,9},{11,1... | collective-permute-start | bytes 98312 | tf_op jit(solution)/shard_map/ppermute | solution.py:486
  41.6 5.9 %all-to-all-start.1 = ((f32[16,1,128]{2,1,0:T(1,128)}), f32[16,1,128]{2,1,0:T(1,128)S(1)}, u32[]{:S(2)}, u32[]{:S(2)}) async-start(f32[16,1,128]{2,1,0:T(1,128)} %bitcast.4), calls=%async_computation.1 | async-start | bytes 16384 | tf_op jit(solution)/shard_map/all_to_all | solution.py:479
  47.5 0.0 collective-permute-done.2.low_image_ref
  47.5 0.0 collective-permute-done.3.high_image_ref
  47.6 1.9 %second_solve.1.image_smooth_ref = f32[2,80,512]{2,1,0:T(8,128)S(1)} custom-call(s32[16]{0:T(128)S(1)} %copy-done.11, f32[64,512]{1,0:T(8,128)S(1)} %copy-done.8, f32[2,64,512]{2,1,0:T(8,128)S(1)} %copy-done.4, f32[2,64,512]{2,1,0:T(8,128)S(1)} %get-tuple-element.16.image_ref, f32[208,512]{1,0:T(8,128)S(1)} %collective-permute-done.low_ref, ...), custom_call_target="tpu_custom_call" | custom-call | flops 10000000 | bytes 4000000 | tf_op jit(solution)/shard_map/second_solve/pallas_call | solution.py:515
  49.5 4.4 %all-to-all-done.1 = f32[16,1,128]{2,1,0:T(1,128)S(1)} async-done(((f32[16,1,128]{2,1,0:T(1,128)}), f32[16,1,128]{2,1,0:T(1,128)S(1)}, u32[]{:S(2)}, u32[]{:S(2)}) %all-to-all-start.1) | async-done | bytes 8224 | tf_op jit(solution)/shard_map/all_to_all | solution.py:479
  53.9 2.8 %copy-done.2 = bf16[48,2,64,512]{3,2,1,0:T(8,128)(2,1)S(1)} copy-done((bf16[48,2,64,512]{3,2,1,0:T(8,128)(2,1)S(1)}, bf16[48,2,64,512]{3,2,1,0:T(8,128)(2,1)}, u32[]{:S(2)}) %copy-start.2) | copy-done | bytes 6291480
  56.7 3.8 %second_turn.1 = (f32[2,64,512]{2,1,0:T(8,128)S(1)}, f32[16,128]{1,0:T(8,128)S(1)}) custom-call(f32[16,128]{1,0:T(8,128)S(1)} %bitcast.13, f32[16,128]{1,0:T(8,128)S(1)} %bitcast.15, f32[48,768]{1,0:T(8,128)S(1)} %copy-done.10, f32[208,512]{1,0:T(8,128)S(1)} %collective-permute-done.low_ref, f32[208,512]{1,0:T(8,128)S(1)} %collective-permute-done.1.high_ref, ...), custom_call_target="tpu_custom_call" | custom-call | flops 20000000 | bytes 4000000 | tf_op jit(solution)/shard_map/second_turn/pallas_call | solution.py:519
  60.5 9.0 %all_to_all.33 = f32[16,1,128]{2,1,0:T(1,128)S(1)} all-to-all(f32[16,1,128]{2,1,0:T(1,128)S(1)} %bitcast.18), channel_id=1, replica_groups=mesh['groups'=2,'sub'=16] {'sub'}, dimensions={0} | all-to-all | bytes 16384 | tf_op jit(solution)/shard_map/all_to_all | solution.py:479
  69.5 1.4 %finish.1 = (f32[2,64,512]{2,1,0:T(8,128)}, f32[3,2]{1,0:T(4,128)S(1)}) custom-call(f32[16,128]{1,0:T(8,128)S(1)} %bitcast.14, f32[16,128]{1,0:T(8,128)S(1)} %bitcast.16, f32[16,128]{1,0:T(8,128)S(1)} %bitcast.17, f32[2,64,512]{2,1,0:T(8,128)S(1)} %get-tuple-element.20.first_direction_ref, f32[2,64,512]{2,1,0:T(8,128)S(1)} %get-tuple-element.21.second_direction_ref), custom_call_target="tpu_custom_call" | custom-call | flops 1000000 | bytes 4000000 | tf_op jit(solution)/shard_map/finish/pallas_call | solution.py:528
  70.8 0.6 copy.12
  (12 shorter events, 0.0 us)
Async XLA Ops:
  0.6 2.8 %copy-start = (bf16[48,2,64,512]{3,2,1,0:T(8,128)(2,1)S(1)}, bf16[48,2,64,512]{3,2,1,0:T(8,128)(2,1)}, u32[]{:S(2)}) copy-start(bf16[48,2,64,512]{3,2,1,0:T(8,128)(2,1)} %basis_ref.5) | copy-start | bytes 18874372
  3.4 0.9 %copy-start.3 = (f32[2,64,512]{2,1,0:T(8,128)S(1)}, f32[2,64,512]{2,1,0:T(8,128)}, u32[]{:S(2)}) copy-start(f32[2,64,512]{2,1,0:T(8,128)} %coup_ref.9) | copy-start | bytes 786436
  4.4 0.9 %copy-start.5 = (f32[2,64,512]{2,1,0:T(8,128)S(1)}, f32[2,64,512]{2,1,0:T(8,128)}, u32[]{:S(2)}) copy-start(f32[2,64,512]{2,1,0:T(8,128)} %rhs_ref.7) | copy-start | bytes 786436
  5.3 0.9 %copy-start.7 = (f32[64,512]{1,0:T(8,128)S(1)}, f32[64,512]{1,0:T(8,128)}, u32[]{:S(2)}) copy-start(f32[64,512]{1,0:T(8,128)} %visc_ref.9) | copy-start | bytes 393220
  6.2 0.9 %copy-start.9 = (f32[48,768]{1,0:T(8,128)S(1)}, f32[48,768]{1,0:T(8,128)}, u32[]{:S(2)}) copy-start(f32[48,768]{1,0:T(8,128)} %inverse_ref.5) | copy-start | bytes 442372
  7.1 16.9 %copy-start.4 = (f32[2,64,512]{2,1,0:T(8,128)S(1)}, f32[2,64,512]{2,1,0:T(8,128)}, u32[]{:S(2)}) copy-start(f32[2,64,512]{2,1,0:T(8,128)} %coup_ref.9) | copy-start | bytes 786436
  7.1 16.9 %copy-start.6 = (f32[2,64,512]{2,1,0:T(8,128)S(1)}, f32[2,64,512]{2,1,0:T(8,128)}, u32[]{:S(2)}) copy-start(f32[2,64,512]{2,1,0:T(8,128)} %rhs_ref.7) | copy-start | bytes 786436
  7.1 17.0 %copy-start.8 = (f32[64,512]{1,0:T(8,128)S(1)}, f32[64,512]{1,0:T(8,128)}, u32[]{:S(2)}) copy-start(f32[64,512]{1,0:T(8,128)} %visc_ref.9) | copy-start | bytes 393220
  7.1 17.0 %copy-start.11 = (s32[16]{0:T(128)S(1)}, s32[16]{0:T(128)}, u32[]{:S(2)}) copy-start(s32[16]{0:T(128)} %margin_ref.3) | copy-start | bytes 196
  7.1 23.2 %copy-start.10 = (f32[48,768]{1,0:T(8,128)S(1)}, f32[48,768]{1,0:T(8,128)}, u32[]{:S(2)}) copy-start(f32[48,768]{1,0:T(8,128)} %inverse_ref.5) | copy-start | bytes 442372
  11.1 13.0 %collective-permute-start = (f32[208,512]{1,0:T(8,128)S(1)}, f32[208,512]{1,0:T(8,128)S(1)}, u32[]{:S(2)}, u32[]{:S(2)}) collective-permute-start(f32[208,512]{1,0:T(8,128)S(1)} %get-tuple-element.13), channel_id=1, source_target_pairs={{0,1},{1,2},{2,3},{3,4},{4,5},{5,6},{6,7},{7,8},{8,9},{9,10},{10,1... | collective-permute-start | bytes 1277960 | tf_op jit(solution)/shard_map/ppermute | solution.py:485
  13.5 10.6 %collective-permute-start.1 = (f32[208,512]{1,0:T(8,128)S(1)}, f32[208,512]{1,0:T(8,128)S(1)}, u32[]{:S(2)}, u32[]{:S(2)}) collective-permute-start(f32[208,512]{1,0:T(8,128)S(1)} %get-tuple-element.14), channel_id=1, source_target_pairs={{1,0},{2,1},{3,2},{4,3},{5,4},{6,5},{7,6},{8,7},{9,8},{10,9},{11,1... | collective-permute-start | bytes 1277960 | tf_op jit(solution)/shard_map/ppermute | solution.py:486
  14.8 15.6 %all-to-all-start = ((f32[16,1,128]{2,1,0:T(1,128)}), f32[16,1,128]{2,1,0:T(1,128)S(1)}, u32[]{:S(2)}, u32[]{:S(2)}) async-start(f32[16,1,128]{2,1,0:T(1,128)} %bitcast.1), calls=%async_computation | async-start | bytes 16384 | tf_op jit(solution)/shard_map/all_to_all | solution.py:479
  30.4 2.8 %copy-start.1 = (bf16[48,2,64,512]{3,2,1,0:T(8,128)(2,1)S(1)}, bf16[48,2,64,512]{3,2,1,0:T(8,128)(2,1)}, u32[]{:S(2)}) copy-start(bf16[48,2,64,512]{3,2,1,0:T(8,128)(2,1)} %basis_ref.5) | copy-start | bytes 18874372
  38.6 8.9 %collective-permute-start.2 = (f32[2,8,512]{2,1,0:T(8,128)S(1)}, f32[2,8,512]{2,1,0:T(8,128)S(1)}, u32[]{:S(2)}, u32[]{:S(2)}) collective-permute-start(f32[2,8,512]{2,1,0:T(8,128)S(1)} %get-tuple-element.17), channel_id=1, source_target_pairs={{0,1},{1,2},{2,3},{3,4},{4,5},{5,6},{6,7},{7,8},{8,9},{9,10},{10,1... | collective-permute-start | bytes 98312 | tf_op jit(solution)/shard_map/ppermute | solution.py:485
  40.3 7.2 %collective-permute-start.3 = (f32[2,8,512]{2,1,0:T(8,128)S(1)}, f32[2,8,512]{2,1,0:T(8,128)S(1)}, u32[]{:S(2)}, u32[]{:S(2)}) collective-permute-start(f32[2,8,512]{2,1,0:T(8,128)S(1)} %get-tuple-element.18), channel_id=1, source_target_pairs={{1,0},{2,1},{3,2},{4,3},{5,4},{6,5},{7,6},{8,7},{9,8},{10,9},{11,1... | collective-permute-start | bytes 98312 | tf_op jit(solution)/shard_map/ppermute | solution.py:486
  41.6 12.2 %all-to-all-start.1 = ((f32[16,1,128]{2,1,0:T(1,128)}), f32[16,1,128]{2,1,0:T(1,128)S(1)}, u32[]{:S(2)}, u32[]{:S(2)}) async-start(f32[16,1,128]{2,1,0:T(1,128)} %bitcast.4), calls=%async_computation.1 | async-start | bytes 16384 | tf_op jit(solution)/shard_map/all_to_all | solution.py:479
  53.9 2.8 %copy-start.2 = (bf16[48,2,64,512]{3,2,1,0:T(8,128)(2,1)S(1)}, bf16[48,2,64,512]{3,2,1,0:T(8,128)(2,1)}, u32[]{:S(2)}) copy-start(bf16[48,2,64,512]{3,2,1,0:T(8,128)(2,1)} %basis_ref.5) | copy-start | bytes 18874372

commit v3 on v2

v3 whole, which is shorter than its diff:
```python
import functools

import jax
import jax.numpy as jnp
from jax import lax
from jax.experimental import pallas as pl
from jax.experimental.pallas import tpu as pltpu
from jax.sharding import PartitionSpec as P

ROWS = 64
CELLS = 512
VECTORS = 48
HALO = 8
EXT = ROWS + 2 * HALO
STRIP = 32
CHUNK = 16
CHUNKS = 2 * ROWS // CHUNK
LANES = 128
SLOTS = 56
EDGE_AT = 5 * HALO
INVERSE_AT = 2 * VECTORS
SWEEPS = 4
RELAX = 0.7
ROW_FACTOR = (1.0, 4.0)
CELL_FACTOR = (4.0, 1.0)

VMEM = pl.BlockSpec(memory_space=pltpu.VMEM)
SMEM = pl.BlockSpec(memory_space=pltpu.SMEM)
HBM = pl.BlockSpec(memory_space=pltpu.HBM)
ANY = pl.BlockSpec(memory_space=pl.ANY)


def coarse_rows(columns):
    return INVERSE_AT + VECTORS * (columns // 512) + (VECTORS // 2) * (columns % 512 // 256)


def cell_sum(field):
    column = lax.broadcasted_iota(jnp.int32, field.shape, 1)
    left = jnp.where(column == 0, 0.0, pltpu.roll(field, 1, 1))
    right = jnp.where(column == CELLS - 1, 0.0, pltpu.roll(field, CELLS - 1, 1))
    return left + right


def row_sum(field):
    count = field.shape[0]
    return pltpu.roll(field, 1, 0) + pltpu.roll(field, count - 1, 0)


def neighbours(field, component):
    rows, cells = row_sum(field), cell_sum(field)
    if component == 0:
        return rows + CELL_FACTOR[0] * cells
    return ROW_FACTOR[1] * rows + cells


def apply_operator(extended, viscosity, coupling):
    inner = slice(HALO, HALO + ROWS)
    images = []
    for a in range(2):
        around = neighbours(extended[a], a)[inner]
        diagonal = 10.0 * viscosity + jnp.abs(coupling[a]) + 0.05
        images.append(
            diagonal * extended[a][inner]
            - viscosity * around
            + coupling[a] * extended[1 - a][inner]
        )
    return images


def basis_copy(i, basis_ref, held, sems):
    rows = pl.ds(pl.multiple_of(CHUNK * (i % 4), CHUNK), CHUNK)
    return pltpu.make_async_copy(basis_ref.at[:, i // 4, rows, :], held.at[i], sems.at[i])


def restrict_chunk(i, held, field, sums):
    a = i // 4
    start = pl.multiple_of((i % 4) * CHUNK, CHUNK)
    parts = [field[a, pl.ds(start, CHUNK), pl.ds(LANES * c, LANES)] for c in range(4)]
    for k in range(VECTORS):
        total = None
        for c in range(4):
            term = held[i, k, :, pl.ds(LANES * c, LANES)].astype(jnp.float32) * parts[c]
            total = term if total is None else total + term
        sums[8 * k : 8 * k + 8, :] += total[:8] + total[8:]


def fold(field):
    total = None
    for part in field:
        for r in range(0, part.shape[0], 8):
            for c in range(0, part.shape[1], LANES):
                term = part[r : r + 8, c : c + LANES]
                total = term if total is None else total + term
    return total


def send_sums(sums, out_ref):
    pick_row = lax.broadcasted_iota(jnp.int32, (LANES, 8 * SLOTS), 0)
    pick_col = lax.broadcasted_iota(jnp.int32, (LANES, 8 * SLOTS), 1)
    pick = (pick_col // 8 == pick_row).astype(jnp.float32)
    by_slot = jnp.dot(
        pick, sums[...], precision=lax.Precision.HIGHEST, preferred_element_type=jnp.float32
    )
    row = lax.dot_general(
        jnp.ones((8, LANES), jnp.float32),
        by_slot,
        (((1,), (1,)), ((), ())),
        precision=lax.Precision.HIGHEST,
        preferred_element_type=jnp.float32,
    )
    out_ref[...] = jnp.broadcast_to(row[:1], out_ref.shape)


def pack_copies(out_ref, first_row, rhs_ref, visc_ref, coup_ref, inverse_ref, sems, at_sem):
    rows = pl.ds(pl.multiple_of(first_row, HALO), HALO)
    moves = [(visc_ref.at[rows, :], 0, HALO, None)]
    for a in range(2):
        moves.append((coup_ref.at[a, rows, :], HALO * (1 + a), HALO, None))
        moves.append((rhs_ref.at[a, rows, :], HALO * (3 + a), HALO, None))
    columns = inverse_ref.shape[1]
    at = EDGE_AT + INVERSE_AT
    for c in range(0, columns - 511, 512):
        moves.append((inverse_ref.at[:, pl.ds(c, 512)], at, VECTORS, None))
        at += VECTORS
    if columns % 512:
        half = VECTORS // 2
        last = pl.ds(columns - 256, 256)
        moves.append((inverse_ref.at[pl.ds(0, half), last], at, half, 0))
        moves.append((inverse_ref.at[pl.ds(half, half), last], at, half, 256))
    copies = []
    for n, (source, at, size, lane) in enumerate(moves):
        place = pl.ds(at, size)
        target = out_ref.at[place, :] if lane is None else out_ref.at[place, pl.ds(lane, 256)]
        copies.append(pltpu.make_async_copy(source, target, sems.at[at_sem + n]))
    return copies


def pack_count(columns):
    return 5 + columns // 512 + 2 * (columns % 512 // 256)


def start_kernel(
    rhs_ref, visc_ref, coup_ref, inverse_ref, basis_ref,
    sums_ref, partner_ref, other_ref,
    held, field, sums, field_sem, sems, pack_sems,
):
    odd = lax.axis_index("sub") % 2
    field_copy = pltpu.make_async_copy(rhs_ref, field, field_sem)
    field_copy.start()
    for i in range(CHUNKS):
        basis_copy(i, basis_ref, held, sems).start()
    packs = []
    for n, (out_ref, up) in enumerate(((partner_ref, 1 - odd), (other_ref, odd))):
        packs += pack_copies(
            out_ref, up * (ROWS - HALO), rhs_ref, visc_ref, coup_ref, inverse_ref, pack_sems,
            n * pack_count(inverse_ref.shape[1]),
        )
    for copy in packs:
        copy.start()
    sums[...] = jnp.zeros_like(sums)
    field_copy.wait()
    sums[8 * VECTORS : 8 * VECTORS + 8] = fold([field[a] * field[a] for a in range(2)])

    def body(i, carry):
        basis_copy(i, basis_ref, held, sems).wait()
        restrict_chunk(i, held, field, sums)
        return carry

    lax.fori_loop(0, CHUNKS, body, 0)
    picker = lax.broadcasted_iota(jnp.int32, (VECTORS, CHUNK * VECTORS), 0) * CHUNK
    place = lax.broadcasted_iota(jnp.int32, (VECTORS, CHUNK * VECTORS), 1)
    for out_ref, up in ((partner_ref, 1 - odd), (other_ref, odd)):
        pick = (place == picker + up * (CHUNK - 1)).astype(jnp.float32).astype(jnp.bfloat16)
        for a in range(2):
            rows = held[4 * a + 3 * up].reshape(CHUNK * VECTORS, CELLS)
            at = EDGE_AT + VECTORS * a
            out_ref[at : at + VECTORS] = jnp.dot(pick, rows, preferred_element_type=jnp.float32)
    for copy in packs:
        copy.wait()
    send_sums(sums, sums_ref)


def fetch(partner_ref, other_ref, low_ref, high_ref, first_row, sems):
    odd = lax.axis_index("sub") % 2
    rows = pl.ds(first_row, low_ref.shape[0])

    def copies(below_ref, above_ref):
        return (
            pltpu.make_async_copy(below_ref.at[rows], low_ref, sems.at[0]),
            pltpu.make_async_copy(above_ref.at[rows], high_ref, sems.at[1]),
        )

    @pl.when(odd == 1)
    def _():
        for copy in copies(partner_ref, other_ref):
            copy.start()

    @pl.when(odd == 0)
    def _():
        for copy in copies(other_ref, partner_ref):
            copy.start()

    def finish():
        for copy in copies(partner_ref, other_ref):
            copy.wait()

    return finish


def solve(count, margin_ref, visc_ref, coup_ref, field_ref, low_ref, high_ref, edges, out_ref):
    rank = lax.axis_index("sub")
    lower = jnp.where(rank > 0, margin_ref[jnp.maximum(rank - 1, 0)], 0)
    upper = jnp.where(rank < count - 1, margin_ref[rank], 0)
    lower_f, upper_f = lower.astype(jnp.float32), upper.astype(jnp.float32)
    low_scale = 2.0 * jnp.maximum(lower_f, 1.0)
    high_scale = 2.0 * jnp.maximum(upper_f, 1.0)

    def masks(first, rows, side):
        place = lax.broadcasted_iota(jnp.int32, (rows, LANES), 0) + first
        place_f = place.astype(jnp.float32)
        rising = lambda base, scale: (place_f - base + 0.5) / scale
        falling = lambda base, scale: (base - place_f - 0.5) / scale
        if side == 0:
            live = (place >= -lower) & (place < ROWS + upper)
            weight = jnp.where(place < lower, rising(-lower_f, low_scale), 1.0)
            weight = jnp.where(
                place >= ROWS - upper, falling(ROWS + upper_f, high_scale), weight
            )
        elif side < 0:
            live = place < lower
            weight = jnp.where(place >= -lower, falling(lower_f, low_scale), 1.0)
        else:
            live = place >= ROWS - upper
            weight = jnp.where(place < ROWS + upper, rising(ROWS - upper_f, high_scale), 1.0)
        wide = lambda x: jnp.concatenate([x] * (CELLS // LANES), 1)
        return wide(live.astype(jnp.float32)), wide(weight)

    def stack(own, at):
        rows = slice(at, at + HALO)
        return jnp.concatenate([low_ref[rows], own, high_ref[rows]], 0)

    def triple(field):
        return jnp.concatenate([field, field[:STRIP], field[EXT - STRIP :]], 0)

    viscosity = stack(visc_ref[...], 0)
    blocks = [masks(-HALO, EXT, 0), masks(-HALO, STRIP, -1), masks(ROWS + HALO - STRIP, STRIP, 1)]
    live = jnp.concatenate([block[0] for block in blocks], 0)
    first, across, other = [], [], []
    for a in range(2):
        coupling = stack(coup_ref[a], HALO * (1 + a))
        field = jnp.concatenate([edges[a][0], field_ref[a], edges[a][1]], 0)
        scale = RELAX / (10.0 * viscosity + jnp.abs(coupling) + 0.05)
        first.append(live * triple(scale * field))
        across.append(live * triple(scale * viscosity))
        other.append(live * triple(scale * coupling))
    solved = list(first)
    for _ in range(SWEEPS - 1):
        solved = [
            (1.0 - RELAX) * solved[a]
            + first[a]
            + across[a] * neighbours(solved[a], a)
            - other[a] * solved[1 - a]
            for a in range(2)
        ]
    for a in range(2):
        shares = solved[a] * jnp.concatenate([block[1] for block in blocks], 0)
        out_ref[a] = shares[:EXT]
        out_ref[a, :STRIP] += shares[EXT : EXT + STRIP]
        out_ref[a, EXT - STRIP :] += shares[EXT + STRIP :]


def first_solve_kernel(
    count, margin_ref, visc_ref, coup_ref, rhs_ref, partner_ref, other_ref,
    out_ref,
    low, high, sems,
):
    fetch(partner_ref, other_ref, low, high, 0, sems)()
    rows = [slice(HALO * (3 + a), HALO * (4 + a)) for a in range(2)]
    edges = [(low[rows[a]], high[rows[a]]) for a in range(2)]
    solve(count, margin_ref, visc_ref, coup_ref, rhs_ref, low, high, edges, out_ref)


def second_solve_kernel(
    count, margin_ref, visc_ref, coup_ref, image_ref, partner_ref, other_ref,
    partner_image_ref, other_image_ref,
    out_ref,
    low, high, low_image, high_image, sems, image_sems,
):
    images = fetch(partner_image_ref, other_image_ref, low_image, high_image, 0, image_sems)
    fetch(partner_ref, other_ref, low, high, 0, sems)()
    images()
    edges = [(low_image[a], high_image[a]) for a in range(2)]
    solve(count, margin_ref, visc_ref, coup_ref, image_ref, low, high, edges, out_ref)


def line_up(residuals):
    devices = residuals.shape[0]
    lane = lax.broadcasted_iota(jnp.int32, (1, LANES), 1)
    tiles = [jnp.zeros((1, LANES), jnp.float32) for _ in range(devices * VECTORS // LANES)]
    for t in range(devices):
        tile, offset = divmod(VECTORS * t, LANES)
        row = jnp.where(lane < VECTORS, residuals[t : t + 1], 0.0)
        if offset:
            row = pltpu.roll(row, offset, 1)
        if offset + VECTORS <= LANES:
            tiles[tile] = tiles[tile] + row
        else:
            tiles[tile] = tiles[tile] + jnp.where(lane >= offset, row, 0.0)
            tiles[tile + 1] = tiles[tile + 1] + jnp.where(lane < offset, row, 0.0)
    return jnp.concatenate(tiles, 1)


def rounded(column):
    return column.astype(jnp.bfloat16).astype(jnp.float32)


def lift(inverse_ref, residual):
    return rounded(jnp.sum(inverse_ref[...] * residual, 1, keepdims=True))


def lift_packed(ref, residual):
    columns = residual.shape[1]
    at, total = INVERSE_AT, None
    for c in range(0, columns - 511, 512):
        term = jnp.sum(ref[at : at + VECTORS] * residual[:, c : c + 512], 1, keepdims=True)
        total = term if total is None else total + term
        at += VECTORS
    if columns % 512:
        half = VECTORS // 2
        last = residual[:, columns - 256 :]
        rows = ref[at : at + half]
        term = jnp.concatenate(
            [
                jnp.sum(rows[:, :256] * last, 1, keepdims=True),
                jnp.sum(rows[:, 256:] * last, 1, keepdims=True),
            ],
            0,
        )
        total = term if total is None else total + term
    return rounded(total)


def edge_values(ref, lifted):
    return [
        jnp.sum(ref[VECTORS * a : VECTORS * (a + 1)] * lifted, 0, keepdims=True)
        for a in range(2)
    ]


def spread(lifted):
    shape = (VECTORS, CHUNK * VECTORS)
    owner = lax.broadcasted_iota(jnp.int32, shape, 1) // CHUNK
    row = lax.broadcasted_iota(jnp.int32, shape, 0)
    line = jnp.sum(jnp.where(owner == row, lifted, 0.0), 0, keepdims=True)
    shape = (CHUNK, CHUNK * VECTORS)
    place = lax.broadcasted_iota(jnp.int32, shape, 1) % CHUNK
    row = lax.broadcasted_iota(jnp.int32, shape, 0)
    return jnp.where(place == row, line, 0.0).astype(jnp.bfloat16)


class Coarse:
    def __init__(self, partner_ref, other_ref, basis_ref, held, low, high, sems, side_sems):
        self.held, self.low, self.high = held, low, high
        self.sides_ready = fetch(partner_ref, other_ref, low, high, EDGE_AT, side_sems)
        self.copies = [basis_copy(i, basis_ref, held, sems) for i in range(CHUNKS)]
        for copy in self.copies:
            copy.start()

    def prolong(self, residual, inverse_ref, smooth, extended):
        matrix = spread(lift(inverse_ref, residual))
        for i, copy in enumerate(self.copies):
            a, start = i // 4, HALO + CHUNK * (i % 4)
            rows = slice(start, start + CHUNK)
            if i == CHUNKS // 2:
                self.prolong_edges(residual, smooth, extended)
            copy.wait()
            coarse = jnp.dot(
                matrix,
                self.held[i].reshape(CHUNK * VECTORS, CELLS),
                preferred_element_type=jnp.float32,
            )
            extended[a, rows] = smooth(a, rows) + coarse

    def prolong_edges(self, residual, smooth, extended):
        self.sides_ready()
        low_edge = edge_values(self.low, lift_packed(self.low, residual))
        high_edge = edge_values(self.high, lift_packed(self.high, residual))
        place = lax.broadcasted_iota(jnp.int32, (HALO, CELLS), 0)
        for a in range(2):
            rows = slice(0, HALO)
            extended[a, rows] = smooth(a, rows) + jnp.where(place == HALO - 1, low_edge[a], 0.0)
            rows = slice(EXT - HALO, EXT)
            extended[a, rows] = smooth(a, rows) + jnp.where(place == 0, high_edge[a], 0.0)


def lane_total(received, lane):
    return jnp.sum(received[:, lane : lane + 1], 0, keepdims=True)


def first_turn_kernel(
    sums_ref, inverse_ref, partner_ref, other_ref, basis_ref, smooth_ref, rhs_ref, visc_ref,
    coup_ref,
    direction_ref, image_ref, partner_rows_ref, other_rows_ref, next_ref,
    held, low, high, sems, side_sems, extended, sums,
):
    coarse = Coarse(partner_ref, other_ref, basis_ref, held, low, high, sems, side_sems)
    received = sums_ref[...]
    over_beta = 1.0 / jnp.sqrt(lane_total(received, VECTORS))
    residual = line_up(received) * over_beta
    coarse.prolong(
        residual,
        inverse_ref,
        lambda a, rows: smooth_ref[a, rows] * over_beta,
        extended,
    )
    images = apply_operator(
        [extended[a] for a in range(2)], visc_ref[...], [coup_ref[a] for a in range(2)]
    )
    odd = lax.axis_index("sub") % 2 == 1
    for a in range(2):
        direction_ref[a] = extended[a, HALO : HALO + ROWS]
        image_ref[a] = images[a]
        head, tail = images[a][:HALO], images[a][ROWS - HALO :]
        partner_rows_ref[a] = jnp.where(odd, head, tail)
        other_rows_ref[a] = jnp.where(odd, tail, head)
    sums[...] = jnp.zeros_like(sums)
    at = 8 * VECTORS
    sums[at : at + 8] = fold([rhs_ref[a] * images[a] for a in range(2)])
    sums[at + 8 : at + 16] = fold([images[a] * images[a] for a in range(2)])

    def body(i, carry):
        restrict_chunk(i, held, image_ref, sums)
        return carry

    lax.fori_loop(0, CHUNKS, body, 0)
    send_sums(sums, next_ref)


def first_column(first, second):
    beta = jnp.sqrt(lane_total(first, VECTORS))
    h_00 = lane_total(second, VECTORS) / beta
    h_10 = jnp.sqrt(lane_total(second, VECTORS + 1) - h_00 * h_00)
    return beta, h_00, h_10


def second_turn_kernel(
    first_ref, second_ref, inverse_ref, partner_ref, other_ref, basis_ref, smooth_ref,
    image_smooth_ref, rhs_ref, image_ref, visc_ref, coup_ref,
    direction_ref, next_ref,
    held, low, high, sems, side_sems, extended, sums,
):
    coarse = Coarse(partner_ref, other_ref, basis_ref, held, low, high, sems, side_sems)
    first, second = first_ref[...], second_ref[...]
    beta, h_00, h_10 = first_column(first, second)
    ratio = h_00 / beta
    over = 1.0 / h_10
    residual = (line_up(second) - ratio * line_up(first)) * over
    coarse.prolong(
        residual,
        inverse_ref,
        lambda a, rows: (image_smooth_ref[a, rows] - ratio * smooth_ref[a, rows]) * over,
        extended,
    )
    images = apply_operator(
        [extended[a] for a in range(2)], visc_ref[...], [coup_ref[a] for a in range(2)]
    )
    sums[...] = jnp.zeros_like(sums)
    sums[0:8] = fold([rhs_ref[a] * images[a] for a in range(2)])
    sums[8:16] = fold([image_ref[a] * images[a] for a in range(2)])
    sums[16:24] = fold([images[a] * images[a] for a in range(2)])
    for a in range(2):
        direction_ref[a] = extended[a, HALO : HALO + ROWS]
    send_sums(sums, next_ref)


def finish_kernel(
    first_ref, second_ref, third_ref, first_direction_ref, second_direction_ref,
    solution_ref, hessenberg_ref,
):
    third = third_ref[...]
    beta, h_00, h_10 = first_column(first_ref[...], second_ref[...])
    h_01 = lane_total(third, 0) / beta
    h_11 = (lane_total(third, 1) - h_00 * h_01) / h_10
    h_21 = jnp.sqrt(lane_total(third, 2) - h_01 * h_01 - h_11 * h_11)
    n_00 = h_00 * h_00 + h_10 * h_10
    n_10 = h_00 * h_01 + h_10 * h_11
    n_11 = h_01 * h_01 + h_11 * h_11 + h_21 * h_21
    l_00 = jnp.sqrt(n_00)
    l_10 = n_10 / l_00
    l_11 = jnp.sqrt(n_11 - l_10 * l_10)
    f_0 = beta * h_00 / l_00
    f_1 = (beta * h_01 - l_10 * f_0) / l_11
    c_1 = f_1 / l_11
    c_0 = (f_0 - l_10 * c_1) / l_00
    for a in range(2):
        solution_ref[a] = c_0 * first_direction_ref[a] + c_1 * second_direction_ref[a]
    shape = hessenberg_ref.shape
    row = lax.broadcasted_iota(jnp.int32, shape, 1)
    column = lax.broadcasted_iota(jnp.int32, shape, 0)
    entries = jnp.zeros(shape, jnp.float32)
    for i, j, value in ((0, 0, h_00), (0, 1, h_01), (1, 0, h_10), (1, 1, h_11), (2, 1, h_21)):
        entries = jnp.where((row == i) & (column == j), value, entries)
    hessenberg_ref[...] = entries


def call(kernel, name, in_specs, outs, flops, scratch=(), traffic=4_000_000):
    return pl.pallas_call(
        kernel,
        name=name,
        in_specs=in_specs,
        out_specs=[VMEM] * len(outs),
        out_shape=outs,
        scratch_shapes=scratch,
        compiler_params=pltpu.CompilerParams(vmem_limit_bytes=16 * 1024 * 1024),
        cost_estimate=pl.CostEstimate(flops=flops, bytes_accessed=traffic, transcendentals=0),
    )


def in_hbm(array):
    return pltpu.with_memory_space_constraint(array, pltpu.HBM)


def from_everyone(rows):
    return lax.all_to_all(rows, "sub", 0, 0, tiled=True)


def from_everyone_reversed(rows):
    order = [list(range(lax.axis_size("sub")))[::-1]]
    return lax.all_to_all(rows, "sub", 0, 0, tiled=True, axis_index_groups=order)


def swap(partner, other):
    count = lax.axis_size("sub")
    both = lambda lows: [pair for i in lows for pair in ((i, i + 1), (i + 1, i))]
    return (
        lax.ppermute(partner, "sub", both(range(0, count, 2))),
        lax.ppermute(other, "sub", both(range(1, count - 1, 2))),
    )


def on_device(rhs, viscosity, coupling, margin_rows, coarse_basis, coarse_inverse):
    count = lax.axis_size("sub")
    columns = coarse_inverse.shape[1]
    f32 = lambda *shape: jax.ShapeDtypeStruct(shape, jnp.float32)
    dma = lambda *shape: pltpu.SemaphoreType.DMA(shape)
    held = pltpu.VMEM((CHUNKS, VECTORS, CHUNK, CELLS), jnp.bfloat16)
    field = pltpu.VMEM((2, ROWS, CELLS), jnp.float32)
    sums = pltpu.VMEM((8 * SLOTS, LANES), jnp.float32)
    edge_scratch = [pltpu.VMEM((EDGE_AT, CELLS), jnp.float32)] * 2
    image_scratch = [pltpu.VMEM((2, HALO, CELLS), jnp.float32)] * 2
    turn_scratch = (
        [held]
        + [pltpu.VMEM((coarse_rows(columns), CELLS), jnp.float32)] * 2
        + [dma(CHUNKS), dma(2), pltpu.VMEM((2, EXT, CELLS), jnp.float32), sums]
    )
    row, whole, edge = f32(count, LANES), f32(2, ROWS, CELLS), f32(2, HALO, CELLS)
    packed, smoothed = f32(EDGE_AT + coarse_rows(columns), CELLS), f32(2, EXT, CELLS)
    basis = in_hbm(coarse_basis)
    first, partner, other = call(
        start_kernel, "start", [HBM] * 5, [row, packed, packed], 10_000_000,
        [held, field, sums, dma(), dma(CHUNKS), dma(2 * pack_count(columns))],
    )(in_hbm(rhs), in_hbm(viscosity), in_hbm(coupling), in_hbm(coarse_inverse), basis)
    partner, other = swap(partner, other)
    first = from_everyone(first)
    (smooth,) = call(
        functools.partial(first_solve_kernel, count), "first_solve",
        [SMEM] + [VMEM] * 3 + [ANY] * 2, [smoothed], 10_000_000, edge_scratch + [dma(2)],
    )(margin_rows, viscosity, coupling, rhs, partner, other)
    partner, other = in_hbm(partner), in_hbm(other)
    direction, image, partner_rows, other_rows, second = call(
        first_turn_kernel, "first_turn", [VMEM] * 2 + [HBM] * 3 + [VMEM] * 4,
        [whole, whole, edge, edge, row], 20_000_000, turn_scratch,
    )(first, coarse_inverse, partner, other, basis, smooth, rhs, viscosity, coupling)
    partner_rows, other_rows = swap(partner_rows, other_rows)
    second = from_everyone(second)
    (image_smooth,) = call(
        functools.partial(second_solve_kernel, count), "second_solve",
        [SMEM] + [VMEM] * 3 + [HBM] * 2 + [ANY] * 2, [smoothed], 0,
        edge_scratch + image_scratch + [dma(2)] * 2, 0,
    )(margin_rows, viscosity, coupling, image, partner, other, partner_rows, other_rows)
    second_direction, third = call(
        second_turn_kernel, "second_turn", [VMEM] * 3 + [HBM] * 3 + [VMEM] * 6, [whole, row],
        20_000_000, turn_scratch,
    )(
        first, second, coarse_inverse, partner, other, basis, smooth, image_smooth, rhs, image,
        viscosity, coupling,
    )
    third = from_everyone_reversed(third)
    result, transposed = call(finish_kernel, "finish", [VMEM] * 5, [whole, f32(2, 3)], 1_000_000)(
        first, second, third, direction, second_direction
    )
    return result, transposed.T


def solution(mesh):
    in_specs = (
        P(None, ("groups", "sub"), None),
        P(("groups", "sub"), None),
        P(None, ("groups", "sub"), None),
        P("groups"),
        P(None, None, ("groups", "sub"), None),
        P(("groups", "sub"), None),
    )
    out_specs = (P(None, ("groups", "sub"), None), P("groups", None))
    return jax.shard_map(
        on_device, mesh=mesh, in_specs=in_specs, out_specs=out_specs, check_vma=False
    )
```

time: 72 us -> 61.3 us (0.85)
  local copies, waits for them, and re-layouts: 12.7 us -> 0.03 us
  Pallas kernels: 18.4 us -> 24.9 us
  starting transfers between devices: 21.8 us -> 20 us
  waiting for transfers between devices: 8.77 us -> 7.43 us
  blocking collectives: 8.98 us -> 7.9 us
    unnamed x24 -> x14, local copies, waits for them, and re-layouts: 12.1 us -> 0.03 us
    pallas_call x4, Pallas kernels: 14.5 us -> 19.7 us  [the longest x1 6.72 us: on_device(): call(first_turn_kernel, 'first_turn', [VMEM] * 2 + [HBM] * 3 + [VMEM] * 4...]
    ppermute x4, starting transfers between devices: 6.66 us -> 2.12 us  [the longest x2 1.33 us: swap(): lax.ppermute(other, 'sub', both(range(1, count - 1, 2)))]
    all_to_all x2, starting transfers between devices: 15.2 us -> 17.8 us  [from_everyone(): return lax.all_to_all(rows, 'sub', 0, 0, tiled=True)]
    all_to_all x2, waiting for transfers between devices: 8.76 us -> 7.42 us  [from_everyone(): return lax.all_to_all(rows, 'sub', 0, 0, tiled=True)]
    all_to_all x1, blocking collectives: 8.98 us -> 7.9 us  [from_everyone_reversed(): lax.all_to_all(rows, 'sub', 0, 0, tiled=True, axis_index_groups=order)]
    pallas_call x1, Pallas kernels: 1.9 us -> 2.97 us  [on_device(): call(functools.partial(second_solve_kernel, count), 'second_solve', [SMEM...]
  transfers between devices with their start and end apart: 6 -> 6, of which waited for: 2 -> 2; matrix products, arithmetic and copies ran while one was open for 0% -> 0% of each run, Pallas kernels for 5% -> 8%
where the time goes in v3:
time: 61.3 us; the launch traced here: 61 us
  Pallas kernels  24.9 us (41%)
  starting transfers between devices  20 us (33%)
  blocking collectives  7.9 us (13%)
  waiting for transfers between devices  7.43 us (12%)
  between operations  0.83 us (1%)
    all_to_all x2, starting transfers between devices, from_everyone(): return lax.all_to_all(rows, 'sub', 0, 0, tiled=True)  17.8 us
    all_to_all x1, blocking collectives, from_everyone_reversed(): lax.all_to_all(rows, 'sub', 0, 0, tiled=True, axis_index_groups=order)  7.9 us
    all_to_all x2, waiting for transfers between devices, from_everyone(): return lax.all_to_all(rows, 'sub', 0, 0, tiled=True)  7.42 us
    pallas_call x1, Pallas kernels, on_device(): call(first_turn_kernel, 'first_turn', [VMEM] * 2 + [HBM] * 3 + [VMEM] * 4...  6.72 us
    pallas_call x1, Pallas kernels, on_device(): call(start_kernel, 'start', [HBM] * 5, [row, packed, packed], 10000000, [...  6.7 us
    pallas_call x1, Pallas kernels, on_device(): call(second_turn_kernel, 'second_turn', [VMEM] * 3 + [HBM] * 3 + [VMEM] *...  4.95 us
    pallas_call x1, Pallas kernels, on_device(): call(functools.partial(second_solve_kernel, count), 'second_solve', [SMEM...  2.97 us
    pallas_call x1, Pallas kernels, on_device(): call(functools.partial(first_solve_kernel, count), 'first_solve', [SMEM]...  2.15 us
  transfers between devices with their start and end apart: 6, of which 2 were waited for; matrix products, arithmetic and copies ran while one was open for 0% of the time, Pallas kernels for 8%

profile of v3, /device:TPU:0, one launch (start us, length us, event | category | flops | bytes accessed | tf_op | source)
XLA Modules:
  0.0 61.0 jit_solution(9340837137363212079)
XLA Ops:
  0.6 0.0 copy-start.2
  0.6 0.0 copy-start.4
  0.7 0.0 copy-start.3
  0.7 0.0 copy-start.5
  0.7 0.0 copy-start.6
  0.7 6.7 %start.1 = (f32[16,128]{1,0:T(8,128)}, f32[208,512]{1,0:T(8,128)S(1)}, f32[208,512]{1,0:T(8,128)S(1)}) custom-call(f32[2,64,512]{2,1,0:T(8,128)} %rhs_ref.7, f32[64,512]{1,0:T(8,128)} %visc_ref.9, f32[2,64,512]{2,1,0:T(8,128)} %coup_ref.9, f32[48,768]{1,0:T(8,128)} %inverse_ref.5, bf16[48,2,64,512]{3,2,1,0:T(8,128)(2,1)} %basis_ref.5), custom_call_target="tpu_custom_call" | custom-call | flops 10000000 | bytes 4000000 | tf_op jit(solution)/shard_map/start/pallas_call | solution.py:559
  7.4 0.5 collective-permute-start
  7.9 0.7 %collective-permute-start.1 = (f32[208,512]{1,0:T(8,128)S(1)}, f32[208,512]{1,0:T(8,128)S(1)}, u32[]{:S(2)}, u32[]{:S(2)}) collective-permute-start(f32[208,512]{1,0:T(8,128)S(1)} %get-tuple-element.16), channel_id=1, source_target_pairs={{1,2},{2,1},{3,4},{4,3},{5,6},{6,5},{7,8},{8,7},{9,10},{10,9},{11,... | collective-permute-start | bytes 1277960 | tf_op jit(solution)/shard_map/ppermute | solution.py:537
  8.6 8.8 %all-to-all-start = ((f32[16,1,128]{2,1,0:T(1,128)}), f32[16,1,128]{2,1,0:T(1,128)S(1)}, u32[]{:S(2)}, u32[]{:S(2)}) async-start(f32[16,1,128]{2,1,0:T(1,128)} %bitcast.1), calls=%async_computation | async-start | bytes 16384 | tf_op jit(solution)/shard_map/all_to_all | solution.py:524
  17.4 0.0 collective-permute-done.partner_ref
  17.4 0.0 copy-start
  17.4 0.0 collective-permute-done.1.other_ref
  17.4 0.0 copy-done.2
  17.4 0.0 copy-done.4
  17.4 0.0 copy-done.3
  17.4 0.0 copy-done.6
  17.5 0.0 copy-start.1
  17.5 2.2 %first_solve.1.smooth_ref = f32[2,80,512]{2,1,0:T(8,128)S(1)} custom-call(s32[16]{0:T(128)S(1)} %copy-done.6, f32[64,512]{1,0:T(8,128)S(1)} %copy-done.4, f32[2,64,512]{2,1,0:T(8,128)S(1)} %copy-done.2, f32[2,64,512]{2,1,0:T(8,128)S(1)} %copy-done.3, f32[208,512]{1,0:T(8,128)S(1)} %collective-permute-done.partner_ref, ...), custom_call_target="tpu_custom_call" | custom-call | flops 10000000 | bytes 4000000 | tf_op jit(solution)/shard_map/first_solve/pallas_call | solution.py:565
  19.6 4.1 %all-to-all-done = f32[16,1,128]{2,1,0:T(1,128)S(1)} async-done(((f32[16,1,128]{2,1,0:T(1,128)}), f32[16,1,128]{2,1,0:T(1,128)S(1)}, u32[]{:S(2)}, u32[]{:S(2)}) %all-to-all-start) | async-done | bytes 8224 | tf_op jit(solution)/shard_map/all_to_all | solution.py:524
  23.7 0.0 copy-done
  23.7 0.0 copy-done.1
  23.7 6.7 %first_turn.1 = (f32[2,64,512]{2,1,0:T(8,128)S(1)}, f32[2,64,512]{2,1,0:T(8,128)S(1)}, f32[2,8,512]{2,1,0:T(8,128)S(1)}, f32[2,8,512]{2,1,0:T(8,128)S(1)}, f32[16,128]{1,0:T(8,128)}) custom-call(f32[16,128]{1,0:T(8,128)S(1)} %bitcast.13, f32[48,768]{1,0:T(8,128)S(1)} %copy-done.5, f32[208,512]{1,0:T(8,128)} %copy-done, f32[208,512]{1,0:T(8,128)} %copy-done.1, ...), custom_call_target="tpu_custom_call" | custom-call | flops 20000000 | bytes 4000000 | tf_op jit(solution)/shard_map/first_turn/pallas_call | solution.py:570
  30.4 0.3 collective-permute-start.2
  30.7 0.7 %collective-permute-start.3 = (f32[2,8,512]{2,1,0:T(8,128)S(1)}, f32[2,8,512]{2,1,0:T(8,128)S(1)}, u32[]{:S(2)}, u32[]{:S(2)}) collective-permute-start(f32[2,8,512]{2,1,0:T(8,128)S(1)} %get-tuple-element.20), channel_id=1, source_target_pairs={{1,2},{2,1},{3,4},{4,3},{5,6},{6,5},{7,8},{8,7},{9,10},{10,9},{11,... | collective-permute-start | bytes 98312 | tf_op jit(solution)/shard_map/ppermute | solution.py:537
  31.4 9.1 %all-to-all-start.1 = ((f32[16,1,128]{2,1,0:T(1,128)}), f32[16,1,128]{2,1,0:T(1,128)S(1)}, u32[]{:S(2)}, u32[]{:S(2)}) async-start(f32[16,1,128]{2,1,0:T(1,128)} %bitcast.4), calls=%async_computation.1 | async-start | bytes 16384 | tf_op jit(solution)/shard_map/all_to_all | solution.py:524
  40.4 0.0 collective-permute-done.2.partner_image_ref
  40.5 0.0 collective-permute-done.3.other_image_ref
  40.5 3.0 %second_solve.1.image_smooth_ref = f32[2,80,512]{2,1,0:T(8,128)S(1)} custom-call(s32[16]{0:T(128)S(1)} %copy-done.6, f32[64,512]{1,0:T(8,128)S(1)} %copy-done.4, f32[2,64,512]{2,1,0:T(8,128)S(1)} %copy-done.2, f32[2,64,512]{2,1,0:T(8,128)S(1)} %get-tuple-element.18.image_ref, f32[208,512]{1,0:T(8,128)} %copy-done, f32[208,512]{1,0:T(8,128)} %copy-done.1, ...), custom_call_target="tpu_custom_call" | custom-call | tf_op jit(solution)/shard_map/second_solve/pallas_call | solution.py:576
  43.4 3.3 %all-to-all-done.1 = f32[16,1,128]{2,1,0:T(1,128)S(1)} async-done(((f32[16,1,128]{2,1,0:T(1,128)}), f32[16,1,128]{2,1,0:T(1,128)S(1)}, u32[]{:S(2)}, u32[]{:S(2)}) %all-to-all-start.1) | async-done | bytes 8224 | tf_op jit(solution)/shard_map/all_to_all | solution.py:524
  46.8 4.9 %second_turn.1 = (f32[2,64,512]{2,1,0:T(8,128)S(1)}, f32[16,128]{1,0:T(8,128)S(1)}) custom-call(f32[16,128]{1,0:T(8,128)S(1)} %bitcast.14, f32[16,128]{1,0:T(8,128)S(1)} %bitcast.16, f32[48,768]{1,0:T(8,128)S(1)} %copy-done.5, f32[208,512]{1,0:T(8,128)} %copy-done, f32[208,512]{1,0:T(8,128)} %copy-done.1, bf16[48,2,64,512]{3,2,1,0:T(8,128)(2,1)} %basis_ref.5, ...), custom_call_target="tpu_custom_call" | custom-call | flops 20000000 | bytes 4000000 | tf_op jit(solution)/shard_map/second_turn/pallas_call | solution.py:581
  51.7 7.9 %all_to_all.33 = f32[16,1,128]{2,1,0:T(1,128)S(1)} all-to-all(f32[16,1,128]{2,1,0:T(1,128)S(1)} %bitcast.19), channel_id=1, replica_groups={{15,14,13,12,11,10,9,8,7,6,5,4,3,2,1,0},{31,30,29,28,27,26,25,24,23,22,..., dimensions={0} | all-to-all | bytes 16384 | tf_op jit(solution)/shard_map/all_to_all | solution.py:529
  59.6 1.4 %finish.1 = (f32[2,64,512]{2,1,0:T(8,128)}, f32[2,3]{1,0:T(2,128)}) custom-call(f32[16,128]{1,0:T(8,128)S(1)} %bitcast.15, f32[16,128]{1,0:T(8,128)S(1)} %bitcast.17, f32[16,128]{1,0:T(8,128)S(1)} %bitcast.18, f32[2,64,512]{2,1,0:T(8,128)S(1)} %get-tuple-element.22.first_direction_ref, f32[2,64,512]{2,1,0:T(8,128)S(1)} %get-tuple-element.23.second_direction_ref), custom_call_target="tpu_custom_call" | custom-call | flops 1000000 | bytes 4000000 | tf_op jit(solution)/shard_map/finish/pallas_call | solution.py:589
  (1 shorter events, 0.0 us)
Async XLA Ops:
  0.6 16.8 %copy-start.2 = (f32[2,64,512]{2,1,0:T(8,128)S(1)}, f32[2,64,512]{2,1,0:T(8,128)}, u32[]{:S(2)}) copy-start(f32[2,64,512]{2,1,0:T(8,128)} %coup_ref.9) | copy-start | bytes 786436
  0.6 16.8 %copy-start.4 = (f32[64,512]{1,0:T(8,128)S(1)}, f32[64,512]{1,0:T(8,128)}, u32[]{:S(2)}) copy-start(f32[64,512]{1,0:T(8,128)} %visc_ref.9) | copy-start | bytes 393220
  0.7 16.8 %copy-start.3 = (f32[2,64,512]{2,1,0:T(8,128)S(1)}, f32[2,64,512]{2,1,0:T(8,128)}, u32[]{:S(2)}) copy-start(f32[2,64,512]{2,1,0:T(8,128)} %rhs_ref.7) | copy-start | bytes 786436
  0.7 23.1 %copy-start.5 = (f32[48,768]{1,0:T(8,128)S(1)}, f32[48,768]{1,0:T(8,128)}, u32[]{:S(2)}) copy-start(f32[48,768]{1,0:T(8,128)} %inverse_ref.5) | copy-start | bytes 442372
  0.7 16.8 %copy-start.6 = (s32[16]{0:T(128)S(1)}, s32[16]{0:T(128)}, u32[]{:S(2)}) copy-start(s32[16]{0:T(128)} %margin_ref.3) | copy-start | bytes 196
  7.4 10.0 %collective-permute-start = (f32[208,512]{1,0:T(8,128)S(1)}, f32[208,512]{1,0:T(8,128)S(1)}, u32[]{:S(2)}, u32[]{:S(2)}) collective-permute-start(f32[208,512]{1,0:T(8,128)S(1)} %get-tuple-element.15), channel_id=1, source_target_pairs={{0,1},{1,0},{2,3},{3,2},{4,5},{5,4},{6,7},{7,6},{8,9},{9,8},{10,11... | collective-permute-start | bytes 1277960 | tf_op jit(solution)/shard_map/ppermute | solution.py:536
  7.9 9.5 %collective-permute-start.1 = (f32[208,512]{1,0:T(8,128)S(1)}, f32[208,512]{1,0:T(8,128)S(1)}, u32[]{:S(2)}, u32[]{:S(2)}) collective-permute-start(f32[208,512]{1,0:T(8,128)S(1)} %get-tuple-element.16), channel_id=1, source_target_pairs={{1,2},{2,1},{3,4},{4,3},{5,6},{6,5},{7,8},{8,7},{9,10},{10,9},{11,... | collective-permute-start | bytes 1277960 | tf_op jit(solution)/shard_map/ppermute | solution.py:537
  8.6 15.1 %all-to-all-start = ((f32[16,1,128]{2,1,0:T(1,128)}), f32[16,1,128]{2,1,0:T(1,128)S(1)}, u32[]{:S(2)}, u32[]{:S(2)}) async-start(f32[16,1,128]{2,1,0:T(1,128)} %bitcast.1), calls=%async_computation | async-start | bytes 16384 | tf_op jit(solution)/shard_map/all_to_all | solution.py:524
  17.4 6.3 %copy-start = (f32[208,512]{1,0:T(8,128)}, f32[208,512]{1,0:T(8,128)S(1)}, u32[]{:S(2)}) copy-start(f32[208,512]{1,0:T(8,128)S(1)} %collective-permute-done.partner_ref) | copy-start | bytes 1277956
  17.5 6.3 %copy-start.1 = (f32[208,512]{1,0:T(8,128)}, f32[208,512]{1,0:T(8,128)S(1)}, u32[]{:S(2)}) copy-start(f32[208,512]{1,0:T(8,128)S(1)} %collective-permute-done.1.other_ref) | copy-start | bytes 1277956
  30.4 10.0 %collective-permute-start.2 = (f32[2,8,512]{2,1,0:T(8,128)S(1)}, f32[2,8,512]{2,1,0:T(8,128)S(1)}, u32[]{:S(2)}, u32[]{:S(2)}) collective-permute-start(f32[2,8,512]{2,1,0:T(8,128)S(1)} %get-tuple-element.19), channel_id=1, source_target_pairs={{0,1},{1,0},{2,3},{3,2},{4,5},{5,4},{6,7},{7,6},{8,9},{9,8},{10,11... | collective-permute-start | bytes 98312 | tf_op jit(solution)/shard_map/ppermute | solution.py:536
  30.7 9.7 %collective-permute-start.3 = (f32[2,8,512]{2,1,0:T(8,128)S(1)}, f32[2,8,512]{2,1,0:T(8,128)S(1)}, u32[]{:S(2)}, u32[]{:S(2)}) collective-permute-start(f32[2,8,512]{2,1,0:T(8,128)S(1)} %get-tuple-element.20), channel_id=1, source_target_pairs={{1,2},{2,1},{3,4},{4,3},{5,6},{6,5},{7,8},{8,7},{9,10},{10,9},{11,... | collective-permute-start | bytes 98312 | tf_op jit(solution)/shard_map/ppermute | solution.py:537
  31.4 15.4 %all-to-all-start.1 = ((f32[16,1,128]{2,1,0:T(1,128)}), f32[16,1,128]{2,1,0:T(1,128)S(1)}, u32[]{:S(2)}, u32[]{:S(2)}) async-start(f32[16,1,128]{2,1,0:T(1,128)} %bitcast.4), calls=%async_computation.1 | async-start | bytes 16384 | tf_op jit(solution)/shard_map/all_to_all | solution.py:524

commit v4 on v3

--- a/solution.py
+++ b/solution.py
@@ -15,6 +15,7 @@
 STRIP = 32
 CHUNK = 16
 CHUNKS = 2 * ROWS // CHUNK
+AHEAD = 3
 LANES = 128
 SLOTS = 56
 EDGE_AT = 5 * HALO
@@ -147,7 +148,7 @@
     odd = lax.axis_index("sub") % 2
     field_copy = pltpu.make_async_copy(rhs_ref, field, field_sem)
     field_copy.start()
-    for i in range(CHUNKS):
+    for i in range(AHEAD):
         basis_copy(i, basis_ref, held, sems).start()
     packs = []
     for n, (out_ref, up) in enumerate(((partner_ref, 1 - odd), (other_ref, odd))):
@@ -163,6 +164,11 @@
 
     def body(i, carry):
         basis_copy(i, basis_ref, held, sems).wait()
+
+        @pl.when(i + AHEAD < CHUNKS)
+        def _():
+            basis_copy(i + AHEAD, basis_ref, held, sems).start()
+
         restrict_chunk(i, held, field, sums)
         return carry
 
@@ -363,7 +369,7 @@
         self.held, self.low, self.high = held, low, high
         self.sides_ready = fetch(partner_ref, other_ref, low, high, EDGE_AT, side_sems)
         self.copies = [basis_copy(i, basis_ref, held, sems) for i in range(CHUNKS)]
-        for copy in self.copies:
+        for copy in self.copies[:AHEAD]:
             copy.start()
 
     def prolong(self, residual, inverse_ref, smooth, extended):
@@ -374,6 +380,8 @@
             if i == CHUNKS // 2:
                 self.prolong_edges(residual, smooth, extended)
             copy.wait()
+            if i + AHEAD < CHUNKS:
+                self.copies[i + AHEAD].start()
             coarse = jnp.dot(
                 matrix,
                 self.held[i].reshape(CHUNK * VECTORS, CELLS),
@@ -524,9 +532,8 @@
     return lax.all_to_all(rows, "sub", 0, 0, tiled=True)
 
 
-def from_everyone_reversed(rows):
-    order = [list(range(lax.axis_size("sub")))[::-1]]
-    return lax.all_to_all(rows, "sub", 0, 0, tiled=True, axis_index_groups=order)
+def gather_blocks(rows):
+    return lax.all_gather(rows[:8], "sub", axis=0)[:, 0]
 
 
 def swap(partner, other):
@@ -585,7 +592,7 @@
         first, second, coarse_inverse, partner, other, basis, smooth, image_smooth, rhs, image,
         viscosity, coupling,
     )
-    third = from_everyone_reversed(third)
+    third = gather_blocks(third)
     result, transposed = call(finish_kernel, "finish", [VMEM] * 5, [whole, f32(2, 3)], 1_000_000)(
         first, second, third, direction, second_direction
     )

time: 61.3 us -> 73.6 us (1.20)
  blocking collectives: 7.9 us -> 18.6 us
  Pallas kernels: 24.9 us -> 26.1 us
    all_gather x0 -> x1, blocking collectives: none -> 18.6 us  [gather_blocks(): return lax.all_gather(rows[:8], 'sub', axis=0)[:, 0]]
    all_to_all x1 -> x0, blocking collectives: 7.9 us -> none  [from_everyone_reversed(): lax.all_to_all(rows, 'sub', 0, 0, tiled=True, axis_index_groups=order)]
  transfers between devices with their start and end apart: 6 -> 6, of which waited for: 2 -> 2; matrix products, arithmetic and copies ran while one was open for 0% -> 0% of each run, Pallas kernels for 8% -> 7%
where the time goes in v4:
time: 73.6 us; the launch traced here: 73.1 us
  Pallas kernels  26.1 us (35%)
  starting transfers between devices  20.1 us (27%)
  blocking collectives  18.6 us (25%)
  waiting for transfers between devices  7.43 us (10%)
  between operations  0.84 us (1%)
    all_gather x1, blocking collectives, gather_blocks(): return lax.all_gather(rows[:8], 'sub', axis=0)[:, 0]  18.6 us
    all_to_all x2, starting transfers between devices, from_everyone(): return lax.all_to_all(rows, 'sub', 0, 0, tiled=True)  17.5 us
    all_to_all x2, waiting for transfers between devices, from_everyone(): return lax.all_to_all(rows, 'sub', 0, 0, tiled=True)  7.42 us
    pallas_call x1, Pallas kernels, on_device(): call(first_turn_kernel, 'first_turn', [VMEM] * 2 + [HBM] * 3 + [VMEM] * 4...  7.27 us
    pallas_call x1, Pallas kernels, on_device(): call(start_kernel, 'start', [HBM] * 5, [row, packed, packed], 10000000, [...  6.81 us
    pallas_call x1, Pallas kernels, on_device(): call(second_turn_kernel, 'second_turn', [VMEM] * 3 + [HBM] * 3 + [VMEM] *...  5.54 us
    pallas_call x1, Pallas kernels, on_device(): call(functools.partial(second_solve_kernel, count), 'second_solve', [SMEM...  2.97 us
    pallas_call x1, Pallas kernels, on_device(): call(functools.partial(first_solve_kernel, count), 'first_solve', [SMEM]...  2.15 us
  transfers between devices with their start and end apart: 6, of which 2 were waited for; matrix products, arithmetic and copies ran while one was open for 0% of the time, Pallas kernels for 7%

profile of v4, /device:TPU:0, one launch (start us, length us, event | category | flops | bytes accessed | tf_op | source)
XLA Modules:
  0.0 73.1 jit_solution(13229817529880386064)
XLA Ops:
  0.6 0.0 copy-start.2
  0.6 0.0 copy-start.4
  0.7 0.0 copy-start.3
  0.7 0.0 copy-start.5
  0.7 0.0 copy-start.6
  0.7 6.8 %start.1 = (f32[16,128]{1,0:T(8,128)}, f32[208,512]{1,0:T(8,128)S(1)}, f32[208,512]{1,0:T(8,128)S(1)}) custom-call(f32[2,64,512]{2,1,0:T(8,128)} %rhs_ref.7, f32[64,512]{1,0:T(8,128)} %visc_ref.9, f32[2,64,512]{2,1,0:T(8,128)} %coup_ref.9, f32[48,768]{1,0:T(8,128)} %inverse_ref.5, bf16[48,2,64,512]{3,2,1,0:T(8,128)(2,1)} %basis_ref.5), custom_call_target="tpu_custom_call" | custom-call | flops 10000000 | bytes 4000000 | tf_op jit(solution)/shard_map/start/pallas_call | solution.py:566
  7.5 0.5 collective-permute-start
  8.0 0.7 collective-permute-start.1
  8.7 8.8 %all-to-all-start = ((f32[16,1,128]{2,1,0:T(1,128)}), f32[16,1,128]{2,1,0:T(1,128)S(1)}, u32[]{:S(2)}, u32[]{:S(2)}) async-start(f32[16,1,128]{2,1,0:T(1,128)} %bitcast.1), calls=%async_computation | async-start | bytes 16384 | tf_op jit(solution)/shard_map/all_to_all | solution.py:532
  17.5 0.0 collective-permute-done.partner_ref
  17.5 0.0 copy-start
  17.5 0.0 collective-permute-done.1.other_ref
  17.5 0.0 copy-done.2
  17.5 0.0 copy-done.4
  17.5 0.0 copy-done.3
  17.6 0.0 copy-done.6
  17.6 0.0 copy-start.1
  17.6 2.2 %first_solve.1.smooth_ref = f32[2,80,512]{2,1,0:T(8,128)S(1)} custom-call(s32[16]{0:T(128)S(1)} %copy-done.6, f32[64,512]{1,0:T(8,128)S(1)} %copy-done.4, f32[2,64,512]{2,1,0:T(8,128)S(1)} %copy-done.2, f32[2,64,512]{2,1,0:T(8,128)S(1)} %copy-done.3, f32[208,512]{1,0:T(8,128)S(1)} %collective-permute-done.partner_ref, ...), custom_call_target="tpu_custom_call" | custom-call | flops 10000000 | bytes 4000000 | tf_op jit(solution)/shard_map/first_solve/pallas_call | solution.py:572
  19.7 4.1 %all-to-all-done = f32[16,1,128]{2,1,0:T(1,128)S(1)} async-done(((f32[16,1,128]{2,1,0:T(1,128)}), f32[16,1,128]{2,1,0:T(1,128)S(1)}, u32[]{:S(2)}, u32[]{:S(2)}) %all-to-all-start) | async-done | bytes 8224 | tf_op jit(solution)/shard_map/all_to_all | solution.py:532
  23.8 0.0 copy-done
  23.8 0.0 copy-done.5
  23.8 7.3 %first_turn.1 = (f32[2,64,512]{2,1,0:T(8,128)S(1)}, f32[2,64,512]{2,1,0:T(8,128)S(1)}, f32[2,8,512]{2,1,0:T(8,128)S(1)}, f32[2,8,512]{2,1,0:T(8,128)S(1)}, f32[16,128]{1,0:T(8,128)}) custom-call(f32[16,128]{1,0:T(8,128)S(1)} %bitcast.13, f32[48,768]{1,0:T(8,128)S(1)} %copy-done.5, f32[208,512]{1,0:T(8,128)} %copy-done, f32[208,512]{1,0:T(8,128)} %copy-done.1, ...), custom_call_target="tpu_custom_call" | custom-call | flops 20000000 | bytes 4000000 | tf_op jit(solution)/shard_map/first_turn/pallas_call | solution.py:577
  31.1 0.7 collective-permute-start.2
  31.8 0.7 collective-permute-start.3
  32.5 8.8 %all-to-all-start.1 = ((f32[16,1,128]{2,1,0:T(1,128)}), f32[16,1,128]{2,1,0:T(1,128)S(1)}, u32[]{:S(2)}, u32[]{:S(2)}) async-start(f32[16,1,128]{2,1,0:T(1,128)} %bitcast.4), calls=%async_computation.1 | async-start | bytes 16384 | tf_op jit(solution)/shard_map/all_to_all | solution.py:532
  41.3 0.0 collective-permute-done.2.partner_image_ref
  41.3 0.0 collective-permute-done.3.other_image_ref
  41.3 3.0 %second_solve.1.image_smooth_ref = f32[2,80,512]{2,1,0:T(8,128)S(1)} custom-call(s32[16]{0:T(128)S(1)} %copy-done.6, f32[64,512]{1,0:T(8,128)S(1)} %copy-done.4, f32[2,64,512]{2,1,0:T(8,128)S(1)} %copy-done.2, f32[2,64,512]{2,1,0:T(8,128)S(1)} %get-tuple-element.18.image_ref, f32[208,512]{1,0:T(8,128)} %copy-done, f32[208,512]{1,0:T(8,128)} %copy-done.1, ...), custom_call_target="tpu_custom_call" | custom-call | tf_op jit(solution)/shard_map/second_solve/pallas_call | solution.py:583
  44.3 3.3 %all-to-all-done.1 = f32[16,1,128]{2,1,0:T(1,128)S(1)} async-done(((f32[16,1,128]{2,1,0:T(1,128)}), f32[16,1,128]{2,1,0:T(1,128)S(1)}, u32[]{:S(2)}, u32[]{:S(2)}) %all-to-all-start.1) | async-done | bytes 8224 | tf_op jit(solution)/shard_map/all_to_all | solution.py:532
  47.6 5.5 %second_turn.1 = (f32[2,64,512]{2,1,0:T(8,128)S(1)}, f32[16,128]{1,0:T(8,128)S(1)}) custom-call(f32[16,128]{1,0:T(8,128)S(1)} %bitcast.14, f32[16,128]{1,0:T(8,128)S(1)} %bitcast.16, f32[48,768]{1,0:T(8,128)S(1)} %copy-done.5, f32[208,512]{1,0:T(8,128)} %copy-done, f32[208,512]{1,0:T(8,128)} %copy-done.1, bf16[48,2,64,512]{3,2,1,0:T(8,128)(2,1)} %basis_ref.5, ...), custom_call_target="tpu_custom_call" | custom-call | flops 20000000 | bytes 4000000 | tf_op jit(solution)/shard_map/second_turn/pallas_call | solution.py:588
  53.1 18.6 %all-gather = f32[128,128]{1,0:T(8,128)S(1)} all-gather(f32[8,128]{1,0:T(8,128)S(1)} %slice.6), channel_id=2, replica_groups=mesh['groups'=2,'sub'=16] {'sub'}, dimensions={0}, use_global_device_ids=true | all-gather | bytes 69632 | tf_op jit(solution)/shard_map/all_gather | solution.py:536
  71.7 1.4 %finish.1 = (f32[2,64,512]{2,1,0:T(8,128)}, f32[2,3]{1,0:T(2,128)}) custom-call(f32[16,128]{1,0:T(8,128)S(1)} %bitcast.15, f32[16,128]{1,0:T(8,128)S(1)} %bitcast.17, f32[16,128]{1,0:T(8,128)S(1)} %bitcast.18, f32[2,64,512]{2,1,0:T(8,128)S(1)} %get-tuple-element.22.first_direction_ref, f32[2,64,512]{2,1,0:T(8,128)S(1)} %get-tuple-element.23.second_direction_ref), custom_call_target="tpu_custom_call" | custom-call | flops 1000000 | bytes 4000000 | tf_op jit(solution)/shard_map/finish/pallas_call | solution.py:596
  (3 shorter events, 0.0 us)
Async XLA Ops:
  0.6 16.9 %copy-start.2 = (f32[2,64,512]{2,1,0:T(8,128)S(1)}, f32[2,64,512]{2,1,0:T(8,128)}, u32[]{:S(2)}) copy-start(f32[2,64,512]{2,1,0:T(8,128)} %coup_ref.9) | copy-start | bytes 786436
  0.6 16.9 %copy-start.4 = (f32[64,512]{1,0:T(8,128)S(1)}, f32[64,512]{1,0:T(8,128)}, u32[]{:S(2)}) copy-start(f32[64,512]{1,0:T(8,128)} %visc_ref.9) | copy-start | bytes 393220
  0.7 16.9 %copy-start.3 = (f32[2,64,512]{2,1,0:T(8,128)S(1)}, f32[2,64,512]{2,1,0:T(8,128)}, u32[]{:S(2)}) copy-start(f32[2,64,512]{2,1,0:T(8,128)} %rhs_ref.7) | copy-start | bytes 786436
  0.7 23.2 %copy-start.5 = (f32[48,768]{1,0:T(8,128)S(1)}, f32[48,768]{1,0:T(8,128)}, u32[]{:S(2)}) copy-start(f32[48,768]{1,0:T(8,128)} %inverse_ref.5) | copy-start | bytes 442372
  0.7 16.9 %copy-start.6 = (s32[16]{0:T(128)S(1)}, s32[16]{0:T(128)}, u32[]{:S(2)}) copy-start(s32[16]{0:T(128)} %margin_ref.3) | copy-start | bytes 196
  7.5 10.0 %collective-permute-start = (f32[208,512]{1,0:T(8,128)S(1)}, f32[208,512]{1,0:T(8,128)S(1)}, u32[]{:S(2)}, u32[]{:S(2)}) collective-permute-start(f32[208,512]{1,0:T(8,128)S(1)} %get-tuple-element.15), channel_id=1, source_target_pairs={{0,1},{1,0},{2,3},{3,2},{4,5},{5,4},{6,7},{7,6},{8,9},{9,8},{10,11... | collective-permute-start | bytes 1277960 | tf_op jit(solution)/shard_map/ppermute | solution.py:543
  8.0 9.5 %collective-permute-start.1 = (f32[208,512]{1,0:T(8,128)S(1)}, f32[208,512]{1,0:T(8,128)S(1)}, u32[]{:S(2)}, u32[]{:S(2)}) collective-permute-start(f32[208,512]{1,0:T(8,128)S(1)} %get-tuple-element.16), channel_id=1, source_target_pairs={{1,2},{2,1},{3,4},{4,3},{5,6},{6,5},{7,8},{8,7},{9,10},{10,9},{11,... | collective-permute-start | bytes 1277960 | tf_op jit(solution)/shard_map/ppermute | solution.py:544
  8.7 15.1 %all-to-all-start = ((f32[16,1,128]{2,1,0:T(1,128)}), f32[16,1,128]{2,1,0:T(1,128)S(1)}, u32[]{:S(2)}, u32[]{:S(2)}) async-start(f32[16,1,128]{2,1,0:T(1,128)} %bitcast.1), calls=%async_computation | async-start | bytes 16384 | tf_op jit(solution)/shard_map/all_to_all | solution.py:532
  17.5 6.3 %copy-start = (f32[208,512]{1,0:T(8,128)}, f32[208,512]{1,0:T(8,128)S(1)}, u32[]{:S(2)}) copy-start(f32[208,512]{1,0:T(8,128)S(1)} %collective-permute-done.partner_ref) | copy-start | bytes 1277956
  17.6 6.3 %copy-start.1 = (f32[208,512]{1,0:T(8,128)}, f32[208,512]{1,0:T(8,128)S(1)}, u32[]{:S(2)}) copy-start(f32[208,512]{1,0:T(8,128)S(1)} %collective-permute-done.1.other_ref) | copy-start | bytes 1277956
  31.1 10.1 %collective-permute-start.2 = (f32[2,8,512]{2,1,0:T(8,128)S(1)}, f32[2,8,512]{2,1,0:T(8,128)S(1)}, u32[]{:S(2)}, u32[]{:S(2)}) collective-permute-start(f32[2,8,512]{2,1,0:T(8,128)S(1)} %get-tuple-element.19), channel_id=1, source_target_pairs={{0,1},{1,0},{2,3},{3,2},{4,5},{5,4},{6,7},{7,6},{8,9},{9,8},{10,11... | collective-permute-start | bytes 98312 | tf_op jit(solution)/shard_map/ppermute | solution.py:543
  31.8 9.4 %collective-permute-start.3 = (f32[2,8,512]{2,1,0:T(8,128)S(1)}, f32[2,8,512]{2,1,0:T(8,128)S(1)}, u32[]{:S(2)}, u32[]{:S(2)}) collective-permute-start(f32[2,8,512]{2,1,0:T(8,128)S(1)} %get-tuple-element.20), channel_id=1, source_target_pairs={{1,2},{2,1},{3,4},{4,3},{5,6},{6,5},{7,8},{8,7},{9,10},{10,9},{11,... | collective-permute-start | bytes 98312 | tf_op jit(solution)/shard_map/ppermute | solution.py:544
  32.5 15.1 %all-to-all-start.1 = ((f32[16,1,128]{2,1,0:T(1,128)}), f32[16,1,128]{2,1,0:T(1,128)S(1)}, u32[]{:S(2)}, u32[]{:S(2)}) async-start(f32[16,1,128]{2,1,0:T(1,128)} %bitcast.4), calls=%async_computation.1 | async-start | bytes 16384 | tf_op jit(solution)/shard_map/all_to_all | solution.py:532

commit v5 on v3

--- a/solution.py
+++ b/solution.py
@@ -15,6 +15,8 @@
 STRIP = 32
 CHUNK = 16
 CHUNKS = 2 * ROWS // CHUNK
+PIECE = 6
+PIECES = VECTORS // PIECE
 LANES = 128
 SLOTS = 56
 EDGE_AT = 5 * HALO
@@ -27,7 +29,6 @@
 VMEM = pl.BlockSpec(memory_space=pltpu.VMEM)
 SMEM = pl.BlockSpec(memory_space=pltpu.SMEM)
 HBM = pl.BlockSpec(memory_space=pltpu.HBM)
-ANY = pl.BlockSpec(memory_space=pl.ANY)
 
 
 def coarse_rows(columns):
@@ -68,20 +69,22 @@
 
 
 def basis_copy(i, basis_ref, held, sems):
-    rows = pl.ds(pl.multiple_of(CHUNK * (i % 4), CHUNK), CHUNK)
-    return pltpu.make_async_copy(basis_ref.at[:, i // 4, rows, :], held.at[i], sems.at[i])
-
-
-def restrict_chunk(i, held, field, sums):
-    a = i // 4
-    start = pl.multiple_of((i % 4) * CHUNK, CHUNK)
-    parts = [field[a, pl.ds(start, CHUNK), pl.ds(LANES * c, LANES)] for c in range(4)]
-    for k in range(VECTORS):
+    vectors = pl.ds(PIECE * i, PIECE)
+    return pltpu.make_async_copy(basis_ref.at[vectors], held.at[vectors], sems.at[i])
+
+
+def restrict_piece(i, held, field, sums):
+    for n in range(PIECE):
+        k = PIECE * i + n
         total = None
-        for c in range(4):
-            term = held[i, k, :, pl.ds(LANES * c, LANES)].astype(jnp.float32) * parts[c]
-            total = term if total is None else total + term
-        sums[8 * k : 8 * k + 8, :] += total[:8] + total[8:]
+        for a in range(2):
+            for r in range(0, ROWS, CHUNK):
+                for c in range(0, CELLS, LANES):
+                    rows, cells = slice(r, r + CHUNK), slice(c, c + LANES)
+                    term = held[k, a, rows, cells].astype(jnp.float32) * field[a, rows, cells]
+                    term = term[:8] + term[8:]
+                    total = term if total is None else total + term
+        sums[pl.ds(pl.multiple_of(8 * k, 8), 8), :] = total
 
 
 def fold(field):
@@ -141,13 +144,13 @@
 
 def start_kernel(
     rhs_ref, visc_ref, coup_ref, inverse_ref, basis_ref,
-    sums_ref, partner_ref, other_ref,
-    held, field, sums, field_sem, sems, pack_sems,
+    sums_ref, partner_ref, other_ref, held,
+    field, sums, field_sem, sems, pack_sems,
 ):
     odd = lax.axis_index("sub") % 2
     field_copy = pltpu.make_async_copy(rhs_ref, field, field_sem)
     field_copy.start()
-    for i in range(CHUNKS):
+    for i in range(PIECES):
         basis_copy(i, basis_ref, held, sems).start()
     packs = []
     for n, (out_ref, up) in enumerate(((partner_ref, 1 - odd), (other_ref, odd))):
@@ -163,16 +166,17 @@
 
     def body(i, carry):
         basis_copy(i, basis_ref, held, sems).wait()
-        restrict_chunk(i, held, field, sums)
+        restrict_piece(i, held, field, sums)
         return carry
 
-    lax.fori_loop(0, CHUNKS, body, 0)
+    lax.fori_loop(0, PIECES, body, 0)
     picker = lax.broadcasted_iota(jnp.int32, (VECTORS, CHUNK * VECTORS), 0) * CHUNK
     place = lax.broadcasted_iota(jnp.int32, (VECTORS, CHUNK * VECTORS), 1)
     for out_ref, up in ((partner_ref, 1 - odd), (other_ref, odd)):
         pick = (place == picker + up * (CHUNK - 1)).astype(jnp.float32).astype(jnp.bfloat16)
+        first_row = pl.multiple_of(up * (ROWS - CHUNK), CHUNK)
         for a in range(2):
-            rows = held[4 * a + 3 * up].reshape(CHUNK * VECTORS, CELLS)
+            rows = held[:, a, pl.ds(first_row, CHUNK), :].reshape(CHUNK * VECTORS, CELLS)
             at = EDGE_AT + VECTORS * a
             out_ref[at : at + VECTORS] = jnp.dot(pick, rows, preferred_element_type=jnp.float32)
     for copy in packs:
@@ -180,31 +184,17 @@
     send_sums(sums, sums_ref)
 
 
-def fetch(partner_ref, other_ref, low_ref, high_ref, first_row, sems):
-    odd = lax.axis_index("sub") % 2
-    rows = pl.ds(first_row, low_ref.shape[0])
-
-    def copies(below_ref, above_ref):
-        return (
-            pltpu.make_async_copy(below_ref.at[rows], low_ref, sems.at[0]),
-            pltpu.make_async_copy(above_ref.at[rows], high_ref, sems.at[1]),
-        )
-
-    @pl.when(odd == 1)
-    def _():
-        for copy in copies(partner_ref, other_ref):
-            copy.start()
-
-    @pl.when(odd == 0)
-    def _():
-        for copy in copies(other_ref, partner_ref):
-            copy.start()
-
-    def finish():
-        for copy in copies(partner_ref, other_ref):
-            copy.wait()
-
-    return finish
+class Neighbour:
+    def __init__(self, first_ref, second_ref):
+        self.odd = lax.axis_index("sub") % 2 == 1
+        self.first, self.second = first_ref, second_ref
+
+    def __getitem__(self, index):
+        return jnp.where(self.odd, self.first[index], self.second[index])
+
+
+def neighbours_of(partner_ref, other_ref):
+    return Neighbour(partner_ref, other_ref), Neighbour(other_ref, partner_ref)
 
 
 def solve(count, margin_ref, visc_ref, coup_ref, field_ref, low_ref, high_ref, edges, out_ref):
@@ -269,30 +259,6 @@
         out_ref[a, EXT - STRIP :] += shares[EXT + STRIP :]
 
 
-def first_solve_kernel(
-    count, margin_ref, visc_ref, coup_ref, rhs_ref, partner_ref, other_ref,
-    out_ref,
-    low, high, sems,
-):
-    fetch(partner_ref, other_ref, low, high, 0, sems)()
-    rows = [slice(HALO * (3 + a), HALO * (4 + a)) for a in range(2)]
-    edges = [(low[rows[a]], high[rows[a]]) for a in range(2)]
-    solve(count, margin_ref, visc_ref, coup_ref, rhs_ref, low, high, edges, out_ref)
-
-
-def second_solve_kernel(
-    count, margin_ref, visc_ref, coup_ref, image_ref, partner_ref, other_ref,
-    partner_image_ref, other_image_ref,
-    out_ref,
-    low, high, low_image, high_image, sems, image_sems,
-):
-    images = fetch(partner_image_ref, other_image_ref, low_image, high_image, 0, image_sems)
-    fetch(partner_ref, other_ref, low, high, 0, sems)()
-    images()
-    edges = [(low_image[a], high_image[a]) for a in range(2)]
-    solve(count, margin_ref, visc_ref, coup_ref, image_ref, low, high, edges, out_ref)
-
-
 def line_up(residuals):
     devices = residuals.shape[0]
     lane = lax.broadcasted_iota(jnp.int32, (1, LANES), 1)
@@ -320,7 +286,7 @@
 
 def lift_packed(ref, residual):
     columns = residual.shape[1]
-    at, total = INVERSE_AT, None
+    at, total = EDGE_AT + INVERSE_AT, None
     for c in range(0, columns - 511, 512):
         term = jnp.sum(ref[at : at + VECTORS] * residual[:, c : c + 512], 1, keepdims=True)
         total = term if total is None else total + term
@@ -341,10 +307,8 @@
 
 
 def edge_values(ref, lifted):
-    return [
-        jnp.sum(ref[VECTORS * a : VECTORS * (a + 1)] * lifted, 0, keepdims=True)
-        for a in range(2)
-    ]
+    starts = [EDGE_AT + VECTORS * a for a in range(2)]
+    return [jnp.sum(ref[at : at + VECTORS] * lifted, 0, keepdims=True) for at in starts]
 
 
 def spread(lifted):
@@ -358,39 +322,27 @@
     return jnp.where(place == row, line, 0.0).astype(jnp.bfloat16)
 
 
-class Coarse:
-    def __init__(self, partner_ref, other_ref, basis_ref, held, low, high, sems, side_sems):
-        self.held, self.low, self.high = held, low, high
-        self.sides_ready = fetch(partner_ref, other_ref, low, high, EDGE_AT, side_sems)
-        self.copies = [basis_copy(i, basis_ref, held, sems) for i in range(CHUNKS)]
-        for copy in self.copies:
-            copy.start()
-
-    def prolong(self, residual, inverse_ref, smooth, extended):
-        matrix = spread(lift(inverse_ref, residual))
-        for i, copy in enumerate(self.copies):
-            a, start = i // 4, HALO + CHUNK * (i % 4)
-            rows = slice(start, start + CHUNK)
-            if i == CHUNKS // 2:
-                self.prolong_edges(residual, smooth, extended)
-            copy.wait()
-            coarse = jnp.dot(
-                matrix,
-                self.held[i].reshape(CHUNK * VECTORS, CELLS),
-                preferred_element_type=jnp.float32,
+def prolong(residual, inverse_ref, held, extended):
+    matrix = spread(lift(inverse_ref, residual))
+    for a in range(2):
+        for r in range(0, ROWS, CHUNK):
+            rows = held[:, a, r : r + CHUNK, :].reshape(CHUNK * VECTORS, CELLS)
+            extended[a, HALO + r : HALO + r + CHUNK] = jnp.dot(
+                matrix, rows, preferred_element_type=jnp.float32
             )
-            extended[a, rows] = smooth(a, rows) + coarse
-
-    def prolong_edges(self, residual, smooth, extended):
-        self.sides_ready()
-        low_edge = edge_values(self.low, lift_packed(self.low, residual))
-        high_edge = edge_values(self.high, lift_packed(self.high, residual))
-        place = lax.broadcasted_iota(jnp.int32, (HALO, CELLS), 0)
-        for a in range(2):
-            rows = slice(0, HALO)
-            extended[a, rows] = smooth(a, rows) + jnp.where(place == HALO - 1, low_edge[a], 0.0)
-            rows = slice(EXT - HALO, EXT)
-            extended[a, rows] = smooth(a, rows) + jnp.where(place == 0, high_edge[a], 0.0)
+
+
+def add_smooth(residual, low, high, smooth, extended):
+    low_edge = edge_values(low, lift_packed(low, residual))
+    high_edge = edge_values(high, lift_packed(high, residual))
+    place = lax.broadcasted_iota(jnp.int32, (HALO, CELLS), 0)
+    for a in range(2):
+        rows = slice(HALO, HALO + ROWS)
+        extended[a, rows] += smooth(a, rows)
+        rows = slice(0, HALO)
+        extended[a, rows] = smooth(a, rows) + jnp.where(place == HALO - 1, low_edge[a], 0.0)
+        rows = slice(EXT - HALO, EXT)
+        extended[a, rows] = smooth(a, rows) + jnp.where(place == 0, high_edge[a], 0.0)
 
 
 def lane_total(received, lane):
@@ -398,20 +350,21 @@
 
 
 def first_turn_kernel(
-    sums_ref, inverse_ref, partner_ref, other_ref, basis_ref, smooth_ref, rhs_ref, visc_ref,
+    count, margin_ref, sums_ref, inverse_ref, partner_ref, other_ref, held, rhs_ref, visc_ref,
     coup_ref,
-    direction_ref, image_ref, partner_rows_ref, other_rows_ref, next_ref,
-    held, low, high, sems, side_sems, extended, sums,
+    direction_ref, image_ref, smooth_ref, partner_rows_ref, other_rows_ref, next_ref,
+    extended, sums,
 ):
-    coarse = Coarse(partner_ref, other_ref, basis_ref, held, low, high, sems, side_sems)
     received = sums_ref[...]
     over_beta = 1.0 / jnp.sqrt(lane_total(received, VECTORS))
     residual = line_up(received) * over_beta
-    coarse.prolong(
-        residual,
-        inverse_ref,
-        lambda a, rows: smooth_ref[a, rows] * over_beta,
-        extended,
+    prolong(residual, inverse_ref, held, extended)
+    low, high = neighbours_of(partner_ref, other_ref)
+    starts = [HALO * (3 + a) for a in range(2)]
+    edges = [(low[at : at + HALO], high[at : at + HALO]) for at in starts]
+    solve(count, margin_ref, visc_ref, coup_ref, rhs_ref, low, high, edges, smooth_ref)
+    add_smooth(
+        residual, low, high, lambda a, rows: smooth_ref[a, rows] * over_beta, extended
     )
     images = apply_operator(
         [extended[a] for a in range(2)], visc_ref[...], [coup_ref[a] for a in range(2)]
@@ -429,10 +382,10 @@
     sums[at + 8 : at + 16] = fold([images[a] * images[a] for a in range(2)])
 
     def body(i, carry):
-        restrict_chunk(i, held, image_ref, sums)
+        restrict_piece(i, held, image_ref, sums)
         return carry
 
-    lax.fori_loop(0, CHUNKS, body, 0)
+    lax.fori_loop(0, PIECES, body, 0)
     send_sums(sums, next_ref)
 
 
@@ -444,21 +397,26 @@
 
 
 def second_turn_kernel(
-    first_ref, second_ref, inverse_ref, partner_ref, other_ref, basis_ref, smooth_ref,
-    image_smooth_ref, rhs_ref, image_ref, visc_ref, coup_ref,
+    count, margin_ref, first_ref, second_ref, inverse_ref, partner_ref, other_ref,
+    partner_rows_ref, other_rows_ref, held, smooth_ref, rhs_ref, image_ref, visc_ref, coup_ref,
     direction_ref, next_ref,
-    held, low, high, sems, side_sems, extended, sums,
+    image_smooth, extended, sums,
 ):
-    coarse = Coarse(partner_ref, other_ref, basis_ref, held, low, high, sems, side_sems)
     first, second = first_ref[...], second_ref[...]
     beta, h_00, h_10 = first_column(first, second)
     ratio = h_00 / beta
     over = 1.0 / h_10
     residual = (line_up(second) - ratio * line_up(first)) * over
-    coarse.prolong(
+    prolong(residual, inverse_ref, held, extended)
+    low, high = neighbours_of(partner_ref, other_ref)
+    low_rows, high_rows = neighbours_of(partner_rows_ref, other_rows_ref)
+    edges = [(low_rows[a], high_rows[a]) for a in range(2)]
+    solve(count, margin_ref, visc_ref, coup_ref, image_ref, low, high, edges, image_smooth)
+    add_smooth(
         residual,
-        inverse_ref,
-        lambda a, rows: (image_smooth_ref[a, rows] - ratio * smooth_ref[a, rows]) * over,
+        low,
+        high,
+        lambda a, rows: (image_smooth[a, rows] - ratio * smooth_ref[a, rows]) * over,
         extended,
     )
     images = apply_operator(
@@ -543,47 +501,31 @@
     columns = coarse_inverse.shape[1]
     f32 = lambda *shape: jax.ShapeDtypeStruct(shape, jnp.float32)
     dma = lambda *shape: pltpu.SemaphoreType.DMA(shape)
-    held = pltpu.VMEM((CHUNKS, VECTORS, CHUNK, CELLS), jnp.bfloat16)
     field = pltpu.VMEM((2, ROWS, CELLS), jnp.float32)
+    extended = pltpu.VMEM((2, EXT, CELLS), jnp.float32)
     sums = pltpu.VMEM((8 * SLOTS, LANES), jnp.float32)
-    edge_scratch = [pltpu.VMEM((EDGE_AT, CELLS), jnp.float32)] * 2
-    image_scratch = [pltpu.VMEM((2, HALO, CELLS), jnp.float32)] * 2
-    turn_scratch = (
-        [held]
-        + [pltpu.VMEM((coarse_rows(columns), CELLS), jnp.float32)] * 2
-        + [dma(CHUNKS), dma(2), pltpu.VMEM((2, EXT, CELLS), jnp.float32), sums]
-    )
     row, whole, edge = f32(count, LANES), f32(2, ROWS, CELLS), f32(2, HALO, CELLS)
     packed, smoothed = f32(EDGE_AT + coarse_rows(columns), CELLS), f32(2, EXT, CELLS)
-    basis = in_hbm(coarse_basis)
-    first, partner, other = call(
-        start_kernel, "start", [HBM] * 5, [row, packed, packed], 10_000_000,
-        [held, field, sums, dma(), dma(CHUNKS), dma(2 * pack_count(columns))],
-    )(in_hbm(rhs), in_hbm(viscosity), in_hbm(coupling), in_hbm(coarse_inverse), basis)
+    basis = jax.ShapeDtypeStruct(coarse_basis.shape, jnp.bfloat16)
+    arguments = (rhs, viscosity, coupling, coarse_inverse, coarse_basis)
+    first, partner, other, held = call(
+        start_kernel, "start", [HBM] * 5, [row, packed, packed, basis], 10_000_000,
+        [field, sums, dma(), dma(PIECES), dma(2 * pack_count(columns))],
+    )(*map(in_hbm, arguments))
     partner, other = swap(partner, other)
     first = from_everyone(first)
-    (smooth,) = call(
-        functools.partial(first_solve_kernel, count), "first_solve",
-        [SMEM] + [VMEM] * 3 + [ANY] * 2, [smoothed], 10_000_000, edge_scratch + [dma(2)],
-    )(margin_rows, viscosity, coupling, rhs, partner, other)
-    partner, other = in_hbm(partner), in_hbm(other)
-    direction, image, partner_rows, other_rows, second = call(
-        first_turn_kernel, "first_turn", [VMEM] * 2 + [HBM] * 3 + [VMEM] * 4,
-        [whole, whole, edge, edge, row], 20_000_000, turn_scratch,
-    )(first, coarse_inverse, partner, other, basis, smooth, rhs, viscosity, coupling)
+    direction, image, smooth, partner_rows, other_rows, second = call(
+        functools.partial(first_turn_kernel, count), "first_turn", [SMEM] + [VMEM] * 8,
+        [whole, whole, smoothed, edge, edge, row], 20_000_000, [extended, sums],
+    )(margin_rows, first, coarse_inverse, partner, other, held, rhs, viscosity, coupling)
     partner_rows, other_rows = swap(partner_rows, other_rows)
     second = from_everyone(second)
-    (image_smooth,) = call(
-        functools.partial(second_solve_kernel, count), "second_solve",
-        [SMEM] + [VMEM] * 3 + [HBM] * 2 + [ANY] * 2, [smoothed], 0,
-        edge_scratch + image_scratch + [dma(2)] * 2, 0,
-    )(margin_rows, viscosity, coupling, image, partner, other, partner_rows, other_rows)
     second_direction, third = call(
-        second_turn_kernel, "second_turn", [VMEM] * 3 + [HBM] * 3 + [VMEM] * 6, [whole, row],
-        20_000_000, turn_scratch,
+        functools.partial(second_turn_kernel, count), "second_turn", [SMEM] + [VMEM] * 13,
+        [whole, row], 20_000_000, [extended, extended, sums],
     )(
-        first, second, coarse_inverse, partner, other, basis, smooth, image_smooth, rhs, image,
-        viscosity, coupling,
+        margin_rows, first, second, coarse_inverse, partner, other, partner_rows, other_rows,
+        held, smooth, rhs, image, viscosity, coupling,
     )
     third = from_everyone_reversed(third)
     result, transposed = call(finish_kernel, "finish", [VMEM] * 5, [whole, f32(2, 3)], 1_000_000)(

time: 61.3 us -> 56.4 us (0.920)
  blocking collectives: 7.9 us -> 37 us
  starting transfers between devices: 20 us -> 1.87 us
  Pallas kernels: 24.9 us -> 16.5 us
  waiting for transfers between devices: 7.43 us -> 0.01 us
    all_to_all x0 -> x2, blocking collectives: none -> 29.1 us  [from_everyone(): return lax.all_to_all(rows, 'sub', 0, 0, tiled=True)]
    all_to_all x2 -> x0, starting transfers between devices: 17.8 us -> none  [from_everyone(): return lax.all_to_all(rows, 'sub', 0, 0, tiled=True)]
    pallas_call x5 -> x3, Pallas kernels: 23.5 us -> 15.1 us  [the longest x1 6.11 us: on_device(): call(start_kernel, 'start', [HBM] * 5, [row, packed, packed, basis], 1000...]
    all_to_all x2 -> x0, waiting for transfers between devices: 7.42 us -> none  [from_everyone(): return lax.all_to_all(rows, 'sub', 0, 0, tiled=True)]
  transfers between devices with their start and end apart: 6 -> 4, of which waited for: 2 -> 0; matrix products, arithmetic and copies ran while one was open for 0% -> 0% of each run, Pallas kernels for 8% -> 0%
where the time goes in v5:
time: 56.4 us; the launch traced here: 56.1 us
  blocking collectives  37 us (66%)
  Pallas kernels  16.5 us (29%)
  starting transfers between devices  1.87 us (3%)
  between operations  0.74 us (1%)
    all_to_all x2, blocking collectives, from_everyone(): return lax.all_to_all(rows, 'sub', 0, 0, tiled=True)  29.1 us
    all_to_all x1, blocking collectives, from_everyone_reversed(): lax.all_to_all(rows, 'sub', 0, 0, tiled=True, axis_index_groups=order)  7.92 us
    pallas_call x1, Pallas kernels, on_device(): call(start_kernel, 'start', [HBM] * 5, [row, packed, packed, basis], 1000...  6.11 us
    pallas_call x1, Pallas kernels, on_device(): call(functools.partial(first_turn_kernel, count), 'first_turn', [SMEM] +...  5.15 us
    pallas_call x1, Pallas kernels, on_device(): call(functools.partial(second_turn_kernel, count), 'second_turn', [SMEM]...  3.86 us
    pallas_call x1, Pallas kernels, on_device(): call(finish_kernel, 'finish', [VMEM] * 5, [whole, f32(2, 3)], 1000000)  1.37 us
    ppermute x2, starting transfers between devices, swap(): lax.ppermute(other, 'sub', both(range(1, count - 1, 2)))  1.36 us
  transfers between devices with their start and end apart: 4, of which 0 were waited for; matrix products, arithmetic and copies ran while one was open for 0% of the time, Pallas kernels for 0%

profile of v5, /device:TPU:0, one launch (start us, length us, event | category | flops | bytes accessed | tf_op | source)
XLA Modules:
  0.0 56.1 jit_solution(9521767952920275696)
XLA Ops:
  0.6 0.0 copy-start.2
  0.6 0.0 copy-start.1
  0.7 0.0 copy-start.3
  0.7 0.0 copy-start
  0.7 0.0 copy-start.4
  0.7 6.1 %start.1 = (f32[16,128]{1,0:T(8,128)S(1)}, f32[208,512]{1,0:T(8,128)S(1)}, f32[208,512]{1,0:T(8,128)S(1)}, bf16[48,2,64,512]{3,2,1,0:T(8,128)(2,1)S(1)}) custom-call(f32[2,64,512]{2,1,0:T(8,128)} %rhs_ref.5, f32[64,512]{1,0:T(8,128)} %visc_ref.5, f32[2,64,512]{2,1,0:T(8,128)} %coup_ref.5, f32[48,768]{1,0:T(8,128)} %inverse_ref.5, ...), custom_call_target="tpu_custom_call" | custom-call | flops 10000000 | bytes 4000000 | tf_op jit(solution)/shard_map/start/pallas_call | solution.py:511
  6.8 0.5 collective-permute-start
  7.3 0.7 %collective-permute-start.1 = (f32[208,512]{1,0:T(8,128)S(1)}, f32[208,512]{1,0:T(8,128)S(1)}, u32[]{:S(2)}, u32[]{:S(2)}) collective-permute-start(f32[208,512]{1,0:T(8,128)S(1)} %get-tuple-element.18), channel_id=1, source_target_pairs={{1,2},{2,1},{3,4},{4,3},{5,6},{6,5},{7,8},{8,7},{9,10},{10,9},{11,... | collective-permute-start | bytes 1277960 | tf_op jit(solution)/shard_map/ppermute | solution.py:495
  8.0 15.0 %all_to_all.33 = f32[16,1,128]{2,1,0:T(1,128)S(1)} all-to-all(f32[16,1,128]{2,1,0:T(1,128)S(1)} %bitcast.20), channel_id=1, replica_groups=mesh['groups'=2,'sub'=16] {'sub'}, dimensions={0} | all-to-all | bytes 16384 | tf_op jit(solution)/shard_map/all_to_all | solution.py:482
  23.0 0.0 collective-permute-done.partner_ref
  23.0 0.0 collective-permute-done.1.other_ref
  23.0 0.0 copy-done.2
  23.0 0.0 copy-done.1
  23.0 0.0 copy-done.3
  23.0 0.0 copy-done
  23.0 0.0 copy-done.4
  23.0 5.1 %first_turn.1 = (f32[2,64,512]{2,1,0:T(8,128)S(1)}, f32[2,64,512]{2,1,0:T(8,128)S(1)}, f32[2,80,512]{2,1,0:T(8,128)S(1)}, f32[2,8,512]{2,1,0:T(8,128)S(1)}, f32[...) custom-call(s32[16]{0:T(128)S(1)} %copy-done.4, f32[16,128]{1,0:T(8,128)S(1)} %bitcast.13, f32[48,768]{1,0:T(8,128)S(1)} %copy-done.2, ...), custom_call_target="tpu_custom_call" | custom-call | flops 20000000 | bytes 4000000 | tf_op jit(solution)/shard_map/first_turn/pallas_call | solution.py:517
  28.2 0.0 collective-permute-start.2
  28.2 0.7 %collective-permute-start.3 = (f32[2,8,512]{2,1,0:T(8,128)S(1)}, f32[2,8,512]{2,1,0:T(8,128)S(1)}, u32[]{:S(2)}, u32[]{:S(2)}) collective-permute-start(f32[2,8,512]{2,1,0:T(8,128)S(1)} %get-tuple-element.22), channel_id=1, source_target_pairs={{1,2},{2,1},{3,4},{4,3},{5,6},{6,5},{7,8},{8,7},{9,10},{10,9},{11,... | collective-permute-start | bytes 98312 | tf_op jit(solution)/shard_map/ppermute | solution.py:495
  28.9 14.1 %all_to_all.34 = f32[16,1,128]{2,1,0:T(1,128)S(1)} all-to-all(f32[16,1,128]{2,1,0:T(1,128)S(1)} %bitcast.19), channel_id=1, replica_groups=mesh['groups'=2,'sub'=16] {'sub'}, dimensions={0} | all-to-all | bytes 16384 | tf_op jit(solution)/shard_map/all_to_all | solution.py:482
  43.0 0.0 collective-permute-done.2.partner_rows_ref
  43.0 0.0 collective-permute-done.3.other_rows_ref
  43.0 3.9 %second_turn.1 = (f32[2,64,512]{2,1,0:T(8,128)S(1)}, f32[16,128]{1,0:T(8,128)S(1)}) custom-call(s32[16]{0:T(128)S(1)} %copy-done.4, f32[16,128]{1,0:T(8,128)S(1)} %bitcast.14, f32[16,128]{1,0:T(8,128)S(1)} %bitcast.16, f32[48,768]{1,0:T(8,128)S(1)} %copy-done.2, f32[208,512]{1,0:T(8,128)S(1)} %collective-permute-done.partner_ref, ...), custom_call_target="tpu_custom_call" | custom-call | flops 20000000 | bytes 4000000 | tf_op jit(solution)/shard_map/second_turn/pallas_call | solution.py:523
  46.8 7.9 %all_to_all.35 = f32[16,1,128]{2,1,0:T(1,128)S(1)} all-to-all(f32[16,1,128]{2,1,0:T(1,128)S(1)} %bitcast.21), channel_id=1, replica_groups={{15,14,13,12,11,10,9,8,7,6,5,4,3,2,1,0},{31,30,29,28,27,26,25,24,23,22,..., dimensions={0} | all-to-all | bytes 16384 | tf_op jit(solution)/shard_map/all_to_all | solution.py:487
  54.8 1.4 %finish.1 = (f32[2,64,512]{2,1,0:T(8,128)}, f32[2,3]{1,0:T(2,128)}) custom-call(f32[16,128]{1,0:T(8,128)S(1)} %bitcast.15, f32[16,128]{1,0:T(8,128)S(1)} %bitcast.17, f32[16,128]{1,0:T(8,128)S(1)} %bitcast.18, f32[2,64,512]{2,1,0:T(8,128)S(1)} %get-tuple-element.26.first_direction_ref, f32[2,64,512]{2,1,0:T(8,128)S(1)} %get-tuple-element.27.second_direction_ref), custom_call_target="tpu_custom_call" | custom-call | flops 1000000 | bytes 4000000 | tf_op jit(solution)/shard_map/finish/pallas_call | solution.py:531
Async XLA Ops:
  0.6 22.4 %copy-start.2 = (f32[48,768]{1,0:T(8,128)S(1)}, f32[48,768]{1,0:T(8,128)}, u32[]{:S(2)}) copy-start(f32[48,768]{1,0:T(8,128)} %inverse_ref.5) | copy-start | bytes 442372
  0.6 22.4 %copy-start.1 = (f32[2,64,512]{2,1,0:T(8,128)S(1)}, f32[2,64,512]{2,1,0:T(8,128)}, u32[]{:S(2)}) copy-start(f32[2,64,512]{2,1,0:T(8,128)} %coup_ref.5) | copy-start | bytes 786436
  0.7 22.4 %copy-start.3 = (f32[64,512]{1,0:T(8,128)S(1)}, f32[64,512]{1,0:T(8,128)}, u32[]{:S(2)}) copy-start(f32[64,512]{1,0:T(8,128)} %visc_ref.5) | copy-start | bytes 393220
  0.7 22.4 %copy-start = (f32[2,64,512]{2,1,0:T(8,128)S(1)}, f32[2,64,512]{2,1,0:T(8,128)}, u32[]{:S(2)}) copy-start(f32[2,64,512]{2,1,0:T(8,128)} %rhs_ref.5) | copy-start | bytes 786436
  0.7 22.4 %copy-start.4 = (s32[16]{0:T(128)S(1)}, s32[16]{0:T(128)}, u32[]{:S(2)}) copy-start(s32[16]{0:T(128)} %margin_ref.3) | copy-start | bytes 196
  6.8 16.2 %collective-permute-start = (f32[208,512]{1,0:T(8,128)S(1)}, f32[208,512]{1,0:T(8,128)S(1)}, u32[]{:S(2)}, u32[]{:S(2)}) collective-permute-start(f32[208,512]{1,0:T(8,128)S(1)} %get-tuple-element.17), channel_id=1, source_target_pairs={{0,1},{1,0},{2,3},{3,2},{4,5},{5,4},{6,7},{7,6},{8,9},{9,8},{10,11... | collective-permute-start | bytes 1277960 | tf_op jit(solution)/shard_map/ppermute | solution.py:494
  7.3 15.7 %collective-permute-start.1 = (f32[208,512]{1,0:T(8,128)S(1)}, f32[208,512]{1,0:T(8,128)S(1)}, u32[]{:S(2)}, u32[]{:S(2)}) collective-permute-start(f32[208,512]{1,0:T(8,128)S(1)} %get-tuple-element.18), channel_id=1, source_target_pairs={{1,2},{2,1},{3,4},{4,3},{5,6},{6,5},{7,8},{8,7},{9,10},{10,9},{11,... | collective-permute-start | bytes 1277960 | tf_op jit(solution)/shard_map/ppermute | solution.py:495
  28.2 14.8 %collective-permute-start.2 = (f32[2,8,512]{2,1,0:T(8,128)S(1)}, f32[2,8,512]{2,1,0:T(8,128)S(1)}, u32[]{:S(2)}, u32[]{:S(2)}) collective-permute-start(f32[2,8,512]{2,1,0:T(8,128)S(1)} %get-tuple-element.21), channel_id=1, source_target_pairs={{0,1},{1,0},{2,3},{3,2},{4,5},{5,4},{6,7},{7,6},{8,9},{9,8},{10,11... | collective-permute-start | bytes 98312 | tf_op jit(solution)/shard_map/ppermute | solution.py:494
  28.2 14.8 %collective-permute-start.3 = (f32[2,8,512]{2,1,0:T(8,128)S(1)}, f32[2,8,512]{2,1,0:T(8,128)S(1)}, u32[]{:S(2)}, u32[]{:S(2)}) collective-permute-start(f32[2,8,512]{2,1,0:T(8,128)S(1)} %get-tuple-element.22), channel_id=1, source_target_pairs={{1,2},{2,1},{3,4},{4,3},{5,6},{6,5},{7,8},{8,7},{9,10},{10,9},{11,... | collective-permute-start | bytes 98312 | tf_op jit(solution)/shard_map/ppermute | solution.py:495

commit v6 on v5

--- a/solution.py
+++ b/solution.py
@@ -17,6 +17,7 @@
 CHUNKS = 2 * ROWS // CHUNK
 PIECE = 6
 PIECES = VECTORS // PIECE
+AHEAD = 4
 LANES = 128
 SLOTS = 56
 EDGE_AT = 5 * HALO
@@ -97,13 +98,12 @@
     return total
 
 
-def send_sums(sums, out_ref):
-    pick_row = lax.broadcasted_iota(jnp.int32, (LANES, 8 * SLOTS), 0)
-    pick_col = lax.broadcasted_iota(jnp.int32, (LANES, 8 * SLOTS), 1)
-    pick = (pick_col // 8 == pick_row).astype(jnp.float32)
-    by_slot = jnp.dot(
-        pick, sums[...], precision=lax.Precision.HIGHEST, preferred_element_type=jnp.float32
-    )
+def send_sums(sums, turned, out_ref):
+    for k in range(SLOTS):
+        turned[pl.ds(k, 8, stride=SLOTS), :] = sums[8 * k : 8 * k + 8, :]
+    by_slot = turned[:SLOTS]
+    for j in range(1, 8):
+        by_slot = by_slot + turned[SLOTS * j : SLOTS * (j + 1)]
     row = lax.dot_general(
         jnp.ones((8, LANES), jnp.float32),
         by_slot,
@@ -111,7 +111,8 @@
         precision=lax.Precision.HIGHEST,
         preferred_element_type=jnp.float32,
     )
-    out_ref[...] = jnp.broadcast_to(row[:1], out_ref.shape)
+    wide = jnp.concatenate([row[:1], jnp.zeros((1, LANES - SLOTS), jnp.float32)], 1)
+    out_ref[...] = jnp.broadcast_to(wide, out_ref.shape)
 
 
 def pack_copies(out_ref, first_row, rhs_ref, visc_ref, coup_ref, inverse_ref, sems, at_sem):
@@ -145,12 +146,12 @@
 def start_kernel(
     rhs_ref, visc_ref, coup_ref, inverse_ref, basis_ref,
     sums_ref, partner_ref, other_ref, held,
-    field, sums, field_sem, sems, pack_sems,
+    field, sums, turned, field_sem, sems, pack_sems,
 ):
     odd = lax.axis_index("sub") % 2
     field_copy = pltpu.make_async_copy(rhs_ref, field, field_sem)
     field_copy.start()
-    for i in range(PIECES):
+    for i in range(AHEAD):
         basis_copy(i, basis_ref, held, sems).start()
     packs = []
     for n, (out_ref, up) in enumerate(((partner_ref, 1 - odd), (other_ref, odd))):
@@ -166,22 +167,26 @@
 
     def body(i, carry):
         basis_copy(i, basis_ref, held, sems).wait()
+
+        @pl.when(i + AHEAD < PIECES)
+        def _():
+            basis_copy(i + AHEAD, basis_ref, held, sems).start()
+
         restrict_piece(i, held, field, sums)
+        for n in range(PIECE):
+            k = PIECE * i + n
+            for a in range(2):
+                top = held[k, a, :CHUNK, :].astype(jnp.float32)[:1]
+                bottom = held[k, a, ROWS - CHUNK :, :].astype(jnp.float32)[CHUNK - 1 :]
+                place = pl.ds(EDGE_AT + VECTORS * a + k, 1)
+                partner_ref[place, :] = jnp.where(odd == 1, top, bottom)
+                other_ref[place, :] = jnp.where(odd == 1, bottom, top)
         return carry
 
     lax.fori_loop(0, PIECES, body, 0)
-    picker = lax.broadcasted_iota(jnp.int32, (VECTORS, CHUNK * VECTORS), 0) * CHUNK
-    place = lax.broadcasted_iota(jnp.int32, (VECTORS, CHUNK * VECTORS), 1)
-    for out_ref, up in ((partner_ref, 1 - odd), (other_ref, odd)):
-        pick = (place == picker + up * (CHUNK - 1)).astype(jnp.float32).astype(jnp.bfloat16)
-        first_row = pl.multiple_of(up * (ROWS - CHUNK), CHUNK)
-        for a in range(2):
-            rows = held[:, a, pl.ds(first_row, CHUNK), :].reshape(CHUNK * VECTORS, CELLS)
-            at = EDGE_AT + VECTORS * a
-            out_ref[at : at + VECTORS] = jnp.dot(pick, rows, preferred_element_type=jnp.float32)
     for copy in packs:
         copy.wait()
-    send_sums(sums, sums_ref)
+    send_sums(sums, turned, sums_ref)
 
 
 class Neighbour:
@@ -353,7 +358,7 @@
     count, margin_ref, sums_ref, inverse_ref, partner_ref, other_ref, held, rhs_ref, visc_ref,
     coup_ref,
     direction_ref, image_ref, smooth_ref, partner_rows_ref, other_rows_ref, next_ref,
-    extended, sums,
+    extended, sums, turned,
 ):
     received = sums_ref[...]
     over_beta = 1.0 / jnp.sqrt(lane_total(received, VECTORS))
@@ -386,7 +391,7 @@
         return carry
 
     lax.fori_loop(0, PIECES, body, 0)
-    send_sums(sums, next_ref)
+    send_sums(sums, turned, next_ref)
 
 
 def first_column(first, second):
@@ -400,7 +405,7 @@
     count, margin_ref, first_ref, second_ref, inverse_ref, partner_ref, other_ref,
     partner_rows_ref, other_rows_ref, held, smooth_ref, rhs_ref, image_ref, visc_ref, coup_ref,
     direction_ref, next_ref,
-    image_smooth, extended, sums,
+    image_smooth, extended, sums, turned,
 ):
     first, second = first_ref[...], second_ref[...]
     beta, h_00, h_10 = first_column(first, second)
@@ -428,7 +433,7 @@
     sums[16:24] = fold([images[a] * images[a] for a in range(2)])
     for a in range(2):
         direction_ref[a] = extended[a, HALO : HALO + ROWS]
-    send_sums(sums, next_ref)
+    send_sums(sums, turned, next_ref)
 
 
 def finish_kernel(
@@ -510,19 +515,19 @@
     arguments = (rhs, viscosity, coupling, coarse_inverse, coarse_basis)
     first, partner, other, held = call(
         start_kernel, "start", [HBM] * 5, [row, packed, packed, basis], 10_000_000,
-        [field, sums, dma(), dma(PIECES), dma(2 * pack_count(columns))],
+        [field, sums, sums, dma(), dma(PIECES), dma(2 * pack_count(columns))],
     )(*map(in_hbm, arguments))
     partner, other = swap(partner, other)
     first = from_everyone(first)
     direction, image, smooth, partner_rows, other_rows, second = call(
         functools.partial(first_turn_kernel, count), "first_turn", [SMEM] + [VMEM] * 8,
-        [whole, whole, smoothed, edge, edge, row], 20_000_000, [extended, sums],
+        [whole, whole, smoothed, edge, edge, row], 20_000_000, [extended, sums, sums],
     )(margin_rows, first, coarse_inverse, partner, other, held, rhs, viscosity, coupling)
     partner_rows, other_rows = swap(partner_rows, other_rows)
     second = from_everyone(second)
     second_direction, third = call(
         functools.partial(second_turn_kernel, count), "second_turn", [SMEM] + [VMEM] * 13,
-        [whole, row], 20_000_000, [extended, extended, sums],
+        [whole, row], 20_000_000, [extended, extended, sums, sums],
     )(
         margin_rows, first, second, coarse_inverse, partner, other, partner_rows, other_rows,
         held, smooth, rhs, image, viscosity, coupling,

time: 56.4 us -> 54.2 us (0.961)
  Pallas kernels: 16.5 us -> 14.2 us
    pallas_call x1, Pallas kernels: 6.11 us -> 4.73 us  [on_device(): call(start_kernel, 'start', [HBM] * 5, [row, packed, packed, basis], 1000...]
where the time goes in v6:
time: 54.2 us; the launch traced here: 53.9 us
  blocking collectives  37 us (68%)
  Pallas kernels  14.2 us (26%)
  starting transfers between devices  1.91 us (4%)
  between operations  0.74 us (1%)
    all_to_all x2, blocking collectives, from_everyone(): return lax.all_to_all(rows, 'sub', 0, 0, tiled=True)  29.1 us
    all_to_all x1, blocking collectives, from_everyone_reversed(): lax.all_to_all(rows, 'sub', 0, 0, tiled=True, axis_index_groups=order)  7.96 us
    pallas_call x1, Pallas kernels, on_device(): call(start_kernel, 'start', [HBM] * 5, [row, packed, packed, basis], 1000...  4.73 us
    pallas_call x1, Pallas kernels, on_device(): call(functools.partial(first_turn_kernel, count), 'first_turn', [SMEM] +...  4.68 us
    pallas_call x1, Pallas kernels, on_device(): call(functools.partial(second_turn_kernel, count), 'second_turn', [SMEM]...  3.41 us
    pallas_call x1, Pallas kernels, on_device(): call(finish_kernel, 'finish', [VMEM] * 5, [whole, f32(2, 3)], 1000000)  1.37 us
    ppermute x2, starting transfers between devices, swap(): lax.ppermute(other, 'sub', both(range(1, count - 1, 2)))  1.37 us
  transfers between devices with their start and end apart: 4, of which 0 were waited for; matrix products, arithmetic and copies ran while one was open for 0% of the time, Pallas kernels for 0%

profile of v6, /device:TPU:0, one launch (start us, length us, event | category | flops | bytes accessed | tf_op | source)
XLA Modules:
  0.0 53.9 jit_solution(18176132192365510665)
XLA Ops:
  0.6 0.0 copy-start.2
  0.6 0.0 copy-start.1
  0.7 0.0 copy-start.3
  0.7 0.0 copy-start
  0.7 0.0 copy-start.4
  0.7 4.7 %start.1 = (f32[16,128]{1,0:T(8,128)S(1)}, f32[208,512]{1,0:T(8,128)S(1)}, f32[208,512]{1,0:T(8,128)S(1)}, bf16[48,2,64,512]{3,2,1,0:T(8,128)(2,1)S(1)}) custom-call(f32[2,64,512]{2,1,0:T(8,128)} %rhs_ref.5, f32[64,512]{1,0:T(8,128)} %visc_ref.5, f32[2,64,512]{2,1,0:T(8,128)} %coup_ref.5, f32[48,768]{1,0:T(8,128)} %inverse_ref.5, ...), custom_call_target="tpu_custom_call" | custom-call | flops 10000000 | bytes 4000000 | tf_op jit(solution)/shard_map/start/pallas_call | solution.py:516
  5.4 0.5 collective-permute-start
  5.9 0.7 %collective-permute-start.1 = (f32[208,512]{1,0:T(8,128)S(1)}, f32[208,512]{1,0:T(8,128)S(1)}, u32[]{:S(2)}, u32[]{:S(2)}) collective-permute-start(f32[208,512]{1,0:T(8,128)S(1)} %get-tuple-element.18), channel_id=1, source_target_pairs={{1,2},{2,1},{3,4},{4,3},{5,6},{6,5},{7,8},{8,7},{9,10},{10,9},{11,... | collective-permute-start | bytes 1277960 | tf_op jit(solution)/shard_map/ppermute | solution.py:500
  6.6 15.0 %all_to_all.33 = f32[16,1,128]{2,1,0:T(1,128)S(1)} all-to-all(f32[16,1,128]{2,1,0:T(1,128)S(1)} %bitcast.20), channel_id=1, replica_groups=mesh['groups'=2,'sub'=16] {'sub'}, dimensions={0} | all-to-all | bytes 16384 | tf_op jit(solution)/shard_map/all_to_all | solution.py:487
  21.6 0.0 collective-permute-done.partner_ref
  21.6 0.0 collective-permute-done.1.other_ref
  21.6 0.0 copy-done.2
  21.6 0.0 copy-done.1
  21.6 0.0 copy-done.3
  21.6 0.0 copy-done
  21.7 0.0 copy-done.4
  21.7 4.7 %first_turn.1 = (f32[2,64,512]{2,1,0:T(8,128)S(1)}, f32[2,64,512]{2,1,0:T(8,128)S(1)}, f32[2,80,512]{2,1,0:T(8,128)S(1)}, f32[2,8,512]{2,1,0:T(8,128)S(1)}, f32[...) custom-call(s32[16]{0:T(128)S(1)} %copy-done.4, f32[16,128]{1,0:T(8,128)S(1)} %bitcast.13, f32[48,768]{1,0:T(8,128)S(1)} %copy-done.2, ...), custom_call_target="tpu_custom_call" | custom-call | flops 20000000 | bytes 4000000 | tf_op jit(solution)/shard_map/first_turn/pallas_call | solution.py:522
  26.3 0.0 collective-permute-start.2
  26.4 0.7 %collective-permute-start.3 = (f32[2,8,512]{2,1,0:T(8,128)S(1)}, f32[2,8,512]{2,1,0:T(8,128)S(1)}, u32[]{:S(2)}, u32[]{:S(2)}) collective-permute-start(f32[2,8,512]{2,1,0:T(8,128)S(1)} %get-tuple-element.22), channel_id=1, source_target_pairs={{1,2},{2,1},{3,4},{4,3},{5,6},{6,5},{7,8},{8,7},{9,10},{10,9},{11,... | collective-permute-start | bytes 98312 | tf_op jit(solution)/shard_map/ppermute | solution.py:500
  27.1 14.1 %all_to_all.34 = f32[16,1,128]{2,1,0:T(1,128)S(1)} all-to-all(f32[16,1,128]{2,1,0:T(1,128)S(1)} %bitcast.19), channel_id=1, replica_groups=mesh['groups'=2,'sub'=16] {'sub'}, dimensions={0} | all-to-all | bytes 16384 | tf_op jit(solution)/shard_map/all_to_all | solution.py:487
  41.2 0.0 collective-permute-done.2.partner_rows_ref
  41.2 0.0 collective-permute-done.3.other_rows_ref
  41.2 3.4 %second_turn.1 = (f32[2,64,512]{2,1,0:T(8,128)S(1)}, f32[16,128]{1,0:T(8,128)S(1)}) custom-call(s32[16]{0:T(128)S(1)} %copy-done.4, f32[16,128]{1,0:T(8,128)S(1)} %bitcast.14, f32[16,128]{1,0:T(8,128)S(1)} %bitcast.16, f32[48,768]{1,0:T(8,128)S(1)} %copy-done.2, f32[208,512]{1,0:T(8,128)S(1)} %collective-permute-done.partner_ref, ...), custom_call_target="tpu_custom_call" | custom-call | flops 20000000 | bytes 4000000 | tf_op jit(solution)/shard_map/second_turn/pallas_call | solution.py:528
  44.6 8.0 %all_to_all.35 = f32[16,1,128]{2,1,0:T(1,128)S(1)} all-to-all(f32[16,1,128]{2,1,0:T(1,128)S(1)} %bitcast.21), channel_id=1, replica_groups={{15,14,13,12,11,10,9,8,7,6,5,4,3,2,1,0},{31,30,29,28,27,26,25,24,23,22,..., dimensions={0} | all-to-all | bytes 16384 | tf_op jit(solution)/shard_map/all_to_all | solution.py:492
  52.5 1.4 %finish.1 = (f32[2,64,512]{2,1,0:T(8,128)}, f32[2,3]{1,0:T(2,128)}) custom-call(f32[16,128]{1,0:T(8,128)S(1)} %bitcast.15, f32[16,128]{1,0:T(8,128)S(1)} %bitcast.17, f32[16,128]{1,0:T(8,128)S(1)} %bitcast.18, f32[2,64,512]{2,1,0:T(8,128)S(1)} %get-tuple-element.26.first_direction_ref, f32[2,64,512]{2,1,0:T(8,128)S(1)} %get-tuple-element.27.second_direction_ref), custom_call_target="tpu_custom_call" | custom-call | flops 1000000 | bytes 4000000 | tf_op jit(solution)/shard_map/finish/pallas_call | solution.py:536
Async XLA Ops:
  0.6 21.0 %copy-start.2 = (f32[48,768]{1,0:T(8,128)S(1)}, f32[48,768]{1,0:T(8,128)}, u32[]{:S(2)}) copy-start(f32[48,768]{1,0:T(8,128)} %inverse_ref.5) | copy-start | bytes 442372
  0.6 21.0 %copy-start.1 = (f32[2,64,512]{2,1,0:T(8,128)S(1)}, f32[2,64,512]{2,1,0:T(8,128)}, u32[]{:S(2)}) copy-start(f32[2,64,512]{2,1,0:T(8,128)} %coup_ref.5) | copy-start | bytes 786436
  0.7 21.0 %copy-start.3 = (f32[64,512]{1,0:T(8,128)S(1)}, f32[64,512]{1,0:T(8,128)}, u32[]{:S(2)}) copy-start(f32[64,512]{1,0:T(8,128)} %visc_ref.5) | copy-start | bytes 393220
  0.7 21.0 %copy-start = (f32[2,64,512]{2,1,0:T(8,128)S(1)}, f32[2,64,512]{2,1,0:T(8,128)}, u32[]{:S(2)}) copy-start(f32[2,64,512]{2,1,0:T(8,128)} %rhs_ref.5) | copy-start | bytes 786436
  0.7 21.0 %copy-start.4 = (s32[16]{0:T(128)S(1)}, s32[16]{0:T(128)}, u32[]{:S(2)}) copy-start(s32[16]{0:T(128)} %margin_ref.3) | copy-start | bytes 196
  5.4 16.2 %collective-permute-start = (f32[208,512]{1,0:T(8,128)S(1)}, f32[208,512]{1,0:T(8,128)S(1)}, u32[]{:S(2)}, u32[]{:S(2)}) collective-permute-start(f32[208,512]{1,0:T(8,128)S(1)} %get-tuple-element.17), channel_id=1, source_target_pairs={{0,1},{1,0},{2,3},{3,2},{4,5},{5,4},{6,7},{7,6},{8,9},{9,8},{10,11... | collective-permute-start | bytes 1277960 | tf_op jit(solution)/shard_map/ppermute | solution.py:499
  5.9 15.7 %collective-permute-start.1 = (f32[208,512]{1,0:T(8,128)S(1)}, f32[208,512]{1,0:T(8,128)S(1)}, u32[]{:S(2)}, u32[]{:S(2)}) collective-permute-start(f32[208,512]{1,0:T(8,128)S(1)} %get-tuple-element.18), channel_id=1, source_target_pairs={{1,2},{2,1},{3,4},{4,3},{5,6},{6,5},{7,8},{8,7},{9,10},{10,9},{11,... | collective-permute-start | bytes 1277960 | tf_op jit(solution)/shard_map/ppermute | solution.py:500
  26.3 14.8 %collective-permute-start.2 = (f32[2,8,512]{2,1,0:T(8,128)S(1)}, f32[2,8,512]{2,1,0:T(8,128)S(1)}, u32[]{:S(2)}, u32[]{:S(2)}) collective-permute-start(f32[2,8,512]{2,1,0:T(8,128)S(1)} %get-tuple-element.21), channel_id=1, source_target_pairs={{0,1},{1,0},{2,3},{3,2},{4,5},{5,4},{6,7},{7,6},{8,9},{9,8},{10,11... | collective-permute-start | bytes 98312 | tf_op jit(solution)/shard_map/ppermute | solution.py:499
  26.4 14.8 %collective-permute-start.3 = (f32[2,8,512]{2,1,0:T(8,128)S(1)}, f32[2,8,512]{2,1,0:T(8,128)S(1)}, u32[]{:S(2)}, u32[]{:S(2)}) collective-permute-start(f32[2,8,512]{2,1,0:T(8,128)S(1)} %get-tuple-element.22), channel_id=1, source_target_pairs={{1,2},{2,1},{3,4},{4,3},{5,6},{6,5},{7,8},{8,7},{9,10},{10,9},{11,... | collective-permute-start | bytes 98312 | tf_op jit(solution)/shard_map/ppermute | solution.py:500

commit v7 on v6

--- a/solution.py
+++ b/solution.py
@@ -37,10 +37,12 @@
 
 
 def cell_sum(field):
-    column = lax.broadcasted_iota(jnp.int32, field.shape, 1)
-    left = jnp.where(column == 0, 0.0, pltpu.roll(field, 1, 1))
-    right = jnp.where(column == CELLS - 1, 0.0, pltpu.roll(field, CELLS - 1, 1))
-    return left + right
+    lane = lax.broadcasted_iota(jnp.int32, (field.shape[0], LANES), 1)
+    left, right = pltpu.roll(field, 1, 1), pltpu.roll(field, CELLS - 1, 1)
+    inner = left[:, LANES:-LANES] + right[:, LANES:-LANES]
+    first = jnp.where(lane == 0, 0.0, left[:, :LANES]) + right[:, :LANES]
+    last = left[:, -LANES:] + jnp.where(lane == LANES - 1, 0.0, right[:, -LANES:])
+    return jnp.concatenate([first, inner, last], 1)
 
 
 def row_sum(field):
@@ -202,7 +204,9 @@
     return Neighbour(partner_ref, other_ref), Neighbour(other_ref, partner_ref)
 
 
-def solve(count, margin_ref, visc_ref, coup_ref, field_ref, low_ref, high_ref, edges, out_ref):
+def solve(
+    count, margin_ref, visc_ref, coup_ref, field_ref, low_ref, high_ref, edges, out_ref, beside
+):
     rank = lax.axis_index("sub")
     lower = jnp.where(rank > 0, margin_ref[jnp.maximum(rank - 1, 0)], 0)
     upper = jnp.where(rank < count - 1, margin_ref[rank], 0)
@@ -249,7 +253,8 @@
         across.append(live * triple(scale * viscosity))
         other.append(live * triple(scale * coupling))
     solved = list(first)
-    for _ in range(SWEEPS - 1):
+    for sweep in range(1, SWEEPS):
+        beside(sweep)
         solved = [
             (1.0 - RELAX) * solved[a]
             + first[a]
@@ -270,7 +275,7 @@
     tiles = [jnp.zeros((1, LANES), jnp.float32) for _ in range(devices * VECTORS // LANES)]
     for t in range(devices):
         tile, offset = divmod(VECTORS * t, LANES)
-        row = jnp.where(lane < VECTORS, residuals[t : t + 1], 0.0)
+        row = jnp.where(lane < VECTORS, residuals[devices - 1 - t : devices - t], 0.0)
         if offset:
             row = pltpu.roll(row, offset, 1)
         if offset + VECTORS <= LANES:
@@ -327,14 +332,18 @@
     return jnp.where(place == row, line, 0.0).astype(jnp.bfloat16)
 
 
-def prolong(residual, inverse_ref, held, extended):
+def prolonging(residual, inverse_ref, held, extended):
     matrix = spread(lift(inverse_ref, residual))
-    for a in range(2):
-        for r in range(0, ROWS, CHUNK):
+    places = [(a, r) for a in range(2) for r in range(0, ROWS, CHUNK)]
+
+    def beside(n):
+        for a, r in places[n - 1 :: SWEEPS - 1]:
             rows = held[:, a, r : r + CHUNK, :].reshape(CHUNK * VECTORS, CELLS)
             extended[a, HALO + r : HALO + r + CHUNK] = jnp.dot(
                 matrix, rows, preferred_element_type=jnp.float32
             )
+
+    return beside
 
 
 def add_smooth(residual, low, high, smooth, extended):
@@ -363,11 +372,11 @@
     received = sums_ref[...]
     over_beta = 1.0 / jnp.sqrt(lane_total(received, VECTORS))
     residual = line_up(received) * over_beta
-    prolong(residual, inverse_ref, held, extended)
+    beside = prolonging(residual, inverse_ref, held, extended)
     low, high = neighbours_of(partner_ref, other_ref)
     starts = [HALO * (3 + a) for a in range(2)]
     edges = [(low[at : at + HALO], high[at : at + HALO]) for at in starts]
-    solve(count, margin_ref, visc_ref, coup_ref, rhs_ref, low, high, edges, smooth_ref)
+    solve(count, margin_ref, visc_ref, coup_ref, rhs_ref, low, high, edges, smooth_ref, beside)
     add_smooth(
         residual, low, high, lambda a, rows: smooth_ref[a, rows] * over_beta, extended
     )
@@ -412,11 +421,13 @@
     ratio = h_00 / beta
     over = 1.0 / h_10
     residual = (line_up(second) - ratio * line_up(first)) * over
-    prolong(residual, inverse_ref, held, extended)
+    beside = prolonging(residual, inverse_ref, held, extended)
     low, high = neighbours_of(partner_ref, other_ref)
     low_rows, high_rows = neighbours_of(partner_rows_ref, other_rows_ref)
     edges = [(low_rows[a], high_rows[a]) for a in range(2)]
-    solve(count, margin_ref, visc_ref, coup_ref, image_ref, low, high, edges, image_smooth)
+    solve(
+        count, margin_ref, visc_ref, coup_ref, image_ref, low, high, edges, image_smooth, beside
+    )
     add_smooth(
         residual,
         low,
@@ -484,10 +495,6 @@
 
 
 def from_everyone(rows):
-    return lax.all_to_all(rows, "sub", 0, 0, tiled=True)
-
-
-def from_everyone_reversed(rows):
     order = [list(range(lax.axis_size("sub")))[::-1]]
     return lax.all_to_all(rows, "sub", 0, 0, tiled=True, axis_index_groups=order)
 
@@ -532,7 +539,7 @@
         margin_rows, first, second, coarse_inverse, partner, other, partner_rows, other_rows,
         held, smooth, rhs, image, viscosity, coupling,
     )
-    third = from_everyone_reversed(third)
+    third = from_everyone(third)
     result, transposed = call(finish_kernel, "finish", [VMEM] * 5, [whole, f32(2, 3)], 1_000_000)(
         first, second, third, direction, second_direction
     )

time: 54.2 us -> 51.2 us (0.945)
  blocking collectives: 37 us -> 34.1 us
    all_to_all x3, blocking collectives: 37 us -> 34.1 us  [from_everyone(): lax.all_to_all(rows, 'sub', 0, 0, tiled=True, axis_index_groups=order)]
where the time goes in v7:
time: 51.2 us; the launch traced here: 50.9 us
  blocking collectives  34.1 us (67%)
  Pallas kernels  14.1 us (28%)
  starting transfers between devices  1.99 us (4%)
  between operations  0.74 us (1%)
    all_to_all x3, blocking collectives, from_everyone(): lax.all_to_all(rows, 'sub', 0, 0, tiled=True, axis_index_groups=order)  34.1 us
    pallas_call x1, Pallas kernels, on_device(): call(start_kernel, 'start', [HBM] * 5, [row, packed, packed, basis], 1000...  4.73 us
    pallas_call x1, Pallas kernels, on_device(): call(functools.partial(first_turn_kernel, count), 'first_turn', [SMEM] +...  4.64 us
    pallas_call x1, Pallas kernels, on_device(): call(functools.partial(second_turn_kernel, count), 'second_turn', [SMEM]...  3.37 us
    pallas_call x1, Pallas kernels, on_device(): call(finish_kernel, 'finish', [VMEM] * 5, [whole, f32(2, 3)], 1000000)  1.37 us
    ppermute x2, starting transfers between devices, swap(): lax.ppermute(other, 'sub', both(range(1, count - 1, 2)))  1.33 us
  transfers between devices with their start and end apart: 4, of which 0 were waited for; matrix products, arithmetic and copies ran while one was open for 0% of the time, Pallas kernels for 0%

profile of v7, /device:TPU:0, one launch (start us, length us, event | category | flops | bytes accessed | tf_op | source)
XLA Modules:
  0.0 50.9 jit_solution(12196515288168269568)
XLA Ops:
  0.6 0.0 copy-start.2
  0.6 0.0 copy-start.1
  0.7 0.0 copy-start.3
  0.7 0.0 copy-start
  0.7 0.0 copy-start.4
  0.7 4.7 %start.1 = (f32[16,128]{1,0:T(8,128)S(1)}, f32[208,512]{1,0:T(8,128)S(1)}, f32[208,512]{1,0:T(8,128)S(1)}, bf16[48,2,64,512]{3,2,1,0:T(8,128)(2,1)S(1)}) custom-call(f32[2,64,512]{2,1,0:T(8,128)} %rhs_ref.5, f32[64,512]{1,0:T(8,128)} %visc_ref.5, f32[2,64,512]{2,1,0:T(8,128)} %coup_ref.5, f32[48,768]{1,0:T(8,128)} %inverse_ref.5, ...), custom_call_target="tpu_custom_call" | custom-call | flops 10000000 | bytes 4000000 | tf_op jit(solution)/shard_map/start/pallas_call | solution.py:523
  5.4 0.5 %collective-permute-start = (f32[208,512]{1,0:T(8,128)S(1)}, f32[208,512]{1,0:T(8,128)S(1)}, u32[]{:S(2)}, u32[]{:S(2)}) collective-permute-start(f32[208,512]{1,0:T(8,128)S(1)} %get-tuple-element.17), channel_id=1, source_target_pairs={{0,1},{1,0},{2,3},{3,2},{4,5},{5,4},{6,7},{7,6},{8,9},{9,8},{10,11... | collective-permute-start | bytes 1277960 | tf_op jit(solution)/shard_map/ppermute | solution.py:506
  5.9 0.7 %collective-permute-start.1 = (f32[208,512]{1,0:T(8,128)S(1)}, f32[208,512]{1,0:T(8,128)S(1)}, u32[]{:S(2)}, u32[]{:S(2)}) collective-permute-start(f32[208,512]{1,0:T(8,128)S(1)} %get-tuple-element.18), channel_id=1, source_target_pairs={{1,2},{2,1},{3,4},{4,3},{5,6},{6,5},{7,8},{8,7},{9,10},{10,9},{11,... | collective-permute-start | bytes 1277960 | tf_op jit(solution)/shard_map/ppermute | solution.py:507
  6.6 13.5 %all_to_all.33 = f32[16,1,128]{2,1,0:T(1,128)S(1)} all-to-all(f32[16,1,128]{2,1,0:T(1,128)S(1)} %bitcast.20), channel_id=1, replica_groups={{15,14,13,12,11,10,9,8,7,6,5,4,3,2,1,0},{31,30,29,28,27,26,25,24,23,22,..., dimensions={0} | all-to-all | bytes 16384 | tf_op jit(solution)/shard_map/all_to_all | solution.py:499
  20.2 0.0 collective-permute-done.partner_ref
  20.2 0.0 collective-permute-done.1.other_ref
  20.2 0.0 copy-done.2
  20.2 0.0 copy-done.1
  20.2 0.0 copy-done.3
  20.2 0.0 copy-done
  20.2 0.0 copy-done.4
  20.2 4.6 %first_turn.1 = (f32[2,64,512]{2,1,0:T(8,128)S(1)}, f32[2,64,512]{2,1,0:T(8,128)S(1)}, f32[2,80,512]{2,1,0:T(8,128)S(1)}, f32[2,8,512]{2,1,0:T(8,128)S(1)}, f32[...) custom-call(s32[16]{0:T(128)S(1)} %copy-done.4, f32[16,128]{1,0:T(8,128)S(1)} %bitcast.13, f32[48,768]{1,0:T(8,128)S(1)} %copy-done.2, ...), custom_call_target="tpu_custom_call" | custom-call | flops 20000000 | bytes 4000000 | tf_op jit(solution)/shard_map/first_turn/pallas_call | solution.py:529
  24.8 0.2 collective-permute-start.2
  25.0 0.7 %collective-permute-start.3 = (f32[2,8,512]{2,1,0:T(8,128)S(1)}, f32[2,8,512]{2,1,0:T(8,128)S(1)}, u32[]{:S(2)}, u32[]{:S(2)}) collective-permute-start(f32[2,8,512]{2,1,0:T(8,128)S(1)} %get-tuple-element.22), channel_id=1, source_target_pairs={{1,2},{2,1},{3,4},{4,3},{5,6},{6,5},{7,8},{8,7},{9,10},{10,9},{11,... | collective-permute-start | bytes 98312 | tf_op jit(solution)/shard_map/ppermute | solution.py:507
  25.7 12.1 %all_to_all.34 = f32[16,1,128]{2,1,0:T(1,128)S(1)} all-to-all(f32[16,1,128]{2,1,0:T(1,128)S(1)} %bitcast.19), channel_id=1, replica_groups={{15,14,13,12,11,10,9,8,7,6,5,4,3,2,1,0},{31,30,29,28,27,26,25,24,23,22,..., dimensions={0} | all-to-all | bytes 16384 | tf_op jit(solution)/shard_map/all_to_all | solution.py:499
  37.8 0.0 collective-permute-done.2.partner_rows_ref
  37.8 0.0 collective-permute-done.3.other_rows_ref
  37.8 3.4 %second_turn.1 = (f32[2,64,512]{2,1,0:T(8,128)S(1)}, f32[16,128]{1,0:T(8,128)S(1)}) custom-call(s32[16]{0:T(128)S(1)} %copy-done.4, f32[16,128]{1,0:T(8,128)S(1)} %bitcast.14, f32[16,128]{1,0:T(8,128)S(1)} %bitcast.16, f32[48,768]{1,0:T(8,128)S(1)} %copy-done.2, f32[208,512]{1,0:T(8,128)S(1)} %collective-permute-done.partner_ref, ...), custom_call_target="tpu_custom_call" | custom-call | flops 20000000 | bytes 4000000 | tf_op jit(solution)/shard_map/second_turn/pallas_call | solution.py:535
  41.2 8.4 %all_to_all.35 = f32[16,1,128]{2,1,0:T(1,128)S(1)} all-to-all(f32[16,1,128]{2,1,0:T(1,128)S(1)} %bitcast.21), channel_id=1, replica_groups={{15,14,13,12,11,10,9,8,7,6,5,4,3,2,1,0},{31,30,29,28,27,26,25,24,23,22,..., dimensions={0} | all-to-all | bytes 16384 | tf_op jit(solution)/shard_map/all_to_all | solution.py:499
  49.6 1.4 %finish.1 = (f32[2,64,512]{2,1,0:T(8,128)}, f32[2,3]{1,0:T(2,128)}) custom-call(f32[16,128]{1,0:T(8,128)S(1)} %bitcast.15, f32[16,128]{1,0:T(8,128)S(1)} %bitcast.17, f32[16,128]{1,0:T(8,128)S(1)} %bitcast.18, f32[2,64,512]{2,1,0:T(8,128)S(1)} %get-tuple-element.26.first_direction_ref, f32[2,64,512]{2,1,0:T(8,128)S(1)} %get-tuple-element.27.second_direction_ref), custom_call_target="tpu_custom_call" | custom-call | flops 1000000 | bytes 4000000 | tf_op jit(solution)/shard_map/finish/pallas_call | solution.py:543
Async XLA Ops:
  0.6 19.5 %copy-start.2 = (f32[48,768]{1,0:T(8,128)S(1)}, f32[48,768]{1,0:T(8,128)}, u32[]{:S(2)}) copy-start(f32[48,768]{1,0:T(8,128)} %inverse_ref.5) | copy-start | bytes 442372
  0.6 19.5 %copy-start.1 = (f32[2,64,512]{2,1,0:T(8,128)S(1)}, f32[2,64,512]{2,1,0:T(8,128)}, u32[]{:S(2)}) copy-start(f32[2,64,512]{2,1,0:T(8,128)} %coup_ref.5) | copy-start | bytes 786436
  0.7 19.5 %copy-start.3 = (f32[64,512]{1,0:T(8,128)S(1)}, f32[64,512]{1,0:T(8,128)}, u32[]{:S(2)}) copy-start(f32[64,512]{1,0:T(8,128)} %visc_ref.5) | copy-start | bytes 393220
  0.7 19.5 %copy-start = (f32[2,64,512]{2,1,0:T(8,128)S(1)}, f32[2,64,512]{2,1,0:T(8,128)}, u32[]{:S(2)}) copy-start(f32[2,64,512]{2,1,0:T(8,128)} %rhs_ref.5) | copy-start | bytes 786436
  0.7 19.5 %copy-start.4 = (s32[16]{0:T(128)S(1)}, s32[16]{0:T(128)}, u32[]{:S(2)}) copy-start(s32[16]{0:T(128)} %margin_ref.3) | copy-start | bytes 196
  5.4 14.7 %collective-permute-start = (f32[208,512]{1,0:T(8,128)S(1)}, f32[208,512]{1,0:T(8,128)S(1)}, u32[]{:S(2)}, u32[]{:S(2)}) collective-permute-start(f32[208,512]{1,0:T(8,128)S(1)} %get-tuple-element.17), channel_id=1, source_target_pairs={{0,1},{1,0},{2,3},{3,2},{4,5},{5,4},{6,7},{7,6},{8,9},{9,8},{10,11... | collective-permute-start | bytes 1277960 | tf_op jit(solution)/shard_map/ppermute | solution.py:506
  5.9 14.2 %collective-permute-start.1 = (f32[208,512]{1,0:T(8,128)S(1)}, f32[208,512]{1,0:T(8,128)S(1)}, u32[]{:S(2)}, u32[]{:S(2)}) collective-permute-start(f32[208,512]{1,0:T(8,128)S(1)} %get-tuple-element.18), channel_id=1, source_target_pairs={{1,2},{2,1},{3,4},{4,3},{5,6},{6,5},{7,8},{8,7},{9,10},{10,9},{11,... | collective-permute-start | bytes 1277960 | tf_op jit(solution)/shard_map/ppermute | solution.py:507
  24.8 12.9 %collective-permute-start.2 = (f32[2,8,512]{2,1,0:T(8,128)S(1)}, f32[2,8,512]{2,1,0:T(8,128)S(1)}, u32[]{:S(2)}, u32[]{:S(2)}) collective-permute-start(f32[2,8,512]{2,1,0:T(8,128)S(1)} %get-tuple-element.21), channel_id=1, source_target_pairs={{0,1},{1,0},{2,3},{3,2},{4,5},{5,4},{6,7},{7,6},{8,9},{9,8},{10,11... | collective-permute-start | bytes 98312 | tf_op jit(solution)/shard_map/ppermute | solution.py:506
  25.0 12.8 %collective-permute-start.3 = (f32[2,8,512]{2,1,0:T(8,128)S(1)}, f32[2,8,512]{2,1,0:T(8,128)S(1)}, u32[]{:S(2)}, u32[]{:S(2)}) collective-permute-start(f32[2,8,512]{2,1,0:T(8,128)S(1)} %get-tuple-element.22), channel_id=1, source_target_pairs={{1,2},{2,1},{3,4},{4,3},{5,6},{6,5},{7,8},{8,7},{9,10},{10,9},{11,... | collective-permute-start | bytes 98312 | tf_op jit(solution)/shard_map/ppermute | solution.py:507

commit v8 on v7

--- a/solution.py
+++ b/solution.py
@@ -17,7 +17,6 @@
 CHUNKS = 2 * ROWS // CHUNK
 PIECE = 6
 PIECES = VECTORS // PIECE
-AHEAD = 4
 LANES = 128
 SLOTS = 56
 EDGE_AT = 5 * HALO
@@ -69,11 +68,6 @@
             + coupling[a] * extended[1 - a][inner]
         )
     return images
-
-
-def basis_copy(i, basis_ref, held, sems):
-    vectors = pl.ds(PIECE * i, PIECE)
-    return pltpu.make_async_copy(basis_ref.at[vectors], held.at[vectors], sems.at[i])
 
 
 def restrict_piece(i, held, field, sums):
@@ -145,49 +139,48 @@
     return 5 + columns // 512 + 2 * (columns % 512 // 256)
 
 
-def start_kernel(
+def pack_kernel(
     rhs_ref, visc_ref, coup_ref, inverse_ref, basis_ref,
-    sums_ref, partner_ref, other_ref, held,
-    field, sums, turned, field_sem, sems, pack_sems,
+    partner_ref, other_ref,
+    groups, group_sems, pack_sems,
 ):
     odd = lax.axis_index("sub") % 2
-    field_copy = pltpu.make_async_copy(rhs_ref, field, field_sem)
-    field_copy.start()
-    for i in range(AHEAD):
-        basis_copy(i, basis_ref, held, sems).start()
-    packs = []
-    for n, (out_ref, up) in enumerate(((partner_ref, 1 - odd), (other_ref, odd))):
+    sides = ((partner_ref, 1 - odd), (other_ref, odd))
+    group_copies, packs = [], []
+    for n, (out_ref, up) in enumerate(sides):
+        for a in range(2):
+            rows = pl.ds(pl.multiple_of(up * (ROWS - CHUNK), CHUNK), CHUNK)
+            group_copies.append(
+                pltpu.make_async_copy(
+                    basis_ref.at[:, a, rows, :], groups.at[2 * n + a], group_sems.at[2 * n + a]
+                )
+            )
         packs += pack_copies(
             out_ref, up * (ROWS - HALO), rhs_ref, visc_ref, coup_ref, inverse_ref, pack_sems,
             n * pack_count(inverse_ref.shape[1]),
         )
-    for copy in packs:
+    for copy in group_copies + packs:
         copy.start()
-    sums[...] = jnp.zeros_like(sums)
-    field_copy.wait()
-    sums[8 * VECTORS : 8 * VECTORS + 8] = fold([field[a] * field[a] for a in range(2)])
-
-    def body(i, carry):
-        basis_copy(i, basis_ref, held, sems).wait()
-
-        @pl.when(i + AHEAD < PIECES)
-        def _():
-            basis_copy(i + AHEAD, basis_ref, held, sems).start()
-
-        restrict_piece(i, held, field, sums)
-        for n in range(PIECE):
-            k = PIECE * i + n
-            for a in range(2):
-                top = held[k, a, :CHUNK, :].astype(jnp.float32)[:1]
-                bottom = held[k, a, ROWS - CHUNK :, :].astype(jnp.float32)[CHUNK - 1 :]
-                place = pl.ds(EDGE_AT + VECTORS * a + k, 1)
-                partner_ref[place, :] = jnp.where(odd == 1, top, bottom)
-                other_ref[place, :] = jnp.where(odd == 1, bottom, top)
-        return carry
-
-    lax.fori_loop(0, PIECES, body, 0)
+    for n, (out_ref, up) in enumerate(sides):
+        for a in range(2):
+            group_copies[2 * n + a].wait()
+            for k in range(VECTORS):
+                rows = groups[2 * n + a, k].astype(jnp.float32)
+                at = EDGE_AT + VECTORS * a + k
+                out_ref[at : at + 1] = jnp.where(up == 1, rows[CHUNK - 1 :], rows[:1])
     for copy in packs:
         copy.wait()
+
+
+def restrict_kernel(rhs_ref, held, sums_ref, sums, turned):
+    sums[...] = jnp.zeros_like(sums)
+    sums[8 * VECTORS : 8 * VECTORS + 8] = fold([rhs_ref[a] * rhs_ref[a] for a in range(2)])
+
+    def body(i, carry):
+        restrict_piece(i, held, rhs_ref, sums)
+        return carry
+
+    lax.fori_loop(0, PIECES, body, 0)
     send_sums(sums, turned, sums_ref)
 
 
@@ -513,18 +506,21 @@
     columns = coarse_inverse.shape[1]
     f32 = lambda *shape: jax.ShapeDtypeStruct(shape, jnp.float32)
     dma = lambda *shape: pltpu.SemaphoreType.DMA(shape)
-    field = pltpu.VMEM((2, ROWS, CELLS), jnp.float32)
     extended = pltpu.VMEM((2, EXT, CELLS), jnp.float32)
     sums = pltpu.VMEM((8 * SLOTS, LANES), jnp.float32)
     row, whole, edge = f32(count, LANES), f32(2, ROWS, CELLS), f32(2, HALO, CELLS)
     packed, smoothed = f32(EDGE_AT + coarse_rows(columns), CELLS), f32(2, EXT, CELLS)
-    basis = jax.ShapeDtypeStruct(coarse_basis.shape, jnp.bfloat16)
     arguments = (rhs, viscosity, coupling, coarse_inverse, coarse_basis)
-    first, partner, other, held = call(
-        start_kernel, "start", [HBM] * 5, [row, packed, packed, basis], 10_000_000,
-        [field, sums, sums, dma(), dma(PIECES), dma(2 * pack_count(columns))],
+    packs = call(
+        pack_kernel, "pack", [HBM] * 5, [packed, packed], 5_000_000,
+        [pltpu.VMEM((4, VECTORS, CHUNK, CELLS), jnp.bfloat16), dma(4)]
+        + [dma(2 * pack_count(columns))],
     )(*map(in_hbm, arguments))
+    held, partner, other = lax.optimization_barrier((coarse_basis, *packs))
     partner, other = swap(partner, other)
+    (first,) = call(
+        restrict_kernel, "restrict", [VMEM] * 2, [row], 10_000_000, [sums, sums]
+    )(rhs, held)
     first = from_everyone(first)
     direction, image, smooth, partner_rows, other_rows, second = call(
         functools.partial(first_turn_kernel, count), "first_turn", [SMEM] + [VMEM] * 8,

time: 51.2 us -> 48.9 us (0.955)
  blocking collectives: 34.1 us -> 32.2 us
  Pallas kernels: 14.1 us -> 13.5 us
    all_to_all x3, blocking collectives: 34.1 us -> 32.2 us  [from_everyone(): lax.all_to_all(rows, 'sub', 0, 0, tiled=True, axis_index_groups=order)]
    pallas_call x1 -> x2, Pallas kernels: 4.73 us -> 4.27 us  [the longest x1 2.55 us: on_device(): call(pack_kernel, 'pack', [HBM] * 5, [packed, packed], 5000000, [pltpu.VM...]
  transfers between devices with their start and end apart: 4 -> 4, of which waited for: 0 -> 0; matrix products, arithmetic and copies ran while one was open for 0% -> 0% of each run, Pallas kernels for 0% -> 4%
where the time goes in v8:
time: 48.9 us; the launch traced here: 48.6 us
  blocking collectives  32.2 us (66%)
  Pallas kernels  13.5 us (28%)
  starting transfers between devices  2.06 us (4%)
  between operations  0.74 us (2%)
    all_to_all x3, blocking collectives, from_everyone(): lax.all_to_all(rows, 'sub', 0, 0, tiled=True, axis_index_groups=order)  32.2 us
    pallas_call x1, Pallas kernels, on_device(): call(functools.partial(first_turn_kernel, count), 'first_turn', [SMEM] +...  4.58 us
    pallas_call x1, Pallas kernels, on_device(): call(functools.partial(second_turn_kernel, count), 'second_turn', [SMEM]...  3.28 us
    pallas_call x1, Pallas kernels, on_device(): call(pack_kernel, 'pack', [HBM] * 5, [packed, packed], 5000000, [pltpu.VM...  2.55 us
    pallas_call x1, Pallas kernels, on_device(): call(restrict_kernel, 'restrict', [VMEM] * 2, [row], 10000000, [sums, sums])  1.72 us
    ppermute x2, starting transfers between devices, swap(): lax.ppermute(other, 'sub', both(range(1, count - 1, 2)))  1.46 us
    pallas_call x1, Pallas kernels, on_device(): call(finish_kernel, 'finish', [VMEM] * 5, [whole, f32(2, 3)], 1000000)  1.37 us
  transfers between devices with their start and end apart: 4, of which 0 were waited for; matrix products, arithmetic and copies ran while one was open for 0% of the time, Pallas kernels for 4%

profile of v8, /device:TPU:0, one launch (start us, length us, event | category | flops | bytes accessed | tf_op | source)
XLA Modules:
  0.0 48.6 jit_solution(2598876987224044968)
XLA Ops:
  0.6 0.0 copy-start.1
  0.6 0.0 copy-start.3
  0.7 0.0 copy-start.2
  0.7 0.0 copy-start.4
  0.7 0.0 copy-start
  0.7 0.0 copy-start.5
  0.7 2.5 %pack.1 = (f32[208,512]{1,0:T(8,128)S(1)}, f32[208,512]{1,0:T(8,128)S(1)}) custom-call(f32[2,64,512]{2,1,0:T(8,128)} %rhs_ref.7, f32[64,512]{1,0:T(8,128)} %visc_ref.5, f32[2,64,512]{2,1,0:T(8,128)} %coup_ref.5, f32[48,768]{1,0:T(8,128)} %inverse_ref.5, bf16[48,2,64,512]{3,2,1,0:T(8,128)(2,1)} %held.2), custom_call_target="tpu_custom_call" | custom-call | flops 5000000 | bytes 4000000 | tf_op jit(solution)/shard_map/pack/pallas_call | solution.py:514
  3.2 0.5 %collective-permute-start = (f32[208,512]{1,0:T(8,128)S(1)}, f32[208,512]{1,0:T(8,128)S(1)}, u32[]{:S(2)}, u32[]{:S(2)}) collective-permute-start(f32[208,512]{1,0:T(8,128)S(1)} %get-tuple-element.20), channel_id=1, source_target_pairs={{0,1},{1,0},{2,3},{3,2},{4,5},{5,4},{6,7},{7,6},{8,9},{9,8},{10,11... | collective-permute-start | bytes 1277960 | tf_op jit(solution)/shard_map/ppermute | solution.py:499
  3.8 0.8 %collective-permute-start.1 = (f32[208,512]{1,0:T(8,128)S(1)}, f32[208,512]{1,0:T(8,128)S(1)}, u32[]{:S(2)}, u32[]{:S(2)}) collective-permute-start(f32[208,512]{1,0:T(8,128)S(1)} %get-tuple-element.21), channel_id=1, source_target_pairs={{1,2},{2,1},{3,4},{4,3},{5,6},{6,5},{7,8},{8,7},{9,10},{10,9},{11,... | collective-permute-start | bytes 1277960 | tf_op jit(solution)/shard_map/ppermute | solution.py:500
  4.6 0.0 copy-done.1
  4.6 0.1 copy-done
  4.7 1.7 %restrict.1 = f32[16,128]{1,0:T(8,128)S(1)} custom-call(f32[2,64,512]{2,1,0:T(8,128)S(1)} %copy-done.1, bf16[48,2,64,512]{3,2,1,0:T(8,128)(2,1)S(1)} %copy-done), custom_call_target="tpu_custom_call" | custom-call | flops 10000000 | bytes 4000000 | tf_op jit(solution)/shard_map/restrict/pallas_call | solution.py:521
  6.4 11.8 %all_to_all.33 = f32[16,1,128]{2,1,0:T(1,128)S(1)} all-to-all(f32[16,1,128]{2,1,0:T(1,128)S(1)} %bitcast.19), channel_id=1, replica_groups={{15,14,13,12,11,10,9,8,7,6,5,4,3,2,1,0},{31,30,29,28,27,26,25,24,23,22,..., dimensions={0} | all-to-all | bytes 16384 | tf_op jit(solution)/shard_map/all_to_all | solution.py:492
  18.2 0.0 collective-permute-done.partner_ref
  18.2 0.0 collective-permute-done.1.other_ref
  18.2 0.0 copy-done.3
  18.2 0.0 copy-done.2
  18.2 0.0 copy-done.4
  18.2 0.0 copy-done.5
  18.2 4.6 %first_turn.1 = (f32[2,64,512]{2,1,0:T(8,128)S(1)}, f32[2,64,512]{2,1,0:T(8,128)S(1)}, f32[2,80,512]{2,1,0:T(8,128)S(1)}, f32[2,8,512]{2,1,0:T(8,128)S(1)}, f32[...) custom-call(s32[16]{0:T(128)S(1)} %copy-done.5, f32[16,128]{1,0:T(8,128)S(1)} %bitcast.13, f32[48,768]{1,0:T(8,128)S(1)} %copy-done.3, ...), custom_call_target="tpu_custom_call" | custom-call | flops 20000000 | bytes 4000000 | tf_op jit(solution)/shard_map/first_turn/pallas_call | solution.py:525
  22.8 0.1 collective-permute-start.2
  22.9 0.7 %collective-permute-start.3 = (f32[2,8,512]{2,1,0:T(8,128)S(1)}, f32[2,8,512]{2,1,0:T(8,128)S(1)}, u32[]{:S(2)}, u32[]{:S(2)}) collective-permute-start(f32[2,8,512]{2,1,0:T(8,128)S(1)} %get-tuple-element.24), channel_id=1, source_target_pairs={{1,2},{2,1},{3,4},{4,3},{5,6},{6,5},{7,8},{8,7},{9,10},{10,9},{11,... | collective-permute-start | bytes 98312 | tf_op jit(solution)/shard_map/ppermute | solution.py:500
  23.5 12.0 %all_to_all.34 = f32[16,1,128]{2,1,0:T(1,128)S(1)} all-to-all(f32[16,1,128]{2,1,0:T(1,128)S(1)} %bitcast.20), channel_id=1, replica_groups={{15,14,13,12,11,10,9,8,7,6,5,4,3,2,1,0},{31,30,29,28,27,26,25,24,23,22,..., dimensions={0} | all-to-all | bytes 16384 | tf_op jit(solution)/shard_map/all_to_all | solution.py:492
  35.5 0.0 collective-permute-done.2.partner_rows_ref
  35.5 0.0 collective-permute-done.3.other_rows_ref
  35.5 3.3 %second_turn.1 = (f32[2,64,512]{2,1,0:T(8,128)S(1)}, f32[16,128]{1,0:T(8,128)S(1)}) custom-call(s32[16]{0:T(128)S(1)} %copy-done.5, f32[16,128]{1,0:T(8,128)S(1)} %bitcast.14, f32[16,128]{1,0:T(8,128)S(1)} %bitcast.16, f32[48,768]{1,0:T(8,128)S(1)} %copy-done.3, f32[208,512]{1,0:T(8,128)S(1)} %collective-permute-done.partner_ref, ...), custom_call_target="tpu_custom_call" | custom-call | flops 20000000 | bytes 4000000 | tf_op jit(solution)/shard_map/second_turn/pallas_call | solution.py:531
  38.8 8.4 %all_to_all.35 = f32[16,1,128]{2,1,0:T(1,128)S(1)} all-to-all(f32[16,1,128]{2,1,0:T(1,128)S(1)} %bitcast.21), channel_id=1, replica_groups={{15,14,13,12,11,10,9,8,7,6,5,4,3,2,1,0},{31,30,29,28,27,26,25,24,23,22,..., dimensions={0} | all-to-all | bytes 16384 | tf_op jit(solution)/shard_map/all_to_all | solution.py:492
  47.2 1.4 %finish.1 = (f32[2,64,512]{2,1,0:T(8,128)}, f32[2,3]{1,0:T(2,128)}) custom-call(f32[16,128]{1,0:T(8,128)S(1)} %bitcast.15, f32[16,128]{1,0:T(8,128)S(1)} %bitcast.17, f32[16,128]{1,0:T(8,128)S(1)} %bitcast.18, f32[2,64,512]{2,1,0:T(8,128)S(1)} %get-tuple-element.28.first_direction_ref, f32[2,64,512]{2,1,0:T(8,128)S(1)} %get-tuple-element.29.second_direction_ref), custom_call_target="tpu_custom_call" | custom-call | flops 1000000 | bytes 4000000 | tf_op jit(solution)/shard_map/finish/pallas_call | solution.py:539
Async XLA Ops:
  0.6 3.9 %copy-start.1 = (f32[2,64,512]{2,1,0:T(8,128)S(1)}, f32[2,64,512]{2,1,0:T(8,128)}, u32[]{:S(2)}) copy-start(f32[2,64,512]{2,1,0:T(8,128)} %rhs_ref.7) | copy-start | bytes 786436
  0.6 17.5 %copy-start.3 = (f32[48,768]{1,0:T(8,128)S(1)}, f32[48,768]{1,0:T(8,128)}, u32[]{:S(2)}) copy-start(f32[48,768]{1,0:T(8,128)} %inverse_ref.5) | copy-start | bytes 442372
  0.7 17.5 %copy-start.2 = (f32[2,64,512]{2,1,0:T(8,128)S(1)}, f32[2,64,512]{2,1,0:T(8,128)}, u32[]{:S(2)}) copy-start(f32[2,64,512]{2,1,0:T(8,128)} %coup_ref.5) | copy-start | bytes 786436
  0.7 17.5 %copy-start.4 = (f32[64,512]{1,0:T(8,128)S(1)}, f32[64,512]{1,0:T(8,128)}, u32[]{:S(2)}) copy-start(f32[64,512]{1,0:T(8,128)} %visc_ref.5) | copy-start | bytes 393220
  0.7 4.0 %copy-start = (bf16[48,2,64,512]{3,2,1,0:T(8,128)(2,1)S(1)}, bf16[48,2,64,512]{3,2,1,0:T(8,128)(2,1)}, u32[]{:S(2)}) copy-start(bf16[48,2,64,512]{3,2,1,0:T(8,128)(2,1)} %held.2) | copy-start | bytes 18874372
  0.7 17.5 %copy-start.5 = (s32[16]{0:T(128)S(1)}, s32[16]{0:T(128)}, u32[]{:S(2)}) copy-start(s32[16]{0:T(128)} %margin_ref.3) | copy-start | bytes 196
  3.2 14.9 %collective-permute-start = (f32[208,512]{1,0:T(8,128)S(1)}, f32[208,512]{1,0:T(8,128)S(1)}, u32[]{:S(2)}, u32[]{:S(2)}) collective-permute-start(f32[208,512]{1,0:T(8,128)S(1)} %get-tuple-element.20), channel_id=1, source_target_pairs={{0,1},{1,0},{2,3},{3,2},{4,5},{5,4},{6,7},{7,6},{8,9},{9,8},{10,11... | collective-permute-start | bytes 1277960 | tf_op jit(solution)/shard_map/ppermute | solution.py:499
  3.8 14.4 %collective-permute-start.1 = (f32[208,512]{1,0:T(8,128)S(1)}, f32[208,512]{1,0:T(8,128)S(1)}, u32[]{:S(2)}, u32[]{:S(2)}) collective-permute-start(f32[208,512]{1,0:T(8,128)S(1)} %get-tuple-element.21), channel_id=1, source_target_pairs={{1,2},{2,1},{3,4},{4,3},{5,6},{6,5},{7,8},{8,7},{9,10},{10,9},{11,... | collective-permute-start | bytes 1277960 | tf_op jit(solution)/shard_map/ppermute | solution.py:500
  22.8 12.7 %collective-permute-start.2 = (f32[2,8,512]{2,1,0:T(8,128)S(1)}, f32[2,8,512]{2,1,0:T(8,128)S(1)}, u32[]{:S(2)}, u32[]{:S(2)}) collective-permute-start(f32[2,8,512]{2,1,0:T(8,128)S(1)} %get-tuple-element.23), channel_id=1, source_target_pairs={{0,1},{1,0},{2,3},{3,2},{4,5},{5,4},{6,7},{7,6},{8,9},{9,8},{10,11... | collective-permute-start | bytes 98312 | tf_op jit(solution)/shard_map/ppermute | solution.py:499
  22.9 12.7 %collective-permute-start.3 = (f32[2,8,512]{2,1,0:T(8,128)S(1)}, f32[2,8,512]{2,1,0:T(8,128)S(1)}, u32[]{:S(2)}, u32[]{:S(2)}) collective-permute-start(f32[2,8,512]{2,1,0:T(8,128)S(1)} %get-tuple-element.24), channel_id=1, source_target_pairs={{1,2},{2,1},{3,4},{4,3},{5,6},{6,5},{7,8},{8,7},{9,10},{10,9},{11,... | collective-permute-start | bytes 98312 | tf_op jit(solution)/shard_map/ppermute | solution.py:500

commit v9 on v8

--- a/solution.py
+++ b/solution.py
@@ -13,6 +13,8 @@
 HALO = 8
 EXT = ROWS + 2 * HALO
 STRIP = 32
+STACKED = EXT + 2 * STRIP
+BLOCK = STACKED // 8
 CHUNK = 16
 CHUNKS = 2 * ROWS // CHUNK
 PIECE = 6
@@ -36,17 +38,21 @@
 
 
 def cell_sum(field):
-    lane = lax.broadcasted_iota(jnp.int32, (field.shape[0], LANES), 1)
-    left, right = pltpu.roll(field, 1, 1), pltpu.roll(field, CELLS - 1, 1)
-    inner = left[:, LANES:-LANES] + right[:, LANES:-LANES]
-    first = jnp.where(lane == 0, 0.0, left[:, :LANES]) + right[:, :LANES]
-    last = left[:, -LANES:] + jnp.where(lane == LANES - 1, 0.0, right[:, -LANES:])
-    return jnp.concatenate([first, inner, last], 1)
+    axis = field.ndim - 1
+    lane = lax.broadcasted_iota(jnp.int32, field.shape[:-1] + (LANES,), axis)
+    left, right = pltpu.roll(field, 1, axis), pltpu.roll(field, CELLS - 1, axis)
+    inner = left[..., LANES:-LANES] + right[..., LANES:-LANES]
+    first = jnp.where(lane == 0, 0.0, left[..., :LANES]) + right[..., :LANES]
+    last = left[..., -LANES:] + jnp.where(lane == LANES - 1, 0.0, right[..., -LANES:])
+    return jnp.concatenate([first, inner, last], axis)
 
 
 def row_sum(field):
-    count = field.shape[0]
-    return pltpu.roll(field, 1, 0) + pltpu.roll(field, count - 1, 0)
+    if field.ndim == 2:
+        return pltpu.roll(field, 1, 0) + pltpu.roll(field, field.shape[0] - 1, 0)
+    below = jnp.concatenate([pltpu.roll(field[-1], 1, 0)[None], field[:-1]], 0)
+    above = jnp.concatenate([field[1:], pltpu.roll(field[0], 7, 0)[None]], 0)
+    return below + above
 
 
 def neighbours(field, component):
@@ -197,8 +203,20 @@
     return Neighbour(partner_ref, other_ref), Neighbour(other_ref, partner_ref)
 
 
+def block_rows(ref, index, field):
+    columns = []
+    for c in range(CELLS // LANES):
+        part = field[:, LANES * c : LANES * (c + 1)]
+        ref[index, c, :EXT] = part
+        ref[index, c, EXT : EXT + STRIP] = part[:STRIP]
+        ref[index, c, EXT + STRIP :] = part[EXT - STRIP :]
+        tiles = [ref[index, c, pl.ds(t, 8, stride=BLOCK), :] for t in range(BLOCK)]
+        columns.append(jnp.stack(tiles))
+    return jnp.concatenate(columns, 2)
+
+
 def solve(
-    count, margin_ref, visc_ref, coup_ref, field_ref, low_ref, high_ref, edges, out_ref, beside
+    count, margin_ref, visc_ref, coup_ref, field_ref, low_ref, high_ref, edges, out_ref, stacked
 ):
     rank = lax.axis_index("sub")
     lower = jnp.where(rank > 0, margin_ref[jnp.maximum(rank - 1, 0)], 0)
@@ -207,47 +225,41 @@
     low_scale = 2.0 * jnp.maximum(lower_f, 1.0)
     high_scale = 2.0 * jnp.maximum(upper_f, 1.0)
 
-    def masks(first, rows, side):
-        place = lax.broadcasted_iota(jnp.int32, (rows, LANES), 0) + first
-        place_f = place.astype(jnp.float32)
-        rising = lambda base, scale: (place_f - base + 0.5) / scale
-        falling = lambda base, scale: (base - place_f - 0.5) / scale
-        if side == 0:
-            live = (place >= -lower) & (place < ROWS + upper)
-            weight = jnp.where(place < lower, rising(-lower_f, low_scale), 1.0)
-            weight = jnp.where(
-                place >= ROWS - upper, falling(ROWS + upper_f, high_scale), weight
-            )
-        elif side < 0:
-            live = place < lower
-            weight = jnp.where(place >= -lower, falling(lower_f, low_scale), 1.0)
-        else:
-            live = place >= ROWS - upper
-            weight = jnp.where(place < ROWS + upper, rising(ROWS - upper_f, high_scale), 1.0)
-        wide = lambda x: jnp.concatenate([x] * (CELLS // LANES), 1)
-        return wide(live.astype(jnp.float32)), wide(weight)
-
-    def stack(own, at):
+    shape = (BLOCK, 8, LANES)
+    row = lax.broadcasted_iota(jnp.int32, shape, 0)
+    row = row + BLOCK * lax.broadcasted_iota(jnp.int32, shape, 1)
+    own, below = row < EXT, row < EXT + STRIP
+    place = row - jnp.where(own, HALO, jnp.where(below, EXT + HALO, EXT + 2 * STRIP - ROWS - HALO))
+    place_f = place.astype(jnp.float32)
+    rising = lambda base, scale: (place_f - base + 0.5) / scale
+    falling = lambda base, scale: (base - place_f - 0.5) / scale
+    own_live = (place >= -lower) & (place < ROWS + upper)
+    own_weight = jnp.where(place < lower, rising(-lower_f, low_scale), 1.0)
+    own_weight = jnp.where(place >= ROWS - upper, falling(ROWS + upper_f, high_scale), own_weight)
+    below_live = place < lower
+    below_weight = jnp.where(place >= -lower, falling(lower_f, low_scale), 1.0)
+    above_live = place >= ROWS - upper
+    above_weight = jnp.where(place < ROWS + upper, rising(ROWS - upper_f, high_scale), 1.0)
+    live = (own & own_live) | (~own & below & below_live) | (~below & above_live)
+    weight = jnp.where(own, own_weight, jnp.where(below, below_weight, above_weight))
+    wide = lambda x: jnp.concatenate([x] * (CELLS // LANES), 2)
+    live, weight = wide(live.astype(jnp.float32)), wide(weight)
+
+    def stack(own_rows, at):
         rows = slice(at, at + HALO)
-        return jnp.concatenate([low_ref[rows], own, high_ref[rows]], 0)
-
-    def triple(field):
-        return jnp.concatenate([field, field[:STRIP], field[EXT - STRIP :]], 0)
+        return jnp.concatenate([low_ref[rows], own_rows, high_ref[rows]], 0)
 
     viscosity = stack(visc_ref[...], 0)
-    blocks = [masks(-HALO, EXT, 0), masks(-HALO, STRIP, -1), masks(ROWS + HALO - STRIP, STRIP, 1)]
-    live = jnp.concatenate([block[0] for block in blocks], 0)
     first, across, other = [], [], []
     for a in range(2):
         coupling = stack(coup_ref[a], HALO * (1 + a))
         field = jnp.concatenate([edges[a][0], field_ref[a], edges[a][1]], 0)
         scale = RELAX / (10.0 * viscosity + jnp.abs(coupling) + 0.05)
-        first.append(live * triple(scale * field))
-        across.append(live * triple(scale * viscosity))
-        other.append(live * triple(scale * coupling))
+        first.append(live * block_rows(stacked, 3 * a, scale * field))
+        across.append(live * block_rows(stacked, 3 * a + 1, scale * viscosity))
+        other.append(live * block_rows(stacked, 3 * a + 2, scale * coupling))
     solved = list(first)
-    for sweep in range(1, SWEEPS):
-        beside(sweep)
+    for _ in range(SWEEPS - 1):
         solved = [
             (1.0 - RELAX) * solved[a]
             + first[a]
@@ -256,10 +268,14 @@
             for a in range(2)
         ]
     for a in range(2):
-        shares = solved[a] * jnp.concatenate([block[1] for block in blocks], 0)
-        out_ref[a] = shares[:EXT]
-        out_ref[a, :STRIP] += shares[EXT : EXT + STRIP]
-        out_ref[a, EXT - STRIP :] += shares[EXT + STRIP :]
+        shares = solved[a] * weight
+        for c in range(CELLS // LANES):
+            cells = slice(LANES * c, LANES * (c + 1))
+            for t in range(BLOCK):
+                stacked[3 * a, c, pl.ds(t, 8, stride=BLOCK), :] = shares[t, :, cells]
+            out_ref[a, :, cells] = stacked[3 * a, c, :EXT]
+            out_ref[a, :STRIP, cells] += stacked[3 * a, c, EXT : EXT + STRIP]
+            out_ref[a, EXT - STRIP :, cells] += stacked[3 * a, c, EXT + STRIP :]
 
 
 def line_up(residuals):
@@ -325,18 +341,14 @@
     return jnp.where(place == row, line, 0.0).astype(jnp.bfloat16)
 
 
-def prolonging(residual, inverse_ref, held, extended):
+def prolong(residual, inverse_ref, held, extended):
     matrix = spread(lift(inverse_ref, residual))
-    places = [(a, r) for a in range(2) for r in range(0, ROWS, CHUNK)]
-
-    def beside(n):
-        for a, r in places[n - 1 :: SWEEPS - 1]:
+    for a in range(2):
+        for r in range(0, ROWS, CHUNK):
             rows = held[:, a, r : r + CHUNK, :].reshape(CHUNK * VECTORS, CELLS)
             extended[a, HALO + r : HALO + r + CHUNK] = jnp.dot(
                 matrix, rows, preferred_element_type=jnp.float32
             )
-
-    return beside
 
 
 def add_smooth(residual, low, high, smooth, extended):
@@ -360,16 +372,16 @@
     count, margin_ref, sums_ref, inverse_ref, partner_ref, other_ref, held, rhs_ref, visc_ref,
     coup_ref,
     direction_ref, image_ref, smooth_ref, partner_rows_ref, other_rows_ref, next_ref,
-    extended, sums, turned,
+    extended, sums, turned, stacked,
 ):
     received = sums_ref[...]
     over_beta = 1.0 / jnp.sqrt(lane_total(received, VECTORS))
     residual = line_up(received) * over_beta
-    beside = prolonging(residual, inverse_ref, held, extended)
+    prolong(residual, inverse_ref, held, extended)
     low, high = neighbours_of(partner_ref, other_ref)
     starts = [HALO * (3 + a) for a in range(2)]
     edges = [(low[at : at + HALO], high[at : at + HALO]) for at in starts]
-    solve(count, margin_ref, visc_ref, coup_ref, rhs_ref, low, high, edges, smooth_ref, beside)
+    solve(count, margin_ref, visc_ref, coup_ref, rhs_ref, low, high, edges, smooth_ref, stacked)
     add_smooth(
         residual, low, high, lambda a, rows: smooth_ref[a, rows] * over_beta, extended
     )
@@ -407,19 +419,19 @@
     count, margin_ref, first_ref, second_ref, inverse_ref, partner_ref, other_ref,
     partner_rows_ref, other_rows_ref, held, smooth_ref, rhs_ref, image_ref, visc_ref, coup_ref,
     direction_ref, next_ref,
-    image_smooth, extended, sums, turned,
+    image_smooth, extended, sums, turned, stacked,
 ):
     first, second = first_ref[...], second_ref[...]
     beta, h_00, h_10 = first_column(first, second)
     ratio = h_00 / beta
     over = 1.0 / h_10
     residual = (line_up(second) - ratio * line_up(first)) * over
-    beside = prolonging(residual, inverse_ref, held, extended)
+    prolong(residual, inverse_ref, held, extended)
     low, high = neighbours_of(partner_ref, other_ref)
     low_rows, high_rows = neighbours_of(partner_rows_ref, other_rows_ref)
     edges = [(low_rows[a], high_rows[a]) for a in range(2)]
     solve(
-        count, margin_ref, visc_ref, coup_ref, image_ref, low, high, edges, image_smooth, beside
+        count, margin_ref, visc_ref, coup_ref, image_ref, low, high, edges, image_smooth, stacked
     )
     add_smooth(
         residual,
@@ -446,18 +458,14 @@
 ):
     third = third_ref[...]
     beta, h_00, h_10 = first_column(first_ref[...], second_ref[...])
+    squares = lane_total(third, 2)
     h_01 = lane_total(third, 0) / beta
     h_11 = (lane_total(third, 1) - h_00 * h_01) / h_10
-    h_21 = jnp.sqrt(lane_total(third, 2) - h_01 * h_01 - h_11 * h_11)
-    n_00 = h_00 * h_00 + h_10 * h_10
-    n_10 = h_00 * h_01 + h_10 * h_11
-    n_11 = h_01 * h_01 + h_11 * h_11 + h_21 * h_21
-    l_00 = jnp.sqrt(n_00)
-    l_10 = n_10 / l_00
-    l_11 = jnp.sqrt(n_11 - l_10 * l_10)
+    h_21 = jnp.sqrt(squares - h_01 * h_01 - h_11 * h_11)
+    l_00 = jnp.sqrt(h_00 * h_00 + h_10 * h_10)
+    l_10 = (h_00 * h_01 + h_10 * h_11) / l_00
     f_0 = beta * h_00 / l_00
-    f_1 = (beta * h_01 - l_10 * f_0) / l_11
-    c_1 = f_1 / l_11
+    c_1 = (beta * h_01 - l_10 * f_0) / (squares - l_10 * l_10)
     c_0 = (f_0 - l_10 * c_1) / l_00
     for a in range(2):
         solution_ref[a] = c_0 * first_direction_ref[a] + c_1 * second_direction_ref[a]
@@ -495,10 +503,8 @@
 def swap(partner, other):
     count = lax.axis_size("sub")
     both = lambda lows: [pair for i in lows for pair in ((i, i + 1), (i + 1, i))]
-    return (
-        lax.ppermute(partner, "sub", both(range(0, count, 2))),
-        lax.ppermute(other, "sub", both(range(1, count - 1, 2))),
-    )
+    other = lax.ppermute(other, "sub", both(range(1, count - 1, 2)))
+    return lax.ppermute(partner, "sub", both(range(0, count, 2))), other
 
 
 def on_device(rhs, viscosity, coupling, margin_rows, coarse_basis, coarse_inverse):
@@ -507,6 +513,7 @@
     f32 = lambda *shape: jax.ShapeDtypeStruct(shape, jnp.float32)
     dma = lambda *shape: pltpu.SemaphoreType.DMA(shape)
     extended = pltpu.VMEM((2, EXT, CELLS), jnp.float32)
+    stacked = pltpu.VMEM((6, CELLS // LANES, STACKED, LANES), jnp.float32)
     sums = pltpu.VMEM((8 * SLOTS, LANES), jnp.float32)
     row, whole, edge = f32(count, LANES), f32(2, ROWS, CELLS), f32(2, HALO, CELLS)
     packed, smoothed = f32(EDGE_AT + coarse_rows(columns), CELLS), f32(2, EXT, CELLS)
@@ -524,13 +531,13 @@
     first = from_everyone(first)
     direction, image, smooth, partner_rows, other_rows, second = call(
         functools.partial(first_turn_kernel, count), "first_turn", [SMEM] + [VMEM] * 8,
-        [whole, whole, smoothed, edge, edge, row], 20_000_000, [extended, sums, sums],
+        [whole, whole, smoothed, edge, edge, row], 20_000_000, [extended, sums, sums, stacked],
     )(margin_rows, first, coarse_inverse, partner, other, held, rhs, viscosity, coupling)
     partner_rows, other_rows = swap(partner_rows, other_rows)
     second = from_everyone(second)
     second_direction, third = call(
         functools.partial(second_turn_kernel, count), "second_turn", [SMEM] + [VMEM] * 13,
-        [whole, row], 20_000_000, [extended, extended, sums, sums],
+        [whole, row], 20_000_000, [extended, extended, sums, sums, stacked],
     )(
         margin_rows, first, second, coarse_inverse, partner, other, partner_rows, other_rows,
         held, smooth, rhs, image, viscosity, coupling,

time: 48.9 us -> 49.2 us (level)
  no operation moved by 1% of the time
where the time goes in v9:
time: 49.2 us; the launch traced here: 48.9 us
  blocking collectives  32.2 us (65%)
  Pallas kernels  13.8 us (28%)
  starting transfers between devices  2.06 us (4%)
  between operations  0.74 us (2%)
    all_to_all x3, blocking collectives, from_everyone(): lax.all_to_all(rows, 'sub', 0, 0, tiled=True, axis_index_groups=order)  32.2 us
    pallas_call x1, Pallas kernels, on_device(): call(functools.partial(first_turn_kernel, count), 'first_turn', [SMEM] +...  4.74 us
    pallas_call x1, Pallas kernels, on_device(): call(functools.partial(second_turn_kernel, count), 'second_turn', [SMEM]...  3.42 us
    pallas_call x1, Pallas kernels, on_device(): call(pack_kernel, 'pack', [HBM] * 5, [packed, packed], 5000000, [pltpu.VM...  2.55 us
    pallas_call x1, Pallas kernels, on_device(): call(restrict_kernel, 'restrict', [VMEM] * 2, [row], 10000000, [sums, sums])  1.72 us
    ppermute x2, starting transfers between devices, swap(): other = lax.ppermute(other, 'sub', both(range(1, count - 1, 2)))  1.46 us
    pallas_call x1, Pallas kernels, on_device(): call(finish_kernel, 'finish', [VMEM] * 5, [whole, f32(2, 3)], 1000000)  1.36 us
  transfers between devices with their start and end apart: 4, of which 0 were waited for; matrix products, arithmetic and copies ran while one was open for 0% of the time, Pallas kernels for 4%

profile of v9, /device:TPU:0, one launch (start us, length us, event | category | flops | bytes accessed | tf_op | source)
XLA Modules:
  0.0 48.9 jit_solution(12246673304300380271)
XLA Ops:
  0.6 0.0 copy-start.1
  0.6 0.0 copy-start.3
  0.7 0.0 copy-start.2
  0.7 0.0 copy-start.4
  0.7 0.0 copy-start
  0.7 0.0 copy-start.5
  0.7 2.5 %pack.1 = (f32[208,512]{1,0:T(8,128)S(1)}, f32[208,512]{1,0:T(8,128)S(1)}) custom-call(f32[2,64,512]{2,1,0:T(8,128)} %rhs_ref.7, f32[64,512]{1,0:T(8,128)} %visc_ref.5, f32[2,64,512]{2,1,0:T(8,128)} %coup_ref.5, f32[48,768]{1,0:T(8,128)} %inverse_ref.5, bf16[48,2,64,512]{3,2,1,0:T(8,128)(2,1)} %held.2), custom_call_target="tpu_custom_call" | custom-call | flops 5000000 | bytes 4000000 | tf_op jit(solution)/shard_map/pack/pallas_call | solution.py:521
  3.2 0.5 %collective-permute-start = (f32[208,512]{1,0:T(8,128)S(1)}, f32[208,512]{1,0:T(8,128)S(1)}, u32[]{:S(2)}, u32[]{:S(2)}) collective-permute-start(f32[208,512]{1,0:T(8,128)S(1)} %get-tuple-element.20), channel_id=1, source_target_pairs={{0,1},{1,0},{2,3},{3,2},{4,5},{5,4},{6,7},{7,6},{8,9},{9,8},{10,11... | collective-permute-start | bytes 1277960 | tf_op jit(solution)/shard_map/ppermute | solution.py:507
  3.8 0.8 %collective-permute-start.1 = (f32[208,512]{1,0:T(8,128)S(1)}, f32[208,512]{1,0:T(8,128)S(1)}, u32[]{:S(2)}, u32[]{:S(2)}) collective-permute-start(f32[208,512]{1,0:T(8,128)S(1)} %get-tuple-element.21), channel_id=1, source_target_pairs={{1,2},{2,1},{3,4},{4,3},{5,6},{6,5},{7,8},{8,7},{9,10},{10,9},{11,... | collective-permute-start | bytes 1277960 | tf_op jit(solution)/shard_map/ppermute | solution.py:506
  4.6 0.0 copy-done.1
  4.6 0.1 copy-done
  4.7 1.7 %restrict.1 = f32[16,128]{1,0:T(8,128)S(1)} custom-call(f32[2,64,512]{2,1,0:T(8,128)S(1)} %copy-done.1, bf16[48,2,64,512]{3,2,1,0:T(8,128)(2,1)S(1)} %copy-done), custom_call_target="tpu_custom_call" | custom-call | flops 10000000 | bytes 4000000 | tf_op jit(solution)/shard_map/restrict/pallas_call | solution.py:528
  6.4 11.8 %all_to_all.33 = f32[16,1,128]{2,1,0:T(1,128)S(1)} all-to-all(f32[16,1,128]{2,1,0:T(1,128)S(1)} %bitcast.19), channel_id=1, replica_groups={{15,14,13,12,11,10,9,8,7,6,5,4,3,2,1,0},{31,30,29,28,27,26,25,24,23,22,..., dimensions={0} | all-to-all | bytes 16384 | tf_op jit(solution)/shard_map/all_to_all | solution.py:500
  18.2 0.0 collective-permute-done.partner_ref
  18.2 0.0 collective-permute-done.1.other_ref
  18.2 0.0 copy-done.3
  18.2 0.0 copy-done.2
  18.2 0.0 copy-done.4
  18.2 0.0 copy-done.5
  18.2 4.7 %first_turn.1 = (f32[2,64,512]{2,1,0:T(8,128)S(1)}, f32[2,64,512]{2,1,0:T(8,128)S(1)}, f32[2,80,512]{2,1,0:T(8,128)S(1)}, f32[2,8,512]{2,1,0:T(8,128)S(1)}, f32[...) custom-call(s32[16]{0:T(128)S(1)} %copy-done.5, f32[16,128]{1,0:T(8,128)S(1)} %bitcast.13, f32[48,768]{1,0:T(8,128)S(1)} %copy-done.3, ...), custom_call_target="tpu_custom_call" | custom-call | flops 20000000 | bytes 4000000 | tf_op jit(solution)/shard_map/first_turn/pallas_call | solution.py:532
  23.0 0.1 collective-permute-start.2
  23.0 0.7 %collective-permute-start.3 = (f32[2,8,512]{2,1,0:T(8,128)S(1)}, f32[2,8,512]{2,1,0:T(8,128)S(1)}, u32[]{:S(2)}, u32[]{:S(2)}) collective-permute-start(f32[2,8,512]{2,1,0:T(8,128)S(1)} %get-tuple-element.24), channel_id=1, source_target_pairs={{1,2},{2,1},{3,4},{4,3},{5,6},{6,5},{7,8},{8,7},{9,10},{10,9},{11,... | collective-permute-start | bytes 98312 | tf_op jit(solution)/shard_map/ppermute | solution.py:506
  23.7 12.0 %all_to_all.34 = f32[16,1,128]{2,1,0:T(1,128)S(1)} all-to-all(f32[16,1,128]{2,1,0:T(1,128)S(1)} %bitcast.20), channel_id=1, replica_groups={{15,14,13,12,11,10,9,8,7,6,5,4,3,2,1,0},{31,30,29,28,27,26,25,24,23,22,..., dimensions={0} | all-to-all | bytes 16384 | tf_op jit(solution)/shard_map/all_to_all | solution.py:500
  35.7 0.0 collective-permute-done.2.partner_rows_ref
  35.7 0.0 collective-permute-done.3.other_rows_ref
  35.7 3.4 %second_turn.1 = (f32[2,64,512]{2,1,0:T(8,128)S(1)}, f32[16,128]{1,0:T(8,128)S(1)}) custom-call(s32[16]{0:T(128)S(1)} %copy-done.5, f32[16,128]{1,0:T(8,128)S(1)} %bitcast.14, f32[16,128]{1,0:T(8,128)S(1)} %bitcast.16, f32[48,768]{1,0:T(8,128)S(1)} %copy-done.3, f32[208,512]{1,0:T(8,128)S(1)} %collective-permute-done.partner_ref, ...), custom_call_target="tpu_custom_call" | custom-call | flops 20000000 | bytes 4000000 | tf_op jit(solution)/shard_map/second_turn/pallas_call | solution.py:538
  39.1 8.4 %all_to_all.35 = f32[16,1,128]{2,1,0:T(1,128)S(1)} all-to-all(f32[16,1,128]{2,1,0:T(1,128)S(1)} %bitcast.21), channel_id=1, replica_groups={{15,14,13,12,11,10,9,8,7,6,5,4,3,2,1,0},{31,30,29,28,27,26,25,24,23,22,..., dimensions={0} | all-to-all | bytes 16384 | tf_op jit(solution)/shard_map/all_to_all | solution.py:500
  47.5 1.4 %finish.1 = (f32[2,64,512]{2,1,0:T(8,128)}, f32[2,3]{1,0:T(2,128)}) custom-call(f32[16,128]{1,0:T(8,128)S(1)} %bitcast.15, f32[16,128]{1,0:T(8,128)S(1)} %bitcast.17, f32[16,128]{1,0:T(8,128)S(1)} %bitcast.18, f32[2,64,512]{2,1,0:T(8,128)S(1)} %get-tuple-element.28.first_direction_ref, f32[2,64,512]{2,1,0:T(8,128)S(1)} %get-tuple-element.29.second_direction_ref), custom_call_target="tpu_custom_call" | custom-call | flops 1000000 | bytes 4000000 | tf_op jit(solution)/shard_map/finish/pallas_call | solution.py:546
Async XLA Ops:
  0.6 3.9 %copy-start.1 = (f32[2,64,512]{2,1,0:T(8,128)S(1)}, f32[2,64,512]{2,1,0:T(8,128)}, u32[]{:S(2)}) copy-start(f32[2,64,512]{2,1,0:T(8,128)} %rhs_ref.7) | copy-start | bytes 786436
  0.6 17.5 %copy-start.3 = (f32[48,768]{1,0:T(8,128)S(1)}, f32[48,768]{1,0:T(8,128)}, u32[]{:S(2)}) copy-start(f32[48,768]{1,0:T(8,128)} %inverse_ref.5) | copy-start | bytes 442372
  0.7 17.5 %copy-start.2 = (f32[2,64,512]{2,1,0:T(8,128)S(1)}, f32[2,64,512]{2,1,0:T(8,128)}, u32[]{:S(2)}) copy-start(f32[2,64,512]{2,1,0:T(8,128)} %coup_ref.5) | copy-start | bytes 786436
  0.7 17.5 %copy-start.4 = (f32[64,512]{1,0:T(8,128)S(1)}, f32[64,512]{1,0:T(8,128)}, u32[]{:S(2)}) copy-start(f32[64,512]{1,0:T(8,128)} %visc_ref.5) | copy-start | bytes 393220
  0.7 4.0 %copy-start = (bf16[48,2,64,512]{3,2,1,0:T(8,128)(2,1)S(1)}, bf16[48,2,64,512]{3,2,1,0:T(8,128)(2,1)}, u32[]{:S(2)}) copy-start(bf16[48,2,64,512]{3,2,1,0:T(8,128)(2,1)} %held.2) | copy-start | bytes 18874372
  0.7 17.5 %copy-start.5 = (s32[16]{0:T(128)S(1)}, s32[16]{0:T(128)}, u32[]{:S(2)}) copy-start(s32[16]{0:T(128)} %margin_ref.3) | copy-start | bytes 196
  3.2 14.9 %collective-permute-start = (f32[208,512]{1,0:T(8,128)S(1)}, f32[208,512]{1,0:T(8,128)S(1)}, u32[]{:S(2)}, u32[]{:S(2)}) collective-permute-start(f32[208,512]{1,0:T(8,128)S(1)} %get-tuple-element.20), channel_id=1, source_target_pairs={{0,1},{1,0},{2,3},{3,2},{4,5},{5,4},{6,7},{7,6},{8,9},{9,8},{10,11... | collective-permute-start | bytes 1277960 | tf_op jit(solution)/shard_map/ppermute | solution.py:507
  3.8 14.4 %collective-permute-start.1 = (f32[208,512]{1,0:T(8,128)S(1)}, f32[208,512]{1,0:T(8,128)S(1)}, u32[]{:S(2)}, u32[]{:S(2)}) collective-permute-start(f32[208,512]{1,0:T(8,128)S(1)} %get-tuple-element.21), channel_id=1, source_target_pairs={{1,2},{2,1},{3,4},{4,3},{5,6},{6,5},{7,8},{8,7},{9,10},{10,9},{11,... | collective-permute-start | bytes 1277960 | tf_op jit(solution)/shard_map/ppermute | solution.py:506
  23.0 12.7 %collective-permute-start.2 = (f32[2,8,512]{2,1,0:T(8,128)S(1)}, f32[2,8,512]{2,1,0:T(8,128)S(1)}, u32[]{:S(2)}, u32[]{:S(2)}) collective-permute-start(f32[2,8,512]{2,1,0:T(8,128)S(1)} %get-tuple-element.23), channel_id=1, source_target_pairs={{0,1},{1,0},{2,3},{3,2},{4,5},{5,4},{6,7},{7,6},{8,9},{9,8},{10,11... | collective-permute-start | bytes 98312 | tf_op jit(solution)/shard_map/ppermute | solution.py:507
  23.0 12.7 %collective-permute-start.3 = (f32[2,8,512]{2,1,0:T(8,128)S(1)}, f32[2,8,512]{2,1,0:T(8,128)S(1)}, u32[]{:S(2)}, u32[]{:S(2)}) collective-permute-start(f32[2,8,512]{2,1,0:T(8,128)S(1)} %get-tuple-element.24), channel_id=1, source_target_pairs={{1,2},{2,1},{3,4},{4,3},{5,6},{6,5},{7,8},{8,7},{9,10},{10,9},{11,... | collective-permute-start | bytes 98312 | tf_op jit(solution)/shard_map/ppermute | solution.py:506

commit v10 on v8

--- a/solution.py
+++ b/solution.py
@@ -13,6 +13,8 @@
 HALO = 8
 EXT = ROWS + 2 * HALO
 STRIP = 32
+STACKED = EXT + 2 * STRIP
+TILE = 8
 CHUNK = 16
 CHUNKS = 2 * ROWS // CHUNK
 PIECE = 6
@@ -44,54 +46,63 @@
     return jnp.concatenate([first, inner, last], 1)
 
 
-def row_sum(field):
-    count = field.shape[0]
-    return pltpu.roll(field, 1, 0) + pltpu.roll(field, count - 1, 0)
-
-
-def neighbours(field, component):
-    rows, cells = row_sum(field), cell_sum(field)
+class Rows:
+    def __init__(self, read, first, last):
+        self.read, self.first, self.last = read, first, last
+        self.tiles, self.down, self.up = {}, {}, {}
+
+    def at(self, t):
+        if t not in self.tiles:
+            self.tiles[t] = self.read(t)
+        return self.tiles[t]
+
+    def moved(self, held, t, by):
+        if t not in held:
+            held[t] = pltpu.roll(self.at(t), by, 0)
+        return held[t]
+
+    def around(self, t):
+        row = lax.broadcasted_iota(jnp.int32, (TILE, CELLS), 0)
+        below, above = self.moved(self.down, t, 1), self.moved(self.up, t, TILE - 1)
+        if t > self.first:
+            below = jnp.where(row == 0, self.moved(self.down, t - 1, 1), below)
+        if t < self.last:
+            above = jnp.where(row == TILE - 1, self.moved(self.up, t + 1, TILE - 1), above)
+        return below + above
+
+
+def neighbours(rows, t, component):
+    around, cells = rows.around(t), cell_sum(rows.at(t))
     if component == 0:
-        return rows + CELL_FACTOR[0] * cells
-    return ROW_FACTOR[1] * rows + cells
-
-
-def apply_operator(extended, viscosity, coupling):
-    inner = slice(HALO, HALO + ROWS)
-    images = []
-    for a in range(2):
-        around = neighbours(extended[a], a)[inner]
-        diagonal = 10.0 * viscosity + jnp.abs(coupling[a]) + 0.05
-        images.append(
-            diagonal * extended[a][inner]
-            - viscosity * around
-            + coupling[a] * extended[1 - a][inner]
-        )
-    return images
+        return around + CELL_FACTOR[0] * cells
+    return ROW_FACTOR[1] * around + cells
 
 
 def restrict_piece(i, held, field, sums):
     for n in range(PIECE):
         k = PIECE * i + n
-        total = None
-        for a in range(2):
-            for r in range(0, ROWS, CHUNK):
-                for c in range(0, CELLS, LANES):
+        totals = []
+        for c in range(0, CELLS, LANES):
+            total = None
+            for a in range(2):
+                for r in range(0, ROWS, CHUNK):
                     rows, cells = slice(r, r + CHUNK), slice(c, c + LANES)
                     term = held[k, a, rows, cells].astype(jnp.float32) * field[a, rows, cells]
-                    term = term[:8] + term[8:]
                     total = term if total is None else total + term
+            totals.append(total[:8] + total[8:])
+        total = (totals[0] + totals[1]) + (totals[2] + totals[3])
         sums[pl.ds(pl.multiple_of(8 * k, 8), 8), :] = total
 
 
-def fold(field):
-    total = None
-    for part in field:
-        for r in range(0, part.shape[0], 8):
-            for c in range(0, part.shape[1], LANES):
-                term = part[r : r + 8, c : c + LANES]
-                total = term if total is None else total + term
+def fold(row):
+    total = row[:, :LANES]
+    for c in range(LANES, CELLS, LANES):
+        total = total + row[:, c : c + LANES]
     return total
+
+
+def tile_rows(t):
+    return slice(TILE * t, TILE * (t + 1))
 
 
 def send_sums(sums, turned, out_ref):
@@ -174,7 +185,12 @@
 
 def restrict_kernel(rhs_ref, held, sums_ref, sums, turned):
     sums[...] = jnp.zeros_like(sums)
-    sums[8 * VECTORS : 8 * VECTORS + 8] = fold([rhs_ref[a] * rhs_ref[a] for a in range(2)])
+    squares = jnp.zeros((TILE, CELLS), jnp.float32)
+    for a in range(2):
+        for t in range(ROWS // TILE):
+            tile = rhs_ref[a, tile_rows(t)]
+            squares = squares + tile * tile
+    sums[8 * VECTORS : 8 * VECTORS + 8] = fold(squares)
 
     def body(i, carry):
         restrict_piece(i, held, rhs_ref, sums)
@@ -197,69 +213,97 @@
     return Neighbour(partner_ref, other_ref), Neighbour(other_ref, partner_ref)
 
 
-def solve(
-    count, margin_ref, visc_ref, coup_ref, field_ref, low_ref, high_ref, edges, out_ref, beside
-):
+def solve(count, margin_ref, visc_ref, coup_ref, field, low, high, out_ref, stacked, solved):
     rank = lax.axis_index("sub")
     lower = jnp.where(rank > 0, margin_ref[jnp.maximum(rank - 1, 0)], 0)
     upper = jnp.where(rank < count - 1, margin_ref[rank], 0)
     lower_f, upper_f = lower.astype(jnp.float32), upper.astype(jnp.float32)
-    low_scale = 2.0 * jnp.maximum(lower_f, 1.0)
-    high_scale = 2.0 * jnp.maximum(upper_f, 1.0)
-
-    def masks(first, rows, side):
-        place = lax.broadcasted_iota(jnp.int32, (rows, LANES), 0) + first
+    low_scale = 1.0 / (2.0 * jnp.maximum(lower_f, 1.0))
+    high_scale = 1.0 / (2.0 * jnp.maximum(upper_f, 1.0))
+    wide = lambda x: jnp.concatenate([x] * (CELLS // LANES), 1)
+    own_tiles = ROWS // TILE
+    strip_tiles = STRIP // TILE
+    last = own_tiles + 1
+    segments = (
+        (0, 0, last + 1),
+        (last + 1, 0, strip_tiles),
+        (last + 1 + strip_tiles, last + 1 - strip_tiles, strip_tiles),
+    )
+
+    def place_of(e):
+        return lax.broadcasted_iota(jnp.int32, (TILE, LANES), 0) + (TILE * e - HALO)
+
+    def live_of(segment, e):
+        place = place_of(e)
+        if segment == 0:
+            live = (place >= -lower) & (place < ROWS + upper)
+        elif segment == 1:
+            live = place < lower
+        else:
+            live = place >= ROWS - upper
+        return wide(live.astype(jnp.float32))
+
+    def weight_of(segment, e):
+        place = place_of(e)
         place_f = place.astype(jnp.float32)
-        rising = lambda base, scale: (place_f - base + 0.5) / scale
-        falling = lambda base, scale: (base - place_f - 0.5) / scale
-        if side == 0:
-            live = (place >= -lower) & (place < ROWS + upper)
+        rising = lambda base, scale: (place_f - base + 0.5) * scale
+        falling = lambda base, scale: (base - place_f - 0.5) * scale
+        if segment == 0:
             weight = jnp.where(place < lower, rising(-lower_f, low_scale), 1.0)
             weight = jnp.where(
                 place >= ROWS - upper, falling(ROWS + upper_f, high_scale), weight
             )
-        elif side < 0:
-            live = place < lower
+        elif segment == 1:
             weight = jnp.where(place >= -lower, falling(lower_f, low_scale), 1.0)
         else:
-            live = place >= ROWS - upper
             weight = jnp.where(place < ROWS + upper, rising(ROWS - upper_f, high_scale), 1.0)
-        wide = lambda x: jnp.concatenate([x] * (CELLS // LANES), 1)
-        return wide(live.astype(jnp.float32)), wide(weight)
-
-    def stack(own, at):
-        rows = slice(at, at + HALO)
-        return jnp.concatenate([low_ref[rows], own, high_ref[rows]], 0)
-
-    def triple(field):
-        return jnp.concatenate([field, field[:STRIP], field[EXT - STRIP :]], 0)
-
-    viscosity = stack(visc_ref[...], 0)
-    blocks = [masks(-HALO, EXT, 0), masks(-HALO, STRIP, -1), masks(ROWS + HALO - STRIP, STRIP, 1)]
-    live = jnp.concatenate([block[0] for block in blocks], 0)
-    first, across, other = [], [], []
-    for a in range(2):
-        coupling = stack(coup_ref[a], HALO * (1 + a))
-        field = jnp.concatenate([edges[a][0], field_ref[a], edges[a][1]], 0)
-        scale = RELAX / (10.0 * viscosity + jnp.abs(coupling) + 0.05)
-        first.append(live * triple(scale * field))
-        across.append(live * triple(scale * viscosity))
-        other.append(live * triple(scale * coupling))
-    solved = list(first)
+        return wide(weight)
+
+    def extended(ref, at, e):
+        if e == 0:
+            return low[at : at + HALO]
+        if e == last:
+            return high[at : at + HALO]
+        return ref[tile_rows(e - 1)]
+
+    for e in range(last + 1):
+        viscosity = extended(visc_ref, 0, e)
+        for a in range(2):
+            coupling = extended(coup_ref.at[a], HALO * (1 + a), e)
+            scale = RELAX / (10.0 * viscosity + jnp.abs(coupling) + 0.05)
+            parts = (scale * field(a, e - 1), scale * viscosity, scale * coupling)
+            for n, (first, begin, size) in enumerate(segments):
+                if not begin <= e < begin + size:
+                    continue
+                rows = tile_rows(first + e - begin)
+                always = n == 0 and 0 < e < last
+                for m, part in enumerate(parts):
+                    stacked[3 * a + m, rows] = part if always else live_of(n, e) * part
+
     for sweep in range(1, SWEEPS):
-        beside(sweep)
-        solved = [
-            (1.0 - RELAX) * solved[a]
-            + first[a]
-            + across[a] * neighbours(solved[a], a)
-            - other[a] * solved[1 - a]
-            for a in range(2)
-        ]
-    for a in range(2):
-        shares = solved[a] * jnp.concatenate([block[1] for block in blocks], 0)
-        out_ref[a] = shares[:EXT]
-        out_ref[a, :STRIP] += shares[EXT : EXT + STRIP]
-        out_ref[a, EXT - STRIP :] += shares[EXT + STRIP :]
+        for n, (first, begin, size) in enumerate(segments):
+            end = first + size - 1
+            if sweep == 1:
+                reads = [lambda t, a=a: stacked[3 * a, tile_rows(t)] for a in range(2)]
+            else:
+                bank = 2 * (sweep % 2)
+                reads = [lambda t, a=a: solved[bank + a, tile_rows(t)] for a in range(2)]
+            fields = [Rows(read, first, end) for read in reads]
+            for t in range(first, end + 1):
+                rows = tile_rows(t)
+                for a in range(2):
+                    value = (
+                        ((1.0 - RELAX) * fields[a].at(t) + stacked[3 * a, rows])
+                        + stacked[3 * a + 1, rows] * neighbours(fields[a], t, a)
+                        - stacked[3 * a + 2, rows] * fields[1 - a].at(t)
+                    )
+                    e = t - first + begin
+                    if sweep < SWEEPS - 1:
+                        solved[2 * ((sweep + 1) % 2) + a, rows] = value
+                    elif n == 0:
+                        out_ref[a, tile_rows(e)] = weight_of(n, e) * value
+                    else:
+                        out_ref[a, tile_rows(e)] += weight_of(n, e) * value
 
 
 def line_up(residuals):
@@ -325,31 +369,43 @@
     return jnp.where(place == row, line, 0.0).astype(jnp.bfloat16)
 
 
-def prolonging(residual, inverse_ref, held, extended):
+def prolong(residual, inverse_ref, held, extended):
     matrix = spread(lift(inverse_ref, residual))
-    places = [(a, r) for a in range(2) for r in range(0, ROWS, CHUNK)]
-
-    def beside(n):
-        for a, r in places[n - 1 :: SWEEPS - 1]:
+    for a in range(2):
+        for r in range(0, ROWS, CHUNK):
             rows = held[:, a, r : r + CHUNK, :].reshape(CHUNK * VECTORS, CELLS)
             extended[a, HALO + r : HALO + r + CHUNK] = jnp.dot(
                 matrix, rows, preferred_element_type=jnp.float32
             )
 
-    return beside
-
-
-def add_smooth(residual, low, high, smooth, extended):
-    low_edge = edge_values(low, lift_packed(low, residual))
-    high_edge = edge_values(high, lift_packed(high, residual))
-    place = lax.broadcasted_iota(jnp.int32, (HALO, CELLS), 0)
-    for a in range(2):
-        rows = slice(HALO, HALO + ROWS)
-        extended[a, rows] += smooth(a, rows)
-        rows = slice(0, HALO)
-        extended[a, rows] = smooth(a, rows) + jnp.where(place == HALO - 1, low_edge[a], 0.0)
-        rows = slice(EXT - HALO, EXT)
-        extended[a, rows] = smooth(a, rows) + jnp.where(place == 0, high_edge[a], 0.0)
+
+def apply_operator(residual, low, high, smooth, extended, visc_ref, coup_ref, direction_ref):
+    edges = [edge_values(side, lift_packed(side, residual)) for side in (low, high)]
+    place = lax.broadcasted_iota(jnp.int32, (TILE, CELLS), 0)
+    tiles = ROWS // TILE
+
+    def read(t, a):
+        if t < 0:
+            return smooth(a, 0) + jnp.where(place == TILE - 1, edges[0][a], 0.0)
+        if t == tiles:
+            return smooth(a, t + 1) + jnp.where(place == 0, edges[1][a], 0.0)
+        tile = smooth(a, t + 1) + extended[a, tile_rows(t + 1)]
+        direction_ref[a, tile_rows(t)] = tile
+        return tile
+
+    fields = [Rows(lambda t, a=a: read(t, a), -1, tiles) for a in range(2)]
+    for t in range(tiles):
+        rows = tile_rows(t)
+        viscosity = visc_ref[rows]
+        for a in range(2):
+            coupling = coup_ref[a, rows]
+            diagonal = 10.0 * viscosity + jnp.abs(coupling) + 0.05
+            image = (
+                diagonal * fields[a].at(t)
+                - viscosity * neighbours(fields[a], t, a)
+                + coupling * fields[1 - a].at(t)
+            )
+            yield t, a, image
 
 
 def lane_total(received, lane):
@@ -360,33 +416,45 @@
     count, margin_ref, sums_ref, inverse_ref, partner_ref, other_ref, held, rhs_ref, visc_ref,
     coup_ref,
     direction_ref, image_ref, smooth_ref, partner_rows_ref, other_rows_ref, next_ref,
-    extended, sums, turned,
+    extended, sums, turned, stacked, solved,
 ):
     received = sums_ref[...]
     over_beta = 1.0 / jnp.sqrt(lane_total(received, VECTORS))
     residual = line_up(received) * over_beta
-    beside = prolonging(residual, inverse_ref, held, extended)
+    prolong(residual, inverse_ref, held, extended)
     low, high = neighbours_of(partner_ref, other_ref)
-    starts = [HALO * (3 + a) for a in range(2)]
-    edges = [(low[at : at + HALO], high[at : at + HALO]) for at in starts]
-    solve(count, margin_ref, visc_ref, coup_ref, rhs_ref, low, high, edges, smooth_ref, beside)
-    add_smooth(
-        residual, low, high, lambda a, rows: smooth_ref[a, rows] * over_beta, extended
-    )
+
+    def field(a, t):
+        at = HALO * (3 + a)
+        if t < 0:
+            return low[at : at + HALO]
+        return high[at : at + HALO] if t == ROWS // TILE else rhs_ref[a, tile_rows(t)]
+
+    solve(
+        count, margin_ref, visc_ref, coup_ref, field, low, high, smooth_ref, stacked, solved
+    )
+    smooth = lambda a, t: smooth_ref[a, tile_rows(t)] * over_beta
     images = apply_operator(
-        [extended[a] for a in range(2)], visc_ref[...], [coup_ref[a] for a in range(2)]
+        residual, low, high, smooth, extended, visc_ref, coup_ref, direction_ref
     )
     odd = lax.axis_index("sub") % 2 == 1
+    products, squares = [jnp.zeros((TILE, CELLS), jnp.float32)] * 2
+    heads, tails = [None] * 2, [None] * 2
+    for t, a, image in images:
+        image_ref[a, tile_rows(t)] = image
+        products = products + rhs_ref[a, tile_rows(t)] * image
+        squares = squares + image * image
+        if t == 0:
+            heads[a] = image
+        if t == ROWS // TILE - 1:
+            tails[a] = image
     for a in range(2):
-        direction_ref[a] = extended[a, HALO : HALO + ROWS]
-        image_ref[a] = images[a]
-        head, tail = images[a][:HALO], images[a][ROWS - HALO :]
-        partner_rows_ref[a] = jnp.where(odd, head, tail)
-        other_rows_ref[a] = jnp.where(odd, tail, head)
+        partner_rows_ref[a] = jnp.where(odd, heads[a], tails[a])
+        other_rows_ref[a] = jnp.where(odd, tails[a], heads[a])
     sums[...] = jnp.zeros_like(sums)
     at = 8 * VECTORS
-    sums[at : at + 8] = fold([rhs_ref[a] * images[a] for a in range(2)])
-    sums[at + 8 : at + 16] = fold([images[a] * images[a] for a in range(2)])
+    sums[at : at + 8] = fold(products)
+    sums[at + 8 : at + 16] = fold(squares)
 
     def body(i, carry):
         restrict_piece(i, held, image_ref, sums)
@@ -407,36 +475,40 @@
     count, margin_ref, first_ref, second_ref, inverse_ref, partner_ref, other_ref,
     partner_rows_ref, other_rows_ref, held, smooth_ref, rhs_ref, image_ref, visc_ref, coup_ref,
     direction_ref, next_ref,
-    image_smooth, extended, sums, turned,
+    image_smooth, extended, sums, turned, stacked, solved,
 ):
     first, second = first_ref[...], second_ref[...]
     beta, h_00, h_10 = first_column(first, second)
     ratio = h_00 / beta
     over = 1.0 / h_10
     residual = (line_up(second) - ratio * line_up(first)) * over
-    beside = prolonging(residual, inverse_ref, held, extended)
+    prolong(residual, inverse_ref, held, extended)
     low, high = neighbours_of(partner_ref, other_ref)
     low_rows, high_rows = neighbours_of(partner_rows_ref, other_rows_ref)
-    edges = [(low_rows[a], high_rows[a]) for a in range(2)]
+
+    def field(a, t):
+        if t < 0:
+            return low_rows[a]
+        return high_rows[a] if t == ROWS // TILE else image_ref[a, tile_rows(t)]
+
     solve(
-        count, margin_ref, visc_ref, coup_ref, image_ref, low, high, edges, image_smooth, beside
-    )
-    add_smooth(
-        residual,
-        low,
-        high,
-        lambda a, rows: (image_smooth[a, rows] - ratio * smooth_ref[a, rows]) * over,
-        extended,
-    )
+        count, margin_ref, visc_ref, coup_ref, field, low, high, image_smooth, stacked, solved
+    )
+
+    def smooth(a, t):
+        rows = tile_rows(t)
+        return (image_smooth[a, rows] - ratio * smooth_ref[a, rows]) * over
+
     images = apply_operator(
-        [extended[a] for a in range(2)], visc_ref[...], [coup_ref[a] for a in range(2)]
-    )
+        residual, low, high, smooth, extended, visc_ref, coup_ref, direction_ref
+    )
+    totals = [jnp.zeros((TILE, CELLS), jnp.float32)] * 3
+    for t, a, image in images:
+        others = (rhs_ref[a, tile_rows(t)], image_ref[a, tile_rows(t)], image)
+        totals = [total + x * image for total, x in zip(totals, others)]
     sums[...] = jnp.zeros_like(sums)
-    sums[0:8] = fold([rhs_ref[a] * images[a] for a in range(2)])
-    sums[8:16] = fold([image_ref[a] * images[a] for a in range(2)])
-    sums[16:24] = fold([images[a] * images[a] for a in range(2)])
-    for a in range(2):
-        direction_ref[a] = extended[a, HALO : HALO + ROWS]
+    for n, total in enumerate(totals):
+        sums[8 * n : 8 * n + 8] = fold(total)
     send_sums(sums, turned, next_ref)
 
 
@@ -446,18 +518,14 @@
 ):
     third = third_ref[...]
     beta, h_00, h_10 = first_column(first_ref[...], second_ref[...])
+    squares = lane_total(third, 2)
     h_01 = lane_total(third, 0) / beta
     h_11 = (lane_total(third, 1) - h_00 * h_01) / h_10
-    h_21 = jnp.sqrt(lane_total(third, 2) - h_01 * h_01 - h_11 * h_11)
-    n_00 = h_00 * h_00 + h_10 * h_10
-    n_10 = h_00 * h_01 + h_10 * h_11
-    n_11 = h_01 * h_01 + h_11 * h_11 + h_21 * h_21
-    l_00 = jnp.sqrt(n_00)
-    l_10 = n_10 / l_00
-    l_11 = jnp.sqrt(n_11 - l_10 * l_10)
+    h_21 = jnp.sqrt(squares - h_01 * h_01 - h_11 * h_11)
+    l_00 = jnp.sqrt(h_00 * h_00 + h_10 * h_10)
+    l_10 = (h_00 * h_01 + h_10 * h_11) / l_00
     f_0 = beta * h_00 / l_00
-    f_1 = (beta * h_01 - l_10 * f_0) / l_11
-    c_1 = f_1 / l_11
+    c_1 = (beta * h_01 - l_10 * f_0) / (squares - l_10 * l_10)
     c_0 = (f_0 - l_10 * c_1) / l_00
     for a in range(2):
         solution_ref[a] = c_0 * first_direction_ref[a] + c_1 * second_direction_ref[a]
@@ -507,6 +575,8 @@
     f32 = lambda *shape: jax.ShapeDtypeStruct(shape, jnp.float32)
     dma = lambda *shape: pltpu.SemaphoreType.DMA(shape)
     extended = pltpu.VMEM((2, EXT, CELLS), jnp.float32)
+    stacked = pltpu.VMEM((6, STACKED, CELLS), jnp.float32)
+    solved = pltpu.VMEM((4, STACKED, CELLS), jnp.float32)
     sums = pltpu.VMEM((8 * SLOTS, LANES), jnp.float32)
     row, whole, edge = f32(count, LANES), f32(2, ROWS, CELLS), f32(2, HALO, CELLS)
     packed, smoothed = f32(EDGE_AT + coarse_rows(columns), CELLS), f32(2, EXT, CELLS)
@@ -524,13 +594,13 @@
     first = from_everyone(first)
     direction, image, smooth, partner_rows, other_rows, second = call(
         functools.partial(first_turn_kernel, count), "first_turn", [SMEM] + [VMEM] * 8,
-        [whole, whole, smoothed, edge, edge, row], 20_000_000, [extended, sums, sums],
+        [whole, whole, smoothed, edge, edge, row], 20_000_000, [extended, sums, sums, stacked, solved],
     )(margin_rows, first, coarse_inverse, partner, other, held, rhs, viscosity, coupling)
     partner_rows, other_rows = swap(partner_rows, other_rows)
     second = from_everyone(second)
     second_direction, third = call(
         functools.partial(second_turn_kernel, count), "second_turn", [SMEM] + [VMEM] * 13,
-        [whole, row], 20_000_000, [extended, extended, sums, sums],
+        [whole, row], 20_000_000, [extended, extended, sums, sums, stacked, solved],
     )(
         margin_rows, first, second, coarse_inverse, partner, other, partner_rows, other_rows,
         held, smooth, rhs, image, viscosity, coupling,

time: 48.9 us -> 48.3 us (0.988)
  Pallas kernels: 13.5 us -> 12.9 us
where the time goes in v10:
time: 48.3 us; the launch traced here: 48 us
  blocking collectives  32.2 us (67%)
  Pallas kernels  12.9 us (27%)
  starting transfers between devices  2.07 us (4%)
  between operations  0.74 us (2%)
    all_to_all x3, blocking collectives, from_everyone(): lax.all_to_all(rows, 'sub', 0, 0, tiled=True, axis_index_groups=order)  32.2 us
    pallas_call x1, Pallas kernels, on_device(): call(functools.partial(first_turn_kernel, count), 'first_turn', [SMEM] +...  4.21 us
    pallas_call x1, Pallas kernels, on_device(): call(functools.partial(second_turn_kernel, count), 'second_turn', [SMEM]...  3.04 us
    pallas_call x1, Pallas kernels, on_device(): call(pack_kernel, 'pack', [HBM] * 5, [packed, packed], 5000000, [pltpu.VM...  2.55 us
    pallas_call x1, Pallas kernels, on_device(): call(restrict_kernel, 'restrict', [VMEM] * 2, [row], 10000000, [sums, sums])  1.71 us
    ppermute x2, starting transfers between devices, swap(): lax.ppermute(other, 'sub', both(range(1, count - 1, 2)))  1.46 us
    pallas_call x1, Pallas kernels, on_device(): call(finish_kernel, 'finish', [VMEM] * 5, [whole, f32(2, 3)], 1000000)  1.36 us
  transfers between devices with their start and end apart: 4, of which 0 were waited for; matrix products, arithmetic and copies ran while one was open for 0% of the time, Pallas kernels for 4%

profile of v10, /device:TPU:0, one launch (start us, length us, event | category | flops | bytes accessed | tf_op | source)
XLA Modules:
  0.0 48.0 jit_solution(2629271585778073664)
XLA Ops:
  0.6 0.0 copy-start.1
  0.6 0.0 copy-start.3
  0.7 0.0 copy-start.2
  0.7 0.0 copy-start.4
  0.7 0.0 copy-start
  0.7 0.0 copy-start.5
  0.7 2.5 %pack.1 = (f32[208,512]{1,0:T(8,128)S(1)}, f32[208,512]{1,0:T(8,128)S(1)}) custom-call(f32[2,64,512]{2,1,0:T(8,128)} %rhs_ref.7, f32[64,512]{1,0:T(8,128)} %visc_ref.5, f32[2,64,512]{2,1,0:T(8,128)} %coup_ref.5, f32[48,768]{1,0:T(8,128)} %inverse_ref.5, bf16[48,2,64,512]{3,2,1,0:T(8,128)(2,1)} %held.2), custom_call_target="tpu_custom_call" | custom-call | flops 5000000 | bytes 4000000 | tf_op jit(solution)/shard_map/pack/pallas_call | solution.py:584
  3.2 0.5 %collective-permute-start = (f32[208,512]{1,0:T(8,128)S(1)}, f32[208,512]{1,0:T(8,128)S(1)}, u32[]{:S(2)}, u32[]{:S(2)}) collective-permute-start(f32[208,512]{1,0:T(8,128)S(1)} %get-tuple-element.20), channel_id=1, source_target_pairs={{0,1},{1,0},{2,3},{3,2},{4,5},{5,4},{6,7},{7,6},{8,9},{9,8},{10,11... | collective-permute-start | bytes 1277960 | tf_op jit(solution)/shard_map/ppermute | solution.py:567
  3.8 0.8 %collective-permute-start.1 = (f32[208,512]{1,0:T(8,128)S(1)}, f32[208,512]{1,0:T(8,128)S(1)}, u32[]{:S(2)}, u32[]{:S(2)}) collective-permute-start(f32[208,512]{1,0:T(8,128)S(1)} %get-tuple-element.21), channel_id=1, source_target_pairs={{1,2},{2,1},{3,4},{4,3},{5,6},{6,5},{7,8},{8,7},{9,10},{10,9},{11,... | collective-permute-start | bytes 1277960 | tf_op jit(solution)/shard_map/ppermute | solution.py:568
  4.6 0.0 copy-done.1
  4.6 0.1 copy-done
  4.7 1.7 %restrict.1 = f32[16,128]{1,0:T(8,128)S(1)} custom-call(f32[2,64,512]{2,1,0:T(8,128)S(1)} %copy-done.1, bf16[48,2,64,512]{3,2,1,0:T(8,128)(2,1)S(1)} %copy-done), custom_call_target="tpu_custom_call" | custom-call | flops 10000000 | bytes 4000000 | tf_op jit(solution)/shard_map/restrict/pallas_call | solution.py:591
  6.4 11.8 %all_to_all.33 = f32[16,1,128]{2,1,0:T(1,128)S(1)} all-to-all(f32[16,1,128]{2,1,0:T(1,128)S(1)} %bitcast.19), channel_id=1, replica_groups={{15,14,13,12,11,10,9,8,7,6,5,4,3,2,1,0},{31,30,29,28,27,26,25,24,23,22,..., dimensions={0} | all-to-all | bytes 16384 | tf_op jit(solution)/shard_map/all_to_all | solution.py:560
  18.2 0.0 collective-permute-done.partner_ref
  18.2 0.0 collective-permute-done.1.other_ref
  18.2 0.0 copy-done.3
  18.2 0.0 copy-done.2
  18.2 0.0 copy-done.4
  18.2 0.0 copy-done.5
  18.2 4.2 %first_turn.1 = (f32[2,64,512]{2,1,0:T(8,128)S(1)}, f32[2,64,512]{2,1,0:T(8,128)S(1)}, f32[2,80,512]{2,1,0:T(8,128)S(1)}, f32[2,8,512]{2,1,0:T(8,128)S(1)}, f32[...) custom-call(s32[16]{0:T(128)S(1)} %copy-done.5, f32[16,128]{1,0:T(8,128)S(1)} %bitcast.13, f32[48,768]{1,0:T(8,128)S(1)} %copy-done.3, ...), custom_call_target="tpu_custom_call" | custom-call | flops 20000000 | bytes 4000000 | tf_op jit(solution)/shard_map/first_turn/pallas_call | solution.py:595
  22.4 0.1 collective-permute-start.2
  22.5 0.7 %collective-permute-start.3 = (f32[2,8,512]{2,1,0:T(8,128)S(1)}, f32[2,8,512]{2,1,0:T(8,128)S(1)}, u32[]{:S(2)}, u32[]{:S(2)}) collective-permute-start(f32[2,8,512]{2,1,0:T(8,128)S(1)} %get-tuple-element.24), channel_id=1, source_target_pairs={{1,2},{2,1},{3,4},{4,3},{5,6},{6,5},{7,8},{8,7},{9,10},{10,9},{11,... | collective-permute-start | bytes 98312 | tf_op jit(solution)/shard_map/ppermute | solution.py:568
  23.2 12.0 %all_to_all.34 = f32[16,1,128]{2,1,0:T(1,128)S(1)} all-to-all(f32[16,1,128]{2,1,0:T(1,128)S(1)} %bitcast.20), channel_id=1, replica_groups={{15,14,13,12,11,10,9,8,7,6,5,4,3,2,1,0},{31,30,29,28,27,26,25,24,23,22,..., dimensions={0} | all-to-all | bytes 16384 | tf_op jit(solution)/shard_map/all_to_all | solution.py:560
  35.2 0.0 collective-permute-done.2.partner_rows_ref
  35.2 0.0 collective-permute-done.3.other_rows_ref
  35.2 3.0 %second_turn.1 = (f32[2,64,512]{2,1,0:T(8,128)S(1)}, f32[16,128]{1,0:T(8,128)S(1)}) custom-call(s32[16]{0:T(128)S(1)} %copy-done.5, f32[16,128]{1,0:T(8,128)S(1)} %bitcast.14, f32[16,128]{1,0:T(8,128)S(1)} %bitcast.16, f32[48,768]{1,0:T(8,128)S(1)} %copy-done.3, f32[208,512]{1,0:T(8,128)S(1)} %collective-permute-done.partner_ref, ...), custom_call_target="tpu_custom_call" | custom-call | flops 20000000 | bytes 4000000 | tf_op jit(solution)/shard_map/second_turn/pallas_call | solution.py:601
  38.2 8.4 %all_to_all.35 = f32[16,1,128]{2,1,0:T(1,128)S(1)} all-to-all(f32[16,1,128]{2,1,0:T(1,128)S(1)} %bitcast.21), channel_id=1, replica_groups={{15,14,13,12,11,10,9,8,7,6,5,4,3,2,1,0},{31,30,29,28,27,26,25,24,23,22,..., dimensions={0} | all-to-all | bytes 16384 | tf_op jit(solution)/shard_map/all_to_all | solution.py:560
  46.6 1.4 %finish.1 = (f32[2,64,512]{2,1,0:T(8,128)}, f32[2,3]{1,0:T(2,128)}) custom-call(f32[16,128]{1,0:T(8,128)S(1)} %bitcast.15, f32[16,128]{1,0:T(8,128)S(1)} %bitcast.17, f32[16,128]{1,0:T(8,128)S(1)} %bitcast.18, f32[2,64,512]{2,1,0:T(8,128)S(1)} %get-tuple-element.28.first_direction_ref, f32[2,64,512]{2,1,0:T(8,128)S(1)} %get-tuple-element.29.second_direction_ref), custom_call_target="tpu_custom_call" | custom-call | flops 1000000 | bytes 4000000 | tf_op jit(solution)/shard_map/finish/pallas_call | solution.py:609
Async XLA Ops:
  0.6 3.9 %copy-start.1 = (f32[2,64,512]{2,1,0:T(8,128)S(1)}, f32[2,64,512]{2,1,0:T(8,128)}, u32[]{:S(2)}) copy-start(f32[2,64,512]{2,1,0:T(8,128)} %rhs_ref.7) | copy-start | bytes 786436
  0.6 17.5 %copy-start.3 = (f32[48,768]{1,0:T(8,128)S(1)}, f32[48,768]{1,0:T(8,128)}, u32[]{:S(2)}) copy-start(f32[48,768]{1,0:T(8,128)} %inverse_ref.5) | copy-start | bytes 442372
  0.7 17.5 %copy-start.2 = (f32[2,64,512]{2,1,0:T(8,128)S(1)}, f32[2,64,512]{2,1,0:T(8,128)}, u32[]{:S(2)}) copy-start(f32[2,64,512]{2,1,0:T(8,128)} %coup_ref.5) | copy-start | bytes 786436
  0.7 17.5 %copy-start.4 = (f32[64,512]{1,0:T(8,128)S(1)}, f32[64,512]{1,0:T(8,128)}, u32[]{:S(2)}) copy-start(f32[64,512]{1,0:T(8,128)} %visc_ref.5) | copy-start | bytes 393220
  0.7 4.0 %copy-start = (bf16[48,2,64,512]{3,2,1,0:T(8,128)(2,1)S(1)}, bf16[48,2,64,512]{3,2,1,0:T(8,128)(2,1)}, u32[]{:S(2)}) copy-start(bf16[48,2,64,512]{3,2,1,0:T(8,128)(2,1)} %held.2) | copy-start | bytes 18874372
  0.7 17.5 %copy-start.5 = (s32[16]{0:T(128)S(1)}, s32[16]{0:T(128)}, u32[]{:S(2)}) copy-start(s32[16]{0:T(128)} %margin_ref.3) | copy-start | bytes 196
  3.2 14.9 %collective-permute-start = (f32[208,512]{1,0:T(8,128)S(1)}, f32[208,512]{1,0:T(8,128)S(1)}, u32[]{:S(2)}, u32[]{:S(2)}) collective-permute-start(f32[208,512]{1,0:T(8,128)S(1)} %get-tuple-element.20), channel_id=1, source_target_pairs={{0,1},{1,0},{2,3},{3,2},{4,5},{5,4},{6,7},{7,6},{8,9},{9,8},{10,11... | collective-permute-start | bytes 1277960 | tf_op jit(solution)/shard_map/ppermute | solution.py:567
  3.8 14.4 %collective-permute-start.1 = (f32[208,512]{1,0:T(8,128)S(1)}, f32[208,512]{1,0:T(8,128)S(1)}, u32[]{:S(2)}, u32[]{:S(2)}) collective-permute-start(f32[208,512]{1,0:T(8,128)S(1)} %get-tuple-element.21), channel_id=1, source_target_pairs={{1,2},{2,1},{3,4},{4,3},{5,6},{6,5},{7,8},{8,7},{9,10},{10,9},{11,... | collective-permute-start | bytes 1277960 | tf_op jit(solution)/shard_map/ppermute | solution.py:568
  22.4 12.8 %collective-permute-start.2 = (f32[2,8,512]{2,1,0:T(8,128)S(1)}, f32[2,8,512]{2,1,0:T(8,128)S(1)}, u32[]{:S(2)}, u32[]{:S(2)}) collective-permute-start(f32[2,8,512]{2,1,0:T(8,128)S(1)} %get-tuple-element.23), channel_id=1, source_target_pairs={{0,1},{1,0},{2,3},{3,2},{4,5},{5,4},{6,7},{7,6},{8,9},{9,8},{10,11... | collective-permute-start | bytes 98312 | tf_op jit(solution)/shard_map/ppermute | solution.py:567
  22.5 12.7 %collective-permute-start.3 = (f32[2,8,512]{2,1,0:T(8,128)S(1)}, f32[2,8,512]{2,1,0:T(8,128)S(1)}, u32[]{:S(2)}, u32[]{:S(2)}) collective-permute-start(f32[2,8,512]{2,1,0:T(8,128)S(1)} %get-tuple-element.24), channel_id=1, source_target_pairs={{1,2},{2,1},{3,4},{4,3},{5,6},{6,5},{7,8},{8,7},{9,10},{10,9},{11,... | collective-permute-start | bytes 98312 | tf_op jit(solution)/shard_map/ppermute | solution.py:568

commit v11 on v10

--- a/solution.py
+++ b/solution.py
@@ -17,10 +17,10 @@
 TILE = 8
 CHUNK = 16
 CHUNKS = 2 * ROWS // CHUNK
-PIECE = 6
+PIECE = 8
 PIECES = VECTORS // PIECE
 LANES = 128
-SLOTS = 56
+SLOTS = 64
 EDGE_AT = 5 * HALO
 INVERSE_AT = 2 * VECTORS
 SWEEPS = 4
@@ -78,20 +78,32 @@
     return ROW_FACTOR[1] * around + cells
 
 
+def sublane_sum(tile):
+    for by in (4, 2, 1):
+        tile = tile + pltpu.roll(tile, by, 0)
+    return tile
+
+
+def in_rows(tiles):
+    row = lax.broadcasted_iota(jnp.int32, (8, LANES), 0)
+    total = jnp.zeros((8, LANES), jnp.float32)
+    for n, tile in enumerate(tiles):
+        total = jnp.where(row == n, sublane_sum(tile), total)
+    return total
+
+
 def restrict_piece(i, held, field, sums):
-    for n in range(PIECE):
-        k = PIECE * i + n
-        totals = []
-        for c in range(0, CELLS, LANES):
-            total = None
-            for a in range(2):
-                for r in range(0, ROWS, CHUNK):
-                    rows, cells = slice(r, r + CHUNK), slice(c, c + LANES)
-                    term = held[k, a, rows, cells].astype(jnp.float32) * field[a, rows, cells]
-                    total = term if total is None else total + term
-            totals.append(total[:8] + total[8:])
-        total = (totals[0] + totals[1]) + (totals[2] + totals[3])
-        sums[pl.ds(pl.multiple_of(8 * k, 8), 8), :] = total
+    totals = [None] * PIECE
+    for a in range(2):
+        for r in range(0, ROWS, CHUNK):
+            for c in range(0, CELLS, LANES):
+                rows, cells = slice(r, r + CHUNK), slice(c, c + LANES)
+                tile = field[a, rows, cells]
+                for n in range(PIECE):
+                    term = held[PIECE * i + n, a, rows, cells].astype(jnp.float32) * tile
+                    totals[n] = term if totals[n] is None else totals[n] + term
+    tiles = [total[:8] + total[8:] for total in totals]
+    sums[pl.ds(pl.multiple_of(PIECE * i, PIECE), PIECE), :] = in_rows(tiles)
 
 
 def fold(row):
@@ -105,17 +117,17 @@
     return slice(TILE * t, TILE * (t + 1))
 
 
-def send_sums(sums, turned, out_ref):
-    for k in range(SLOTS):
-        turned[pl.ds(k, 8, stride=SLOTS), :] = sums[8 * k : 8 * k + 8, :]
-    by_slot = turned[:SLOTS]
-    for j in range(1, 8):
-        by_slot = by_slot + turned[SLOTS * j : SLOTS * (j + 1)]
+def send_sums(sums, out_ref):
+    rest = sums[...]
+    parts = []
+    for _ in range(3):
+        part = rest.astype(jnp.bfloat16)
+        parts.append(part)
+        rest = rest - part.astype(jnp.float32)
     row = lax.dot_general(
-        jnp.ones((8, LANES), jnp.float32),
-        by_slot,
+        jnp.ones((CHUNK, 3 * LANES), jnp.bfloat16),
+        jnp.concatenate(parts, 1),
         (((1,), (1,)), ((), ())),
-        precision=lax.Precision.HIGHEST,
         preferred_element_type=jnp.float32,
     )
     wide = jnp.concatenate([row[:1], jnp.zeros((1, LANES - SLOTS), jnp.float32)], 1)
@@ -183,21 +195,21 @@
         copy.wait()
 
 
-def restrict_kernel(rhs_ref, held, sums_ref, sums, turned):
+def restrict_kernel(rhs_ref, held, sums_ref, sums):
     sums[...] = jnp.zeros_like(sums)
     squares = jnp.zeros((TILE, CELLS), jnp.float32)
     for a in range(2):
         for t in range(ROWS // TILE):
             tile = rhs_ref[a, tile_rows(t)]
             squares = squares + tile * tile
-    sums[8 * VECTORS : 8 * VECTORS + 8] = fold(squares)
+    sums[VECTORS : VECTORS + 8] = in_rows([fold(squares)])
 
     def body(i, carry):
         restrict_piece(i, held, rhs_ref, sums)
         return carry
 
     lax.fori_loop(0, PIECES, body, 0)
-    send_sums(sums, turned, sums_ref)
+    send_sums(sums, sums_ref)
 
 
 class Neighbour:
@@ -213,7 +225,9 @@
     return Neighbour(partner_ref, other_ref), Neighbour(other_ref, partner_ref)
 
 
-def solve(count, margin_ref, visc_ref, coup_ref, field, low, high, out_ref, stacked, solved):
+def solve(count, margin_ref, visc_ref, coup_ref, field, low, high, out_ref, stacked, solved, steps):
+    waiting, done = list(steps), 0
+    every = (SWEEPS - 1) * (STACKED // TILE) // len(waiting)
     rank = lax.axis_index("sub")
     lower = jnp.where(rank > 0, margin_ref[jnp.maximum(rank - 1, 0)], 0)
     upper = jnp.where(rank < count - 1, margin_ref[rank], 0)
@@ -291,6 +305,9 @@
             fields = [Rows(read, first, end) for read in reads]
             for t in range(first, end + 1):
                 rows = tile_rows(t)
+                if done % every == 0 and waiting:
+                    waiting.pop(0)()
+                done += 1
                 for a in range(2):
                     value = (
                         ((1.0 - RELAX) * fields[a].at(t) + stacked[3 * a, rows])
@@ -369,14 +386,16 @@
     return jnp.where(place == row, line, 0.0).astype(jnp.bfloat16)
 
 
-def prolong(residual, inverse_ref, held, extended):
+def prolonging(residual, inverse_ref, held, extended):
     matrix = spread(lift(inverse_ref, residual))
-    for a in range(2):
-        for r in range(0, ROWS, CHUNK):
-            rows = held[:, a, r : r + CHUNK, :].reshape(CHUNK * VECTORS, CELLS)
-            extended[a, HALO + r : HALO + r + CHUNK] = jnp.dot(
-                matrix, rows, preferred_element_type=jnp.float32
-            )
+
+    def step(a, r):
+        rows = held[:, a, r : r + CHUNK, :].reshape(CHUNK * VECTORS, CELLS)
+        extended[a, HALO + r : HALO + r + CHUNK] = jnp.dot(
+            matrix, rows, preferred_element_type=jnp.float32
+        )
+
+    return [functools.partial(step, a, r) for a in range(2) for r in range(0, ROWS, CHUNK)]
 
 
 def apply_operator(residual, low, high, smooth, extended, visc_ref, coup_ref, direction_ref):
@@ -416,12 +435,12 @@
     count, margin_ref, sums_ref, inverse_ref, partner_ref, other_ref, held, rhs_ref, visc_ref,
     coup_ref,
     direction_ref, image_ref, smooth_ref, partner_rows_ref, other_rows_ref, next_ref,
-    extended, sums, turned, stacked, solved,
+    extended, sums, stacked, solved,
 ):
     received = sums_ref[...]
     over_beta = 1.0 / jnp.sqrt(lane_total(received, VECTORS))
     residual = line_up(received) * over_beta
-    prolong(residual, inverse_ref, held, extended)
+    steps = prolonging(residual, inverse_ref, held, extended)
     low, high = neighbours_of(partner_ref, other_ref)
 
     def field(a, t):
@@ -431,7 +450,8 @@
         return high[at : at + HALO] if t == ROWS // TILE else rhs_ref[a, tile_rows(t)]
 
     solve(
-        count, margin_ref, visc_ref, coup_ref, field, low, high, smooth_ref, stacked, solved
+        count, margin_ref, visc_ref, coup_ref, field, low, high, smooth_ref, stacked, solved,
+        steps,
     )
     smooth = lambda a, t: smooth_ref[a, tile_rows(t)] * over_beta
     images = apply_operator(
@@ -452,16 +472,14 @@
         partner_rows_ref[a] = jnp.where(odd, heads[a], tails[a])
         other_rows_ref[a] = jnp.where(odd, tails[a], heads[a])
     sums[...] = jnp.zeros_like(sums)
-    at = 8 * VECTORS
-    sums[at : at + 8] = fold(products)
-    sums[at + 8 : at + 16] = fold(squares)
+    sums[VECTORS : VECTORS + 8] = in_rows([fold(products), fold(squares)])
 
     def body(i, carry):
         restrict_piece(i, held, image_ref, sums)
         return carry
 
     lax.fori_loop(0, PIECES, body, 0)
-    send_sums(sums, turned, next_ref)
+    send_sums(sums, next_ref)
 
 
 def first_column(first, second):
@@ -475,14 +493,14 @@
     count, margin_ref, first_ref, second_ref, inverse_ref, partner_ref, other_ref,
     partner_rows_ref, other_rows_ref, held, smooth_ref, rhs_ref, image_ref, visc_ref, coup_ref,
     direction_ref, next_ref,
-    image_smooth, extended, sums, turned, stacked, solved,
+    image_smooth, extended, sums, stacked, solved,
 ):
     first, second = first_ref[...], second_ref[...]
     beta, h_00, h_10 = first_column(first, second)
     ratio = h_00 / beta
     over = 1.0 / h_10
     residual = (line_up(second) - ratio * line_up(first)) * over
-    prolong(residual, inverse_ref, held, extended)
+    steps = prolonging(residual, inverse_ref, held, extended)
     low, high = neighbours_of(partner_ref, other_ref)
     low_rows, high_rows = neighbours_of(partner_rows_ref, other_rows_ref)
 
@@ -492,7 +510,8 @@
         return high_rows[a] if t == ROWS // TILE else image_ref[a, tile_rows(t)]
 
     solve(
-        count, margin_ref, visc_ref, coup_ref, field, low, high, image_smooth, stacked, solved
+        count, margin_ref, visc_ref, coup_ref, field, low, high, image_smooth, stacked, solved,
+        steps,
     )
 
     def smooth(a, t):
@@ -507,9 +526,8 @@
         others = (rhs_ref[a, tile_rows(t)], image_ref[a, tile_rows(t)], image)
         totals = [total + x * image for total, x in zip(totals, others)]
     sums[...] = jnp.zeros_like(sums)
-    for n, total in enumerate(totals):
-        sums[8 * n : 8 * n + 8] = fold(total)
-    send_sums(sums, turned, next_ref)
+    sums[:8] = in_rows([fold(total) for total in totals])
+    send_sums(sums, next_ref)
 
 
 def finish_kernel(
@@ -577,7 +595,7 @@
     extended = pltpu.VMEM((2, EXT, CELLS), jnp.float32)
     stacked = pltpu.VMEM((6, STACKED, CELLS), jnp.float32)
     solved = pltpu.VMEM((4, STACKED, CELLS), jnp.float32)
-    sums = pltpu.VMEM((8 * SLOTS, LANES), jnp.float32)
+    sums = pltpu.VMEM((SLOTS, LANES), jnp.float32)
     row, whole, edge = f32(count, LANES), f32(2, ROWS, CELLS), f32(2, HALO, CELLS)
     packed, smoothed = f32(EDGE_AT + coarse_rows(columns), CELLS), f32(2, EXT, CELLS)
     arguments = (rhs, viscosity, coupling, coarse_inverse, coarse_basis)
@@ -589,18 +607,18 @@
     held, partner, other = lax.optimization_barrier((coarse_basis, *packs))
     partner, other = swap(partner, other)
     (first,) = call(
-        restrict_kernel, "restrict", [VMEM] * 2, [row], 10_000_000, [sums, sums]
+        restrict_kernel, "restrict", [VMEM] * 2, [row], 10_000_000, [sums]
     )(rhs, held)
     first = from_everyone(first)
     direction, image, smooth, partner_rows, other_rows, second = call(
         functools.partial(first_turn_kernel, count), "first_turn", [SMEM] + [VMEM] * 8,
-        [whole, whole, smoothed, edge, edge, row], 20_000_000, [extended, sums, sums, stacked, solved],
+        [whole, whole, smoothed, edge, edge, row], 20_000_000, [extended, sums, stacked, solved],
     )(margin_rows, first, coarse_inverse, partner, other, held, rhs, viscosity, coupling)
     partner_rows, other_rows = swap(partner_rows, other_rows)
     second = from_everyone(second)
     second_direction, third = call(
         functools.partial(second_turn_kernel, count), "second_turn", [SMEM] + [VMEM] * 13,
-        [whole, row], 20_000_000, [extended, extended, sums, sums, stacked, solved],
+        [whole, row], 20_000_000, [extended, extended, sums, stacked, solved],
     )(
         margin_rows, first, second, coarse_inverse, partner, other, partner_rows, other_rows,
         held, smooth, rhs, image, viscosity, coupling,

time: 48.3 us -> 47.8 us (0.990)
  Pallas kernels: 12.9 us -> 12.3 us
  transfers between devices with their start and end apart: 4 -> 4, of which waited for: 0 -> 0; matrix products, arithmetic and copies ran while one was open for 0% -> 0% of each run, Pallas kernels for 4% -> 3%
where the time goes in v11:
time: 47.8 us; the launch traced here: 47.5 us
  blocking collectives  32.2 us (67%)
  Pallas kernels  12.3 us (26%)
  starting transfers between devices  2.21 us (5%)
  between operations  0.74 us (2%)
    all_to_all x3, blocking collectives, from_everyone(): lax.all_to_all(rows, 'sub', 0, 0, tiled=True, axis_index_groups=order)  32.2 us
    pallas_call x1, Pallas kernels, on_device(): call(functools.partial(first_turn_kernel, count), 'first_turn', [SMEM] +...  4.07 us
    pallas_call x1, Pallas kernels, on_device(): call(functools.partial(second_turn_kernel, count), 'second_turn', [SMEM]...  2.85 us
    pallas_call x1, Pallas kernels, on_device(): call(pack_kernel, 'pack', [HBM] * 5, [packed, packed], 5000000, [pltpu.VM...  2.55 us
    pallas_call x1, Pallas kernels, on_device(): call(restrict_kernel, 'restrict', [VMEM] * 2, [row], 10000000, [sums])  1.47 us
    ppermute x2, starting transfers between devices, swap(): lax.ppermute(other, 'sub', both(range(1, count - 1, 2)))  1.46 us
    pallas_call x1, Pallas kernels, on_device(): call(finish_kernel, 'finish', [VMEM] * 5, [whole, f32(2, 3)], 1000000)  1.36 us
  transfers between devices with their start and end apart: 4, of which 0 were waited for; matrix products, arithmetic and copies ran while one was open for 0% of the time, Pallas kernels for 3%

profile of v11, /device:TPU:0, one launch (start us, length us, event | category | flops | bytes accessed | tf_op | source)
XLA Modules:
  0.0 47.5 jit_solution(349755468258313304)
XLA Ops:
  0.6 0.0 copy-start.1
  0.6 0.0 copy-start.3
  0.7 0.0 copy-start.2
  0.7 0.0 copy-start.4
  0.7 0.0 copy-start
  0.7 0.0 copy-start.5
  0.7 2.5 %pack.1 = (f32[208,512]{1,0:T(8,128)S(1)}, f32[208,512]{1,0:T(8,128)S(1)}) custom-call(f32[2,64,512]{2,1,0:T(8,128)} %rhs_ref.7, f32[64,512]{1,0:T(8,128)} %visc_ref.5, f32[2,64,512]{2,1,0:T(8,128)} %coup_ref.5, f32[48,768]{1,0:T(8,128)} %inverse_ref.5, bf16[48,2,64,512]{3,2,1,0:T(8,128)(2,1)} %held.2), custom_call_target="tpu_custom_call" | custom-call | flops 5000000 | bytes 4000000 | tf_op jit(solution)/shard_map/pack/pallas_call | solution.py:602
  3.2 0.5 %collective-permute-start = (f32[208,512]{1,0:T(8,128)S(1)}, f32[208,512]{1,0:T(8,128)S(1)}, u32[]{:S(2)}, u32[]{:S(2)}) collective-permute-start(f32[208,512]{1,0:T(8,128)S(1)} %get-tuple-element.20), channel_id=1, source_target_pairs={{0,1},{1,0},{2,3},{3,2},{4,5},{5,4},{6,7},{7,6},{8,9},{9,8},{10,11... | collective-permute-start | bytes 1277960 | tf_op jit(solution)/shard_map/ppermute | solution.py:585
  3.8 0.8 %collective-permute-start.1 = (f32[208,512]{1,0:T(8,128)S(1)}, f32[208,512]{1,0:T(8,128)S(1)}, u32[]{:S(2)}, u32[]{:S(2)}) collective-permute-start(f32[208,512]{1,0:T(8,128)S(1)} %get-tuple-element.21), channel_id=1, source_target_pairs={{1,2},{2,1},{3,4},{4,3},{5,6},{6,5},{7,8},{8,7},{9,10},{10,9},{11,... | collective-permute-start | bytes 1277960 | tf_op jit(solution)/shard_map/ppermute | solution.py:586
  4.6 0.0 copy-done.1
  4.6 0.1 copy-done
  4.7 1.5 %restrict.1 = f32[16,128]{1,0:T(8,128)S(1)} custom-call(f32[2,64,512]{2,1,0:T(8,128)S(1)} %copy-done.1, bf16[48,2,64,512]{3,2,1,0:T(8,128)(2,1)S(1)} %copy-done), custom_call_target="tpu_custom_call" | custom-call | flops 10000000 | bytes 4000000 | tf_op jit(solution)/shard_map/restrict/pallas_call | solution.py:609
  6.1 11.8 %all_to_all.33 = f32[16,1,128]{2,1,0:T(1,128)S(1)} all-to-all(f32[16,1,128]{2,1,0:T(1,128)S(1)} %bitcast.19), channel_id=1, replica_groups={{15,14,13,12,11,10,9,8,7,6,5,4,3,2,1,0},{31,30,29,28,27,26,25,24,23,22,..., dimensions={0} | all-to-all | bytes 16384 | tf_op jit(solution)/shard_map/all_to_all | solution.py:578
  18.0 0.0 collective-permute-done.partner_ref
  18.0 0.0 collective-permute-done.1.other_ref
  18.0 0.0 copy-done.3
  18.0 0.0 copy-done.2
  18.0 0.0 copy-done.4
  18.0 0.0 copy-done.5
  18.0 4.1 %first_turn.1 = (f32[2,64,512]{2,1,0:T(8,128)S(1)}, f32[2,64,512]{2,1,0:T(8,128)S(1)}, f32[2,80,512]{2,1,0:T(8,128)S(1)}, f32[2,8,512]{2,1,0:T(8,128)S(1)}, f32[...) custom-call(s32[16]{0:T(128)S(1)} %copy-done.5, f32[16,128]{1,0:T(8,128)S(1)} %bitcast.13, f32[48,768]{1,0:T(8,128)S(1)} %copy-done.3, ...), custom_call_target="tpu_custom_call" | custom-call | flops 20000000 | bytes 4000000 | tf_op jit(solution)/shard_map/first_turn/pallas_call | solution.py:613
  22.1 0.2 collective-permute-start.2
  22.3 0.7 %collective-permute-start.3 = (f32[2,8,512]{2,1,0:T(8,128)S(1)}, f32[2,8,512]{2,1,0:T(8,128)S(1)}, u32[]{:S(2)}, u32[]{:S(2)}) collective-permute-start(f32[2,8,512]{2,1,0:T(8,128)S(1)} %get-tuple-element.24), channel_id=1, source_target_pairs={{1,2},{2,1},{3,4},{4,3},{5,6},{6,5},{7,8},{8,7},{9,10},{10,9},{11,... | collective-permute-start | bytes 98312 | tf_op jit(solution)/shard_map/ppermute | solution.py:586
  23.0 12.0 %all_to_all.34 = f32[16,1,128]{2,1,0:T(1,128)S(1)} all-to-all(f32[16,1,128]{2,1,0:T(1,128)S(1)} %bitcast.20), channel_id=1, replica_groups={{15,14,13,12,11,10,9,8,7,6,5,4,3,2,1,0},{31,30,29,28,27,26,25,24,23,22,..., dimensions={0} | all-to-all | bytes 16384 | tf_op jit(solution)/shard_map/all_to_all | solution.py:578
  35.0 0.0 collective-permute-done.2.partner_rows_ref
  35.0 0.0 collective-permute-done.3.other_rows_ref
  35.0 2.8 %second_turn.1 = (f32[2,64,512]{2,1,0:T(8,128)S(1)}, f32[16,128]{1,0:T(8,128)S(1)}) custom-call(s32[16]{0:T(128)S(1)} %copy-done.5, f32[16,128]{1,0:T(8,128)S(1)} %bitcast.14, f32[16,128]{1,0:T(8,128)S(1)} %bitcast.16, f32[48,768]{1,0:T(8,128)S(1)} %copy-done.3, f32[208,512]{1,0:T(8,128)S(1)} %collective-permute-done.partner_ref, ...), custom_call_target="tpu_custom_call" | custom-call | flops 20000000 | bytes 4000000 | tf_op jit(solution)/shard_map/second_turn/pallas_call | solution.py:619
  37.8 8.4 %all_to_all.35 = f32[16,1,128]{2,1,0:T(1,128)S(1)} all-to-all(f32[16,1,128]{2,1,0:T(1,128)S(1)} %bitcast.21), channel_id=1, replica_groups={{15,14,13,12,11,10,9,8,7,6,5,4,3,2,1,0},{31,30,29,28,27,26,25,24,23,22,..., dimensions={0} | all-to-all | bytes 16384 | tf_op jit(solution)/shard_map/all_to_all | solution.py:578
  46.2 1.4 %finish.1 = (f32[2,64,512]{2,1,0:T(8,128)}, f32[2,3]{1,0:T(2,128)}) custom-call(f32[16,128]{1,0:T(8,128)S(1)} %bitcast.15, f32[16,128]{1,0:T(8,128)S(1)} %bitcast.17, f32[16,128]{1,0:T(8,128)S(1)} %bitcast.18, f32[2,64,512]{2,1,0:T(8,128)S(1)} %get-tuple-element.28.first_direction_ref, f32[2,64,512]{2,1,0:T(8,128)S(1)} %get-tuple-element.29.second_direction_ref), custom_call_target="tpu_custom_call" | custom-call | flops 1000000 | bytes 4000000 | tf_op jit(solution)/shard_map/finish/pallas_call | solution.py:627
Async XLA Ops:
  0.6 3.9 %copy-start.1 = (f32[2,64,512]{2,1,0:T(8,128)S(1)}, f32[2,64,512]{2,1,0:T(8,128)}, u32[]{:S(2)}) copy-start(f32[2,64,512]{2,1,0:T(8,128)} %rhs_ref.7) | copy-start | bytes 786436
  0.6 17.3 %copy-start.3 = (f32[48,768]{1,0:T(8,128)S(1)}, f32[48,768]{1,0:T(8,128)}, u32[]{:S(2)}) copy-start(f32[48,768]{1,0:T(8,128)} %inverse_ref.5) | copy-start | bytes 442372
  0.7 17.3 %copy-start.2 = (f32[2,64,512]{2,1,0:T(8,128)S(1)}, f32[2,64,512]{2,1,0:T(8,128)}, u32[]{:S(2)}) copy-start(f32[2,64,512]{2,1,0:T(8,128)} %coup_ref.5) | copy-start | bytes 786436
  0.7 17.3 %copy-start.4 = (f32[64,512]{1,0:T(8,128)S(1)}, f32[64,512]{1,0:T(8,128)}, u32[]{:S(2)}) copy-start(f32[64,512]{1,0:T(8,128)} %visc_ref.5) | copy-start | bytes 393220
  0.7 4.0 %copy-start = (bf16[48,2,64,512]{3,2,1,0:T(8,128)(2,1)S(1)}, bf16[48,2,64,512]{3,2,1,0:T(8,128)(2,1)}, u32[]{:S(2)}) copy-start(bf16[48,2,64,512]{3,2,1,0:T(8,128)(2,1)} %held.2) | copy-start | bytes 18874372
  0.7 17.3 %copy-start.5 = (s32[16]{0:T(128)S(1)}, s32[16]{0:T(128)}, u32[]{:S(2)}) copy-start(s32[16]{0:T(128)} %margin_ref.3) | copy-start | bytes 196
  3.2 14.7 %collective-permute-start = (f32[208,512]{1,0:T(8,128)S(1)}, f32[208,512]{1,0:T(8,128)S(1)}, u32[]{:S(2)}, u32[]{:S(2)}) collective-permute-start(f32[208,512]{1,0:T(8,128)S(1)} %get-tuple-element.20), channel_id=1, source_target_pairs={{0,1},{1,0},{2,3},{3,2},{4,5},{5,4},{6,7},{7,6},{8,9},{9,8},{10,11... | collective-permute-start | bytes 1277960 | tf_op jit(solution)/shard_map/ppermute | solution.py:585
  3.8 14.2 %collective-permute-start.1 = (f32[208,512]{1,0:T(8,128)S(1)}, f32[208,512]{1,0:T(8,128)S(1)}, u32[]{:S(2)}, u32[]{:S(2)}) collective-permute-start(f32[208,512]{1,0:T(8,128)S(1)} %get-tuple-element.21), channel_id=1, source_target_pairs={{1,2},{2,1},{3,4},{4,3},{5,6},{6,5},{7,8},{8,7},{9,10},{10,9},{11,... | collective-permute-start | bytes 1277960 | tf_op jit(solution)/shard_map/ppermute | solution.py:586
  22.1 12.9 %collective-permute-start.2 = (f32[2,8,512]{2,1,0:T(8,128)S(1)}, f32[2,8,512]{2,1,0:T(8,128)S(1)}, u32[]{:S(2)}, u32[]{:S(2)}) collective-permute-start(f32[2,8,512]{2,1,0:T(8,128)S(1)} %get-tuple-element.23), channel_id=1, source_target_pairs={{0,1},{1,0},{2,3},{3,2},{4,5},{5,4},{6,7},{7,6},{8,9},{9,8},{10,11... | collective-permute-start | bytes 98312 | tf_op jit(solution)/shard_map/ppermute | solution.py:585
  22.3 12.7 %collective-permute-start.3 = (f32[2,8,512]{2,1,0:T(8,128)S(1)}, f32[2,8,512]{2,1,0:T(8,128)S(1)}, u32[]{:S(2)}, u32[]{:S(2)}) collective-permute-start(f32[2,8,512]{2,1,0:T(8,128)S(1)} %get-tuple-element.24), channel_id=1, source_target_pairs={{1,2},{2,1},{3,4},{4,3},{5,6},{6,5},{7,8},{8,7},{9,10},{10,9},{11,... | collective-permute-start | bytes 98312 | tf_op jit(solution)/shard_map/ppermute | solution.py:586

commit v12 on v11

--- a/solution.py
+++ b/solution.py
@@ -31,6 +31,7 @@
 VMEM = pl.BlockSpec(memory_space=pltpu.VMEM)
 SMEM = pl.BlockSpec(memory_space=pltpu.SMEM)
 HBM = pl.BlockSpec(memory_space=pltpu.HBM)
+ANY = pl.BlockSpec(memory_space=pl.ANY)
 
 
 def coarse_rows(columns):
@@ -134,7 +135,7 @@
     out_ref[...] = jnp.broadcast_to(wide, out_ref.shape)
 
 
-def pack_copies(out_ref, first_row, rhs_ref, visc_ref, coup_ref, inverse_ref, sems, at_sem):
+def pack_copies(out_ref, first_row, rhs_ref, visc_ref, coup_ref, inverse_ref, sems):
     rows = pl.ds(pl.multiple_of(first_row, HALO), HALO)
     moves = [(visc_ref.at[rows, :], 0, HALO, None)]
     for a in range(2):
@@ -154,7 +155,7 @@
     for n, (source, at, size, lane) in enumerate(moves):
         place = pl.ds(at, size)
         target = out_ref.at[place, :] if lane is None else out_ref.at[place, pl.ds(lane, 256)]
-        copies.append(pltpu.make_async_copy(source, target, sems.at[at_sem + n]))
+        copies.append(pltpu.make_async_copy(source, target, sems.at[n]))
     return copies
 
 
@@ -162,35 +163,39 @@
     return 5 + columns // 512 + 2 * (columns % 512 // 256)
 
 
-def pack_kernel(
-    rhs_ref, visc_ref, coup_ref, inverse_ref, basis_ref,
-    partner_ref, other_ref,
-    groups, group_sems, pack_sems,
-):
-    odd = lax.axis_index("sub") % 2
-    sides = ((partner_ref, 1 - odd), (other_ref, odd))
-    group_copies, packs = [], []
-    for n, (out_ref, up) in enumerate(sides):
-        for a in range(2):
-            rows = pl.ds(pl.multiple_of(up * (ROWS - CHUNK), CHUNK), CHUNK)
-            group_copies.append(
-                pltpu.make_async_copy(
-                    basis_ref.at[:, a, rows, :], groups.at[2 * n + a], group_sems.at[2 * n + a]
-                )
-            )
-        packs += pack_copies(
-            out_ref, up * (ROWS - HALO), rhs_ref, visc_ref, coup_ref, inverse_ref, pack_sems,
-            n * pack_count(inverse_ref.shape[1]),
-        )
+def pack_kernel(flip, rhs_ref, visc_ref, coup_ref, inverse_ref, basis_ref, *refs):
+    out_ref, groups, group_sems, sems = refs[-4:]
+    up = (lax.axis_index("sub") + flip + 1) % 2
+    rows = pl.ds(pl.multiple_of(up * (ROWS - CHUNK), CHUNK), CHUNK)
+    group_copies = [
+        pltpu.make_async_copy(basis_ref.at[:, a, rows, :], groups.at[a], group_sems.at[a])
+        for a in range(2)
+    ]
+    packs = pack_copies(
+        out_ref, up * (ROWS - HALO), rhs_ref, visc_ref, coup_ref, inverse_ref, sems
+    )
     for copy in group_copies + packs:
         copy.start()
-    for n, (out_ref, up) in enumerate(sides):
-        for a in range(2):
-            group_copies[2 * n + a].wait()
-            for k in range(VECTORS):
-                rows = groups[2 * n + a, k].astype(jnp.float32)
-                at = EDGE_AT + VECTORS * a + k
-                out_ref[at : at + 1] = jnp.where(up == 1, rows[CHUNK - 1 :], rows[:1])
+
+    def take(a, row):
+        for k in range(0, VECTORS, TILE):
+            lines = [
+                groups[a, k + n].astype(jnp.float32)[row : row + 1] for n in range(TILE)
+            ]
+            at = EDGE_AT + VECTORS * a + k
+            out_ref[at : at + TILE] = jnp.concatenate(lines, 0)
+
+    for a in range(2):
+        group_copies[a].wait()
+
+        @pl.when(up == 1)
+        def _():
+            take(a, CHUNK - 1)
+
+        @pl.when(up == 0)
+        def _():
+            take(a, 0)
+
     for copy in packs:
         copy.wait()
 
@@ -599,21 +604,24 @@
     row, whole, edge = f32(count, LANES), f32(2, ROWS, CELLS), f32(2, HALO, CELLS)
     packed, smoothed = f32(EDGE_AT + coarse_rows(columns), CELLS), f32(2, EXT, CELLS)
     arguments = (rhs, viscosity, coupling, coarse_inverse, coarse_basis)
-    packs = call(
-        pack_kernel, "pack", [HBM] * 5, [packed, packed], 5_000_000,
-        [pltpu.VMEM((4, VECTORS, CHUNK, CELLS), jnp.bfloat16), dma(4)]
-        + [dma(2 * pack_count(columns))],
-    )(*map(in_hbm, arguments))
-    held, partner, other = lax.optimization_barrier((coarse_basis, *packs))
+    in_place = [in_hbm(x) for x in arguments]
+    scratch = [pltpu.VMEM((2, VECTORS, CHUNK, CELLS), jnp.bfloat16), dma(2)]
+    scratch.append(dma(pack_count(columns)))
+    pack = lambda flip, name, *before: call(
+        functools.partial(pack_kernel, flip), name, [HBM] * 5 + [ANY] * len(before), [packed],
+        5_000_000, scratch,
+    )(*in_place, *before)[0]
+    other = pack(1, "pack_other")
+    partner = pack(0, "pack_partner", other)
     partner, other = swap(partner, other)
     (first,) = call(
         restrict_kernel, "restrict", [VMEM] * 2, [row], 10_000_000, [sums]
-    )(rhs, held)
+    )(rhs, coarse_basis)
     first = from_everyone(first)
     direction, image, smooth, partner_rows, other_rows, second = call(
         functools.partial(first_turn_kernel, count), "first_turn", [SMEM] + [VMEM] * 8,
         [whole, whole, smoothed, edge, edge, row], 20_000_000, [extended, sums, stacked, solved],
-    )(margin_rows, first, coarse_inverse, partner, other, held, rhs, viscosity, coupling)
+    )(margin_rows, first, coarse_inverse, partner, other, coarse_basis, rhs, viscosity, coupling)
     partner_rows, other_rows = swap(partner_rows, other_rows)
     second = from_everyone(second)
     second_direction, third = call(
@@ -621,7 +629,7 @@
         [whole, row], 20_000_000, [extended, extended, sums, stacked, solved],
     )(
         margin_rows, first, second, coarse_inverse, partner, other, partner_rows, other_rows,
-        held, smooth, rhs, image, viscosity, coupling,
+        coarse_basis, smooth, rhs, image, viscosity, coupling,
     )
     third = from_everyone(third)
     result, transposed = call(finish_kernel, "finish", [VMEM] * 5, [whole, f32(2, 3)], 1_000_000)(

time: 47.8 us -> 48.9 us (1.023)
  Pallas kernels: 12.3 us -> 13.4 us
    pallas_call x1 -> x2, Pallas kernels: 2.55 us -> 3.67 us  [on_device(): call(functools.partial(pack_kernel, flip), name, [HBM] * 5 + [ANY] * len(...]
where the time goes in v12:
time: 48.9 us; the launch traced here: 48.7 us
  blocking collectives  32.5 us (66%)
  Pallas kernels  13.4 us (27%)
  starting transfers between devices  1.95 us (4%)
  between operations  0.78 us (2%)
    all_to_all x3, blocking collectives, from_everyone(): lax.all_to_all(rows, 'sub', 0, 0, tiled=True, axis_index_groups=order)  32.5 us
    pallas_call x1, Pallas kernels, on_device(): call(functools.partial(first_turn_kernel, count), 'first_turn', [SMEM] +...  4.07 us
    pallas_call x2, Pallas kernels, on_device(): call(functools.partial(pack_kernel, flip), name, [HBM] * 5 + [ANY] * len(...  3.67 us
    pallas_call x1, Pallas kernels, on_device(): call(functools.partial(second_turn_kernel, count), 'second_turn', [SMEM]...  2.85 us
    pallas_call x1, Pallas kernels, on_device(): call(restrict_kernel, 'restrict', [VMEM] * 2, [row], 10000000, [sums])  1.47 us
    pallas_call x1, Pallas kernels, on_device(): call(finish_kernel, 'finish', [VMEM] * 5, [whole, f32(2, 3)], 1000000)  1.36 us
    ppermute x2, starting transfers between devices, swap(): lax.ppermute(other, 'sub', both(range(1, count - 1, 2)))  1.33 us
  transfers between devices with their start and end apart: 4, of which 0 were waited for; matrix products, arithmetic and copies ran while one was open for 0% of the time, Pallas kernels for 3%

profile of v12, /device:TPU:0, one launch (start us, length us, event | category | flops | bytes accessed | tf_op | source)
XLA Modules:
  0.0 48.7 jit_solution(8313271094450305190)
XLA Ops:
  0.6 0.0 slice-start
  0.6 0.0 copy-start
  0.7 1.9 %pack_other.1.refs_0_ = f32[208,512]{1,0:T(8,128)S(1)} custom-call(f32[2,64,512]{2,1,0:T(8,128)} %rhs_ref.9, f32[64,512]{1,0:T(8,128)} %visc_ref.7, f32[2,64,512]{2,1,0:T(8,128)} %coup_ref.7, f32[48,768]{1,0:T(8,128)} %inverse_ref.7, bf16[48,2,64,512]{3,2,1,0:T(8,128)(2,1)} %held.5), custom_call_target="tpu_custom_call" | custom-call | flops 5000000 | bytes 4000000 | tf_op jit(solution)/shard_map/pack_other/pallas_call | solution.py:610
  2.5 0.0 slice-start.1
  2.5 0.0 copy-start.1
  2.5 0.0 copy-start.2
  2.5 0.0 copy-start.3
  2.6 0.0 copy-start.4
  2.6 1.8 %pack_partner.1 = f32[208,512]{1,0:T(8,128)S(1)} custom-call(f32[2,64,512]{2,1,0:T(8,128)} %rhs_ref.9, f32[64,512]{1,0:T(8,128)} %visc_ref.7, f32[2,64,512]{2,1,0:T(8,128)} %coup_ref.7, f32[48,768]{1,0:T(8,128)} %inverse_ref.7, bf16[48,2,64,512]{3,2,1,0:T(8,128)(2,1)} %held.5, f32[208,512]{1,0:T(8,128)S(1)} %pack_other.1.refs_0_), custom_call_target="tpu_custom_call" | custom-call | flops 5000000 | bytes 4000000 | tf_op jit(solution)/shard_map/pack_partner/pallas_call | solution.py:610
  4.4 0.5 %collective-permute-start = (f32[208,512]{1,0:T(8,128)S(1)}, f32[208,512]{1,0:T(8,128)S(1)}, u32[]{:S(2)}, u32[]{:S(2)}) collective-permute-start(f32[208,512]{1,0:T(8,128)S(1)} %pack_partner.1), channel_id=1, source_target_pairs={{0,1},{1,0},{2,3},{3,2},{4,5},{5,4},{6,7},{7,6},{8,9},{9,8},{10,11... | collective-permute-start | bytes 1277960 | tf_op jit(solution)/shard_map/ppermute | solution.py:590
  4.9 0.7 %collective-permute-start.1 = (f32[208,512]{1,0:T(8,128)S(1)}, f32[208,512]{1,0:T(8,128)S(1)}, u32[]{:S(2)}, u32[]{:S(2)}) collective-permute-start(f32[208,512]{1,0:T(8,128)S(1)} %pack_other.1.refs_0_), channel_id=1, source_target_pairs={{1,2},{2,1},{3,4},{4,3},{5,6},{6,5},{7,8},{8,7},{9,10},{10,9},{11,... | collective-permute-start | bytes 1277960 | tf_op jit(solution)/shard_map/ppermute | solution.py:591
  5.6 0.0 slice-done
  5.6 0.0 copy-done
  5.6 0.0 slice-done.1
  5.6 1.5 %restrict.1 = f32[16,128]{1,0:T(8,128)S(1)} custom-call(f32[2,64,512]{2,1,0:T(8,128)S(1)} %copy-done, bf16[48,2,64,512]{3,2,1,0:T(8,128)(2,1)S(1)} %bitcast.14), custom_call_target="tpu_custom_call" | custom-call | flops 10000000 | bytes 4000000 | tf_op jit(solution)/shard_map/restrict/pallas_call | solution.py:617
  7.1 12.0 %all_to_all.33 = f32[16,1,128]{2,1,0:T(1,128)S(1)} all-to-all(f32[16,1,128]{2,1,0:T(1,128)S(1)} %bitcast.21), channel_id=1, replica_groups={{15,14,13,12,11,10,9,8,7,6,5,4,3,2,1,0},{31,30,29,28,27,26,25,24,23,22,..., dimensions={0} | all-to-all | bytes 16384 | tf_op jit(solution)/shard_map/all_to_all | solution.py:583
  19.1 0.0 collective-permute-done.partner_ref
  19.1 0.0 collective-permute-done.1.other_ref
  19.1 0.0 copy-done.1
  19.1 0.0 copy-done.2
  19.1 0.0 copy-done.3
  19.2 0.0 copy-done.4
  19.2 4.1 %first_turn.1 = (f32[2,64,512]{2,1,0:T(8,128)S(1)}, f32[2,64,512]{2,1,0:T(8,128)S(1)}, f32[2,80,512]{2,1,0:T(8,128)S(1)}, f32[2,8,512]{2,1,0:T(8,128)S(1)}, f32[...) custom-call(s32[16]{0:T(128)S(1)} %copy-done.4, f32[16,128]{1,0:T(8,128)S(1)} %bitcast.15, f32[48,768]{1,0:T(8,128)S(1)} %copy-done.2, ...), custom_call_target="tpu_custom_call" | custom-call | flops 20000000 | bytes 4000000 | tf_op jit(solution)/shard_map/first_turn/pallas_call | solution.py:621
  23.2 0.1 collective-permute-start.2
  23.3 0.7 %collective-permute-start.3 = (f32[2,8,512]{2,1,0:T(8,128)S(1)}, f32[2,8,512]{2,1,0:T(8,128)S(1)}, u32[]{:S(2)}, u32[]{:S(2)}) collective-permute-start(f32[2,8,512]{2,1,0:T(8,128)S(1)} %get-tuple-element.14), channel_id=1, source_target_pairs={{1,2},{2,1},{3,4},{4,3},{5,6},{6,5},{7,8},{8,7},{9,10},{10,9},{11,... | collective-permute-start | bytes 98312 | tf_op jit(solution)/shard_map/ppermute | solution.py:591
  24.0 12.1 %all_to_all.34 = f32[16,1,128]{2,1,0:T(1,128)S(1)} all-to-all(f32[16,1,128]{2,1,0:T(1,128)S(1)} %bitcast.22), channel_id=1, replica_groups={{15,14,13,12,11,10,9,8,7,6,5,4,3,2,1,0},{31,30,29,28,27,26,25,24,23,22,..., dimensions={0} | all-to-all | bytes 16384 | tf_op jit(solution)/shard_map/all_to_all | solution.py:583
  36.1 0.0 collective-permute-done.2.partner_rows_ref
  36.1 0.0 collective-permute-done.3.other_rows_ref
  36.1 2.8 %second_turn.1 = (f32[2,64,512]{2,1,0:T(8,128)S(1)}, f32[16,128]{1,0:T(8,128)S(1)}) custom-call(s32[16]{0:T(128)S(1)} %copy-done.4, f32[16,128]{1,0:T(8,128)S(1)} %bitcast.16, f32[16,128]{1,0:T(8,128)S(1)} %bitcast.18, f32[48,768]{1,0:T(8,128)S(1)} %copy-done.2, f32[208,512]{1,0:T(8,128)S(1)} %collective-permute-done.partner_ref, ...), custom_call_target="tpu_custom_call" | custom-call | flops 20000000 | bytes 4000000 | tf_op jit(solution)/shard_map/second_turn/pallas_call | solution.py:627
  39.0 8.4 %all_to_all.35 = f32[16,1,128]{2,1,0:T(1,128)S(1)} all-to-all(f32[16,1,128]{2,1,0:T(1,128)S(1)} %bitcast.23), channel_id=1, replica_groups={{15,14,13,12,11,10,9,8,7,6,5,4,3,2,1,0},{31,30,29,28,27,26,25,24,23,22,..., dimensions={0} | all-to-all | bytes 16384 | tf_op jit(solution)/shard_map/all_to_all | solution.py:583
  47.3 1.4 %finish.1 = (f32[2,64,512]{2,1,0:T(8,128)}, f32[2,3]{1,0:T(2,128)}) custom-call(f32[16,128]{1,0:T(8,128)S(1)} %bitcast.17, f32[16,128]{1,0:T(8,128)S(1)} %bitcast.19, f32[16,128]{1,0:T(8,128)S(1)} %bitcast.20, f32[2,64,512]{2,1,0:T(8,128)S(1)} %get-tuple-element.18.first_direction_ref, f32[2,64,512]{2,1,0:T(8,128)S(1)} %get-tuple-element.19.second_direction_ref), custom_call_target="tpu_custom_call" | custom-call | flops 1000000 | bytes 4000000 | tf_op jit(solution)/shard_map/finish/pallas_call | solution.py:635
  (1 shorter events, 0.0 us)
Async XLA Ops:
  0.6 5.0 %slice-start = ((s8[6291456]{0:T(1024)(128)(4,1)}), s8[4194304]{0:T(1024)(128)(4,1)S(1)}, s32[]{:S(2)}) async-start(s8[6291456]{0:T(1024)(128)(4,1)} %bitcast.13), calls=%async_computation.3 | async-start | bytes 8388608
  0.6 5.0 %copy-start = (f32[2,64,512]{2,1,0:T(8,128)S(1)}, f32[2,64,512]{2,1,0:T(8,128)}, u32[]{:S(2)}) copy-start(f32[2,64,512]{2,1,0:T(8,128)} %rhs_ref.9) | copy-start | bytes 786436
  2.5 3.1 %slice-start.1 = ((s8[6291456]{0:T(1024)(128)(4,1)}), s8[2097152]{0:T(1024)(128)(4,1)S(1)}, s32[]{:S(2)}) async-start(s8[6291456]{0:T(1024)(128)(4,1)} %bitcast.13), calls=%async_computation.4 | async-start | bytes 4194304
  2.5 16.6 %copy-start.1 = (f32[2,64,512]{2,1,0:T(8,128)S(1)}, f32[2,64,512]{2,1,0:T(8,128)}, u32[]{:S(2)}) copy-start(f32[2,64,512]{2,1,0:T(8,128)} %coup_ref.7) | copy-start | bytes 786436
  2.5 16.6 %copy-start.2 = (f32[48,768]{1,0:T(8,128)S(1)}, f32[48,768]{1,0:T(8,128)}, u32[]{:S(2)}) copy-start(f32[48,768]{1,0:T(8,128)} %inverse_ref.7) | copy-start | bytes 442372
  2.5 16.6 %copy-start.3 = (f32[64,512]{1,0:T(8,128)S(1)}, f32[64,512]{1,0:T(8,128)}, u32[]{:S(2)}) copy-start(f32[64,512]{1,0:T(8,128)} %visc_ref.7) | copy-start | bytes 393220
  2.6 16.6 %copy-start.4 = (s32[16]{0:T(128)S(1)}, s32[16]{0:T(128)}, u32[]{:S(2)}) copy-start(s32[16]{0:T(128)} %margin_ref.3) | copy-start | bytes 196
  4.4 14.7 %collective-permute-start = (f32[208,512]{1,0:T(8,128)S(1)}, f32[208,512]{1,0:T(8,128)S(1)}, u32[]{:S(2)}, u32[]{:S(2)}) collective-permute-start(f32[208,512]{1,0:T(8,128)S(1)} %pack_partner.1), channel_id=1, source_target_pairs={{0,1},{1,0},{2,3},{3,2},{4,5},{5,4},{6,7},{7,6},{8,9},{9,8},{10,11... | collective-permute-start | bytes 1277960 | tf_op jit(solution)/shard_map/ppermute | solution.py:590
  4.9 14.2 %collective-permute-start.1 = (f32[208,512]{1,0:T(8,128)S(1)}, f32[208,512]{1,0:T(8,128)S(1)}, u32[]{:S(2)}, u32[]{:S(2)}) collective-permute-start(f32[208,512]{1,0:T(8,128)S(1)} %pack_other.1.refs_0_), channel_id=1, source_target_pairs={{1,2},{2,1},{3,4},{4,3},{5,6},{6,5},{7,8},{8,7},{9,10},{10,9},{11,... | collective-permute-start | bytes 1277960 | tf_op jit(solution)/shard_map/ppermute | solution.py:591
  23.2 12.9 %collective-permute-start.2 = (f32[2,8,512]{2,1,0:T(8,128)S(1)}, f32[2,8,512]{2,1,0:T(8,128)S(1)}, u32[]{:S(2)}, u32[]{:S(2)}) collective-permute-start(f32[2,8,512]{2,1,0:T(8,128)S(1)} %get-tuple-element.13), channel_id=1, source_target_pairs={{0,1},{1,0},{2,3},{3,2},{4,5},{5,4},{6,7},{7,6},{8,9},{9,8},{10,11... | collective-permute-start | bytes 98312 | tf_op jit(solution)/shard_map/ppermute | solution.py:590
  23.3 12.8 %collective-permute-start.3 = (f32[2,8,512]{2,1,0:T(8,128)S(1)}, f32[2,8,512]{2,1,0:T(8,128)S(1)}, u32[]{:S(2)}, u32[]{:S(2)}) collective-permute-start(f32[2,8,512]{2,1,0:T(8,128)S(1)} %get-tuple-element.14), channel_id=1, source_target_pairs={{1,2},{2,1},{3,4},{4,3},{5,6},{6,5},{7,8},{8,7},{9,10},{10,9},{11,... | collective-permute-start | bytes 98312 | tf_op jit(solution)/shard_map/ppermute | solution.py:591

commit v13 on v11

--- a/solution.py
+++ b/solution.py
@@ -184,13 +184,29 @@
         )
     for copy in group_copies + packs:
         copy.start()
-    for n, (out_ref, up) in enumerate(sides):
+
+    def take(out_ref, group, a, row):
+        for k in range(0, VECTORS, TILE):
+            lines = [groups[group, k + n].astype(jnp.float32)[row : row + 1] for n in range(TILE)]
+            at = EDGE_AT + VECTORS * a + k
+            out_ref[at : at + TILE] = jnp.concatenate(lines, 0)
+
+    for n in range(2):
         for a in range(2):
             group_copies[2 * n + a].wait()
-            for k in range(VECTORS):
-                rows = groups[2 * n + a, k].astype(jnp.float32)
-                at = EDGE_AT + VECTORS * a + k
-                out_ref[at : at + 1] = jnp.where(up == 1, rows[CHUNK - 1 :], rows[:1])
+
+    @pl.when(odd == 0)
+    def _():
+        for a in range(2):
+            take(partner_ref, a, a, CHUNK - 1)
+            take(other_ref, 2 + a, a, 0)
+
+    @pl.when(odd == 1)
+    def _():
+        for a in range(2):
+            take(partner_ref, a, a, 0)
+            take(other_ref, 2 + a, a, CHUNK - 1)
+
     for copy in packs:
         copy.wait()
 
@@ -432,7 +448,7 @@
 
 
 def first_turn_kernel(
-    count, margin_ref, sums_ref, inverse_ref, partner_ref, other_ref, held, rhs_ref, visc_ref,
+    count, margin_ref, sums_ref, inverse_ref, other_ref, partner_ref, held, rhs_ref, visc_ref,
     coup_ref,
     direction_ref, image_ref, smooth_ref, partner_rows_ref, other_rows_ref, next_ref,
     extended, sums, stacked, solved,
@@ -468,9 +484,11 @@
             heads[a] = image
         if t == ROWS // TILE - 1:
             tails[a] = image
-    for a in range(2):
-        partner_rows_ref[a] = jnp.where(odd, heads[a], tails[a])
-        other_rows_ref[a] = jnp.where(odd, tails[a], heads[a])
+    half = lax.broadcasted_iota(jnp.int32, (TILE, CELLS), 0) < TILE // 2
+    head = jnp.where(half, heads[0], pltpu.roll(heads[1], TILE // 2, 0))
+    tail = jnp.where(half, pltpu.roll(tails[1], TILE // 2, 0), tails[0])
+    partner_rows_ref[...] = jnp.where(odd, head, tail)
+    other_rows_ref[...] = jnp.where(odd, tail, head)
     sums[...] = jnp.zeros_like(sums)
     sums[VECTORS : VECTORS + 8] = in_rows([fold(products), fold(squares)])
 
@@ -490,8 +508,8 @@
 
 
 def second_turn_kernel(
-    count, margin_ref, first_ref, second_ref, inverse_ref, partner_ref, other_ref,
-    partner_rows_ref, other_rows_ref, held, smooth_ref, rhs_ref, image_ref, visc_ref, coup_ref,
+    count, margin_ref, first_ref, second_ref, inverse_ref, other_ref, partner_ref,
+    other_rows_ref, partner_rows_ref, held, smooth_ref, rhs_ref, image_ref, visc_ref, coup_ref,
     direction_ref, next_ref,
     image_smooth, extended, sums, stacked, solved,
 ):
@@ -505,9 +523,10 @@
     low_rows, high_rows = neighbours_of(partner_rows_ref, other_rows_ref)
 
     def field(a, t):
-        if t < 0:
-            return low_rows[a]
-        return high_rows[a] if t == ROWS // TILE else image_ref[a, tile_rows(t)]
+        if 0 <= t < ROWS // TILE:
+            return image_ref[a, tile_rows(t)]
+        rows = low_rows[...] if t < 0 else high_rows[...]
+        return pltpu.roll(rows, TILE // 2, 0) if a else rows
 
     solve(
         count, margin_ref, visc_ref, coup_ref, field, low, high, image_smooth, stacked, solved,
@@ -596,7 +615,7 @@
     stacked = pltpu.VMEM((6, STACKED, CELLS), jnp.float32)
     solved = pltpu.VMEM((4, STACKED, CELLS), jnp.float32)
     sums = pltpu.VMEM((SLOTS, LANES), jnp.float32)
-    row, whole, edge = f32(count, LANES), f32(2, ROWS, CELLS), f32(2, HALO, CELLS)
+    row, whole, edge = f32(count, LANES), f32(2, ROWS, CELLS), f32(TILE, CELLS)
     packed, smoothed = f32(EDGE_AT + coarse_rows(columns), CELLS), f32(2, EXT, CELLS)
     arguments = (rhs, viscosity, coupling, coarse_inverse, coarse_basis)
     packs = call(
@@ -613,14 +632,14 @@
     direction, image, smooth, partner_rows, other_rows, second = call(
         functools.partial(first_turn_kernel, count), "first_turn", [SMEM] + [VMEM] * 8,
         [whole, whole, smoothed, edge, edge, row], 20_000_000, [extended, sums, stacked, solved],
-    )(margin_rows, first, coarse_inverse, partner, other, held, rhs, viscosity, coupling)
+    )(margin_rows, first, coarse_inverse, other, partner, held, rhs, viscosity, coupling)
     partner_rows, other_rows = swap(partner_rows, other_rows)
     second = from_everyone(second)
     second_direction, third = call(
         functools.partial(second_turn_kernel, count), "second_turn", [SMEM] + [VMEM] * 13,
         [whole, row], 20_000_000, [extended, extended, sums, stacked, solved],
     )(
-        margin_rows, first, second, coarse_inverse, partner, other, partner_rows, other_rows,
+        margin_rows, first, second, coarse_inverse, other, partner, other_rows, partner_rows,
         held, smooth, rhs, image, viscosity, coupling,
     )
     third = from_everyone(third)

time: 47.8 us -> 47.9 us (level)
  starting transfers between devices: 2.21 us -> 9.62 us
  blocking collectives: 32.2 us -> 24.8 us
    all_to_all x3, blocking collectives: 32.2 us -> 24.8 us  [from_everyone(): lax.all_to_all(rows, 'sub', 0, 0, tiled=True, axis_index_groups=order)]
    ppermute x2, starting transfers between devices: 0.75 us -> 8.14 us  [swap(): lax.ppermute(partner, 'sub', both(range(0, count, 2)))]
where the time goes in v13:
time: 47.9 us; the launch traced here: 47.6 us
  blocking collectives  24.8 us (52%)
  Pallas kernels  12.4 us (26%)
  starting transfers between devices  9.62 us (20%)
  between operations  0.74 us (2%)
    all_to_all x3, blocking collectives, from_everyone(): lax.all_to_all(rows, 'sub', 0, 0, tiled=True, axis_index_groups=order)  24.8 us
    ppermute x2, starting transfers between devices, swap(): lax.ppermute(partner, 'sub', both(range(0, count, 2)))  8.14 us
    pallas_call x1, Pallas kernels, on_device(): call(functools.partial(first_turn_kernel, count), 'first_turn', [SMEM] +...  4.07 us
    pallas_call x1, Pallas kernels, on_device(): call(functools.partial(second_turn_kernel, count), 'second_turn', [SMEM]...  2.86 us
    pallas_call x1, Pallas kernels, on_device(): call(pack_kernel, 'pack', [HBM] * 5, [packed, packed], 5000000, [pltpu.VM...  2.68 us
    ppermute x2, starting transfers between devices, swap(): lax.ppermute(other, 'sub', both(range(1, count - 1, 2)))  1.49 us
    pallas_call x1, Pallas kernels, on_device(): call(restrict_kernel, 'restrict', [VMEM] * 2, [row], 10000000, [sums])  1.47 us
    pallas_call x1, Pallas kernels, on_device(): call(finish_kernel, 'finish', [VMEM] * 5, [whole, f32(2, 3)], 1000000)  1.36 us
  transfers between devices with their start and end apart: 4, of which 0 were waited for; matrix products, arithmetic and copies ran while one was open for 0% of the time, Pallas kernels for 3%

profile of v13, /device:TPU:0, one launch (start us, length us, event | category | flops | bytes accessed | tf_op | source)
XLA Modules:
  0.0 47.6 jit_solution(3358766039408110755)
XLA Ops:
  0.6 0.0 copy-start.1
  0.6 0.0 copy-start.3
  0.7 0.0 copy-start.2
  0.7 0.0 copy-start.4
  0.7 0.0 copy-start
  0.7 0.0 copy-start.5
  0.7 2.7 %pack.1 = (f32[208,512]{1,0:T(8,128)S(1)}, f32[208,512]{1,0:T(8,128)S(1)}) custom-call(f32[2,64,512]{2,1,0:T(8,128)} %rhs_ref.7, f32[64,512]{1,0:T(8,128)} %visc_ref.5, f32[2,64,512]{2,1,0:T(8,128)} %coup_ref.5, f32[48,768]{1,0:T(8,128)} %inverse_ref.5, bf16[48,2,64,512]{3,2,1,0:T(8,128)(2,1)} %held.2), custom_call_target="tpu_custom_call" | custom-call | flops 5000000 | bytes 4000000 | tf_op jit(solution)/shard_map/pack/pallas_call | solution.py:621
  3.4 0.8 %collective-permute-start = (f32[208,512]{1,0:T(8,128)S(1)}, f32[208,512]{1,0:T(8,128)S(1)}, u32[]{:S(2)}, u32[]{:S(2)}) collective-permute-start(f32[208,512]{1,0:T(8,128)S(1)} %get-tuple-element.20), channel_id=1, source_target_pairs={{1,2},{2,1},{3,4},{4,3},{5,6},{6,5},{7,8},{8,7},{9,10},{10,9},{11,... | collective-permute-start | bytes 1277960 | tf_op jit(solution)/shard_map/ppermute | solution.py:605
  4.2 4.4 %collective-permute-start.1 = (f32[208,512]{1,0:T(8,128)S(1)}, f32[208,512]{1,0:T(8,128)S(1)}, u32[]{:S(2)}, u32[]{:S(2)}) collective-permute-start(f32[208,512]{1,0:T(8,128)S(1)} %get-tuple-element.21), channel_id=1, source_target_pairs={{0,1},{1,0},{2,3},{3,2},{4,5},{5,4},{6,7},{7,6},{8,9},{9,8},{10,11... | collective-permute-start | bytes 1277960 | tf_op jit(solution)/shard_map/ppermute | solution.py:604
  8.6 0.0 copy-done.1
  8.6 0.0 copy-done
  8.6 1.5 %restrict.1 = f32[16,128]{1,0:T(8,128)S(1)} custom-call(f32[2,64,512]{2,1,0:T(8,128)S(1)} %copy-done.1, bf16[48,2,64,512]{3,2,1,0:T(8,128)(2,1)S(1)} %copy-done), custom_call_target="tpu_custom_call" | custom-call | flops 10000000 | bytes 4000000 | tf_op jit(solution)/shard_map/restrict/pallas_call | solution.py:628
  10.0 8.2 %all_to_all.33 = f32[16,1,128]{2,1,0:T(1,128)S(1)} all-to-all(f32[16,1,128]{2,1,0:T(1,128)S(1)} %bitcast.19), channel_id=1, replica_groups={{15,14,13,12,11,10,9,8,7,6,5,4,3,2,1,0},{31,30,29,28,27,26,25,24,23,22,..., dimensions={0} | all-to-all | bytes 16384 | tf_op jit(solution)/shard_map/all_to_all | solution.py:597
  18.3 0.0 collective-permute-done.other_ref
  18.3 0.0 collective-permute-done.1.partner_ref
  18.3 0.0 copy-done.3
  18.3 0.0 copy-done.2
  18.3 0.0 copy-done.4
  18.3 0.0 copy-done.5
  18.3 4.1 %first_turn.1 = (f32[2,64,512]{2,1,0:T(8,128)S(1)}, f32[2,64,512]{2,1,0:T(8,128)S(1)}, f32[2,80,512]{2,1,0:T(8,128)S(1)}, f32[8,512]{1,0:T(8,128)S(1)}, f32[8,512]{1,0:T(8,128)S(1)}, /*index=5*/f32[16,128]{1,0:T(8,128)S(1)}) custom-call(s32[16]{0:T(128)S(1)} %copy-done.5, f32[16,128]{1,0:T(8,128)S(1)} %bitcast.13, f32[48,768]{1,0:T(8,128)S(1)} %copy-done.3, ...), custom_call_target="tpu_custom_call" | custom-call | flops 20000000 | bytes 4000000 | tf_op jit(solution)/shard_map/first_turn/pallas_call | solution.py:632
  22.4 0.7 %collective-permute-start.2 = (f32[8,512]{1,0:T(8,128)S(1)}, f32[8,512]{1,0:T(8,128)S(1)}, u32[]{:S(2)}, u32[]{:S(2)}) collective-permute-start(f32[8,512]{1,0:T(8,128)S(1)} %get-tuple-element.23), channel_id=1, source_target_pairs={{1,2},{2,1},{3,4},{4,3},{5,6},{6,5},{7,8},{8,7},{9,10},{10,9},{11,... | collective-permute-start | bytes 49160 | tf_op jit(solution)/shard_map/ppermute | solution.py:605
  23.1 3.8 %collective-permute-start.3 = (f32[8,512]{1,0:T(8,128)S(1)}, f32[8,512]{1,0:T(8,128)S(1)}, u32[]{:S(2)}, u32[]{:S(2)}) collective-permute-start(f32[8,512]{1,0:T(8,128)S(1)} %get-tuple-element.24), channel_id=1, source_target_pairs={{0,1},{1,0},{2,3},{3,2},{4,5},{5,4},{6,7},{7,6},{8,9},{9,8},{10,11... | collective-permute-start | bytes 49160 | tf_op jit(solution)/shard_map/ppermute | solution.py:604
  26.9 8.2 %all_to_all.34 = f32[16,1,128]{2,1,0:T(1,128)S(1)} all-to-all(f32[16,1,128]{2,1,0:T(1,128)S(1)} %bitcast.20), channel_id=1, replica_groups={{15,14,13,12,11,10,9,8,7,6,5,4,3,2,1,0},{31,30,29,28,27,26,25,24,23,22,..., dimensions={0} | all-to-all | bytes 16384 | tf_op jit(solution)/shard_map/all_to_all | solution.py:597
  35.0 0.0 collective-permute-done.2.other_rows_ref
  35.0 0.0 collective-permute-done.3.partner_rows_ref
  35.0 2.9 %second_turn.1 = (f32[2,64,512]{2,1,0:T(8,128)S(1)}, f32[16,128]{1,0:T(8,128)S(1)}) custom-call(s32[16]{0:T(128)S(1)} %copy-done.5, f32[16,128]{1,0:T(8,128)S(1)} %bitcast.14, f32[16,128]{1,0:T(8,128)S(1)} %bitcast.16, f32[48,768]{1,0:T(8,128)S(1)} %copy-done.3, f32[208,512]{1,0:T(8,128)S(1)} %collective-permute-done.other_ref, ...), custom_call_target="tpu_custom_call" | custom-call | flops 20000000 | bytes 4000000 | tf_op jit(solution)/shard_map/second_turn/pallas_call | solution.py:638
  37.9 8.4 %all_to_all.35 = f32[16,1,128]{2,1,0:T(1,128)S(1)} all-to-all(f32[16,1,128]{2,1,0:T(1,128)S(1)} %bitcast.21), channel_id=1, replica_groups={{15,14,13,12,11,10,9,8,7,6,5,4,3,2,1,0},{31,30,29,28,27,26,25,24,23,22,..., dimensions={0} | all-to-all | bytes 16384 | tf_op jit(solution)/shard_map/all_to_all | solution.py:597
  46.2 1.4 %finish.1 = (f32[2,64,512]{2,1,0:T(8,128)}, f32[2,3]{1,0:T(2,128)}) custom-call(f32[16,128]{1,0:T(8,128)S(1)} %bitcast.15, f32[16,128]{1,0:T(8,128)S(1)} %bitcast.17, f32[16,128]{1,0:T(8,128)S(1)} %bitcast.18, f32[2,64,512]{2,1,0:T(8,128)S(1)} %get-tuple-element.28.first_direction_ref, f32[2,64,512]{2,1,0:T(8,128)S(1)} %get-tuple-element.29.second_direction_ref), custom_call_target="tpu_custom_call" | custom-call | flops 1000000 | bytes 4000000 | tf_op jit(solution)/shard_map/finish/pallas_call | solution.py:646
Async XLA Ops:
  0.6 7.9 %copy-start.1 = (f32[2,64,512]{2,1,0:T(8,128)S(1)}, f32[2,64,512]{2,1,0:T(8,128)}, u32[]{:S(2)}) copy-start(f32[2,64,512]{2,1,0:T(8,128)} %rhs_ref.7) | copy-start | bytes 786436
  0.6 17.7 %copy-start.3 = (f32[48,768]{1,0:T(8,128)S(1)}, f32[48,768]{1,0:T(8,128)}, u32[]{:S(2)}) copy-start(f32[48,768]{1,0:T(8,128)} %inverse_ref.5) | copy-start | bytes 442372
  0.7 17.7 %copy-start.2 = (f32[2,64,512]{2,1,0:T(8,128)S(1)}, f32[2,64,512]{2,1,0:T(8,128)}, u32[]{:S(2)}) copy-start(f32[2,64,512]{2,1,0:T(8,128)} %coup_ref.5) | copy-start | bytes 786436
  0.7 17.7 %copy-start.4 = (f32[64,512]{1,0:T(8,128)S(1)}, f32[64,512]{1,0:T(8,128)}, u32[]{:S(2)}) copy-start(f32[64,512]{1,0:T(8,128)} %visc_ref.5) | copy-start | bytes 393220
  0.7 7.9 %copy-start = (bf16[48,2,64,512]{3,2,1,0:T(8,128)(2,1)S(1)}, bf16[48,2,64,512]{3,2,1,0:T(8,128)(2,1)}, u32[]{:S(2)}) copy-start(bf16[48,2,64,512]{3,2,1,0:T(8,128)(2,1)} %held.2) | copy-start | bytes 18874372
  0.7 17.6 %copy-start.5 = (s32[16]{0:T(128)S(1)}, s32[16]{0:T(128)}, u32[]{:S(2)}) copy-start(s32[16]{0:T(128)} %margin_ref.3) | copy-start | bytes 196
  3.4 14.9 %collective-permute-start = (f32[208,512]{1,0:T(8,128)S(1)}, f32[208,512]{1,0:T(8,128)S(1)}, u32[]{:S(2)}, u32[]{:S(2)}) collective-permute-start(f32[208,512]{1,0:T(8,128)S(1)} %get-tuple-element.20), channel_id=1, source_target_pairs={{1,2},{2,1},{3,4},{4,3},{5,6},{6,5},{7,8},{8,7},{9,10},{10,9},{11,... | collective-permute-start | bytes 1277960 | tf_op jit(solution)/shard_map/ppermute | solution.py:605
  4.2 14.1 %collective-permute-start.1 = (f32[208,512]{1,0:T(8,128)S(1)}, f32[208,512]{1,0:T(8,128)S(1)}, u32[]{:S(2)}, u32[]{:S(2)}) collective-permute-start(f32[208,512]{1,0:T(8,128)S(1)} %get-tuple-element.21), channel_id=1, source_target_pairs={{0,1},{1,0},{2,3},{3,2},{4,5},{5,4},{6,7},{7,6},{8,9},{9,8},{10,11... | collective-permute-start | bytes 1277960 | tf_op jit(solution)/shard_map/ppermute | solution.py:604
  22.4 12.6 %collective-permute-start.2 = (f32[8,512]{1,0:T(8,128)S(1)}, f32[8,512]{1,0:T(8,128)S(1)}, u32[]{:S(2)}, u32[]{:S(2)}) collective-permute-start(f32[8,512]{1,0:T(8,128)S(1)} %get-tuple-element.23), channel_id=1, source_target_pairs={{1,2},{2,1},{3,4},{4,3},{5,6},{6,5},{7,8},{8,7},{9,10},{10,9},{11,... | collective-permute-start | bytes 49160 | tf_op jit(solution)/shard_map/ppermute | solution.py:605
  23.1 11.9 %collective-permute-start.3 = (f32[8,512]{1,0:T(8,128)S(1)}, f32[8,512]{1,0:T(8,128)S(1)}, u32[]{:S(2)}, u32[]{:S(2)}) collective-permute-start(f32[8,512]{1,0:T(8,128)S(1)} %get-tuple-element.24), channel_id=1, source_target_pairs={{0,1},{1,0},{2,3},{3,2},{4,5},{5,4},{6,7},{7,6},{8,9},{9,8},{10,11... | collective-permute-start | bytes 49160 | tf_op jit(solution)/shard_map/ppermute | solution.py:604

commit v14 on v13

--- a/solution.py
+++ b/solution.py
@@ -13,6 +13,7 @@
 HALO = 8
 EXT = ROWS + 2 * HALO
 STRIP = 32
+GROUP = 16
 STACKED = EXT + 2 * STRIP
 TILE = 8
 CHUNK = 16
@@ -170,14 +171,18 @@
     odd = lax.axis_index("sub") % 2
     sides = ((partner_ref, 1 - odd), (other_ref, odd))
     group_copies, packs = [], []
+    for k in range(0, VECTORS, GROUP):
+        for n, (out_ref, up) in enumerate(sides):
+            rows = pl.ds(pl.multiple_of(up * (ROWS - CHUNK), CHUNK), CHUNK)
+            for a in range(2):
+                group_copies.append(
+                    pltpu.make_async_copy(
+                        basis_ref.at[pl.ds(k, GROUP), a, rows, :],
+                        groups.at[2 * n + a, pl.ds(k, GROUP)],
+                        group_sems.at[len(group_copies)],
+                    )
+                )
     for n, (out_ref, up) in enumerate(sides):
-        for a in range(2):
-            rows = pl.ds(pl.multiple_of(up * (ROWS - CHUNK), CHUNK), CHUNK)
-            group_copies.append(
-                pltpu.make_async_copy(
-                    basis_ref.at[:, a, rows, :], groups.at[2 * n + a], group_sems.at[2 * n + a]
-                )
-            )
         packs += pack_copies(
             out_ref, up * (ROWS - HALO), rhs_ref, visc_ref, coup_ref, inverse_ref, pack_sems,
             n * pack_count(inverse_ref.shape[1]),
@@ -185,27 +190,27 @@
     for copy in group_copies + packs:
         copy.start()
 
-    def take(out_ref, group, a, row):
-        for k in range(0, VECTORS, TILE):
+    def take(out_ref, group, first, row):
+        for k in range(first, first + GROUP, TILE):
             lines = [groups[group, k + n].astype(jnp.float32)[row : row + 1] for n in range(TILE)]
-            at = EDGE_AT + VECTORS * a + k
+            at = EDGE_AT + VECTORS * (group % 2) + k
             out_ref[at : at + TILE] = jnp.concatenate(lines, 0)
 
-    for n in range(2):
-        for a in range(2):
-            group_copies[2 * n + a].wait()
-
-    @pl.when(odd == 0)
-    def _():
-        for a in range(2):
-            take(partner_ref, a, a, CHUNK - 1)
-            take(other_ref, 2 + a, a, 0)
-
-    @pl.when(odd == 1)
-    def _():
-        for a in range(2):
-            take(partner_ref, a, a, 0)
-            take(other_ref, 2 + a, a, CHUNK - 1)
+    for first in range(0, VECTORS, GROUP):
+        for _ in range(4):
+            group_copies.pop(0).wait()
+
+        @pl.when(odd == 0)
+        def _():
+            for a in range(2):
+                take(partner_ref, a, first, CHUNK - 1)
+                take(other_ref, 2 + a, first, 0)
+
+        @pl.when(odd == 1)
+        def _():
+            for a in range(2):
+                take(partner_ref, a, first, 0)
+                take(other_ref, 2 + a, first, CHUNK - 1)
 
     for copy in packs:
         copy.wait()
@@ -448,7 +453,7 @@
 
 
 def first_turn_kernel(
-    count, margin_ref, sums_ref, inverse_ref, other_ref, partner_ref, held, rhs_ref, visc_ref,
+    count, margin_ref, sums_ref, inverse_ref, partner_ref, other_ref, held, rhs_ref, visc_ref,
     coup_ref,
     direction_ref, image_ref, smooth_ref, partner_rows_ref, other_rows_ref, next_ref,
     extended, sums, stacked, solved,
@@ -508,8 +513,8 @@
 
 
 def second_turn_kernel(
-    count, margin_ref, first_ref, second_ref, inverse_ref, other_ref, partner_ref,
-    other_rows_ref, partner_rows_ref, held, smooth_ref, rhs_ref, image_ref, visc_ref, coup_ref,
+    count, margin_ref, first_ref, second_ref, inverse_ref, partner_ref, other_ref,
+    partner_rows_ref, other_rows_ref, held, smooth_ref, rhs_ref, image_ref, visc_ref, coup_ref,
     direction_ref, next_ref,
     image_smooth, extended, sums, stacked, solved,
 ):
@@ -620,7 +625,7 @@
     arguments = (rhs, viscosity, coupling, coarse_inverse, coarse_basis)
     packs = call(
         pack_kernel, "pack", [HBM] * 5, [packed, packed], 5_000_000,
-        [pltpu.VMEM((4, VECTORS, CHUNK, CELLS), jnp.bfloat16), dma(4)]
+        [pltpu.VMEM((4, VECTORS, CHUNK, CELLS), jnp.bfloat16), dma(4 * VECTORS // GROUP)]
         + [dma(2 * pack_count(columns))],
     )(*map(in_hbm, arguments))
     held, partner, other = lax.optimization_barrier((coarse_basis, *packs))
@@ -632,14 +637,14 @@
     direction, image, smooth, partner_rows, other_rows, second = call(
         functools.partial(first_turn_kernel, count), "first_turn", [SMEM] + [VMEM] * 8,
         [whole, whole, smoothed, edge, edge, row], 20_000_000, [extended, sums, stacked, solved],
-    )(margin_rows, first, coarse_inverse, other, partner, held, rhs, viscosity, coupling)
+    )(margin_rows, first, coarse_inverse, partner, other, held, rhs, viscosity, coupling)
     partner_rows, other_rows = swap(partner_rows, other_rows)
     second = from_everyone(second)
     second_direction, third = call(
         functools.partial(second_turn_kernel, count), "second_turn", [SMEM] + [VMEM] * 13,
         [whole, row], 20_000_000, [extended, extended, sums, stacked, solved],
     )(
-        margin_rows, first, second, coarse_inverse, other, partner, other_rows, partner_rows,
+        margin_rows, first, second, coarse_inverse, partner, other, partner_rows, other_rows,
         held, smooth, rhs, image, viscosity, coupling,
     )
     third = from_everyone(third)

time: 47.9 us -> 47.8 us (level)
  starting transfers between devices: 9.62 us -> 2.21 us
  blocking collectives: 24.8 us -> 32.2 us
    all_to_all x3, blocking collectives: 24.8 us -> 32.2 us  [from_everyone(): lax.all_to_all(rows, 'sub', 0, 0, tiled=True, axis_index_groups=order)]
    ppermute x2, starting transfers between devices: 8.14 us -> 0.75 us  [swap(): lax.ppermute(partner, 'sub', both(range(0, count, 2)))]
where the time goes in v14:
time: 47.8 us; the launch traced here: 47.5 us
  blocking collectives  32.2 us (67%)
  Pallas kernels  12.3 us (26%)
  starting transfers between devices  2.21 us (5%)
  between operations  0.74 us (2%)
    all_to_all x3, blocking collectives, from_everyone(): lax.all_to_all(rows, 'sub', 0, 0, tiled=True, axis_index_groups=order)  32.2 us
    pallas_call x1, Pallas kernels, on_device(): call(functools.partial(first_turn_kernel, count), 'first_turn', [SMEM] +...  4.07 us
    pallas_call x1, Pallas kernels, on_device(): call(functools.partial(second_turn_kernel, count), 'second_turn', [SMEM]...  2.86 us
    pallas_call x1, Pallas kernels, on_device(): call(pack_kernel, 'pack', [HBM] * 5, [packed, packed], 5000000, [pltpu.VM...  2.52 us
    pallas_call x1, Pallas kernels, on_device(): call(restrict_kernel, 'restrict', [VMEM] * 2, [row], 10000000, [sums])  1.47 us
    ppermute x2, starting transfers between devices, swap(): lax.ppermute(other, 'sub', both(range(1, count - 1, 2)))  1.46 us
    pallas_call x1, Pallas kernels, on_device(): call(finish_kernel, 'finish', [VMEM] * 5, [whole, f32(2, 3)], 1000000)  1.36 us
  transfers between devices with their start and end apart: 4, of which 0 were waited for; matrix products, arithmetic and copies ran while one was open for 0% of the time, Pallas kernels for 3%

profile of v14, /device:TPU:0, one launch (start us, length us, event | category | flops | bytes accessed | tf_op | source)
XLA Modules:
  0.0 47.5 jit_solution(2125686726001453310)
XLA Ops:
  0.6 0.0 copy-start.1
  0.6 0.0 copy-start.3
  0.7 0.0 copy-start.2
  0.7 0.0 copy-start.4
  0.7 0.0 copy-start
  0.7 0.0 copy-start.5
  0.7 2.5 %pack.1 = (f32[208,512]{1,0:T(8,128)S(1)}, f32[208,512]{1,0:T(8,128)S(1)}) custom-call(f32[2,64,512]{2,1,0:T(8,128)} %rhs_ref.7, f32[64,512]{1,0:T(8,128)} %visc_ref.5, f32[2,64,512]{2,1,0:T(8,128)} %coup_ref.5, f32[48,768]{1,0:T(8,128)} %inverse_ref.5, bf16[48,2,64,512]{3,2,1,0:T(8,128)(2,1)} %held.2), custom_call_target="tpu_custom_call" | custom-call | flops 5000000 | bytes 4000000 | tf_op jit(solution)/shard_map/pack/pallas_call | solution.py:626
  3.2 0.5 %collective-permute-start = (f32[208,512]{1,0:T(8,128)S(1)}, f32[208,512]{1,0:T(8,128)S(1)}, u32[]{:S(2)}, u32[]{:S(2)}) collective-permute-start(f32[208,512]{1,0:T(8,128)S(1)} %get-tuple-element.20), channel_id=1, source_target_pairs={{0,1},{1,0},{2,3},{3,2},{4,5},{5,4},{6,7},{7,6},{8,9},{9,8},{10,11... | collective-permute-start | bytes 1277960 | tf_op jit(solution)/shard_map/ppermute | solution.py:609
  3.7 0.8 %collective-permute-start.1 = (f32[208,512]{1,0:T(8,128)S(1)}, f32[208,512]{1,0:T(8,128)S(1)}, u32[]{:S(2)}, u32[]{:S(2)}) collective-permute-start(f32[208,512]{1,0:T(8,128)S(1)} %get-tuple-element.21), channel_id=1, source_target_pairs={{1,2},{2,1},{3,4},{4,3},{5,6},{6,5},{7,8},{8,7},{9,10},{10,9},{11,... | collective-permute-start | bytes 1277960 | tf_op jit(solution)/shard_map/ppermute | solution.py:610
  4.5 0.0 copy-done.1
  4.6 0.1 copy-done
  4.6 1.5 %restrict.1 = f32[16,128]{1,0:T(8,128)S(1)} custom-call(f32[2,64,512]{2,1,0:T(8,128)S(1)} %copy-done.1, bf16[48,2,64,512]{3,2,1,0:T(8,128)(2,1)S(1)} %copy-done), custom_call_target="tpu_custom_call" | custom-call | flops 10000000 | bytes 4000000 | tf_op jit(solution)/shard_map/restrict/pallas_call | solution.py:633
  6.1 11.8 %all_to_all.33 = f32[16,1,128]{2,1,0:T(1,128)S(1)} all-to-all(f32[16,1,128]{2,1,0:T(1,128)S(1)} %bitcast.19), channel_id=1, replica_groups={{15,14,13,12,11,10,9,8,7,6,5,4,3,2,1,0},{31,30,29,28,27,26,25,24,23,22,..., dimensions={0} | all-to-all | bytes 16384 | tf_op jit(solution)/shard_map/all_to_all | solution.py:602
  17.9 0.0 collective-permute-done.partner_ref
  17.9 0.0 collective-permute-done.1.other_ref
  17.9 0.0 copy-done.3
  18.0 0.0 copy-done.2
  18.0 0.0 copy-done.4
  18.0 0.0 copy-done.5
  18.0 4.1 %first_turn.1 = (f32[2,64,512]{2,1,0:T(8,128)S(1)}, f32[2,64,512]{2,1,0:T(8,128)S(1)}, f32[2,80,512]{2,1,0:T(8,128)S(1)}, f32[8,512]{1,0:T(8,128)S(1)}, f32[8,512]{1,0:T(8,128)S(1)}, /*index=5*/f32[16,128]{1,0:T(8,128)S(1)}) custom-call(s32[16]{0:T(128)S(1)} %copy-done.5, f32[16,128]{1,0:T(8,128)S(1)} %bitcast.13, f32[48,768]{1,0:T(8,128)S(1)} %copy-done.3, ...), custom_call_target="tpu_custom_call" | custom-call | flops 20000000 | bytes 4000000 | tf_op jit(solution)/shard_map/first_turn/pallas_call | solution.py:637
  22.1 0.2 collective-permute-start.2
  22.3 0.7 %collective-permute-start.3 = (f32[8,512]{1,0:T(8,128)S(1)}, f32[8,512]{1,0:T(8,128)S(1)}, u32[]{:S(2)}, u32[]{:S(2)}) collective-permute-start(f32[8,512]{1,0:T(8,128)S(1)} %get-tuple-element.24), channel_id=1, source_target_pairs={{1,2},{2,1},{3,4},{4,3},{5,6},{6,5},{7,8},{8,7},{9,10},{10,9},{11,... | collective-permute-start | bytes 49160 | tf_op jit(solution)/shard_map/ppermute | solution.py:610
  23.0 12.0 %all_to_all.34 = f32[16,1,128]{2,1,0:T(1,128)S(1)} all-to-all(f32[16,1,128]{2,1,0:T(1,128)S(1)} %bitcast.20), channel_id=1, replica_groups={{15,14,13,12,11,10,9,8,7,6,5,4,3,2,1,0},{31,30,29,28,27,26,25,24,23,22,..., dimensions={0} | all-to-all | bytes 16384 | tf_op jit(solution)/shard_map/all_to_all | solution.py:602
  34.9 0.0 collective-permute-done.2.partner_rows_ref
  35.0 0.0 collective-permute-done.3.other_rows_ref
  35.0 2.9 %second_turn.1 = (f32[2,64,512]{2,1,0:T(8,128)S(1)}, f32[16,128]{1,0:T(8,128)S(1)}) custom-call(s32[16]{0:T(128)S(1)} %copy-done.5, f32[16,128]{1,0:T(8,128)S(1)} %bitcast.14, f32[16,128]{1,0:T(8,128)S(1)} %bitcast.16, f32[48,768]{1,0:T(8,128)S(1)} %copy-done.3, f32[208,512]{1,0:T(8,128)S(1)} %collective-permute-done.partner_ref, ...), custom_call_target="tpu_custom_call" | custom-call | flops 20000000 | bytes 4000000 | tf_op jit(solution)/shard_map/second_turn/pallas_call | solution.py:643
  37.8 8.4 %all_to_all.35 = f32[16,1,128]{2,1,0:T(1,128)S(1)} all-to-all(f32[16,1,128]{2,1,0:T(1,128)S(1)} %bitcast.21), channel_id=1, replica_groups={{15,14,13,12,11,10,9,8,7,6,5,4,3,2,1,0},{31,30,29,28,27,26,25,24,23,22,..., dimensions={0} | all-to-all | bytes 16384 | tf_op jit(solution)/shard_map/all_to_all | solution.py:602
  46.2 1.4 %finish.1 = (f32[2,64,512]{2,1,0:T(8,128)}, f32[2,3]{1,0:T(2,128)}) custom-call(f32[16,128]{1,0:T(8,128)S(1)} %bitcast.15, f32[16,128]{1,0:T(8,128)S(1)} %bitcast.17, f32[16,128]{1,0:T(8,128)S(1)} %bitcast.18, f32[2,64,512]{2,1,0:T(8,128)S(1)} %get-tuple-element.28.first_direction_ref, f32[2,64,512]{2,1,0:T(8,128)S(1)} %get-tuple-element.29.second_direction_ref), custom_call_target="tpu_custom_call" | custom-call | flops 1000000 | bytes 4000000 | tf_op jit(solution)/shard_map/finish/pallas_call | solution.py:651
Async XLA Ops:
  0.6 3.9 %copy-start.1 = (f32[2,64,512]{2,1,0:T(8,128)S(1)}, f32[2,64,512]{2,1,0:T(8,128)}, u32[]{:S(2)}) copy-start(f32[2,64,512]{2,1,0:T(8,128)} %rhs_ref.7) | copy-start | bytes 786436
  0.6 17.3 %copy-start.3 = (f32[48,768]{1,0:T(8,128)S(1)}, f32[48,768]{1,0:T(8,128)}, u32[]{:S(2)}) copy-start(f32[48,768]{1,0:T(8,128)} %inverse_ref.5) | copy-start | bytes 442372
  0.7 17.3 %copy-start.2 = (f32[2,64,512]{2,1,0:T(8,128)S(1)}, f32[2,64,512]{2,1,0:T(8,128)}, u32[]{:S(2)}) copy-start(f32[2,64,512]{2,1,0:T(8,128)} %coup_ref.5) | copy-start | bytes 786436
  0.7 17.3 %copy-start.4 = (f32[64,512]{1,0:T(8,128)S(1)}, f32[64,512]{1,0:T(8,128)}, u32[]{:S(2)}) copy-start(f32[64,512]{1,0:T(8,128)} %visc_ref.5) | copy-start | bytes 393220
  0.7 4.0 %copy-start = (bf16[48,2,64,512]{3,2,1,0:T(8,128)(2,1)S(1)}, bf16[48,2,64,512]{3,2,1,0:T(8,128)(2,1)}, u32[]{:S(2)}) copy-start(bf16[48,2,64,512]{3,2,1,0:T(8,128)(2,1)} %held.2) | copy-start | bytes 18874372
  0.7 17.3 %copy-start.5 = (s32[16]{0:T(128)S(1)}, s32[16]{0:T(128)}, u32[]{:S(2)}) copy-start(s32[16]{0:T(128)} %margin_ref.3) | copy-start | bytes 196
  3.2 14.7 %collective-permute-start = (f32[208,512]{1,0:T(8,128)S(1)}, f32[208,512]{1,0:T(8,128)S(1)}, u32[]{:S(2)}, u32[]{:S(2)}) collective-permute-start(f32[208,512]{1,0:T(8,128)S(1)} %get-tuple-element.20), channel_id=1, source_target_pairs={{0,1},{1,0},{2,3},{3,2},{4,5},{5,4},{6,7},{7,6},{8,9},{9,8},{10,11... | collective-permute-start | bytes 1277960 | tf_op jit(solution)/shard_map/ppermute | solution.py:609
  3.7 14.2 %collective-permute-start.1 = (f32[208,512]{1,0:T(8,128)S(1)}, f32[208,512]{1,0:T(8,128)S(1)}, u32[]{:S(2)}, u32[]{:S(2)}) collective-permute-start(f32[208,512]{1,0:T(8,128)S(1)} %get-tuple-element.21), channel_id=1, source_target_pairs={{1,2},{2,1},{3,4},{4,3},{5,6},{6,5},{7,8},{8,7},{9,10},{10,9},{11,... | collective-permute-start | bytes 1277960 | tf_op jit(solution)/shard_map/ppermute | solution.py:610
  22.1 12.9 %collective-permute-start.2 = (f32[8,512]{1,0:T(8,128)S(1)}, f32[8,512]{1,0:T(8,128)S(1)}, u32[]{:S(2)}, u32[]{:S(2)}) collective-permute-start(f32[8,512]{1,0:T(8,128)S(1)} %get-tuple-element.23), channel_id=1, source_target_pairs={{0,1},{1,0},{2,3},{3,2},{4,5},{5,4},{6,7},{7,6},{8,9},{9,8},{10,11... | collective-permute-start | bytes 49160 | tf_op jit(solution)/shard_map/ppermute | solution.py:609
  22.3 12.7 %collective-permute-start.3 = (f32[8,512]{1,0:T(8,128)S(1)}, f32[8,512]{1,0:T(8,128)S(1)}, u32[]{:S(2)}, u32[]{:S(2)}) collective-permute-start(f32[8,512]{1,0:T(8,128)S(1)} %get-tuple-element.24), channel_id=1, source_target_pairs={{1,2},{2,1},{3,4},{4,3},{5,6},{6,5},{7,8},{8,7},{9,10},{10,9},{11,... | collective-permute-start | bytes 49160 | tf_op jit(solution)/shard_map/ppermute | solution.py:610

commit v15 on v14

--- a/solution.py
+++ b/solution.py
@@ -19,7 +19,6 @@
 CHUNK = 16
 CHUNKS = 2 * ROWS // CHUNK
 PIECE = 8
-PIECES = VECTORS // PIECE
 LANES = 128
 SLOTS = 64
 EDGE_AT = 5 * HALO
@@ -93,18 +92,40 @@
     return total
 
 
-def restrict_piece(i, held, field, sums):
-    totals = [None] * PIECE
-    for a in range(2):
-        for r in range(0, ROWS, CHUNK):
+MATRIX_GROUPS = tuple((1, r) for r in range(CHUNK, ROWS, CHUNK))
+VECTOR_GROUPS = ((0, 0), (0, 16), (0, 32), (0, 48), (1, 0))
+
+
+def restrict(held, field, sums, lines):
+    lines[2 * CHUNK :] = jnp.zeros((LANES - 2 * CHUNK, lines.shape[1]), jnp.bfloat16)
+    blocks = []
+    for g, (a, r) in enumerate(MATRIX_GROUPS):
+        part, cells = field[a, r : r + CHUNK], slice(CELLS * g, CELLS * (g + 1))
+        high = part.astype(jnp.bfloat16)
+        lines[:CHUNK, cells] = high
+        lines[CHUNK : 2 * CHUNK, cells] = (part - high.astype(jnp.float32)).astype(jnp.bfloat16)
+        blocks.append(held[:, a, r : r + CHUNK, :].reshape(CHUNK * VECTORS, CELLS))
+    products = lax.dot_general(
+        jnp.concatenate(blocks, 1),
+        lines[...],
+        (((1,), (1,)), ((), ())),
+        preferred_element_type=jnp.float32,
+    )
+    row = lax.broadcasted_iota(jnp.int32, (CHUNK, LANES), 0)
+    equal = row == lax.broadcasted_iota(jnp.int32, (CHUNK, LANES), 1) % CHUNK
+    for first in range(0, VECTORS, PIECE):
+        totals = [
+            jnp.where(equal, products[CHUNK * k : CHUNK * (k + 1)], 0.0)
+            for k in range(first, first + PIECE)
+        ]
+        for a, r in VECTOR_GROUPS:
             for c in range(0, CELLS, LANES):
                 rows, cells = slice(r, r + CHUNK), slice(c, c + LANES)
                 tile = field[a, rows, cells]
                 for n in range(PIECE):
-                    term = held[PIECE * i + n, a, rows, cells].astype(jnp.float32) * tile
-                    totals[n] = term if totals[n] is None else totals[n] + term
-    tiles = [total[:8] + total[8:] for total in totals]
-    sums[pl.ds(pl.multiple_of(PIECE * i, PIECE), PIECE), :] = in_rows(tiles)
+                    term = held[first + n, a, rows, cells].astype(jnp.float32) * tile
+                    totals[n] = totals[n] + term
+        sums[first : first + PIECE] = in_rows([total[:8] + total[8:] for total in totals])
 
 
 def fold(row):
@@ -216,7 +237,7 @@
         copy.wait()
 
 
-def restrict_kernel(rhs_ref, held, sums_ref, sums):
+def restrict_kernel(rhs_ref, held, sums_ref, sums, lines):
     sums[...] = jnp.zeros_like(sums)
     squares = jnp.zeros((TILE, CELLS), jnp.float32)
     for a in range(2):
@@ -225,11 +246,7 @@
             squares = squares + tile * tile
     sums[VECTORS : VECTORS + 8] = in_rows([fold(squares)])
 
-    def body(i, carry):
-        restrict_piece(i, held, rhs_ref, sums)
-        return carry
-
-    lax.fori_loop(0, PIECES, body, 0)
+    restrict(held, rhs_ref, sums, lines)
     send_sums(sums, sums_ref)
 
 
@@ -455,12 +472,13 @@
 def first_turn_kernel(
     count, margin_ref, sums_ref, inverse_ref, partner_ref, other_ref, held, rhs_ref, visc_ref,
     coup_ref,
-    direction_ref, image_ref, smooth_ref, partner_rows_ref, other_rows_ref, next_ref,
-    extended, sums, stacked, solved,
+    direction_ref, image_ref, smooth_ref, residual_ref, partner_rows_ref, other_rows_ref, next_ref,
+    extended, sums, stacked, solved, lines,
 ):
     received = sums_ref[...]
     over_beta = 1.0 / jnp.sqrt(lane_total(received, VECTORS))
     residual = line_up(received) * over_beta
+    residual_ref[...] = residual
     steps = prolonging(residual, inverse_ref, held, extended)
     low, high = neighbours_of(partner_ref, other_ref)
 
@@ -497,11 +515,7 @@
     sums[...] = jnp.zeros_like(sums)
     sums[VECTORS : VECTORS + 8] = in_rows([fold(products), fold(squares)])
 
-    def body(i, carry):
-        restrict_piece(i, held, image_ref, sums)
-        return carry
-
-    lax.fori_loop(0, PIECES, body, 0)
+    restrict(held, image_ref, sums, lines)
     send_sums(sums, next_ref)
 
 
@@ -513,7 +527,7 @@
 
 
 def second_turn_kernel(
-    count, margin_ref, first_ref, second_ref, inverse_ref, partner_ref, other_ref,
+    count, margin_ref, first_ref, second_ref, residual_ref, inverse_ref, partner_ref, other_ref,
     partner_rows_ref, other_rows_ref, held, smooth_ref, rhs_ref, image_ref, visc_ref, coup_ref,
     direction_ref, next_ref,
     image_smooth, extended, sums, stacked, solved,
@@ -522,7 +536,7 @@
     beta, h_00, h_10 = first_column(first, second)
     ratio = h_00 / beta
     over = 1.0 / h_10
-    residual = (line_up(second) - ratio * line_up(first)) * over
+    residual = (line_up(second) - h_00 * residual_ref[...]) * over
     steps = prolonging(residual, inverse_ref, held, extended)
     low, high = neighbours_of(partner_ref, other_ref)
     low_rows, high_rows = neighbours_of(partner_rows_ref, other_rows_ref)
@@ -620,6 +634,7 @@
     stacked = pltpu.VMEM((6, STACKED, CELLS), jnp.float32)
     solved = pltpu.VMEM((4, STACKED, CELLS), jnp.float32)
     sums = pltpu.VMEM((SLOTS, LANES), jnp.float32)
+    lines = pltpu.VMEM((LANES, len(MATRIX_GROUPS) * CELLS), jnp.bfloat16)
     row, whole, edge = f32(count, LANES), f32(2, ROWS, CELLS), f32(TILE, CELLS)
     packed, smoothed = f32(EDGE_AT + coarse_rows(columns), CELLS), f32(2, EXT, CELLS)
     arguments = (rhs, viscosity, coupling, coarse_inverse, coarse_basis)
@@ -631,20 +646,21 @@
     held, partner, other = lax.optimization_barrier((coarse_basis, *packs))
     partner, other = swap(partner, other)
     (first,) = call(
-        restrict_kernel, "restrict", [VMEM] * 2, [row], 10_000_000, [sums]
+        restrict_kernel, "restrict", [VMEM] * 2, [row], 10_000_000, [sums, lines]
     )(rhs, held)
     first = from_everyone(first)
-    direction, image, smooth, partner_rows, other_rows, second = call(
+    direction, image, smooth, residual, partner_rows, other_rows, second = call(
         functools.partial(first_turn_kernel, count), "first_turn", [SMEM] + [VMEM] * 8,
-        [whole, whole, smoothed, edge, edge, row], 20_000_000, [extended, sums, stacked, solved],
+        [whole, whole, smoothed, f32(1, columns), edge, edge, row], 20_000_000,
+        [extended, sums, stacked, solved, lines],
     )(margin_rows, first, coarse_inverse, partner, other, held, rhs, viscosity, coupling)
     partner_rows, other_rows = swap(partner_rows, other_rows)
     second = from_everyone(second)
     second_direction, third = call(
-        functools.partial(second_turn_kernel, count), "second_turn", [SMEM] + [VMEM] * 13,
+        functools.partial(second_turn_kernel, count), "second_turn", [SMEM] + [VMEM] * 14,
         [whole, row], 20_000_000, [extended, extended, sums, stacked, solved],
     )(
-        margin_rows, first, second, coarse_inverse, partner, other, partner_rows, other_rows,
+        margin_rows, first, second, residual, coarse_inverse, partner, other, partner_rows, other_rows,
         held, smooth, rhs, image, viscosity, coupling,
     )
     third = from_everyone(third)

time: 47.8 us -> 47.3 us (0.990)
  Pallas kernels: 12.3 us -> 11.8 us
where the time goes in v15:
time: 47.3 us; the launch traced here: 47 us
  blocking collectives  32.1 us (68%)
  Pallas kernels  11.8 us (25%)
  starting transfers between devices  2.19 us (5%)
  between operations  0.74 us (2%)
    all_to_all x3, blocking collectives, from_everyone(): lax.all_to_all(rows, 'sub', 0, 0, tiled=True, axis_index_groups=order)  32.1 us
    pallas_call x1, Pallas kernels, on_device(): call(functools.partial(first_turn_kernel, count), 'first_turn', [SMEM] +...  3.87 us
    pallas_call x1, Pallas kernels, on_device(): call(functools.partial(second_turn_kernel, count), 'second_turn', [SMEM]...  2.53 us
    pallas_call x1, Pallas kernels, on_device(): call(pack_kernel, 'pack', [HBM] * 5, [packed, packed], 5000000, [pltpu.VM...  2.52 us
    pallas_call x1, Pallas kernels, on_device(): call(restrict_kernel, 'restrict', [VMEM] * 2, [row], 10000000, [sums, lin...  1.54 us
    ppermute x2, starting transfers between devices, swap(): lax.ppermute(other, 'sub', both(range(1, count - 1, 2)))  1.46 us
    pallas_call x1, Pallas kernels, on_device(): call(finish_kernel, 'finish', [VMEM] * 5, [whole, f32(2, 3)], 1000000)  1.36 us
  transfers between devices with their start and end apart: 4, of which 0 were waited for; matrix products, arithmetic and copies ran while one was open for 0% of the time, Pallas kernels for 3%

profile of v15, /device:TPU:0, one launch (start us, length us, event | category | flops | bytes accessed | tf_op | source)
XLA Modules:
  0.0 47.0 jit_solution(11040992488719518053)
XLA Ops:
  0.6 0.0 copy-start.1
  0.6 0.0 copy-start.3
  0.7 0.0 copy-start.2
  0.7 0.0 copy-start.4
  0.7 0.0 copy-start
  0.7 0.0 copy-start.5
  0.7 2.5 %pack.1 = (f32[208,512]{1,0:T(8,128)S(1)}, f32[208,512]{1,0:T(8,128)S(1)}) custom-call(f32[2,64,512]{2,1,0:T(8,128)} %rhs_ref.7, f32[64,512]{1,0:T(8,128)} %visc_ref.5, f32[2,64,512]{2,1,0:T(8,128)} %coup_ref.5, f32[48,768]{1,0:T(8,128)} %inverse_ref.5, bf16[48,2,64,512]{3,2,1,0:T(8,128)(2,1)} %held.2), custom_call_target="tpu_custom_call" | custom-call | flops 5000000 | bytes 4000000 | tf_op jit(solution)/shard_map/pack/pallas_call | solution.py:641
  3.2 0.5 %collective-permute-start = (f32[208,512]{1,0:T(8,128)S(1)}, f32[208,512]{1,0:T(8,128)S(1)}, u32[]{:S(2)}, u32[]{:S(2)}) collective-permute-start(f32[208,512]{1,0:T(8,128)S(1)} %get-tuple-element.21), channel_id=1, source_target_pairs={{0,1},{1,0},{2,3},{3,2},{4,5},{5,4},{6,7},{7,6},{8,9},{9,8},{10,11... | collective-permute-start | bytes 1277960 | tf_op jit(solution)/shard_map/ppermute | solution.py:623
  3.7 0.8 %collective-permute-start.1 = (f32[208,512]{1,0:T(8,128)S(1)}, f32[208,512]{1,0:T(8,128)S(1)}, u32[]{:S(2)}, u32[]{:S(2)}) collective-permute-start(f32[208,512]{1,0:T(8,128)S(1)} %get-tuple-element.22), channel_id=1, source_target_pairs={{1,2},{2,1},{3,4},{4,3},{5,6},{6,5},{7,8},{8,7},{9,10},{10,9},{11,... | collective-permute-start | bytes 1277960 | tf_op jit(solution)/shard_map/ppermute | solution.py:624
  4.5 0.0 copy-done.1
  4.6 0.1 copy-done
  4.6 1.5 %restrict.1 = f32[16,128]{1,0:T(8,128)S(1)} custom-call(f32[2,64,512]{2,1,0:T(8,128)S(1)} %copy-done.1, bf16[48,2,64,512]{3,2,1,0:T(8,128)(2,1)S(1)} %copy-done), custom_call_target="tpu_custom_call" | custom-call | flops 10000000 | bytes 4000000 | tf_op jit(solution)/shard_map/restrict/pallas_call | solution.py:648
  6.2 11.8 %all_to_all.33 = f32[16,1,128]{2,1,0:T(1,128)S(1)} all-to-all(f32[16,1,128]{2,1,0:T(1,128)S(1)} %bitcast.19), channel_id=1, replica_groups={{15,14,13,12,11,10,9,8,7,6,5,4,3,2,1,0},{31,30,29,28,27,26,25,24,23,22,..., dimensions={0} | all-to-all | bytes 16384 | tf_op jit(solution)/shard_map/all_to_all | solution.py:616
  18.0 0.0 collective-permute-done.partner_ref
  18.0 0.0 collective-permute-done.1.other_ref
  18.0 0.0 copy-done.3
  18.0 0.0 copy-done.2
  18.0 0.0 copy-done.4
  18.0 0.0 copy-done.5
  18.0 3.9 %first_turn.1 = (f32[2,64,512]{2,1,0:T(8,128)S(1)}, f32[2,64,512]{2,1,0:T(8,128)S(1)}, f32[2,80,512]{2,1,0:T(8,128)S(1)}, f32[1,768]{1,0:T(1,128)S(1)}, f32[8,51...) custom-call(s32[16]{0:T(128)S(1)} %copy-done.5, f32[16,128]{1,0:T(8,128)S(1)} %bitcast.13, ...), custom_call_target="tpu_custom_call" | custom-call | flops 20000000 | bytes 4000000 | tf_op jit(solution)/shard_map/first_turn/pallas_call | solution.py:652
  21.9 0.2 collective-permute-start.2
  22.1 0.7 %collective-permute-start.3 = (f32[8,512]{1,0:T(8,128)S(1)}, f32[8,512]{1,0:T(8,128)S(1)}, u32[]{:S(2)}, u32[]{:S(2)}) collective-permute-start(f32[8,512]{1,0:T(8,128)S(1)} %get-tuple-element.26), channel_id=1, source_target_pairs={{1,2},{2,1},{3,4},{4,3},{5,6},{6,5},{7,8},{8,7},{9,10},{10,9},{11,... | collective-permute-start | bytes 49160 | tf_op jit(solution)/shard_map/ppermute | solution.py:624
  22.8 12.0 %all_to_all.34 = f32[16,1,128]{2,1,0:T(1,128)S(1)} all-to-all(f32[16,1,128]{2,1,0:T(1,128)S(1)} %bitcast.20), channel_id=1, replica_groups={{15,14,13,12,11,10,9,8,7,6,5,4,3,2,1,0},{31,30,29,28,27,26,25,24,23,22,..., dimensions={0} | all-to-all | bytes 16384 | tf_op jit(solution)/shard_map/all_to_all | solution.py:616
  34.7 0.0 collective-permute-done.2.partner_rows_ref
  34.8 0.0 collective-permute-done.3.other_rows_ref
  34.8 2.5 %second_turn.1 = (f32[2,64,512]{2,1,0:T(8,128)S(1)}, f32[16,128]{1,0:T(8,128)S(1)}) custom-call(s32[16]{0:T(128)S(1)} %copy-done.5, f32[16,128]{1,0:T(8,128)S(1)} %bitcast.14, f32[16,128]{1,0:T(8,128)S(1)} %bitcast.16, f32[1,768]{1,0:T(1,128)S(1)} %get-tuple-element.24.residual_ref, f32[48,768]{1,0:T(8,128)S(1)} %copy-done.3, ...), custom_call_target="tpu_custom_call" | custom-call | flops 20000000 | bytes 4000000 | tf_op jit(solution)/shard_map/second_turn/pallas_call | solution.py:659
  37.3 8.4 %all_to_all.35 = f32[16,1,128]{2,1,0:T(1,128)S(1)} all-to-all(f32[16,1,128]{2,1,0:T(1,128)S(1)} %bitcast.21), channel_id=1, replica_groups={{15,14,13,12,11,10,9,8,7,6,5,4,3,2,1,0},{31,30,29,28,27,26,25,24,23,22,..., dimensions={0} | all-to-all | bytes 16384 | tf_op jit(solution)/shard_map/all_to_all | solution.py:616
  45.6 1.4 %finish.1 = (f32[2,64,512]{2,1,0:T(8,128)}, f32[2,3]{1,0:T(2,128)}) custom-call(f32[16,128]{1,0:T(8,128)S(1)} %bitcast.15, f32[16,128]{1,0:T(8,128)S(1)} %bitcast.17, f32[16,128]{1,0:T(8,128)S(1)} %bitcast.18, f32[2,64,512]{2,1,0:T(8,128)S(1)} %get-tuple-element.30.first_direction_ref, f32[2,64,512]{2,1,0:T(8,128)S(1)} %get-tuple-element.31.second_direction_ref), custom_call_target="tpu_custom_call" | custom-call | flops 1000000 | bytes 4000000 | tf_op jit(solution)/shard_map/finish/pallas_call | solution.py:667
Async XLA Ops:
  0.6 3.9 %copy-start.1 = (f32[2,64,512]{2,1,0:T(8,128)S(1)}, f32[2,64,512]{2,1,0:T(8,128)}, u32[]{:S(2)}) copy-start(f32[2,64,512]{2,1,0:T(8,128)} %rhs_ref.7) | copy-start | bytes 786436
  0.6 17.3 %copy-start.3 = (f32[48,768]{1,0:T(8,128)S(1)}, f32[48,768]{1,0:T(8,128)}, u32[]{:S(2)}) copy-start(f32[48,768]{1,0:T(8,128)} %inverse_ref.5) | copy-start | bytes 442372
  0.7 17.3 %copy-start.2 = (f32[2,64,512]{2,1,0:T(8,128)S(1)}, f32[2,64,512]{2,1,0:T(8,128)}, u32[]{:S(2)}) copy-start(f32[2,64,512]{2,1,0:T(8,128)} %coup_ref.5) | copy-start | bytes 786436
  0.7 17.3 %copy-start.4 = (f32[64,512]{1,0:T(8,128)S(1)}, f32[64,512]{1,0:T(8,128)}, u32[]{:S(2)}) copy-start(f32[64,512]{1,0:T(8,128)} %visc_ref.5) | copy-start | bytes 393220
  0.7 4.0 %copy-start = (bf16[48,2,64,512]{3,2,1,0:T(8,128)(2,1)S(1)}, bf16[48,2,64,512]{3,2,1,0:T(8,128)(2,1)}, u32[]{:S(2)}) copy-start(bf16[48,2,64,512]{3,2,1,0:T(8,128)(2,1)} %held.2) | copy-start | bytes 18874372
  0.7 17.3 %copy-start.5 = (s32[16]{0:T(128)S(1)}, s32[16]{0:T(128)}, u32[]{:S(2)}) copy-start(s32[16]{0:T(128)} %margin_ref.3) | copy-start | bytes 196
  3.2 14.8 %collective-permute-start = (f32[208,512]{1,0:T(8,128)S(1)}, f32[208,512]{1,0:T(8,128)S(1)}, u32[]{:S(2)}, u32[]{:S(2)}) collective-permute-start(f32[208,512]{1,0:T(8,128)S(1)} %get-tuple-element.21), channel_id=1, source_target_pairs={{0,1},{1,0},{2,3},{3,2},{4,5},{5,4},{6,7},{7,6},{8,9},{9,8},{10,11... | collective-permute-start | bytes 1277960 | tf_op jit(solution)/shard_map/ppermute | solution.py:623
  3.7 14.2 %collective-permute-start.1 = (f32[208,512]{1,0:T(8,128)S(1)}, f32[208,512]{1,0:T(8,128)S(1)}, u32[]{:S(2)}, u32[]{:S(2)}) collective-permute-start(f32[208,512]{1,0:T(8,128)S(1)} %get-tuple-element.22), channel_id=1, source_target_pairs={{1,2},{2,1},{3,4},{4,3},{5,6},{6,5},{7,8},{8,7},{9,10},{10,9},{11,... | collective-permute-start | bytes 1277960 | tf_op jit(solution)/shard_map/ppermute | solution.py:624
  21.9 12.9 %collective-permute-start.2 = (f32[8,512]{1,0:T(8,128)S(1)}, f32[8,512]{1,0:T(8,128)S(1)}, u32[]{:S(2)}, u32[]{:S(2)}) collective-permute-start(f32[8,512]{1,0:T(8,128)S(1)} %get-tuple-element.25), channel_id=1, source_target_pairs={{0,1},{1,0},{2,3},{3,2},{4,5},{5,4},{6,7},{7,6},{8,9},{9,8},{10,11... | collective-permute-start | bytes 49160 | tf_op jit(solution)/shard_map/ppermute | solution.py:623
  22.1 12.7 %collective-permute-start.3 = (f32[8,512]{1,0:T(8,128)S(1)}, f32[8,512]{1,0:T(8,128)S(1)}, u32[]{:S(2)}, u32[]{:S(2)}) collective-permute-start(f32[8,512]{1,0:T(8,128)S(1)} %get-tuple-element.26), channel_id=1, source_target_pairs={{1,2},{2,1},{3,4},{4,3},{5,6},{6,5},{7,8},{8,7},{9,10},{10,9},{11,... | collective-permute-start | bytes 49160 | tf_op jit(solution)/shard_map/ppermute | solution.py:624

commit v16 on v15

--- a/solution.py
+++ b/solution.py
@@ -114,17 +114,17 @@
     row = lax.broadcasted_iota(jnp.int32, (CHUNK, LANES), 0)
     equal = row == lax.broadcasted_iota(jnp.int32, (CHUNK, LANES), 1) % CHUNK
     for first in range(0, VECTORS, PIECE):
-        totals = [
-            jnp.where(equal, products[CHUNK * k : CHUNK * (k + 1)], 0.0)
-            for k in range(first, first + PIECE)
-        ]
+        totals = [None] * PIECE
         for a, r in VECTOR_GROUPS:
             for c in range(0, CELLS, LANES):
                 rows, cells = slice(r, r + CHUNK), slice(c, c + LANES)
                 tile = field[a, rows, cells]
                 for n in range(PIECE):
                     term = held[first + n, a, rows, cells].astype(jnp.float32) * tile
-                    totals[n] = totals[n] + term
+                    totals[n] = term if totals[n] is None else totals[n] + term
+        for n in range(PIECE):
+            at = CHUNK * (first + n)
+            totals[n] = totals[n] + jnp.where(equal, products[at : at + CHUNK], 0.0)
         sums[first : first + PIECE] = in_rows([total[:8] + total[8:] for total in totals])
 
 
@@ -139,7 +139,7 @@
     return slice(TILE * t, TILE * (t + 1))
 
 
-def send_sums(sums, out_ref):
+def send_sums(sums, out_ref, turn):
     rest = sums[...]
     parts = []
     for _ in range(3):
@@ -152,8 +152,14 @@
         (((1,), (1,)), ((), ())),
         preferred_element_type=jnp.float32,
     )
-    wide = jnp.concatenate([row[:1], jnp.zeros((1, LANES - SLOTS), jnp.float32)], 1)
-    out_ref[...] = jnp.broadcast_to(wide, out_ref.shape)
+    wide = jnp.concatenate([row[:8], jnp.zeros((8, LANES - SLOTS), jnp.float32)], 1)
+    wide = pltpu.roll(wide, turn, 1)
+    for r in range(0, out_ref.shape[0], 8):
+        out_ref[r : r + 8] = wide
+
+
+def own_turn():
+    return VECTORS * lax.axis_index("sub") % LANES
 
 
 def pack_copies(out_ref, first_row, rhs_ref, visc_ref, coup_ref, inverse_ref, sems, at_sem):
@@ -247,7 +253,7 @@
     sums[VECTORS : VECTORS + 8] = in_rows([fold(squares)])
 
     restrict(held, rhs_ref, sums, lines)
-    send_sums(sums, sums_ref)
+    send_sums(sums, sums_ref, own_turn())
 
 
 class Neighbour:
@@ -361,49 +367,59 @@
                         out_ref[a, tile_rows(e)] += weight_of(n, e) * value
 
 
-def line_up(residuals):
-    devices = residuals.shape[0]
-    lane = lax.broadcasted_iota(jnp.int32, (1, LANES), 1)
-    tiles = [jnp.zeros((1, LANES), jnp.float32) for _ in range(devices * VECTORS // LANES)]
-    for t in range(devices):
-        tile, offset = divmod(VECTORS * t, LANES)
-        row = jnp.where(lane < VECTORS, residuals[devices - 1 - t : devices - t], 0.0)
-        if offset:
-            row = pltpu.roll(row, offset, 1)
-        if offset + VECTORS <= LANES:
-            tiles[tile] = tiles[tile] + row
-        else:
-            tiles[tile] = tiles[tile] + jnp.where(lane >= offset, row, 0.0)
-            tiles[tile + 1] = tiles[tile + 1] + jnp.where(lane < offset, row, 0.0)
+def place_in_line(shape):
+    rank = shape[0] - 1 - lax.broadcasted_iota(jnp.int32, shape, 0)
+    return rank, lax.broadcasted_iota(jnp.int32, shape, 1)
+
+
+def add_rows(field):
+    total = field[:8]
+    for r in range(8, field.shape[0], 8):
+        total = total + field[r : r + 8]
+    return sublane_sum(total)
+
+
+def line_up(received):
+    rank, lane = place_in_line(received.shape)
+    first = lane - VECTORS * rank
+    tiles = []
+    for at in range(0, VECTORS * received.shape[0], LANES):
+        own = (first + at >= 0) & (first + at < VECTORS)
+        tiles.append(add_rows(jnp.where(own, received, 0.0)))
     return jnp.concatenate(tiles, 1)
+
+
+def turned_total(received, slot):
+    rank, lane = place_in_line(received.shape)
+    own = lane == (VECTORS * rank + slot) % LANES
+    return jnp.sum(jnp.where(own, received, 0.0), keepdims=True)
 
 
 def rounded(column):
     return column.astype(jnp.bfloat16).astype(jnp.float32)
 
 
+def times(matrix, line):
+    tall = matrix.reshape(-1, 8, matrix.shape[1])
+    return jnp.sum(tall * line[None], 2, keepdims=True).reshape(-1, 1)
+
+
 def lift(inverse_ref, residual):
-    return rounded(jnp.sum(inverse_ref[...] * residual, 1, keepdims=True))
+    return rounded(times(inverse_ref[...], residual))
 
 
 def lift_packed(ref, residual):
     columns = residual.shape[1]
     at, total = EDGE_AT + INVERSE_AT, None
     for c in range(0, columns - 511, 512):
-        term = jnp.sum(ref[at : at + VECTORS] * residual[:, c : c + 512], 1, keepdims=True)
+        term = times(ref[at : at + VECTORS], residual[:, c : c + 512])
         total = term if total is None else total + term
         at += VECTORS
     if columns % 512:
         half = VECTORS // 2
         last = residual[:, columns - 256 :]
         rows = ref[at : at + half]
-        term = jnp.concatenate(
-            [
-                jnp.sum(rows[:, :256] * last, 1, keepdims=True),
-                jnp.sum(rows[:, 256:] * last, 1, keepdims=True),
-            ],
-            0,
-        )
+        term = jnp.concatenate([times(rows[:, :256], last), times(rows[:, 256:], last)], 0)
         total = term if total is None else total + term
     return rounded(total)
 
@@ -476,7 +492,7 @@
     extended, sums, stacked, solved, lines,
 ):
     received = sums_ref[...]
-    over_beta = 1.0 / jnp.sqrt(lane_total(received, VECTORS))
+    over_beta = 1.0 / jnp.sqrt(turned_total(received, VECTORS))
     residual = line_up(received) * over_beta
     residual_ref[...] = residual
     steps = prolonging(residual, inverse_ref, held, extended)
@@ -516,13 +532,13 @@
     sums[VECTORS : VECTORS + 8] = in_rows([fold(products), fold(squares)])
 
     restrict(held, image_ref, sums, lines)
-    send_sums(sums, next_ref)
+    send_sums(sums, next_ref, own_turn())
 
 
 def first_column(first, second):
-    beta = jnp.sqrt(lane_total(first, VECTORS))
-    h_00 = lane_total(second, VECTORS) / beta
-    h_10 = jnp.sqrt(lane_total(second, VECTORS + 1) - h_00 * h_00)
+    beta = jnp.sqrt(turned_total(first, VECTORS))
+    h_00 = turned_total(second, VECTORS) / beta
+    h_10 = jnp.sqrt(turned_total(second, VECTORS + 1) - h_00 * h_00)
     return beta, h_00, h_10
 
 
@@ -565,7 +581,7 @@
         totals = [total + x * image for total, x in zip(totals, others)]
     sums[...] = jnp.zeros_like(sums)
     sums[:8] = in_rows([fold(total) for total in totals])
-    send_sums(sums, next_ref)
+    send_sums(sums, next_ref, 0)
 
 
 def finish_kernel(
@@ -651,7 +667,7 @@
     first = from_everyone(first)
     direction, image, smooth, residual, partner_rows, other_rows, second = call(
         functools.partial(first_turn_kernel, count), "first_turn", [SMEM] + [VMEM] * 8,
-        [whole, whole, smoothed, f32(1, columns), edge, edge, row], 20_000_000,
+        [whole, whole, smoothed, f32(8, columns), edge, edge, row], 20_000_000,
         [extended, sums, stacked, solved, lines],
     )(margin_rows, first, coarse_inverse, partner, other, held, rhs, viscosity, coupling)
     partner_rows, other_rows = swap(partner_rows, other_rows)

time: 47.3 us -> 48 us (1.015)
  Pallas kernels: 11.8 us -> 12.7 us
    pallas_call x1, Pallas kernels: 3.87 us -> 4.41 us  [on_device(): call(functools.partial(first_turn_kernel, count), 'first_turn', [SMEM] +...]
  transfers between devices with their start and end apart: 4 -> 4, of which waited for: 0 -> 0; matrix products, arithmetic and copies ran while one was open for 0% -> 0% of each run, Pallas kernels for 3% -> 4%
where the time goes in v16:
time: 48 us; the launch traced here: 47.7 us
  blocking collectives  32.1 us (67%)
  Pallas kernels  12.7 us (26%)
  starting transfers between devices  2.04 us (4%)
  between operations  0.74 us (2%)
    all_to_all x3, blocking collectives, from_everyone(): lax.all_to_all(rows, 'sub', 0, 0, tiled=True, axis_index_groups=order)  32.1 us
    pallas_call x1, Pallas kernels, on_device(): call(functools.partial(first_turn_kernel, count), 'first_turn', [SMEM] +...  4.41 us
    pallas_call x1, Pallas kernels, on_device(): call(functools.partial(second_turn_kernel, count), 'second_turn', [SMEM]...  2.83 us
    pallas_call x1, Pallas kernels, on_device(): call(pack_kernel, 'pack', [HBM] * 5, [packed, packed], 5000000, [pltpu.VM...  2.52 us
    pallas_call x1, Pallas kernels, on_device(): call(restrict_kernel, 'restrict', [VMEM] * 2, [row], 10000000, [sums, lin...  1.69 us
    ppermute x2, starting transfers between devices, swap(): lax.ppermute(other, 'sub', both(range(1, count - 1, 2)))  1.46 us
    pallas_call x1, Pallas kernels, on_device(): call(finish_kernel, 'finish', [VMEM] * 5, [whole, f32(2, 3)], 1000000)  1.21 us
  transfers between devices with their start and end apart: 4, of which 0 were waited for; matrix products, arithmetic and copies ran while one was open for 0% of the time, Pallas kernels for 4%

profile of v16, /device:TPU:0, one launch (start us, length us, event | category | flops | bytes accessed | tf_op | source)
XLA Modules:
  0.0 47.7 jit_solution(1931831803955297394)
XLA Ops:
  0.6 0.0 copy-start.1
  0.6 0.0 copy-start.3
  0.7 0.0 copy-start.2
  0.7 0.0 copy-start.4
  0.7 0.0 copy-start
  0.7 0.0 copy-start.5
  0.7 2.5 %pack.1 = (f32[208,512]{1,0:T(8,128)S(1)}, f32[208,512]{1,0:T(8,128)S(1)}) custom-call(f32[2,64,512]{2,1,0:T(8,128)} %rhs_ref.7, f32[64,512]{1,0:T(8,128)} %visc_ref.5, f32[2,64,512]{2,1,0:T(8,128)} %coup_ref.5, f32[48,768]{1,0:T(8,128)} %inverse_ref.5, bf16[48,2,64,512]{3,2,1,0:T(8,128)(2,1)} %held.2), custom_call_target="tpu_custom_call" | custom-call | flops 5000000 | bytes 4000000 | tf_op jit(solution)/shard_map/pack/pallas_call | solution.py:657
  3.2 0.5 %collective-permute-start = (f32[208,512]{1,0:T(8,128)S(1)}, f32[208,512]{1,0:T(8,128)S(1)}, u32[]{:S(2)}, u32[]{:S(2)}) collective-permute-start(f32[208,512]{1,0:T(8,128)S(1)} %get-tuple-element.21), channel_id=1, source_target_pairs={{0,1},{1,0},{2,3},{3,2},{4,5},{5,4},{6,7},{7,6},{8,9},{9,8},{10,11... | collective-permute-start | bytes 1277960 | tf_op jit(solution)/shard_map/ppermute | solution.py:639
  3.7 0.8 %collective-permute-start.1 = (f32[208,512]{1,0:T(8,128)S(1)}, f32[208,512]{1,0:T(8,128)S(1)}, u32[]{:S(2)}, u32[]{:S(2)}) collective-permute-start(f32[208,512]{1,0:T(8,128)S(1)} %get-tuple-element.22), channel_id=1, source_target_pairs={{1,2},{2,1},{3,4},{4,3},{5,6},{6,5},{7,8},{8,7},{9,10},{10,9},{11,... | collective-permute-start | bytes 1277960 | tf_op jit(solution)/shard_map/ppermute | solution.py:640
  4.5 0.0 copy-done.1
  4.6 0.1 copy-done
  4.6 1.7 %restrict.1 = f32[16,128]{1,0:T(8,128)S(1)} custom-call(f32[2,64,512]{2,1,0:T(8,128)S(1)} %copy-done.1, bf16[48,2,64,512]{3,2,1,0:T(8,128)(2,1)S(1)} %copy-done), custom_call_target="tpu_custom_call" | custom-call | flops 10000000 | bytes 4000000 | tf_op jit(solution)/shard_map/restrict/pallas_call | solution.py:664
  6.3 11.8 %all_to_all.33 = f32[16,1,128]{2,1,0:T(1,128)S(1)} all-to-all(f32[16,1,128]{2,1,0:T(1,128)S(1)} %bitcast.19), channel_id=1, replica_groups={{15,14,13,12,11,10,9,8,7,6,5,4,3,2,1,0},{31,30,29,28,27,26,25,24,23,22,..., dimensions={0} | all-to-all | bytes 16384 | tf_op jit(solution)/shard_map/all_to_all | solution.py:632
  18.1 0.0 collective-permute-done.partner_ref
  18.1 0.0 collective-permute-done.1.other_ref
  18.1 0.0 copy-done.3
  18.1 0.0 copy-done.2
  18.1 0.0 copy-done.4
  18.1 0.0 copy-done.5
  18.2 4.4 %first_turn.1 = (f32[2,64,512]{2,1,0:T(8,128)S(1)}, f32[2,64,512]{2,1,0:T(8,128)S(1)}, f32[2,80,512]{2,1,0:T(8,128)S(1)}, f32[8,768]{1,0:T(8,128)S(1)}, f32[8,51...) custom-call(s32[16]{0:T(128)S(1)} %copy-done.5, f32[16,128]{1,0:T(8,128)S(1)} %bitcast.13, ...), custom_call_target="tpu_custom_call" | custom-call | flops 20000000 | bytes 4000000 | tf_op jit(solution)/shard_map/first_turn/pallas_call | solution.py:668
  22.6 0.1 collective-permute-start.2
  22.6 0.7 %collective-permute-start.3 = (f32[8,512]{1,0:T(8,128)S(1)}, f32[8,512]{1,0:T(8,128)S(1)}, u32[]{:S(2)}, u32[]{:S(2)}) collective-permute-start(f32[8,512]{1,0:T(8,128)S(1)} %get-tuple-element.26), channel_id=1, source_target_pairs={{1,2},{2,1},{3,4},{4,3},{5,6},{6,5},{7,8},{8,7},{9,10},{10,9},{11,... | collective-permute-start | bytes 49160 | tf_op jit(solution)/shard_map/ppermute | solution.py:640
  23.3 12.0 %all_to_all.34 = f32[16,1,128]{2,1,0:T(1,128)S(1)} all-to-all(f32[16,1,128]{2,1,0:T(1,128)S(1)} %bitcast.20), channel_id=1, replica_groups={{15,14,13,12,11,10,9,8,7,6,5,4,3,2,1,0},{31,30,29,28,27,26,25,24,23,22,..., dimensions={0} | all-to-all | bytes 16384 | tf_op jit(solution)/shard_map/all_to_all | solution.py:632
  35.3 0.0 collective-permute-done.2.partner_rows_ref
  35.3 0.0 collective-permute-done.3.other_rows_ref
  35.3 2.8 %second_turn.1 = (f32[2,64,512]{2,1,0:T(8,128)S(1)}, f32[16,128]{1,0:T(8,128)S(1)}) custom-call(s32[16]{0:T(128)S(1)} %copy-done.5, f32[16,128]{1,0:T(8,128)S(1)} %bitcast.14, f32[16,128]{1,0:T(8,128)S(1)} %bitcast.16, f32[8,768]{1,0:T(8,128)S(1)} %get-tuple-element.24.residual_ref, f32[48,768]{1,0:T(8,128)S(1)} %copy-done.3, ...), custom_call_target="tpu_custom_call" | custom-call | flops 20000000 | bytes 4000000 | tf_op jit(solution)/shard_map/second_turn/pallas_call | solution.py:675
  38.1 8.4 %all_to_all.35 = f32[16,1,128]{2,1,0:T(1,128)S(1)} all-to-all(f32[16,1,128]{2,1,0:T(1,128)S(1)} %bitcast.21), channel_id=1, replica_groups={{15,14,13,12,11,10,9,8,7,6,5,4,3,2,1,0},{31,30,29,28,27,26,25,24,23,22,..., dimensions={0} | all-to-all | bytes 16384 | tf_op jit(solution)/shard_map/all_to_all | solution.py:632
  46.5 1.2 %finish.1 = (f32[2,64,512]{2,1,0:T(8,128)}, f32[2,3]{1,0:T(2,128)}) custom-call(f32[16,128]{1,0:T(8,128)S(1)} %bitcast.15, f32[16,128]{1,0:T(8,128)S(1)} %bitcast.17, f32[16,128]{1,0:T(8,128)S(1)} %bitcast.18, f32[2,64,512]{2,1,0:T(8,128)S(1)} %get-tuple-element.30.first_direction_ref, f32[2,64,512]{2,1,0:T(8,128)S(1)} %get-tuple-element.31.second_direction_ref), custom_call_target="tpu_custom_call" | custom-call | flops 1000000 | bytes 4000000 | tf_op jit(solution)/shard_map/finish/pallas_call | solution.py:683
Async XLA Ops:
  0.6 3.9 %copy-start.1 = (f32[2,64,512]{2,1,0:T(8,128)S(1)}, f32[2,64,512]{2,1,0:T(8,128)}, u32[]{:S(2)}) copy-start(f32[2,64,512]{2,1,0:T(8,128)} %rhs_ref.7) | copy-start | bytes 786436
  0.6 17.5 %copy-start.3 = (f32[48,768]{1,0:T(8,128)S(1)}, f32[48,768]{1,0:T(8,128)}, u32[]{:S(2)}) copy-start(f32[48,768]{1,0:T(8,128)} %inverse_ref.5) | copy-start | bytes 442372
  0.7 17.5 %copy-start.2 = (f32[2,64,512]{2,1,0:T(8,128)S(1)}, f32[2,64,512]{2,1,0:T(8,128)}, u32[]{:S(2)}) copy-start(f32[2,64,512]{2,1,0:T(8,128)} %coup_ref.5) | copy-start | bytes 786436
  0.7 17.5 %copy-start.4 = (f32[64,512]{1,0:T(8,128)S(1)}, f32[64,512]{1,0:T(8,128)}, u32[]{:S(2)}) copy-start(f32[64,512]{1,0:T(8,128)} %visc_ref.5) | copy-start | bytes 393220
  0.7 4.0 %copy-start = (bf16[48,2,64,512]{3,2,1,0:T(8,128)(2,1)S(1)}, bf16[48,2,64,512]{3,2,1,0:T(8,128)(2,1)}, u32[]{:S(2)}) copy-start(bf16[48,2,64,512]{3,2,1,0:T(8,128)(2,1)} %held.2) | copy-start | bytes 18874372
  0.7 17.5 %copy-start.5 = (s32[16]{0:T(128)S(1)}, s32[16]{0:T(128)}, u32[]{:S(2)}) copy-start(s32[16]{0:T(128)} %margin_ref.3) | copy-start | bytes 196
  3.2 14.9 %collective-permute-start = (f32[208,512]{1,0:T(8,128)S(1)}, f32[208,512]{1,0:T(8,128)S(1)}, u32[]{:S(2)}, u32[]{:S(2)}) collective-permute-start(f32[208,512]{1,0:T(8,128)S(1)} %get-tuple-element.21), channel_id=1, source_target_pairs={{0,1},{1,0},{2,3},{3,2},{4,5},{5,4},{6,7},{7,6},{8,9},{9,8},{10,11... | collective-permute-start | bytes 1277960 | tf_op jit(solution)/shard_map/ppermute | solution.py:639
  3.7 14.4 %collective-permute-start.1 = (f32[208,512]{1,0:T(8,128)S(1)}, f32[208,512]{1,0:T(8,128)S(1)}, u32[]{:S(2)}, u32[]{:S(2)}) collective-permute-start(f32[208,512]{1,0:T(8,128)S(1)} %get-tuple-element.22), channel_id=1, source_target_pairs={{1,2},{2,1},{3,4},{4,3},{5,6},{6,5},{7,8},{8,7},{9,10},{10,9},{11,... | collective-permute-start | bytes 1277960 | tf_op jit(solution)/shard_map/ppermute | solution.py:640
  22.6 12.7 %collective-permute-start.2 = (f32[8,512]{1,0:T(8,128)S(1)}, f32[8,512]{1,0:T(8,128)S(1)}, u32[]{:S(2)}, u32[]{:S(2)}) collective-permute-start(f32[8,512]{1,0:T(8,128)S(1)} %get-tuple-element.25), channel_id=1, source_target_pairs={{0,1},{1,0},{2,3},{3,2},{4,5},{5,4},{6,7},{7,6},{8,9},{9,8},{10,11... | collective-permute-start | bytes 49160 | tf_op jit(solution)/shard_map/ppermute | solution.py:639
  22.6 12.7 %collective-permute-start.3 = (f32[8,512]{1,0:T(8,128)S(1)}, f32[8,512]{1,0:T(8,128)S(1)}, u32[]{:S(2)}, u32[]{:S(2)}) collective-permute-start(f32[8,512]{1,0:T(8,128)S(1)} %get-tuple-element.26), channel_id=1, source_target_pairs={{1,2},{2,1},{3,4},{4,3},{5,6},{6,5},{7,8},{8,7},{9,10},{10,9},{11,... | collective-permute-start | bytes 49160 | tf_op jit(solution)/shard_map/ppermute | solution.py:640

commit v17 on v15

--- a/solution.py
+++ b/solution.py
@@ -90,6 +90,20 @@
     for n, tile in enumerate(tiles):
         total = jnp.where(row == n, sublane_sum(tile), total)
     return total
+
+
+def restrict_piece(i, held, field, sums):
+    totals = [None] * PIECE
+    for a in range(2):
+        for r in range(0, ROWS, CHUNK):
+            for c in range(0, CELLS, LANES):
+                rows, cells = slice(r, r + CHUNK), slice(c, c + LANES)
+                tile = field[a, rows, cells]
+                for n in range(PIECE):
+                    term = held[PIECE * i + n, a, rows, cells].astype(jnp.float32) * tile
+                    totals[n] = term if totals[n] is None else totals[n] + term
+    tiles = [total[:8] + total[8:] for total in totals]
+    sums[pl.ds(pl.multiple_of(PIECE * i, PIECE), PIECE), :] = in_rows(tiles)
 
 
 MATRIX_GROUPS = tuple((1, r) for r in range(CHUNK, ROWS, CHUNK))
@@ -237,7 +251,7 @@
         copy.wait()
 
 
-def restrict_kernel(rhs_ref, held, sums_ref, sums, lines):
+def restrict_kernel(rhs_ref, held, sums_ref, sums):
     sums[...] = jnp.zeros_like(sums)
     squares = jnp.zeros((TILE, CELLS), jnp.float32)
     for a in range(2):
@@ -246,7 +260,11 @@
             squares = squares + tile * tile
     sums[VECTORS : VECTORS + 8] = in_rows([fold(squares)])
 
-    restrict(held, rhs_ref, sums, lines)
+    def body(i, carry):
+        restrict_piece(i, held, rhs_ref, sums)
+        return carry
+
+    lax.fori_loop(0, VECTORS // PIECE, body, 0)
     send_sums(sums, sums_ref)
 
 
@@ -361,20 +379,25 @@
                         out_ref[a, tile_rows(e)] += weight_of(n, e) * value
 
 
-def line_up(residuals):
-    devices = residuals.shape[0]
-    lane = lax.broadcasted_iota(jnp.int32, (1, LANES), 1)
-    tiles = [jnp.zeros((1, LANES), jnp.float32) for _ in range(devices * VECTORS // LANES)]
-    for t in range(devices):
-        tile, offset = divmod(VECTORS * t, LANES)
-        row = jnp.where(lane < VECTORS, residuals[devices - 1 - t : devices - t], 0.0)
-        if offset:
-            row = pltpu.roll(row, offset, 1)
-        if offset + VECTORS <= LANES:
-            tiles[tile] = tiles[tile] + row
-        else:
-            tiles[tile] = tiles[tile] + jnp.where(lane >= offset, row, 0.0)
-            tiles[tile + 1] = tiles[tile + 1] + jnp.where(lane < offset, row, 0.0)
+def place_in_line(shape):
+    rank = shape[0] - 1 - lax.broadcasted_iota(jnp.int32, shape, 0)
+    return rank, lax.broadcasted_iota(jnp.int32, shape, 1)
+
+
+def line_up(received):
+    devices = received.shape[0]
+    rank, lane = place_in_line(received.shape)
+    turned, by = received, VECTORS * rank % LANES
+    for step in (64, 32, 16):
+        turned = jnp.where(by & step != 0, pltpu.roll(turned, step, 1), turned)
+    first = lane - VECTORS * rank
+    tiles = []
+    for at in range(0, VECTORS * devices, LANES):
+        own = jnp.where((first + at >= 0) & (first + at < VECTORS), turned, 0.0)
+        total = own[:8]
+        for r in range(8, devices, 8):
+            total = total + own[r : r + 8]
+        tiles.append(sublane_sum(total))
     return jnp.concatenate(tiles, 1)
 
 
@@ -382,28 +405,26 @@
     return column.astype(jnp.bfloat16).astype(jnp.float32)
 
 
+def times(matrix, line):
+    return jnp.sum(matrix * jnp.concatenate([line] * (matrix.shape[0] // 8), 0), 1, keepdims=True)
+
+
 def lift(inverse_ref, residual):
-    return rounded(jnp.sum(inverse_ref[...] * residual, 1, keepdims=True))
+    return rounded(times(inverse_ref[...], residual))
 
 
 def lift_packed(ref, residual):
     columns = residual.shape[1]
     at, total = EDGE_AT + INVERSE_AT, None
     for c in range(0, columns - 511, 512):
-        term = jnp.sum(ref[at : at + VECTORS] * residual[:, c : c + 512], 1, keepdims=True)
+        term = times(ref[at : at + VECTORS], residual[:, c : c + 512])
         total = term if total is None else total + term
         at += VECTORS
     if columns % 512:
         half = VECTORS // 2
         last = residual[:, columns - 256 :]
         rows = ref[at : at + half]
-        term = jnp.concatenate(
-            [
-                jnp.sum(rows[:, :256] * last, 1, keepdims=True),
-                jnp.sum(rows[:, 256:] * last, 1, keepdims=True),
-            ],
-            0,
-        )
+        term = jnp.concatenate([times(rows[:, :256], last), times(rows[:, 256:], last)], 0)
         total = term if total is None else total + term
     return rounded(total)
 
@@ -466,7 +487,8 @@
 
 
 def lane_total(received, lane):
-    return jnp.sum(received[:, lane : lane + 1], 0, keepdims=True)
+    place = lax.broadcasted_iota(jnp.int32, received.shape, 1)
+    return jnp.sum(jnp.where(place == lane, received, 0.0), keepdims=True)
 
 
 def first_turn_kernel(
@@ -646,12 +668,12 @@
     held, partner, other = lax.optimization_barrier((coarse_basis, *packs))
     partner, other = swap(partner, other)
     (first,) = call(
-        restrict_kernel, "restrict", [VMEM] * 2, [row], 10_000_000, [sums, lines]
+        restrict_kernel, "restrict", [VMEM] * 2, [row], 10_000_000, [sums]
     )(rhs, held)
     first = from_everyone(first)
     direction, image, smooth, residual, partner_rows, other_rows, second = call(
         functools.partial(first_turn_kernel, count), "first_turn", [SMEM] + [VMEM] * 8,
-        [whole, whole, smoothed, f32(1, columns), edge, edge, row], 20_000_000,
+        [whole, whole, smoothed, f32(8, columns), edge, edge, row], 20_000_000,
         [extended, sums, stacked, solved, lines],
     )(margin_rows, first, coarse_inverse, partner, other, held, rhs, viscosity, coupling)
     partner_rows, other_rows = swap(partner_rows, other_rows)

time: 47.3 us -> 47.7 us (level)
    pallas_call x1, Pallas kernels: 3.87 us -> 4.41 us  [on_device(): call(functools.partial(first_turn_kernel, count), 'first_turn', [SMEM] +...]
where the time goes in v17:
time: 47.7 us; the launch traced here: 47.4 us
  blocking collectives  32.2 us (68%)
  Pallas kernels  12.2 us (26%)
  starting transfers between devices  2.21 us (5%)
  between operations  0.74 us (2%)
    all_to_all x3, blocking collectives, from_everyone(): lax.all_to_all(rows, 'sub', 0, 0, tiled=True, axis_index_groups=order)  32.2 us
    pallas_call x1, Pallas kernels, on_device(): call(functools.partial(first_turn_kernel, count), 'first_turn', [SMEM] +...  4.41 us
    pallas_call x1, Pallas kernels, on_device(): call(functools.partial(second_turn_kernel, count), 'second_turn', [SMEM]...  2.87 us
    pallas_call x1, Pallas kernels, on_device(): call(pack_kernel, 'pack', [HBM] * 5, [packed, packed], 5000000, [pltpu.VM...  2.52 us
    pallas_call x1, Pallas kernels, on_device(): call(restrict_kernel, 'restrict', [VMEM] * 2, [row], 10000000, [sums])  1.48 us
    ppermute x2, starting transfers between devices, swap(): lax.ppermute(other, 'sub', both(range(1, count - 1, 2)))  1.46 us
  transfers between devices with their start and end apart: 4, of which 0 were waited for; matrix products, arithmetic and copies ran while one was open for 0% of the time, Pallas kernels for 3%

profile of v17, /device:TPU:0, one launch (start us, length us, event | category | flops | bytes accessed | tf_op | source)
XLA Modules:
  0.0 47.4 jit_solution(10721645285583373244)
XLA Ops:
  0.6 0.0 copy-start.1
  0.6 0.0 copy-start.3
  0.7 0.0 copy-start.2
  0.7 0.0 copy-start.4
  0.7 0.0 copy-start
  0.7 0.0 copy-start.5
  0.7 2.5 %pack.1 = (f32[208,512]{1,0:T(8,128)S(1)}, f32[208,512]{1,0:T(8,128)S(1)}) custom-call(f32[2,64,512]{2,1,0:T(8,128)} %rhs_ref.7, f32[64,512]{1,0:T(8,128)} %visc_ref.5, f32[2,64,512]{2,1,0:T(8,128)} %coup_ref.5, f32[48,768]{1,0:T(8,128)} %inverse_ref.5, bf16[48,2,64,512]{3,2,1,0:T(8,128)(2,1)} %held.2), custom_call_target="tpu_custom_call" | custom-call | flops 5000000 | bytes 4000000 | tf_op jit(solution)/shard_map/pack/pallas_call | solution.py:663
  3.2 0.5 %collective-permute-start = (f32[208,512]{1,0:T(8,128)S(1)}, f32[208,512]{1,0:T(8,128)S(1)}, u32[]{:S(2)}, u32[]{:S(2)}) collective-permute-start(f32[208,512]{1,0:T(8,128)S(1)} %get-tuple-element.21), channel_id=1, source_target_pairs={{0,1},{1,0},{2,3},{3,2},{4,5},{5,4},{6,7},{7,6},{8,9},{9,8},{10,11... | collective-permute-start | bytes 1277960 | tf_op jit(solution)/shard_map/ppermute | solution.py:645
  3.7 0.8 %collective-permute-start.1 = (f32[208,512]{1,0:T(8,128)S(1)}, f32[208,512]{1,0:T(8,128)S(1)}, u32[]{:S(2)}, u32[]{:S(2)}) collective-permute-start(f32[208,512]{1,0:T(8,128)S(1)} %get-tuple-element.22), channel_id=1, source_target_pairs={{1,2},{2,1},{3,4},{4,3},{5,6},{6,5},{7,8},{8,7},{9,10},{10,9},{11,... | collective-permute-start | bytes 1277960 | tf_op jit(solution)/shard_map/ppermute | solution.py:646
  4.5 0.0 copy-done.1
  4.6 0.1 copy-done
  4.6 1.5 %restrict.1 = f32[16,128]{1,0:T(8,128)S(1)} custom-call(f32[2,64,512]{2,1,0:T(8,128)S(1)} %copy-done.1, bf16[48,2,64,512]{3,2,1,0:T(8,128)(2,1)S(1)} %copy-done), custom_call_target="tpu_custom_call" | custom-call | flops 10000000 | bytes 4000000 | tf_op jit(solution)/shard_map/restrict/pallas_call | solution.py:670
  6.1 11.8 %all_to_all.33 = f32[16,1,128]{2,1,0:T(1,128)S(1)} all-to-all(f32[16,1,128]{2,1,0:T(1,128)S(1)} %bitcast.19), channel_id=1, replica_groups={{15,14,13,12,11,10,9,8,7,6,5,4,3,2,1,0},{31,30,29,28,27,26,25,24,23,22,..., dimensions={0} | all-to-all | bytes 16384 | tf_op jit(solution)/shard_map/all_to_all | solution.py:638
  17.9 0.0 collective-permute-done.partner_ref
  17.9 0.0 collective-permute-done.1.other_ref
  17.9 0.0 copy-done.3
  18.0 0.0 copy-done.2
  18.0 0.0 copy-done.4
  18.0 0.0 copy-done.5
  18.0 4.4 %first_turn.1 = (f32[2,64,512]{2,1,0:T(8,128)S(1)}, f32[2,64,512]{2,1,0:T(8,128)S(1)}, f32[2,80,512]{2,1,0:T(8,128)S(1)}, f32[8,768]{1,0:T(8,128)S(1)}, f32[8,51...) custom-call(s32[16]{0:T(128)S(1)} %copy-done.5, f32[16,128]{1,0:T(8,128)S(1)} %bitcast.13, ...), custom_call_target="tpu_custom_call" | custom-call | flops 20000000 | bytes 4000000 | tf_op jit(solution)/shard_map/first_turn/pallas_call | solution.py:674
  22.4 0.2 collective-permute-start.2
  22.6 0.7 %collective-permute-start.3 = (f32[8,512]{1,0:T(8,128)S(1)}, f32[8,512]{1,0:T(8,128)S(1)}, u32[]{:S(2)}, u32[]{:S(2)}) collective-permute-start(f32[8,512]{1,0:T(8,128)S(1)} %get-tuple-element.26), channel_id=1, source_target_pairs={{1,2},{2,1},{3,4},{4,3},{5,6},{6,5},{7,8},{8,7},{9,10},{10,9},{11,... | collective-permute-start | bytes 49160 | tf_op jit(solution)/shard_map/ppermute | solution.py:646
  23.3 12.0 %all_to_all.34 = f32[16,1,128]{2,1,0:T(1,128)S(1)} all-to-all(f32[16,1,128]{2,1,0:T(1,128)S(1)} %bitcast.20), channel_id=1, replica_groups={{15,14,13,12,11,10,9,8,7,6,5,4,3,2,1,0},{31,30,29,28,27,26,25,24,23,22,..., dimensions={0} | all-to-all | bytes 16384 | tf_op jit(solution)/shard_map/all_to_all | solution.py:638
  35.3 0.0 collective-permute-done.2.partner_rows_ref
  35.3 0.0 collective-permute-done.3.other_rows_ref
  35.3 2.9 %second_turn.1 = (f32[2,64,512]{2,1,0:T(8,128)S(1)}, f32[16,128]{1,0:T(8,128)S(1)}) custom-call(s32[16]{0:T(128)S(1)} %copy-done.5, f32[16,128]{1,0:T(8,128)S(1)} %bitcast.14, f32[16,128]{1,0:T(8,128)S(1)} %bitcast.16, f32[8,768]{1,0:T(8,128)S(1)} %get-tuple-element.24.residual_ref, f32[48,768]{1,0:T(8,128)S(1)} %copy-done.3, ...), custom_call_target="tpu_custom_call" | custom-call | flops 20000000 | bytes 4000000 | tf_op jit(solution)/shard_map/second_turn/pallas_call | solution.py:681
  38.2 8.4 %all_to_all.35 = f32[16,1,128]{2,1,0:T(1,128)S(1)} all-to-all(f32[16,1,128]{2,1,0:T(1,128)S(1)} %bitcast.21), channel_id=1, replica_groups={{15,14,13,12,11,10,9,8,7,6,5,4,3,2,1,0},{31,30,29,28,27,26,25,24,23,22,..., dimensions={0} | all-to-all | bytes 16384 | tf_op jit(solution)/shard_map/all_to_all | solution.py:638
  46.5 0.9 %finish.1 = (f32[2,64,512]{2,1,0:T(8,128)}, f32[2,3]{1,0:T(2,128)}) custom-call(f32[16,128]{1,0:T(8,128)S(1)} %bitcast.15, f32[16,128]{1,0:T(8,128)S(1)} %bitcast.17, f32[16,128]{1,0:T(8,128)S(1)} %bitcast.18, f32[2,64,512]{2,1,0:T(8,128)S(1)} %get-tuple-element.30.first_direction_ref, f32[2,64,512]{2,1,0:T(8,128)S(1)} %get-tuple-element.31.second_direction_ref), custom_call_target="tpu_custom_call" | custom-call | flops 1000000 | bytes 4000000 | tf_op jit(solution)/shard_map/finish/pallas_call | solution.py:689
Async XLA Ops:
  0.6 3.9 %copy-start.1 = (f32[2,64,512]{2,1,0:T(8,128)S(1)}, f32[2,64,512]{2,1,0:T(8,128)}, u32[]{:S(2)}) copy-start(f32[2,64,512]{2,1,0:T(8,128)} %rhs_ref.7) | copy-start | bytes 786436
  0.6 17.3 %copy-start.3 = (f32[48,768]{1,0:T(8,128)S(1)}, f32[48,768]{1,0:T(8,128)}, u32[]{:S(2)}) copy-start(f32[48,768]{1,0:T(8,128)} %inverse_ref.5) | copy-start | bytes 442372
  0.7 17.3 %copy-start.2 = (f32[2,64,512]{2,1,0:T(8,128)S(1)}, f32[2,64,512]{2,1,0:T(8,128)}, u32[]{:S(2)}) copy-start(f32[2,64,512]{2,1,0:T(8,128)} %coup_ref.5) | copy-start | bytes 786436
  0.7 17.3 %copy-start.4 = (f32[64,512]{1,0:T(8,128)S(1)}, f32[64,512]{1,0:T(8,128)}, u32[]{:S(2)}) copy-start(f32[64,512]{1,0:T(8,128)} %visc_ref.5) | copy-start | bytes 393220
  0.7 4.0 %copy-start = (bf16[48,2,64,512]{3,2,1,0:T(8,128)(2,1)S(1)}, bf16[48,2,64,512]{3,2,1,0:T(8,128)(2,1)}, u32[]{:S(2)}) copy-start(bf16[48,2,64,512]{3,2,1,0:T(8,128)(2,1)} %held.2) | copy-start | bytes 18874372
  0.7 17.3 %copy-start.5 = (s32[16]{0:T(128)S(1)}, s32[16]{0:T(128)}, u32[]{:S(2)}) copy-start(s32[16]{0:T(128)} %margin_ref.3) | copy-start | bytes 196
  3.2 14.7 %collective-permute-start = (f32[208,512]{1,0:T(8,128)S(1)}, f32[208,512]{1,0:T(8,128)S(1)}, u32[]{:S(2)}, u32[]{:S(2)}) collective-permute-start(f32[208,512]{1,0:T(8,128)S(1)} %get-tuple-element.21), channel_id=1, source_target_pairs={{0,1},{1,0},{2,3},{3,2},{4,5},{5,4},{6,7},{7,6},{8,9},{9,8},{10,11... | collective-permute-start | bytes 1277960 | tf_op jit(solution)/shard_map/ppermute | solution.py:645
  3.7 14.2 %collective-permute-start.1 = (f32[208,512]{1,0:T(8,128)S(1)}, f32[208,512]{1,0:T(8,128)S(1)}, u32[]{:S(2)}, u32[]{:S(2)}) collective-permute-start(f32[208,512]{1,0:T(8,128)S(1)} %get-tuple-element.22), channel_id=1, source_target_pairs={{1,2},{2,1},{3,4},{4,3},{5,6},{6,5},{7,8},{8,7},{9,10},{10,9},{11,... | collective-permute-start | bytes 1277960 | tf_op jit(solution)/shard_map/ppermute | solution.py:646
  22.4 12.9 %collective-permute-start.2 = (f32[8,512]{1,0:T(8,128)S(1)}, f32[8,512]{1,0:T(8,128)S(1)}, u32[]{:S(2)}, u32[]{:S(2)}) collective-permute-start(f32[8,512]{1,0:T(8,128)S(1)} %get-tuple-element.25), channel_id=1, source_target_pairs={{0,1},{1,0},{2,3},{3,2},{4,5},{5,4},{6,7},{7,6},{8,9},{9,8},{10,11... | collective-permute-start | bytes 49160 | tf_op jit(solution)/shard_map/ppermute | solution.py:645
  22.6 12.7 %collective-permute-start.3 = (f32[8,512]{1,0:T(8,128)S(1)}, f32[8,512]{1,0:T(8,128)S(1)}, u32[]{:S(2)}, u32[]{:S(2)}) collective-permute-start(f32[8,512]{1,0:T(8,128)S(1)} %get-tuple-element.26), channel_id=1, source_target_pairs={{1,2},{2,1},{3,4},{4,3},{5,6},{6,5},{7,8},{8,7},{9,10},{10,9},{11,... | collective-permute-start | bytes 49160 | tf_op jit(solution)/shard_map/ppermute | solution.py:646

commit v18 on v15

--- a/solution.py
+++ b/solution.py
@@ -90,6 +90,20 @@
     for n, tile in enumerate(tiles):
         total = jnp.where(row == n, sublane_sum(tile), total)
     return total
+
+
+def restrict_piece(i, held, field, sums):
+    totals = [None] * PIECE
+    for a in range(2):
+        for r in range(0, ROWS, CHUNK):
+            for c in range(0, CELLS, LANES):
+                rows, cells = slice(r, r + CHUNK), slice(c, c + LANES)
+                tile = field[a, rows, cells]
+                for n in range(PIECE):
+                    term = held[PIECE * i + n, a, rows, cells].astype(jnp.float32) * tile
+                    totals[n] = term if totals[n] is None else totals[n] + term
+    tiles = [total[:8] + total[8:] for total in totals]
+    sums[pl.ds(pl.multiple_of(PIECE * i, PIECE), PIECE), :] = in_rows(tiles)
 
 
 MATRIX_GROUPS = tuple((1, r) for r in range(CHUNK, ROWS, CHUNK))
@@ -237,7 +251,7 @@
         copy.wait()
 
 
-def restrict_kernel(rhs_ref, held, sums_ref, sums, lines):
+def restrict_kernel(rhs_ref, held, sums_ref, sums):
     sums[...] = jnp.zeros_like(sums)
     squares = jnp.zeros((TILE, CELLS), jnp.float32)
     for a in range(2):
@@ -246,7 +260,11 @@
             squares = squares + tile * tile
     sums[VECTORS : VECTORS + 8] = in_rows([fold(squares)])
 
-    restrict(held, rhs_ref, sums, lines)
+    def body(i, carry):
+        restrict_piece(i, held, rhs_ref, sums)
+        return carry
+
+    lax.fori_loop(0, VECTORS // PIECE, body, 0)
     send_sums(sums, sums_ref)
 
 
@@ -266,6 +284,7 @@
 def solve(count, margin_ref, visc_ref, coup_ref, field, low, high, out_ref, stacked, solved, steps):
     waiting, done = list(steps), 0
     every = (SWEEPS - 1) * (STACKED // TILE) // len(waiting)
+    assert every > 0
     rank = lax.axis_index("sub")
     lower = jnp.where(rank > 0, margin_ref[jnp.maximum(rank - 1, 0)], 0)
     upper = jnp.where(rank < count - 1, margin_ref[rank], 0)
@@ -424,20 +443,38 @@
     return jnp.where(place == row, line, 0.0).astype(jnp.bfloat16)
 
 
-def prolonging(residual, inverse_ref, held, extended):
-    matrix = spread(lift(inverse_ref, residual))
-
-    def step(a, r):
-        rows = held[:, a, r : r + CHUNK, :].reshape(CHUNK * VECTORS, CELLS)
-        extended[a, HALO + r : HALO + r + CHUNK] = jnp.dot(
-            matrix, rows, preferred_element_type=jnp.float32
+class Coarse:
+    def __init__(self, begin, inverse_ref, low, high, held, extended):
+        self.inverse, self.sides, self.held, self.extended = inverse_ref, (low, high), held, extended
+        self.lifted, self.edges = [None] * 2, [None] * 2
+        self.steps = begin(self) + [self.lift_own, self.make_matrix]
+        for a in range(2):
+            for r in range(0, ROWS, CHUNK):
+                self.steps.append(functools.partial(self.prolong, a, r))
+        for n in range(2):
+            self.steps.insert(len(self.steps) - 6, functools.partial(self.lift_side, n))
+            self.steps.append(functools.partial(self.edge, n))
+
+    def lift_own(self):
+        self.own = lift(self.inverse, self.residual)
+
+    def make_matrix(self):
+        self.matrix = spread(self.own)
+
+    def prolong(self, a, r):
+        rows = self.held[:, a, r : r + CHUNK, :].reshape(CHUNK * VECTORS, CELLS)
+        self.extended[a, HALO + r : HALO + r + CHUNK] = jnp.dot(
+            self.matrix, rows, preferred_element_type=jnp.float32
         )
 
-    return [functools.partial(step, a, r) for a in range(2) for r in range(0, ROWS, CHUNK)]
-
-
-def apply_operator(residual, low, high, smooth, extended, visc_ref, coup_ref, direction_ref):
-    edges = [edge_values(side, lift_packed(side, residual)) for side in (low, high)]
+    def lift_side(self, n):
+        self.lifted[n] = lift_packed(self.sides[n], self.residual)
+
+    def edge(self, n):
+        self.edges[n] = edge_values(self.sides[n], self.lifted[n])
+
+
+def apply_operator(edges, smooth, extended, visc_ref, coup_ref, direction_ref):
     place = lax.broadcasted_iota(jnp.int32, (TILE, CELLS), 0)
     tiles = ROWS // TILE
 
@@ -466,7 +503,8 @@
 
 
 def lane_total(received, lane):
-    return jnp.sum(received[:, lane : lane + 1], 0, keepdims=True)
+    place = lax.broadcasted_iota(jnp.int32, received.shape, 1)
+    return jnp.sum(jnp.where(place == lane, received, 0.0), keepdims=True)
 
 
 def first_turn_kernel(
@@ -475,12 +513,19 @@
     direction_ref, image_ref, smooth_ref, residual_ref, partner_rows_ref, other_rows_ref, next_ref,
     extended, sums, stacked, solved, lines,
 ):
-    received = sums_ref[...]
-    over_beta = 1.0 / jnp.sqrt(lane_total(received, VECTORS))
-    residual = line_up(received) * over_beta
-    residual_ref[...] = residual
-    steps = prolonging(residual, inverse_ref, held, extended)
     low, high = neighbours_of(partner_ref, other_ref)
+
+    def begin(coarse):
+        def scale():
+            coarse.over_beta = 1.0 / jnp.sqrt(lane_total(sums_ref[...], VECTORS))
+
+        def line():
+            coarse.residual = line_up(sums_ref[...]) * coarse.over_beta
+            residual_ref[...] = coarse.residual
+
+        return [scale, line]
+
+    coarse = Coarse(begin, inverse_ref, low, high, held, extended)
 
     def field(a, t):
         at = HALO * (3 + a)
@@ -490,11 +535,11 @@
 
     solve(
         count, margin_ref, visc_ref, coup_ref, field, low, high, smooth_ref, stacked, solved,
-        steps,
-    )
-    smooth = lambda a, t: smooth_ref[a, tile_rows(t)] * over_beta
+        coarse.steps,
+    )
+    smooth = lambda a, t: smooth_ref[a, tile_rows(t)] * coarse.over_beta
     images = apply_operator(
-        residual, low, high, smooth, extended, visc_ref, coup_ref, direction_ref
+        coarse.edges, smooth, extended, visc_ref, coup_ref, direction_ref
     )
     odd = lax.axis_index("sub") % 2 == 1
     products, squares = [jnp.zeros((TILE, CELLS), jnp.float32)] * 2
@@ -532,13 +577,20 @@
     direction_ref, next_ref,
     image_smooth, extended, sums, stacked, solved,
 ):
-    first, second = first_ref[...], second_ref[...]
-    beta, h_00, h_10 = first_column(first, second)
-    ratio = h_00 / beta
-    over = 1.0 / h_10
-    residual = (line_up(second) - h_00 * residual_ref[...]) * over
-    steps = prolonging(residual, inverse_ref, held, extended)
     low, high = neighbours_of(partner_ref, other_ref)
+
+    def begin(coarse):
+        def scale():
+            beta, h_00, h_10 = first_column(first_ref[...], second_ref[...])
+            coarse.h_00, coarse.ratio, coarse.over = h_00, h_00 / beta, 1.0 / h_10
+
+        def line():
+            lined = line_up(second_ref[...])
+            coarse.residual = (lined - coarse.h_00 * residual_ref[...]) * coarse.over
+
+        return [scale, line]
+
+    coarse = Coarse(begin, inverse_ref, low, high, held, extended)
     low_rows, high_rows = neighbours_of(partner_rows_ref, other_rows_ref)
 
     def field(a, t):
@@ -549,15 +601,15 @@
 
     solve(
         count, margin_ref, visc_ref, coup_ref, field, low, high, image_smooth, stacked, solved,
-        steps,
+        coarse.steps,
     )
 
     def smooth(a, t):
         rows = tile_rows(t)
-        return (image_smooth[a, rows] - ratio * smooth_ref[a, rows]) * over
+        return (image_smooth[a, rows] - coarse.ratio * smooth_ref[a, rows]) * coarse.over
 
     images = apply_operator(
-        residual, low, high, smooth, extended, visc_ref, coup_ref, direction_ref
+        coarse.edges, smooth, extended, visc_ref, coup_ref, direction_ref
     )
     totals = [jnp.zeros((TILE, CELLS), jnp.float32)] * 3
     for t, a, image in images:
@@ -646,7 +698,7 @@
     held, partner, other = lax.optimization_barrier((coarse_basis, *packs))
     partner, other = swap(partner, other)
     (first,) = call(
-        restrict_kernel, "restrict", [VMEM] * 2, [row], 10_000_000, [sums, lines]
+        restrict_kernel, "restrict", [VMEM] * 2, [row], 10_000_000, [sums]
     )(rhs, held)
     first = from_everyone(first)
     direction, image, smooth, residual, partner_rows, other_rows, second = call(

time: 47.3 us -> 46.9 us (level)
  Pallas kernels: 11.8 us -> 11.3 us
where the time goes in v18:
time: 46.9 us; the launch traced here: 46.6 us
  blocking collectives  32.2 us (69%)
  Pallas kernels  11.3 us (24%)
  starting transfers between devices  2.21 us (5%)
  between operations  0.74 us (2%)
    all_to_all x3, blocking collectives, from_everyone(): lax.all_to_all(rows, 'sub', 0, 0, tiled=True, axis_index_groups=order)  32.2 us
    pallas_call x1, Pallas kernels, on_device(): call(functools.partial(first_turn_kernel, count), 'first_turn', [SMEM] +...  3.9 us
    pallas_call x1, Pallas kernels, on_device(): call(functools.partial(second_turn_kernel, count), 'second_turn', [SMEM]...  2.58 us
    pallas_call x1, Pallas kernels, on_device(): call(pack_kernel, 'pack', [HBM] * 5, [packed, packed], 5000000, [pltpu.VM...  2.52 us
    ppermute x2, starting transfers between devices, swap(): lax.ppermute(other, 'sub', both(range(1, count - 1, 2)))  1.46 us
    pallas_call x1, Pallas kernels, on_device(): call(restrict_kernel, 'restrict', [VMEM] * 2, [row], 10000000, [sums])  1.44 us
  transfers between devices with their start and end apart: 4, of which 0 were waited for; matrix products, arithmetic and copies ran while one was open for 0% of the time, Pallas kernels for 3%

profile of v18, /device:TPU:0, one launch (start us, length us, event | category | flops | bytes accessed | tf_op | source)
XLA Modules:
  0.0 46.6 jit_solution(3106420258921021264)
XLA Ops:
  0.6 0.0 copy-start.1
  0.6 0.0 copy-start.3
  0.7 0.0 copy-start.2
  0.7 0.0 copy-start.4
  0.7 0.0 copy-start
  0.7 0.0 copy-start.5
  0.7 2.5 %pack.1 = (f32[208,512]{1,0:T(8,128)S(1)}, f32[208,512]{1,0:T(8,128)S(1)}) custom-call(f32[2,64,512]{2,1,0:T(8,128)} %rhs_ref.7, f32[64,512]{1,0:T(8,128)} %visc_ref.5, f32[2,64,512]{2,1,0:T(8,128)} %coup_ref.5, f32[48,768]{1,0:T(8,128)} %inverse_ref.5, bf16[48,2,64,512]{3,2,1,0:T(8,128)(2,1)} %held.2), custom_call_target="tpu_custom_call" | custom-call | flops 5000000 | bytes 4000000 | tf_op jit(solution)/shard_map/pack/pallas_call | solution.py:693
  3.2 0.5 %collective-permute-start = (f32[208,512]{1,0:T(8,128)S(1)}, f32[208,512]{1,0:T(8,128)S(1)}, u32[]{:S(2)}, u32[]{:S(2)}) collective-permute-start(f32[208,512]{1,0:T(8,128)S(1)} %get-tuple-element.21), channel_id=1, source_target_pairs={{0,1},{1,0},{2,3},{3,2},{4,5},{5,4},{6,7},{7,6},{8,9},{9,8},{10,11... | collective-permute-start | bytes 1277960 | tf_op jit(solution)/shard_map/ppermute | solution.py:675
  3.7 0.8 %collective-permute-start.1 = (f32[208,512]{1,0:T(8,128)S(1)}, f32[208,512]{1,0:T(8,128)S(1)}, u32[]{:S(2)}, u32[]{:S(2)}) collective-permute-start(f32[208,512]{1,0:T(8,128)S(1)} %get-tuple-element.22), channel_id=1, source_target_pairs={{1,2},{2,1},{3,4},{4,3},{5,6},{6,5},{7,8},{8,7},{9,10},{10,9},{11,... | collective-permute-start | bytes 1277960 | tf_op jit(solution)/shard_map/ppermute | solution.py:676
  4.5 0.0 copy-done.1
  4.6 0.1 copy-done
  4.6 1.4 %restrict.1 = f32[16,128]{1,0:T(8,128)S(1)} custom-call(f32[2,64,512]{2,1,0:T(8,128)S(1)} %copy-done.1, bf16[48,2,64,512]{3,2,1,0:T(8,128)(2,1)S(1)} %copy-done), custom_call_target="tpu_custom_call" | custom-call | flops 10000000 | bytes 4000000 | tf_op jit(solution)/shard_map/restrict/pallas_call | solution.py:700
  6.1 11.9 %all_to_all.33 = f32[16,1,128]{2,1,0:T(1,128)S(1)} all-to-all(f32[16,1,128]{2,1,0:T(1,128)S(1)} %bitcast.19), channel_id=1, replica_groups={{15,14,13,12,11,10,9,8,7,6,5,4,3,2,1,0},{31,30,29,28,27,26,25,24,23,22,..., dimensions={0} | all-to-all | bytes 16384 | tf_op jit(solution)/shard_map/all_to_all | solution.py:668
  17.9 0.0 collective-permute-done.partner_ref
  17.9 0.0 collective-permute-done.1.other_ref
  17.9 0.0 copy-done.3
  18.0 0.0 copy-done.2
  18.0 0.0 copy-done.4
  18.0 0.0 copy-done.5
  18.0 3.9 %first_turn.1 = (f32[2,64,512]{2,1,0:T(8,128)S(1)}, f32[2,64,512]{2,1,0:T(8,128)S(1)}, f32[2,80,512]{2,1,0:T(8,128)S(1)}, f32[1,768]{1,0:T(1,128)S(1)}, f32[8,51...) custom-call(s32[16]{0:T(128)S(1)} %copy-done.5, f32[16,128]{1,0:T(8,128)S(1)} %bitcast.13, ...), custom_call_target="tpu_custom_call" | custom-call | flops 20000000 | bytes 4000000 | tf_op jit(solution)/shard_map/first_turn/pallas_call | solution.py:704
  21.9 0.2 collective-permute-start.2
  22.1 0.7 %collective-permute-start.3 = (f32[8,512]{1,0:T(8,128)S(1)}, f32[8,512]{1,0:T(8,128)S(1)}, u32[]{:S(2)}, u32[]{:S(2)}) collective-permute-start(f32[8,512]{1,0:T(8,128)S(1)} %get-tuple-element.26), channel_id=1, source_target_pairs={{1,2},{2,1},{3,4},{4,3},{5,6},{6,5},{7,8},{8,7},{9,10},{10,9},{11,... | collective-permute-start | bytes 49160 | tf_op jit(solution)/shard_map/ppermute | solution.py:676
  22.8 12.0 %all_to_all.34 = f32[16,1,128]{2,1,0:T(1,128)S(1)} all-to-all(f32[16,1,128]{2,1,0:T(1,128)S(1)} %bitcast.20), channel_id=1, replica_groups={{15,14,13,12,11,10,9,8,7,6,5,4,3,2,1,0},{31,30,29,28,27,26,25,24,23,22,..., dimensions={0} | all-to-all | bytes 16384 | tf_op jit(solution)/shard_map/all_to_all | solution.py:668
  34.8 0.0 collective-permute-done.2.partner_rows_ref
  34.8 0.0 collective-permute-done.3.other_rows_ref
  34.8 2.6 %second_turn.1 = (f32[2,64,512]{2,1,0:T(8,128)S(1)}, f32[16,128]{1,0:T(8,128)S(1)}) custom-call(s32[16]{0:T(128)S(1)} %copy-done.5, f32[16,128]{1,0:T(8,128)S(1)} %bitcast.14, f32[16,128]{1,0:T(8,128)S(1)} %bitcast.16, f32[1,768]{1,0:T(1,128)S(1)} %get-tuple-element.24.residual_ref, f32[48,768]{1,0:T(8,128)S(1)} %copy-done.3, ...), custom_call_target="tpu_custom_call" | custom-call | flops 20000000 | bytes 4000000 | tf_op jit(solution)/shard_map/second_turn/pallas_call | solution.py:711
  37.4 8.4 %all_to_all.35 = f32[16,1,128]{2,1,0:T(1,128)S(1)} all-to-all(f32[16,1,128]{2,1,0:T(1,128)S(1)} %bitcast.21), channel_id=1, replica_groups={{15,14,13,12,11,10,9,8,7,6,5,4,3,2,1,0},{31,30,29,28,27,26,25,24,23,22,..., dimensions={0} | all-to-all | bytes 16384 | tf_op jit(solution)/shard_map/all_to_all | solution.py:668
  45.7 0.9 %finish.1 = (f32[2,64,512]{2,1,0:T(8,128)}, f32[2,3]{1,0:T(2,128)}) custom-call(f32[16,128]{1,0:T(8,128)S(1)} %bitcast.15, f32[16,128]{1,0:T(8,128)S(1)} %bitcast.17, f32[16,128]{1,0:T(8,128)S(1)} %bitcast.18, f32[2,64,512]{2,1,0:T(8,128)S(1)} %get-tuple-element.30.first_direction_ref, f32[2,64,512]{2,1,0:T(8,128)S(1)} %get-tuple-element.31.second_direction_ref), custom_call_target="tpu_custom_call" | custom-call | flops 1000000 | bytes 4000000 | tf_op jit(solution)/shard_map/finish/pallas_call | solution.py:719
Async XLA Ops:
  0.6 3.9 %copy-start.1 = (f32[2,64,512]{2,1,0:T(8,128)S(1)}, f32[2,64,512]{2,1,0:T(8,128)}, u32[]{:S(2)}) copy-start(f32[2,64,512]{2,1,0:T(8,128)} %rhs_ref.7) | copy-start | bytes 786436
  0.6 17.3 %copy-start.3 = (f32[48,768]{1,0:T(8,128)S(1)}, f32[48,768]{1,0:T(8,128)}, u32[]{:S(2)}) copy-start(f32[48,768]{1,0:T(8,128)} %inverse_ref.5) | copy-start | bytes 442372
  0.7 17.3 %copy-start.2 = (f32[2,64,512]{2,1,0:T(8,128)S(1)}, f32[2,64,512]{2,1,0:T(8,128)}, u32[]{:S(2)}) copy-start(f32[2,64,512]{2,1,0:T(8,128)} %coup_ref.5) | copy-start | bytes 786436
  0.7 17.3 %copy-start.4 = (f32[64,512]{1,0:T(8,128)S(1)}, f32[64,512]{1,0:T(8,128)}, u32[]{:S(2)}) copy-start(f32[64,512]{1,0:T(8,128)} %visc_ref.5) | copy-start | bytes 393220
  0.7 4.0 %copy-start = (bf16[48,2,64,512]{3,2,1,0:T(8,128)(2,1)S(1)}, bf16[48,2,64,512]{3,2,1,0:T(8,128)(2,1)}, u32[]{:S(2)}) copy-start(bf16[48,2,64,512]{3,2,1,0:T(8,128)(2,1)} %held.2) | copy-start | bytes 18874372
  0.7 17.3 %copy-start.5 = (s32[16]{0:T(128)S(1)}, s32[16]{0:T(128)}, u32[]{:S(2)}) copy-start(s32[16]{0:T(128)} %margin_ref.3) | copy-start | bytes 196
  3.2 14.7 %collective-permute-start = (f32[208,512]{1,0:T(8,128)S(1)}, f32[208,512]{1,0:T(8,128)S(1)}, u32[]{:S(2)}, u32[]{:S(2)}) collective-permute-start(f32[208,512]{1,0:T(8,128)S(1)} %get-tuple-element.21), channel_id=1, source_target_pairs={{0,1},{1,0},{2,3},{3,2},{4,5},{5,4},{6,7},{7,6},{8,9},{9,8},{10,11... | collective-permute-start | bytes 1277960 | tf_op jit(solution)/shard_map/ppermute | solution.py:675
  3.7 14.2 %collective-permute-start.1 = (f32[208,512]{1,0:T(8,128)S(1)}, f32[208,512]{1,0:T(8,128)S(1)}, u32[]{:S(2)}, u32[]{:S(2)}) collective-permute-start(f32[208,512]{1,0:T(8,128)S(1)} %get-tuple-element.22), channel_id=1, source_target_pairs={{1,2},{2,1},{3,4},{4,3},{5,6},{6,5},{7,8},{8,7},{9,10},{10,9},{11,... | collective-permute-start | bytes 1277960 | tf_op jit(solution)/shard_map/ppermute | solution.py:676
  21.9 12.9 %collective-permute-start.2 = (f32[8,512]{1,0:T(8,128)S(1)}, f32[8,512]{1,0:T(8,128)S(1)}, u32[]{:S(2)}, u32[]{:S(2)}) collective-permute-start(f32[8,512]{1,0:T(8,128)S(1)} %get-tuple-element.25), channel_id=1, source_target_pairs={{0,1},{1,0},{2,3},{3,2},{4,5},{5,4},{6,7},{7,6},{8,9},{9,8},{10,11... | collective-permute-start | bytes 49160 | tf_op jit(solution)/shard_map/ppermute | solution.py:675
  22.1 12.7 %collective-permute-start.3 = (f32[8,512]{1,0:T(8,128)S(1)}, f32[8,512]{1,0:T(8,128)S(1)}, u32[]{:S(2)}, u32[]{:S(2)}) collective-permute-start(f32[8,512]{1,0:T(8,128)S(1)} %get-tuple-element.26), channel_id=1, source_target_pairs={{1,2},{2,1},{3,4},{4,3},{5,6},{6,5},{7,8},{8,7},{9,10},{10,9},{11,... | collective-permute-start | bytes 49160 | tf_op jit(solution)/shard_map/ppermute | solution.py:676

commit v19 on v18

--- a/solution.py
+++ b/solution.py
@@ -21,7 +21,9 @@
 PIECE = 8
 LANES = 128
 SLOTS = 64
-EDGE_AT = 5 * HALO
+COUPLING_AT = HALO
+RHS_AT = 2 * HALO
+EDGE_AT = 3 * HALO
 INVERSE_AT = 2 * VECTORS
 SWEEPS = 4
 RELAX = 0.7
@@ -170,12 +172,9 @@
     out_ref[...] = jnp.broadcast_to(wide, out_ref.shape)
 
 
-def pack_copies(out_ref, first_row, rhs_ref, visc_ref, coup_ref, inverse_ref, sems, at_sem):
+def pack_copies(out_ref, first_row, visc_ref, inverse_ref, sems, at_sem):
     rows = pl.ds(pl.multiple_of(first_row, HALO), HALO)
     moves = [(visc_ref.at[rows, :], 0, HALO, None)]
-    for a in range(2):
-        moves.append((coup_ref.at[a, rows, :], HALO * (1 + a), HALO, None))
-        moves.append((rhs_ref.at[a, rows, :], HALO * (3 + a), HALO, None))
     columns = inverse_ref.shape[1]
     at = EDGE_AT + INVERSE_AT
     for c in range(0, columns - 511, 512):
@@ -195,13 +194,25 @@
 
 
 def pack_count(columns):
-    return 5 + columns // 512 + 2 * (columns % 512 // 256)
+    return 1 + columns // 512 + 2 * (columns % 512 // 256)
+
+
+def outer_rows(head, tail):
+    half = lax.broadcasted_iota(jnp.int32, (TILE, CELLS), 0) < TILE // 2
+    return (
+        jnp.where(half, head[0], pltpu.roll(head[1], TILE // 2, 0)),
+        jnp.where(half, pltpu.roll(tail[1], TILE // 2, 0), tail[0]),
+    )
+
+
+def component(rows, a):
+    return pltpu.roll(rows, TILE // 2, 0) if a else rows
 
 
 def pack_kernel(
     rhs_ref, visc_ref, coup_ref, inverse_ref, basis_ref,
     partner_ref, other_ref,
-    groups, group_sems, pack_sems,
+    groups, staged, group_sems, stage_sems, pack_sems,
 ):
     odd = lax.axis_index("sub") % 2
     sides = ((partner_ref, 1 - odd), (other_ref, odd))
@@ -219,11 +230,25 @@
                 )
     for n, (out_ref, up) in enumerate(sides):
         packs += pack_copies(
-            out_ref, up * (ROWS - HALO), rhs_ref, visc_ref, coup_ref, inverse_ref, pack_sems,
+            out_ref, up * (ROWS - HALO), visc_ref, inverse_ref, pack_sems,
             n * pack_count(inverse_ref.shape[1]),
         )
-    for copy in group_copies + packs:
+    stages = []
+    for m, ref in enumerate((coup_ref, rhs_ref)):
+        for n, first_row in enumerate((0, ROWS - HALO)):
+            stages.append(
+                pltpu.make_async_copy(
+                    ref.at[:, pl.ds(first_row, HALO), :], staged.at[m, n], stage_sems.at[2 * m + n]
+                )
+            )
+    for copy in stages + group_copies + packs:
         copy.start()
+    for copy in stages:
+        copy.wait()
+    for m, at in enumerate((COUPLING_AT, RHS_AT)):
+        head, tail = outer_rows(staged[m, 0], staged[m, 1])
+        partner_ref[at : at + HALO] = jnp.where(odd == 1, head, tail)
+        other_ref[at : at + HALO] = jnp.where(odd == 1, tail, head)
 
     def take(out_ref, group, first, row):
         for k in range(first, first + GROUP, TILE):
@@ -281,7 +306,7 @@
     return Neighbour(partner_ref, other_ref), Neighbour(other_ref, partner_ref)
 
 
-def solve(count, margin_ref, visc_ref, coup_ref, field, low, high, out_ref, stacked, solved, steps):
+def solve(count, margin_ref, factors_ref, make, field, out_ref, first_ref, solved, steps):
     waiting, done = list(steps), 0
     every = (SWEEPS - 1) * (STACKED // TILE) // len(waiting)
     assert every > 0
@@ -330,32 +355,26 @@
             weight = jnp.where(place < ROWS + upper, rising(ROWS - upper_f, high_scale), 1.0)
         return wide(weight)
 
-    def extended(ref, at, e):
-        if e == 0:
-            return low[at : at + HALO]
-        if e == last:
-            return high[at : at + HALO]
-        return ref[tile_rows(e - 1)]
-
     for e in range(last + 1):
-        viscosity = extended(visc_ref, 0, e)
         for a in range(2):
-            coupling = extended(coup_ref.at[a], HALO * (1 + a), e)
-            scale = RELAX / (10.0 * viscosity + jnp.abs(coupling) + 0.05)
-            parts = (scale * field(a, e - 1), scale * viscosity, scale * coupling)
+            parts = make(a, e) if make else None
+            value = field(a, e - 1)
             for n, (first, begin, size) in enumerate(segments):
                 if not begin <= e < begin + size:
                     continue
                 rows = tile_rows(first + e - begin)
-                always = n == 0 and 0 < e < last
-                for m, part in enumerate(parts):
-                    stacked[3 * a + m, rows] = part if always else live_of(n, e) * part
+                if make:
+                    always = n == 0 and 0 < e < last
+                    live = None if always else live_of(n, e)
+                    for m, part in enumerate(parts):
+                        factors_ref[3 * a + m, rows] = part if always else live * part
+                first_ref[a, rows] = factors_ref[3 * a, rows] * value
 
     for sweep in range(1, SWEEPS):
         for n, (first, begin, size) in enumerate(segments):
             end = first + size - 1
             if sweep == 1:
-                reads = [lambda t, a=a: stacked[3 * a, tile_rows(t)] for a in range(2)]
+                reads = [lambda t, a=a: first_ref[a, tile_rows(t)] for a in range(2)]
             else:
                 bank = 2 * (sweep % 2)
                 reads = [lambda t, a=a: solved[bank + a, tile_rows(t)] for a in range(2)]
@@ -367,9 +386,9 @@
                 done += 1
                 for a in range(2):
                     value = (
-                        ((1.0 - RELAX) * fields[a].at(t) + stacked[3 * a, rows])
-                        + stacked[3 * a + 1, rows] * neighbours(fields[a], t, a)
-                        - stacked[3 * a + 2, rows] * fields[1 - a].at(t)
+                        ((1.0 - RELAX) * fields[a].at(t) + first_ref[a, rows])
+                        + factors_ref[3 * a + 1, rows] * neighbours(fields[a], t, a)
+                        - factors_ref[3 * a + 2, rows] * fields[1 - a].at(t)
                     )
                     e = t - first + begin
                     if sweep < SWEEPS - 1:
@@ -510,8 +529,9 @@
 def first_turn_kernel(
     count, margin_ref, sums_ref, inverse_ref, partner_ref, other_ref, held, rhs_ref, visc_ref,
     coup_ref,
-    direction_ref, image_ref, smooth_ref, residual_ref, partner_rows_ref, other_rows_ref, next_ref,
-    extended, sums, stacked, solved, lines,
+    direction_ref, image_ref, smooth_ref, residual_ref, factors_ref, partner_rows_ref, other_rows_ref,
+    next_ref,
+    extended, sums, first_ref, solved, lines,
 ):
     low, high = neighbours_of(partner_ref, other_ref)
 
@@ -528,14 +548,22 @@
     coarse = Coarse(begin, inverse_ref, low, high, held, extended)
 
     def field(a, t):
-        at = HALO * (3 + a)
-        if t < 0:
-            return low[at : at + HALO]
-        return high[at : at + HALO] if t == ROWS // TILE else rhs_ref[a, tile_rows(t)]
+        if 0 <= t < ROWS // TILE:
+            return rhs_ref[a, tile_rows(t)]
+        return component((low if t < 0 else high)[RHS_AT : RHS_AT + HALO], a)
+
+    def make(a, e):
+        if 0 < e <= ROWS // TILE:
+            viscosity, coupling = visc_ref[tile_rows(e - 1)], coup_ref[a, tile_rows(e - 1)]
+        else:
+            side = low if e == 0 else high
+            viscosity = side[:HALO]
+            coupling = component(side[COUPLING_AT : COUPLING_AT + HALO], a)
+        scale = RELAX / (10.0 * viscosity + jnp.abs(coupling) + 0.05)
+        return scale, scale * viscosity, scale * coupling
 
     solve(
-        count, margin_ref, visc_ref, coup_ref, field, low, high, smooth_ref, stacked, solved,
-        coarse.steps,
+        count, margin_ref, factors_ref, make, field, smooth_ref, first_ref, solved, coarse.steps
     )
     smooth = lambda a, t: smooth_ref[a, tile_rows(t)] * coarse.over_beta
     images = apply_operator(
@@ -552,9 +580,7 @@
             heads[a] = image
         if t == ROWS // TILE - 1:
             tails[a] = image
-    half = lax.broadcasted_iota(jnp.int32, (TILE, CELLS), 0) < TILE // 2
-    head = jnp.where(half, heads[0], pltpu.roll(heads[1], TILE // 2, 0))
-    tail = jnp.where(half, pltpu.roll(tails[1], TILE // 2, 0), tails[0])
+    head, tail = outer_rows(heads, tails)
     partner_rows_ref[...] = jnp.where(odd, head, tail)
     other_rows_ref[...] = jnp.where(odd, tail, head)
     sums[...] = jnp.zeros_like(sums)
@@ -572,16 +598,16 @@
 
 
 def second_turn_kernel(
-    count, margin_ref, first_ref, second_ref, residual_ref, inverse_ref, partner_ref, other_ref,
+    count, margin_ref, sums_ref, second_ref, residual_ref, factors_ref, inverse_ref, partner_ref, other_ref,
     partner_rows_ref, other_rows_ref, held, smooth_ref, rhs_ref, image_ref, visc_ref, coup_ref,
     direction_ref, next_ref,
-    image_smooth, extended, sums, stacked, solved,
+    image_smooth, extended, sums, first_ref, solved,
 ):
     low, high = neighbours_of(partner_ref, other_ref)
 
     def begin(coarse):
         def scale():
-            beta, h_00, h_10 = first_column(first_ref[...], second_ref[...])
+            beta, h_00, h_10 = first_column(sums_ref[...], second_ref[...])
             coarse.h_00, coarse.ratio, coarse.over = h_00, h_00 / beta, 1.0 / h_10
 
         def line():
@@ -597,11 +623,10 @@
         if 0 <= t < ROWS // TILE:
             return image_ref[a, tile_rows(t)]
         rows = low_rows[...] if t < 0 else high_rows[...]
-        return pltpu.roll(rows, TILE // 2, 0) if a else rows
+        return component(rows, a)
 
     solve(
-        count, margin_ref, visc_ref, coup_ref, field, low, high, image_smooth, stacked, solved,
-        coarse.steps,
+        count, margin_ref, factors_ref, None, field, image_smooth, first_ref, solved, coarse.steps
     )
 
     def smooth(a, t):
@@ -683,7 +708,7 @@
     f32 = lambda *shape: jax.ShapeDtypeStruct(shape, jnp.float32)
     dma = lambda *shape: pltpu.SemaphoreType.DMA(shape)
     extended = pltpu.VMEM((2, EXT, CELLS), jnp.float32)
-    stacked = pltpu.VMEM((6, STACKED, CELLS), jnp.float32)
+    stacked = pltpu.VMEM((2, STACKED, CELLS), jnp.float32)
     solved = pltpu.VMEM((4, STACKED, CELLS), jnp.float32)
     sums = pltpu.VMEM((SLOTS, LANES), jnp.float32)
     lines = pltpu.VMEM((LANES, len(MATRIX_GROUPS) * CELLS), jnp.bfloat16)
@@ -692,7 +717,8 @@
     arguments = (rhs, viscosity, coupling, coarse_inverse, coarse_basis)
     packs = call(
         pack_kernel, "pack", [HBM] * 5, [packed, packed], 5_000_000,
-        [pltpu.VMEM((4, VECTORS, CHUNK, CELLS), jnp.bfloat16), dma(4 * VECTORS // GROUP)]
+        [pltpu.VMEM((4, VECTORS, CHUNK, CELLS), jnp.bfloat16)]
+        + [pltpu.VMEM((2, 2, 2, HALO, CELLS), jnp.float32), dma(4 * VECTORS // GROUP), dma(4)]
         + [dma(2 * pack_count(columns))],
     )(*map(in_hbm, arguments))
     held, partner, other = lax.optimization_barrier((coarse_basis, *packs))
@@ -701,18 +727,18 @@
         restrict_kernel, "restrict", [VMEM] * 2, [row], 10_000_000, [sums]
     )(rhs, held)
     first = from_everyone(first)
-    direction, image, smooth, residual, partner_rows, other_rows, second = call(
+    direction, image, smooth, residual, factors, partner_rows, other_rows, second = call(
         functools.partial(first_turn_kernel, count), "first_turn", [SMEM] + [VMEM] * 8,
-        [whole, whole, smoothed, f32(1, columns), edge, edge, row], 20_000_000,
+        [whole, whole, smoothed, f32(1, columns), f32(6, STACKED, CELLS), edge, edge, row], 20_000_000,
         [extended, sums, stacked, solved, lines],
     )(margin_rows, first, coarse_inverse, partner, other, held, rhs, viscosity, coupling)
     partner_rows, other_rows = swap(partner_rows, other_rows)
     second = from_everyone(second)
     second_direction, third = call(
-        functools.partial(second_turn_kernel, count), "second_turn", [SMEM] + [VMEM] * 14,
+        functools.partial(second_turn_kernel, count), "second_turn", [SMEM] + [VMEM] * 15,
         [whole, row], 20_000_000, [extended, extended, sums, stacked, solved],
     )(
-        margin_rows, first, second, residual, coarse_inverse, partner, other, partner_rows, other_rows,
+        margin_rows, first, second, residual, factors, coarse_inverse, partner, other, partner_rows, other_rows,
         held, smooth, rhs, image, viscosity, coupling,
     )
     third = from_everyone(third)

time: 46.9 us -> 46.1 us (0.983)
  blocking collectives: 32.2 us -> 31.7 us
    all_to_all x3, blocking collectives: 32.2 us -> 31.7 us  [from_everyone(): lax.all_to_all(rows, 'sub', 0, 0, tiled=True, axis_index_groups=order)]
where the time goes in v19:
time: 46.1 us; the launch traced here: 45.9 us
  blocking collectives  31.7 us (69%)
  Pallas kernels  11.3 us (25%)
  starting transfers between devices  1.99 us (4%)
  between operations  0.74 us (2%)
    all_to_all x3, blocking collectives, from_everyone(): lax.all_to_all(rows, 'sub', 0, 0, tiled=True, axis_index_groups=order)  31.7 us
    pallas_call x1, Pallas kernels, on_device(): call(functools.partial(first_turn_kernel, count), 'first_turn', [SMEM] +...  3.93 us
    pallas_call x1, Pallas kernels, on_device(): call(functools.partial(second_turn_kernel, count), 'second_turn', [SMEM]...  2.54 us
    pallas_call x1, Pallas kernels, on_device(): call(pack_kernel, 'pack', [HBM] * 5, [packed, packed], 5000000, [pltpu.VM...  2.47 us
    ppermute x2, starting transfers between devices, swap(): lax.ppermute(other, 'sub', both(range(1, count - 1, 2)))  1.48 us
    pallas_call x1, Pallas kernels, on_device(): call(restrict_kernel, 'restrict', [VMEM] * 2, [row], 10000000, [sums])  1.44 us
  transfers between devices with their start and end apart: 4, of which 0 were waited for; matrix products, arithmetic and copies ran while one was open for 0% of the time, Pallas kernels for 3%

profile of v19, /device:TPU:0, one launch (start us, length us, event | category | flops | bytes accessed | tf_op | source)
XLA Modules:
  0.0 45.9 jit_solution(3655213222163030626)
XLA Ops:
  0.6 0.0 copy-start.1
  0.6 0.0 copy-start.3
  0.7 0.0 copy-start.2
  0.7 0.0 copy-start.4
  0.7 0.0 copy-start
  0.7 0.0 copy-start.5
  0.7 2.5 %pack.1 = (f32[192,512]{1,0:T(8,128)S(1)}, f32[192,512]{1,0:T(8,128)S(1)}) custom-call(f32[2,64,512]{2,1,0:T(8,128)} %rhs_ref.7, f32[64,512]{1,0:T(8,128)} %visc_ref.5, f32[2,64,512]{2,1,0:T(8,128)} %coup_ref.5, f32[48,768]{1,0:T(8,128)} %inverse_ref.5, bf16[48,2,64,512]{3,2,1,0:T(8,128)(2,1)} %held.2), custom_call_target="tpu_custom_call" | custom-call | flops 5000000 | bytes 4000000 | tf_op jit(solution)/shard_map/pack/pallas_call | solution.py:718
  3.2 0.5 %collective-permute-start = (f32[192,512]{1,0:T(8,128)S(1)}, f32[192,512]{1,0:T(8,128)S(1)}, u32[]{:S(2)}, u32[]{:S(2)}) collective-permute-start(f32[192,512]{1,0:T(8,128)S(1)} %get-tuple-element.22), channel_id=1, source_target_pairs={{0,1},{1,0},{2,3},{3,2},{4,5},{5,4},{6,7},{7,6},{8,9},{9,8},{10,11... | collective-permute-start | bytes 1179656 | tf_op jit(solution)/shard_map/ppermute | solution.py:700
  3.7 0.8 %collective-permute-start.1 = (f32[192,512]{1,0:T(8,128)S(1)}, f32[192,512]{1,0:T(8,128)S(1)}, u32[]{:S(2)}, u32[]{:S(2)}) collective-permute-start(f32[192,512]{1,0:T(8,128)S(1)} %get-tuple-element.23), channel_id=1, source_target_pairs={{1,2},{2,1},{3,4},{4,3},{5,6},{6,5},{7,8},{8,7},{9,10},{10,9},{11,... | collective-permute-start | bytes 1179656 | tf_op jit(solution)/shard_map/ppermute | solution.py:701
  4.5 0.0 copy-done.1
  4.5 0.1 copy-done
  4.6 1.4 %restrict.1 = f32[16,128]{1,0:T(8,128)S(1)} custom-call(f32[2,64,512]{2,1,0:T(8,128)S(1)} %copy-done.1, bf16[48,2,64,512]{3,2,1,0:T(8,128)(2,1)S(1)} %copy-done), custom_call_target="tpu_custom_call" | custom-call | flops 10000000 | bytes 4000000 | tf_op jit(solution)/shard_map/restrict/pallas_call | solution.py:726
  6.1 11.7 %all_to_all.33 = f32[16,1,128]{2,1,0:T(1,128)S(1)} all-to-all(f32[16,1,128]{2,1,0:T(1,128)S(1)} %bitcast.19), channel_id=1, replica_groups={{15,14,13,12,11,10,9,8,7,6,5,4,3,2,1,0},{31,30,29,28,27,26,25,24,23,22,..., dimensions={0} | all-to-all | bytes 16384 | tf_op jit(solution)/shard_map/all_to_all | solution.py:693
  17.8 0.0 collective-permute-done.partner_ref
  17.8 0.0 collective-permute-done.1.other_ref
  17.8 0.0 copy-done.3
  17.8 0.0 copy-done.2
  17.8 0.0 copy-done.4
  17.8 0.0 copy-done.5
  17.8 3.9 %first_turn.1 = (f32[2,64,512]{2,1,0:T(8,128)S(1)}, f32[2,64,512]{2,1,0:T(8,128)S(1)}, f32[2,80,512]{2,1,0:T(8,128)S(1)}, f32[1,768]{1,0:T(1,128)S(1)}, f32[6,14...) custom-call(s32[16]{0:T(128)S(1)} %copy-done.5, ...), custom_call_target="tpu_custom_call" | custom-call | flops 20000000 | bytes 4000000 | tf_op jit(solution)/shard_map/first_turn/pallas_call | solution.py:730
  21.8 0.0 collective-permute-start.2
  21.8 0.7 %collective-permute-start.3 = (f32[8,512]{1,0:T(8,128)S(1)}, f32[8,512]{1,0:T(8,128)S(1)}, u32[]{:S(2)}, u32[]{:S(2)}) collective-permute-start(f32[8,512]{1,0:T(8,128)S(1)} %get-tuple-element.28), channel_id=1, source_target_pairs={{1,2},{2,1},{3,4},{4,3},{5,6},{6,5},{7,8},{8,7},{9,10},{10,9},{11,... | collective-permute-start | bytes 49160 | tf_op jit(solution)/shard_map/ppermute | solution.py:701
  22.5 11.6 %all_to_all.34 = f32[16,1,128]{2,1,0:T(1,128)S(1)} all-to-all(f32[16,1,128]{2,1,0:T(1,128)S(1)} %bitcast.20), channel_id=1, replica_groups={{15,14,13,12,11,10,9,8,7,6,5,4,3,2,1,0},{31,30,29,28,27,26,25,24,23,22,..., dimensions={0} | all-to-all | bytes 16384 | tf_op jit(solution)/shard_map/all_to_all | solution.py:693
  34.0 0.0 collective-permute-done.2.partner_rows_ref
  34.1 0.0 collective-permute-done.3.other_rows_ref
  34.1 2.5 %second_turn.1 = (f32[2,64,512]{2,1,0:T(8,128)S(1)}, f32[16,128]{1,0:T(8,128)S(1)}) custom-call(s32[16]{0:T(128)S(1)} %copy-done.5, f32[16,128]{1,0:T(8,128)S(1)} %bitcast.14, f32[16,128]{1,0:T(8,128)S(1)} %bitcast.16, f32[1,768]{1,0:T(1,128)S(1)} %get-tuple-element.25.residual_ref, f32[6,144,512]{2,1,0:T(8,128)S(1)} %get-tuple-element.26.factors_ref, ...), custom_call_target="tpu_custom_call" | custom-call | flops 20000000 | bytes 4000000 | tf_op jit(solution)/shard_map/second_turn/pallas_call | solution.py:737
  36.6 8.4 %all_to_all.35 = f32[16,1,128]{2,1,0:T(1,128)S(1)} all-to-all(f32[16,1,128]{2,1,0:T(1,128)S(1)} %bitcast.21), channel_id=1, replica_groups={{15,14,13,12,11,10,9,8,7,6,5,4,3,2,1,0},{31,30,29,28,27,26,25,24,23,22,..., dimensions={0} | all-to-all | bytes 16384 | tf_op jit(solution)/shard_map/all_to_all | solution.py:693
  45.0 0.9 %finish.1 = (f32[2,64,512]{2,1,0:T(8,128)}, f32[2,3]{1,0:T(2,128)}) custom-call(f32[16,128]{1,0:T(8,128)S(1)} %bitcast.15, f32[16,128]{1,0:T(8,128)S(1)} %bitcast.17, f32[16,128]{1,0:T(8,128)S(1)} %bitcast.18, f32[2,64,512]{2,1,0:T(8,128)S(1)} %get-tuple-element.32.first_direction_ref, f32[2,64,512]{2,1,0:T(8,128)S(1)} %get-tuple-element.33.second_direction_ref), custom_call_target="tpu_custom_call" | custom-call | flops 1000000 | bytes 4000000 | tf_op jit(solution)/shard_map/finish/pallas_call | solution.py:745
Async XLA Ops:
  0.6 3.9 %copy-start.1 = (f32[2,64,512]{2,1,0:T(8,128)S(1)}, f32[2,64,512]{2,1,0:T(8,128)}, u32[]{:S(2)}) copy-start(f32[2,64,512]{2,1,0:T(8,128)} %rhs_ref.7) | copy-start | bytes 786436
  0.6 17.2 %copy-start.3 = (f32[48,768]{1,0:T(8,128)S(1)}, f32[48,768]{1,0:T(8,128)}, u32[]{:S(2)}) copy-start(f32[48,768]{1,0:T(8,128)} %inverse_ref.5) | copy-start | bytes 442372
  0.7 17.2 %copy-start.2 = (f32[2,64,512]{2,1,0:T(8,128)S(1)}, f32[2,64,512]{2,1,0:T(8,128)}, u32[]{:S(2)}) copy-start(f32[2,64,512]{2,1,0:T(8,128)} %coup_ref.5) | copy-start | bytes 786436
  0.7 17.2 %copy-start.4 = (f32[64,512]{1,0:T(8,128)S(1)}, f32[64,512]{1,0:T(8,128)}, u32[]{:S(2)}) copy-start(f32[64,512]{1,0:T(8,128)} %visc_ref.5) | copy-start | bytes 393220
  0.7 3.9 %copy-start = (bf16[48,2,64,512]{3,2,1,0:T(8,128)(2,1)S(1)}, bf16[48,2,64,512]{3,2,1,0:T(8,128)(2,1)}, u32[]{:S(2)}) copy-start(bf16[48,2,64,512]{3,2,1,0:T(8,128)(2,1)} %held.2) | copy-start | bytes 18874372
  0.7 17.2 %copy-start.5 = (s32[16]{0:T(128)S(1)}, s32[16]{0:T(128)}, u32[]{:S(2)}) copy-start(s32[16]{0:T(128)} %margin_ref.3) | copy-start | bytes 196
  3.2 14.6 %collective-permute-start = (f32[192,512]{1,0:T(8,128)S(1)}, f32[192,512]{1,0:T(8,128)S(1)}, u32[]{:S(2)}, u32[]{:S(2)}) collective-permute-start(f32[192,512]{1,0:T(8,128)S(1)} %get-tuple-element.22), channel_id=1, source_target_pairs={{0,1},{1,0},{2,3},{3,2},{4,5},{5,4},{6,7},{7,6},{8,9},{9,8},{10,11... | collective-permute-start | bytes 1179656 | tf_op jit(solution)/shard_map/ppermute | solution.py:700
  3.7 14.1 %collective-permute-start.1 = (f32[192,512]{1,0:T(8,128)S(1)}, f32[192,512]{1,0:T(8,128)S(1)}, u32[]{:S(2)}, u32[]{:S(2)}) collective-permute-start(f32[192,512]{1,0:T(8,128)S(1)} %get-tuple-element.23), channel_id=1, source_target_pairs={{1,2},{2,1},{3,4},{4,3},{5,6},{6,5},{7,8},{8,7},{9,10},{10,9},{11,... | collective-permute-start | bytes 1179656 | tf_op jit(solution)/shard_map/ppermute | solution.py:701
  21.8 12.3 %collective-permute-start.2 = (f32[8,512]{1,0:T(8,128)S(1)}, f32[8,512]{1,0:T(8,128)S(1)}, u32[]{:S(2)}, u32[]{:S(2)}) collective-permute-start(f32[8,512]{1,0:T(8,128)S(1)} %get-tuple-element.27), channel_id=1, source_target_pairs={{0,1},{1,0},{2,3},{3,2},{4,5},{5,4},{6,7},{7,6},{8,9},{9,8},{10,11... | collective-permute-start | bytes 49160 | tf_op jit(solution)/shard_map/ppermute | solution.py:700
  21.8 12.3 %collective-permute-start.3 = (f32[8,512]{1,0:T(8,128)S(1)}, f32[8,512]{1,0:T(8,128)S(1)}, u32[]{:S(2)}, u32[]{:S(2)}) collective-permute-start(f32[8,512]{1,0:T(8,128)S(1)} %get-tuple-element.28), channel_id=1, source_target_pairs={{1,2},{2,1},{3,4},{4,3},{5,6},{6,5},{7,8},{8,7},{9,10},{10,9},{11,... | collective-permute-start | bytes 49160 | tf_op jit(solution)/shard_map/ppermute | solution.py:701

commit v20 on v19

--- a/solution.py
+++ b/solution.py
@@ -108,8 +108,8 @@
     sums[pl.ds(pl.multiple_of(PIECE * i, PIECE), PIECE), :] = in_rows(tiles)
 
 
-MATRIX_GROUPS = tuple((1, r) for r in range(CHUNK, ROWS, CHUNK))
-VECTOR_GROUPS = ((0, 0), (0, 16), (0, 32), (0, 48), (1, 0))
+VECTOR_GROUPS = tuple((0, r) for r in range(0, ROWS, CHUNK))
+MATRIX_GROUPS = tuple((1, r) for r in range(0, ROWS, CHUNK))
 
 
 def restrict(held, field, sums, lines):
@@ -242,7 +242,7 @@
                 )
             )
     for copy in stages + group_copies + packs:
-        copy.start()
+        copy.start(priority=1)
     for copy in stages:
         copy.wait()
     for m, at in enumerate((COUPLING_AT, RHS_AT)):

time: 46.1 us -> 45.8 us (level)
  no operation moved by 1% of the time
where the time goes in v20:
time: 45.8 us; the launch traced here: 45.6 us
  blocking collectives  31.7 us (69%)
  Pallas kernels  11 us (24%)
  starting transfers between devices  1.99 us (4%)
  between operations  0.74 us (2%)
    all_to_all x3, blocking collectives, from_everyone(): lax.all_to_all(rows, 'sub', 0, 0, tiled=True, axis_index_groups=order)  31.7 us
    pallas_call x1, Pallas kernels, on_device(): call(functools.partial(first_turn_kernel, count), 'first_turn', [SMEM] +...  3.64 us
    pallas_call x1, Pallas kernels, on_device(): call(functools.partial(second_turn_kernel, count), 'second_turn', [SMEM]...  2.54 us
    pallas_call x1, Pallas kernels, on_device(): call(pack_kernel, 'pack', [HBM] * 5, [packed, packed], 5000000, [pltpu.VM...  2.47 us
    ppermute x2, starting transfers between devices, swap(): lax.ppermute(other, 'sub', both(range(1, count - 1, 2)))  1.48 us
    pallas_call x1, Pallas kernels, on_device(): call(restrict_kernel, 'restrict', [VMEM] * 2, [row], 10000000, [sums])  1.44 us
  transfers between devices with their start and end apart: 4, of which 0 were waited for; matrix products, arithmetic and copies ran while one was open for 0% of the time, Pallas kernels for 3%

profile of v20, /device:TPU:0, one launch (start us, length us, event | category | flops | bytes accessed | tf_op | source)
XLA Modules:
  0.0 45.6 jit_solution(11902616685053763776)
XLA Ops:
  0.6 0.0 copy-start.1
  0.6 0.0 copy-start.3
  0.7 0.0 copy-start.2
  0.7 0.0 copy-start.4
  0.7 0.0 copy-start
  0.7 0.0 copy-start.5
  0.7 2.5 %pack.1 = (f32[192,512]{1,0:T(8,128)S(1)}, f32[192,512]{1,0:T(8,128)S(1)}) custom-call(f32[2,64,512]{2,1,0:T(8,128)} %rhs_ref.7, f32[64,512]{1,0:T(8,128)} %visc_ref.5, f32[2,64,512]{2,1,0:T(8,128)} %coup_ref.5, f32[48,768]{1,0:T(8,128)} %inverse_ref.5, bf16[48,2,64,512]{3,2,1,0:T(8,128)(2,1)} %held.2), custom_call_target="tpu_custom_call" | custom-call | flops 5000000 | bytes 4000000 | tf_op jit(solution)/shard_map/pack/pallas_call | solution.py:718
  3.2 0.5 %collective-permute-start = (f32[192,512]{1,0:T(8,128)S(1)}, f32[192,512]{1,0:T(8,128)S(1)}, u32[]{:S(2)}, u32[]{:S(2)}) collective-permute-start(f32[192,512]{1,0:T(8,128)S(1)} %get-tuple-element.22), channel_id=1, source_target_pairs={{0,1},{1,0},{2,3},{3,2},{4,5},{5,4},{6,7},{7,6},{8,9},{9,8},{10,11... | collective-permute-start | bytes 1179656 | tf_op jit(solution)/shard_map/ppermute | solution.py:700
  3.7 0.8 %collective-permute-start.1 = (f32[192,512]{1,0:T(8,128)S(1)}, f32[192,512]{1,0:T(8,128)S(1)}, u32[]{:S(2)}, u32[]{:S(2)}) collective-permute-start(f32[192,512]{1,0:T(8,128)S(1)} %get-tuple-element.23), channel_id=1, source_target_pairs={{1,2},{2,1},{3,4},{4,3},{5,6},{6,5},{7,8},{8,7},{9,10},{10,9},{11,... | collective-permute-start | bytes 1179656 | tf_op jit(solution)/shard_map/ppermute | solution.py:701
  4.5 0.0 copy-done.1
  4.5 0.1 copy-done
  4.6 1.4 %restrict.1 = f32[16,128]{1,0:T(8,128)S(1)} custom-call(f32[2,64,512]{2,1,0:T(8,128)S(1)} %copy-done.1, bf16[48,2,64,512]{3,2,1,0:T(8,128)(2,1)S(1)} %copy-done), custom_call_target="tpu_custom_call" | custom-call | flops 10000000 | bytes 4000000 | tf_op jit(solution)/shard_map/restrict/pallas_call | solution.py:726
  6.1 11.7 %all_to_all.33 = f32[16,1,128]{2,1,0:T(1,128)S(1)} all-to-all(f32[16,1,128]{2,1,0:T(1,128)S(1)} %bitcast.19), channel_id=1, replica_groups={{15,14,13,12,11,10,9,8,7,6,5,4,3,2,1,0},{31,30,29,28,27,26,25,24,23,22,..., dimensions={0} | all-to-all | bytes 16384 | tf_op jit(solution)/shard_map/all_to_all | solution.py:693
  17.8 0.0 collective-permute-done.partner_ref
  17.8 0.0 collective-permute-done.1.other_ref
  17.8 0.0 copy-done.3
  17.8 0.0 copy-done.2
  17.8 0.0 copy-done.4
  17.8 0.0 copy-done.5
  17.8 3.6 %first_turn.1 = (f32[2,64,512]{2,1,0:T(8,128)S(1)}, f32[2,64,512]{2,1,0:T(8,128)S(1)}, f32[2,80,512]{2,1,0:T(8,128)S(1)}, f32[1,768]{1,0:T(1,128)S(1)}, f32[6,14...) custom-call(s32[16]{0:T(128)S(1)} %copy-done.5, ...), custom_call_target="tpu_custom_call" | custom-call | flops 20000000 | bytes 4000000 | tf_op jit(solution)/shard_map/first_turn/pallas_call | solution.py:730
  21.5 0.0 collective-permute-start.2
  21.5 0.7 %collective-permute-start.3 = (f32[8,512]{1,0:T(8,128)S(1)}, f32[8,512]{1,0:T(8,128)S(1)}, u32[]{:S(2)}, u32[]{:S(2)}) collective-permute-start(f32[8,512]{1,0:T(8,128)S(1)} %get-tuple-element.28), channel_id=1, source_target_pairs={{1,2},{2,1},{3,4},{4,3},{5,6},{6,5},{7,8},{8,7},{9,10},{10,9},{11,... | collective-permute-start | bytes 49160 | tf_op jit(solution)/shard_map/ppermute | solution.py:701
  22.2 11.6 %all_to_all.34 = f32[16,1,128]{2,1,0:T(1,128)S(1)} all-to-all(f32[16,1,128]{2,1,0:T(1,128)S(1)} %bitcast.20), channel_id=1, replica_groups={{15,14,13,12,11,10,9,8,7,6,5,4,3,2,1,0},{31,30,29,28,27,26,25,24,23,22,..., dimensions={0} | all-to-all | bytes 16384 | tf_op jit(solution)/shard_map/all_to_all | solution.py:693
  33.8 0.0 collective-permute-done.2.partner_rows_ref
  33.8 0.0 collective-permute-done.3.other_rows_ref
  33.8 2.5 %second_turn.1 = (f32[2,64,512]{2,1,0:T(8,128)S(1)}, f32[16,128]{1,0:T(8,128)S(1)}) custom-call(s32[16]{0:T(128)S(1)} %copy-done.5, f32[16,128]{1,0:T(8,128)S(1)} %bitcast.14, f32[16,128]{1,0:T(8,128)S(1)} %bitcast.16, f32[1,768]{1,0:T(1,128)S(1)} %get-tuple-element.25.residual_ref, f32[6,144,512]{2,1,0:T(8,128)S(1)} %get-tuple-element.26.factors_ref, ...), custom_call_target="tpu_custom_call" | custom-call | flops 20000000 | bytes 4000000 | tf_op jit(solution)/shard_map/second_turn/pallas_call | solution.py:737
  36.3 8.4 %all_to_all.35 = f32[16,1,128]{2,1,0:T(1,128)S(1)} all-to-all(f32[16,1,128]{2,1,0:T(1,128)S(1)} %bitcast.21), channel_id=1, replica_groups={{15,14,13,12,11,10,9,8,7,6,5,4,3,2,1,0},{31,30,29,28,27,26,25,24,23,22,..., dimensions={0} | all-to-all | bytes 16384 | tf_op jit(solution)/shard_map/all_to_all | solution.py:693
  44.7 0.9 %finish.1 = (f32[2,64,512]{2,1,0:T(8,128)}, f32[2,3]{1,0:T(2,128)}) custom-call(f32[16,128]{1,0:T(8,128)S(1)} %bitcast.15, f32[16,128]{1,0:T(8,128)S(1)} %bitcast.17, f32[16,128]{1,0:T(8,128)S(1)} %bitcast.18, f32[2,64,512]{2,1,0:T(8,128)S(1)} %get-tuple-element.32.first_direction_ref, f32[2,64,512]{2,1,0:T(8,128)S(1)} %get-tuple-element.33.second_direction_ref), custom_call_target="tpu_custom_call" | custom-call | flops 1000000 | bytes 4000000 | tf_op jit(solution)/shard_map/finish/pallas_call | solution.py:745
Async XLA Ops:
  0.6 3.9 %copy-start.1 = (f32[2,64,512]{2,1,0:T(8,128)S(1)}, f32[2,64,512]{2,1,0:T(8,128)}, u32[]{:S(2)}) copy-start(f32[2,64,512]{2,1,0:T(8,128)} %rhs_ref.7) | copy-start | bytes 786436
  0.6 17.2 %copy-start.3 = (f32[48,768]{1,0:T(8,128)S(1)}, f32[48,768]{1,0:T(8,128)}, u32[]{:S(2)}) copy-start(f32[48,768]{1,0:T(8,128)} %inverse_ref.5) | copy-start | bytes 442372
  0.7 17.2 %copy-start.2 = (f32[2,64,512]{2,1,0:T(8,128)S(1)}, f32[2,64,512]{2,1,0:T(8,128)}, u32[]{:S(2)}) copy-start(f32[2,64,512]{2,1,0:T(8,128)} %coup_ref.5) | copy-start | bytes 786436
  0.7 17.2 %copy-start.4 = (f32[64,512]{1,0:T(8,128)S(1)}, f32[64,512]{1,0:T(8,128)}, u32[]{:S(2)}) copy-start(f32[64,512]{1,0:T(8,128)} %visc_ref.5) | copy-start | bytes 393220
  0.7 3.9 %copy-start = (bf16[48,2,64,512]{3,2,1,0:T(8,128)(2,1)S(1)}, bf16[48,2,64,512]{3,2,1,0:T(8,128)(2,1)}, u32[]{:S(2)}) copy-start(bf16[48,2,64,512]{3,2,1,0:T(8,128)(2,1)} %held.2) | copy-start | bytes 18874372
  0.7 17.2 %copy-start.5 = (s32[16]{0:T(128)S(1)}, s32[16]{0:T(128)}, u32[]{:S(2)}) copy-start(s32[16]{0:T(128)} %margin_ref.3) | copy-start | bytes 196
  3.2 14.6 %collective-permute-start = (f32[192,512]{1,0:T(8,128)S(1)}, f32[192,512]{1,0:T(8,128)S(1)}, u32[]{:S(2)}, u32[]{:S(2)}) collective-permute-start(f32[192,512]{1,0:T(8,128)S(1)} %get-tuple-element.22), channel_id=1, source_target_pairs={{0,1},{1,0},{2,3},{3,2},{4,5},{5,4},{6,7},{7,6},{8,9},{9,8},{10,11... | collective-permute-start | bytes 1179656 | tf_op jit(solution)/shard_map/ppermute | solution.py:700
  3.7 14.1 %collective-permute-start.1 = (f32[192,512]{1,0:T(8,128)S(1)}, f32[192,512]{1,0:T(8,128)S(1)}, u32[]{:S(2)}, u32[]{:S(2)}) collective-permute-start(f32[192,512]{1,0:T(8,128)S(1)} %get-tuple-element.23), channel_id=1, source_target_pairs={{1,2},{2,1},{3,4},{4,3},{5,6},{6,5},{7,8},{8,7},{9,10},{10,9},{11,... | collective-permute-start | bytes 1179656 | tf_op jit(solution)/shard_map/ppermute | solution.py:701
  21.5 12.3 %collective-permute-start.2 = (f32[8,512]{1,0:T(8,128)S(1)}, f32[8,512]{1,0:T(8,128)S(1)}, u32[]{:S(2)}, u32[]{:S(2)}) collective-permute-start(f32[8,512]{1,0:T(8,128)S(1)} %get-tuple-element.27), channel_id=1, source_target_pairs={{0,1},{1,0},{2,3},{3,2},{4,5},{5,4},{6,7},{7,6},{8,9},{9,8},{10,11... | collective-permute-start | bytes 49160 | tf_op jit(solution)/shard_map/ppermute | solution.py:700
  21.5 12.3 %collective-permute-start.3 = (f32[8,512]{1,0:T(8,128)S(1)}, f32[8,512]{1,0:T(8,128)S(1)}, u32[]{:S(2)}, u32[]{:S(2)}) collective-permute-start(f32[8,512]{1,0:T(8,128)S(1)} %get-tuple-element.28), channel_id=1, source_target_pairs={{1,2},{2,1},{3,4},{4,3},{5,6},{6,5},{7,8},{8,7},{9,10},{10,9},{11,... | collective-permute-start | bytes 49160 | tf_op jit(solution)/shard_map/ppermute | solution.py:701

commit v21 on v20

--- a/solution.py
+++ b/solution.py
@@ -94,22 +94,8 @@
     return total
 
 
-def restrict_piece(i, held, field, sums):
-    totals = [None] * PIECE
-    for a in range(2):
-        for r in range(0, ROWS, CHUNK):
-            for c in range(0, CELLS, LANES):
-                rows, cells = slice(r, r + CHUNK), slice(c, c + LANES)
-                tile = field[a, rows, cells]
-                for n in range(PIECE):
-                    term = held[PIECE * i + n, a, rows, cells].astype(jnp.float32) * tile
-                    totals[n] = term if totals[n] is None else totals[n] + term
-    tiles = [total[:8] + total[8:] for total in totals]
-    sums[pl.ds(pl.multiple_of(PIECE * i, PIECE), PIECE), :] = in_rows(tiles)
-
-
-VECTOR_GROUPS = tuple((0, r) for r in range(0, ROWS, CHUNK))
-MATRIX_GROUPS = tuple((1, r) for r in range(0, ROWS, CHUNK))
+GROUPS = tuple((a, r) for a in range(2) for r in range(0, ROWS, CHUNK))
+VECTOR_GROUPS, MATRIX_GROUPS = GROUPS[:2], GROUPS[2:]
 
 
 def restrict(held, field, sums, lines):
@@ -276,7 +262,7 @@
         copy.wait()
 
 
-def restrict_kernel(rhs_ref, held, sums_ref, sums):
+def restrict_kernel(rhs_ref, held, sums_ref, sums, lines):
     sums[...] = jnp.zeros_like(sums)
     squares = jnp.zeros((TILE, CELLS), jnp.float32)
     for a in range(2):
@@ -285,11 +271,7 @@
             squares = squares + tile * tile
     sums[VECTORS : VECTORS + 8] = in_rows([fold(squares)])
 
-    def body(i, carry):
-        restrict_piece(i, held, rhs_ref, sums)
-        return carry
-
-    lax.fori_loop(0, VECTORS // PIECE, body, 0)
+    restrict(held, rhs_ref, sums, lines)
     send_sums(sums, sums_ref)
 
 
@@ -724,7 +706,7 @@
     held, partner, other = lax.optimization_barrier((coarse_basis, *packs))
     partner, other = swap(partner, other)
     (first,) = call(
-        restrict_kernel, "restrict", [VMEM] * 2, [row], 10_000_000, [sums]
+        restrict_kernel, "restrict", [VMEM] * 2, [row], 10_000_000, [sums, lines]
     )(rhs, held)
     first = from_everyone(first)
     direction, image, smooth, residual, factors, partner_rows, other_rows, second = call(

time: 45.8 us -> 46 us (level)
  transfers between devices with their start and end apart: 4 -> 4, of which waited for: 0 -> 0; matrix products, arithmetic and copies ran while one was open for 0% -> 0% of each run, Pallas kernels for 3% -> 4%
where the time goes in v21:
time: 46 us; the launch traced here: 45.8 us
  blocking collectives  31.5 us (68%)
  Pallas kernels  11.4 us (25%)
  starting transfers between devices  1.99 us (4%)
  between operations  0.74 us (2%)
    all_to_all x3, blocking collectives, from_everyone(): lax.all_to_all(rows, 'sub', 0, 0, tiled=True, axis_index_groups=order)  31.5 us
    pallas_call x1, Pallas kernels, on_device(): call(functools.partial(first_turn_kernel, count), 'first_turn', [SMEM] +...  3.82 us
    pallas_call x1, Pallas kernels, on_device(): call(functools.partial(second_turn_kernel, count), 'second_turn', [SMEM]...  2.54 us
    pallas_call x1, Pallas kernels, on_device(): call(pack_kernel, 'pack', [HBM] * 5, [packed, packed], 5000000, [pltpu.VM...  2.47 us
    pallas_call x1, Pallas kernels, on_device(): call(restrict_kernel, 'restrict', [VMEM] * 2, [row], 10000000, [sums, lin...  1.68 us
    ppermute x2, starting transfers between devices, swap(): lax.ppermute(other, 'sub', both(range(1, count - 1, 2)))  1.48 us
  transfers between devices with their start and end apart: 4, of which 0 were waited for; matrix products, arithmetic and copies ran while one was open for 0% of the time, Pallas kernels for 4%

profile of v21, /device:TPU:0, one launch (start us, length us, event | category | flops | bytes accessed | tf_op | source)
XLA Modules:
  0.0 45.8 jit_solution(6239773723681660801)
XLA Ops:
  0.6 0.0 copy-start.1
  0.6 0.0 copy-start.3
  0.7 0.0 copy-start.2
  0.7 0.0 copy-start.4
  0.7 0.0 copy-start
  0.7 0.0 copy-start.5
  0.7 2.5 %pack.1 = (f32[192,512]{1,0:T(8,128)S(1)}, f32[192,512]{1,0:T(8,128)S(1)}) custom-call(f32[2,64,512]{2,1,0:T(8,128)} %rhs_ref.7, f32[64,512]{1,0:T(8,128)} %visc_ref.5, f32[2,64,512]{2,1,0:T(8,128)} %coup_ref.5, f32[48,768]{1,0:T(8,128)} %inverse_ref.5, bf16[48,2,64,512]{3,2,1,0:T(8,128)(2,1)} %held.2), custom_call_target="tpu_custom_call" | custom-call | flops 5000000 | bytes 4000000 | tf_op jit(solution)/shard_map/pack/pallas_call | solution.py:700
  3.2 0.5 %collective-permute-start = (f32[192,512]{1,0:T(8,128)S(1)}, f32[192,512]{1,0:T(8,128)S(1)}, u32[]{:S(2)}, u32[]{:S(2)}) collective-permute-start(f32[192,512]{1,0:T(8,128)S(1)} %get-tuple-element.22), channel_id=1, source_target_pairs={{0,1},{1,0},{2,3},{3,2},{4,5},{5,4},{6,7},{7,6},{8,9},{9,8},{10,11... | collective-permute-start | bytes 1179656 | tf_op jit(solution)/shard_map/ppermute | solution.py:682
  3.7 0.8 %collective-permute-start.1 = (f32[192,512]{1,0:T(8,128)S(1)}, f32[192,512]{1,0:T(8,128)S(1)}, u32[]{:S(2)}, u32[]{:S(2)}) collective-permute-start(f32[192,512]{1,0:T(8,128)S(1)} %get-tuple-element.23), channel_id=1, source_target_pairs={{1,2},{2,1},{3,4},{4,3},{5,6},{6,5},{7,8},{8,7},{9,10},{10,9},{11,... | collective-permute-start | bytes 1179656 | tf_op jit(solution)/shard_map/ppermute | solution.py:683
  4.5 0.0 copy-done.1
  4.5 0.1 copy-done
  4.6 1.7 %restrict.1 = f32[16,128]{1,0:T(8,128)S(1)} custom-call(f32[2,64,512]{2,1,0:T(8,128)S(1)} %copy-done.1, bf16[48,2,64,512]{3,2,1,0:T(8,128)(2,1)S(1)} %copy-done), custom_call_target="tpu_custom_call" | custom-call | flops 10000000 | bytes 4000000 | tf_op jit(solution)/shard_map/restrict/pallas_call | solution.py:708
  6.3 11.8 %all_to_all.33 = f32[16,1,128]{2,1,0:T(1,128)S(1)} all-to-all(f32[16,1,128]{2,1,0:T(1,128)S(1)} %bitcast.19), channel_id=1, replica_groups={{15,14,13,12,11,10,9,8,7,6,5,4,3,2,1,0},{31,30,29,28,27,26,25,24,23,22,..., dimensions={0} | all-to-all | bytes 16384 | tf_op jit(solution)/shard_map/all_to_all | solution.py:675
  18.1 0.0 collective-permute-done.partner_ref
  18.1 0.0 collective-permute-done.1.other_ref
  18.1 0.0 copy-done.3
  18.1 0.0 copy-done.2
  18.1 0.0 copy-done.4
  18.1 0.0 copy-done.5
  18.1 3.8 %first_turn.1 = (f32[2,64,512]{2,1,0:T(8,128)S(1)}, f32[2,64,512]{2,1,0:T(8,128)S(1)}, f32[2,80,512]{2,1,0:T(8,128)S(1)}, f32[1,768]{1,0:T(1,128)S(1)}, f32[6,14...) custom-call(s32[16]{0:T(128)S(1)} %copy-done.5, ...), custom_call_target="tpu_custom_call" | custom-call | flops 20000000 | bytes 4000000 | tf_op jit(solution)/shard_map/first_turn/pallas_call | solution.py:712
  21.9 0.0 collective-permute-start.2
  21.9 0.7 %collective-permute-start.3 = (f32[8,512]{1,0:T(8,128)S(1)}, f32[8,512]{1,0:T(8,128)S(1)}, u32[]{:S(2)}, u32[]{:S(2)}) collective-permute-start(f32[8,512]{1,0:T(8,128)S(1)} %get-tuple-element.28), channel_id=1, source_target_pairs={{1,2},{2,1},{3,4},{4,3},{5,6},{6,5},{7,8},{8,7},{9,10},{10,9},{11,... | collective-permute-start | bytes 49160 | tf_op jit(solution)/shard_map/ppermute | solution.py:683
  22.6 11.3 %all_to_all.34 = f32[16,1,128]{2,1,0:T(1,128)S(1)} all-to-all(f32[16,1,128]{2,1,0:T(1,128)S(1)} %bitcast.20), channel_id=1, replica_groups={{15,14,13,12,11,10,9,8,7,6,5,4,3,2,1,0},{31,30,29,28,27,26,25,24,23,22,..., dimensions={0} | all-to-all | bytes 16384 | tf_op jit(solution)/shard_map/all_to_all | solution.py:675
  33.9 0.0 collective-permute-done.2.partner_rows_ref
  33.9 0.0 collective-permute-done.3.other_rows_ref
  33.9 2.5 %second_turn.1 = (f32[2,64,512]{2,1,0:T(8,128)S(1)}, f32[16,128]{1,0:T(8,128)S(1)}) custom-call(s32[16]{0:T(128)S(1)} %copy-done.5, f32[16,128]{1,0:T(8,128)S(1)} %bitcast.14, f32[16,128]{1,0:T(8,128)S(1)} %bitcast.16, f32[1,768]{1,0:T(1,128)S(1)} %get-tuple-element.25.residual_ref, f32[6,144,512]{2,1,0:T(8,128)S(1)} %get-tuple-element.26.factors_ref, ...), custom_call_target="tpu_custom_call" | custom-call | flops 20000000 | bytes 4000000 | tf_op jit(solution)/shard_map/second_turn/pallas_call | solution.py:719
  36.5 8.4 %all_to_all.35 = f32[16,1,128]{2,1,0:T(1,128)S(1)} all-to-all(f32[16,1,128]{2,1,0:T(1,128)S(1)} %bitcast.21), channel_id=1, replica_groups={{15,14,13,12,11,10,9,8,7,6,5,4,3,2,1,0},{31,30,29,28,27,26,25,24,23,22,..., dimensions={0} | all-to-all | bytes 16384 | tf_op jit(solution)/shard_map/all_to_all | solution.py:675
  44.8 0.9 %finish.1 = (f32[2,64,512]{2,1,0:T(8,128)}, f32[2,3]{1,0:T(2,128)}) custom-call(f32[16,128]{1,0:T(8,128)S(1)} %bitcast.15, f32[16,128]{1,0:T(8,128)S(1)} %bitcast.17, f32[16,128]{1,0:T(8,128)S(1)} %bitcast.18, f32[2,64,512]{2,1,0:T(8,128)S(1)} %get-tuple-element.32.first_direction_ref, f32[2,64,512]{2,1,0:T(8,128)S(1)} %get-tuple-element.33.second_direction_ref), custom_call_target="tpu_custom_call" | custom-call | flops 1000000 | bytes 4000000 | tf_op jit(solution)/shard_map/finish/pallas_call | solution.py:727
Async XLA Ops:
  0.6 3.9 %copy-start.1 = (f32[2,64,512]{2,1,0:T(8,128)S(1)}, f32[2,64,512]{2,1,0:T(8,128)}, u32[]{:S(2)}) copy-start(f32[2,64,512]{2,1,0:T(8,128)} %rhs_ref.7) | copy-start | bytes 786436
  0.6 17.4 %copy-start.3 = (f32[48,768]{1,0:T(8,128)S(1)}, f32[48,768]{1,0:T(8,128)}, u32[]{:S(2)}) copy-start(f32[48,768]{1,0:T(8,128)} %inverse_ref.5) | copy-start | bytes 442372
  0.7 17.4 %copy-start.2 = (f32[2,64,512]{2,1,0:T(8,128)S(1)}, f32[2,64,512]{2,1,0:T(8,128)}, u32[]{:S(2)}) copy-start(f32[2,64,512]{2,1,0:T(8,128)} %coup_ref.5) | copy-start | bytes 786436
  0.7 17.4 %copy-start.4 = (f32[64,512]{1,0:T(8,128)S(1)}, f32[64,512]{1,0:T(8,128)}, u32[]{:S(2)}) copy-start(f32[64,512]{1,0:T(8,128)} %visc_ref.5) | copy-start | bytes 393220
  0.7 3.9 %copy-start = (bf16[48,2,64,512]{3,2,1,0:T(8,128)(2,1)S(1)}, bf16[48,2,64,512]{3,2,1,0:T(8,128)(2,1)}, u32[]{:S(2)}) copy-start(bf16[48,2,64,512]{3,2,1,0:T(8,128)(2,1)} %held.2) | copy-start | bytes 18874372
  0.7 17.4 %copy-start.5 = (s32[16]{0:T(128)S(1)}, s32[16]{0:T(128)}, u32[]{:S(2)}) copy-start(s32[16]{0:T(128)} %margin_ref.3) | copy-start | bytes 196
  3.2 14.9 %collective-permute-start = (f32[192,512]{1,0:T(8,128)S(1)}, f32[192,512]{1,0:T(8,128)S(1)}, u32[]{:S(2)}, u32[]{:S(2)}) collective-permute-start(f32[192,512]{1,0:T(8,128)S(1)} %get-tuple-element.22), channel_id=1, source_target_pairs={{0,1},{1,0},{2,3},{3,2},{4,5},{5,4},{6,7},{7,6},{8,9},{9,8},{10,11... | collective-permute-start | bytes 1179656 | tf_op jit(solution)/shard_map/ppermute | solution.py:682
  3.7 14.4 %collective-permute-start.1 = (f32[192,512]{1,0:T(8,128)S(1)}, f32[192,512]{1,0:T(8,128)S(1)}, u32[]{:S(2)}, u32[]{:S(2)}) collective-permute-start(f32[192,512]{1,0:T(8,128)S(1)} %get-tuple-element.23), channel_id=1, source_target_pairs={{1,2},{2,1},{3,4},{4,3},{5,6},{6,5},{7,8},{8,7},{9,10},{10,9},{11,... | collective-permute-start | bytes 1179656 | tf_op jit(solution)/shard_map/ppermute | solution.py:683
  21.9 12.0 %collective-permute-start.2 = (f32[8,512]{1,0:T(8,128)S(1)}, f32[8,512]{1,0:T(8,128)S(1)}, u32[]{:S(2)}, u32[]{:S(2)}) collective-permute-start(f32[8,512]{1,0:T(8,128)S(1)} %get-tuple-element.27), channel_id=1, source_target_pairs={{0,1},{1,0},{2,3},{3,2},{4,5},{5,4},{6,7},{7,6},{8,9},{9,8},{10,11... | collective-permute-start | bytes 49160 | tf_op jit(solution)/shard_map/ppermute | solution.py:682
  21.9 12.0 %collective-permute-start.3 = (f32[8,512]{1,0:T(8,128)S(1)}, f32[8,512]{1,0:T(8,128)S(1)}, u32[]{:S(2)}, u32[]{:S(2)}) collective-permute-start(f32[8,512]{1,0:T(8,128)S(1)} %get-tuple-element.28), channel_id=1, source_target_pairs={{1,2},{2,1},{3,4},{4,3},{5,6},{6,5},{7,8},{8,7},{9,10},{10,9},{11,... | collective-permute-start | bytes 49160 | tf_op jit(solution)/shard_map/ppermute | solution.py:683

commit v22 on v21

--- a/solution.py
+++ b/solution.py
@@ -87,19 +87,18 @@
 
 
 def in_rows(tiles):
-    row = lax.broadcasted_iota(jnp.int32, (8, LANES), 0)
-    total = jnp.zeros((8, LANES), jnp.float32)
+    row = lax.broadcasted_iota(jnp.int32, tiles[0].shape, 0)
+    total = jnp.zeros(tiles[0].shape, jnp.float32)
     for n, tile in enumerate(tiles):
         total = jnp.where(row == n, sublane_sum(tile), total)
     return total
 
 
-GROUPS = tuple((a, r) for a in range(2) for r in range(0, ROWS, CHUNK))
-VECTOR_GROUPS, MATRIX_GROUPS = GROUPS[:2], GROUPS[2:]
-
-
-def restrict(held, field, sums, lines):
-    lines[2 * CHUNK :] = jnp.zeros((LANES - 2 * CHUNK, lines.shape[1]), jnp.bfloat16)
+VECTOR_GROUPS = tuple((0, r) for r in range(0, ROWS, CHUNK))
+MATRIX_GROUPS = tuple((1, r) for r in range(0, ROWS, CHUNK))
+
+
+def restrict(held, field, sums, lines, others):
     blocks = []
     for g, (a, r) in enumerate(MATRIX_GROUPS):
         part, cells = field[a, r : r + CHUNK], slice(CELLS * g, CELLS * (g + 1))
@@ -113,21 +112,25 @@
         (((1,), (1,)), ((), ())),
         preferred_element_type=jnp.float32,
     )
-    row = lax.broadcasted_iota(jnp.int32, (CHUNK, LANES), 0)
-    equal = row == lax.broadcasted_iota(jnp.int32, (CHUNK, LANES), 1) % CHUNK
+    row = lax.broadcasted_iota(jnp.int32, (CHUNK, 2 * CHUNK), 0)
+    equal = row == lax.broadcasted_iota(jnp.int32, (CHUNK, 2 * CHUNK), 1) % CHUNK
+    others[...] = jnp.zeros_like(others)
     for first in range(0, VECTORS, PIECE):
-        totals = [
-            jnp.where(equal, products[CHUNK * k : CHUNK * (k + 1)], 0.0)
-            for k in range(first, first + PIECE)
-        ]
+        totals = [None] * PIECE
         for a, r in VECTOR_GROUPS:
             for c in range(0, CELLS, LANES):
                 rows, cells = slice(r, r + CHUNK), slice(c, c + LANES)
                 tile = field[a, rows, cells]
                 for n in range(PIECE):
                     term = held[first + n, a, rows, cells].astype(jnp.float32) * tile
-                    totals[n] = totals[n] + term
+                    totals[n] = term if totals[n] is None else totals[n] + term
         sums[first : first + PIECE] = in_rows([total[:8] + total[8:] for total in totals])
+        kept = [
+            jnp.where(equal, products[CHUNK * k : CHUNK * (k + 1)], 0.0)
+            for k in range(first, first + PIECE)
+        ]
+        others[first : first + PIECE, : 2 * CHUNK] = in_rows([x[:8] + x[8:] for x in kept])
+    sums[:VECTORS] += others[...]
 
 
 def fold(row):
@@ -262,7 +265,7 @@
         copy.wait()
 
 
-def restrict_kernel(rhs_ref, held, sums_ref, sums, lines):
+def restrict_kernel(rhs_ref, held, sums_ref, sums, lines, others):
     sums[...] = jnp.zeros_like(sums)
     squares = jnp.zeros((TILE, CELLS), jnp.float32)
     for a in range(2):
@@ -271,7 +274,7 @@
             squares = squares + tile * tile
     sums[VECTORS : VECTORS + 8] = in_rows([fold(squares)])
 
-    restrict(held, rhs_ref, sums, lines)
+    restrict(held, rhs_ref, sums, lines, others)
     send_sums(sums, sums_ref)
 
 
@@ -513,7 +516,7 @@
     coup_ref,
     direction_ref, image_ref, smooth_ref, residual_ref, factors_ref, partner_rows_ref, other_rows_ref,
     next_ref,
-    extended, sums, first_ref, solved, lines,
+    extended, sums, first_ref, solved, lines, others,
 ):
     low, high = neighbours_of(partner_ref, other_ref)
 
@@ -568,7 +571,7 @@
     sums[...] = jnp.zeros_like(sums)
     sums[VECTORS : VECTORS + 8] = in_rows([fold(products), fold(squares)])
 
-    restrict(held, image_ref, sums, lines)
+    restrict(held, image_ref, sums, lines, others)
     send_sums(sums, next_ref)
 
 
@@ -693,7 +696,8 @@
     stacked = pltpu.VMEM((2, STACKED, CELLS), jnp.float32)
     solved = pltpu.VMEM((4, STACKED, CELLS), jnp.float32)
     sums = pltpu.VMEM((SLOTS, LANES), jnp.float32)
-    lines = pltpu.VMEM((LANES, len(MATRIX_GROUPS) * CELLS), jnp.bfloat16)
+    lines = pltpu.VMEM((2 * CHUNK, len(MATRIX_GROUPS) * CELLS), jnp.bfloat16)
+    others = pltpu.VMEM((VECTORS, LANES), jnp.float32)
     row, whole, edge = f32(count, LANES), f32(2, ROWS, CELLS), f32(TILE, CELLS)
     packed, smoothed = f32(EDGE_AT + coarse_rows(columns), CELLS), f32(2, EXT, CELLS)
     arguments = (rhs, viscosity, coupling, coarse_inverse, coarse_basis)
@@ -706,13 +710,13 @@
     held, partner, other = lax.optimization_barrier((coarse_basis, *packs))
     partner, other = swap(partner, other)
     (first,) = call(
-        restrict_kernel, "restrict", [VMEM] * 2, [row], 10_000_000, [sums, lines]
+        restrict_kernel, "restrict", [VMEM] * 2, [row], 10_000_000, [sums, lines, others]
     )(rhs, held)
     first = from_everyone(first)
     direction, image, smooth, residual, factors, partner_rows, other_rows, second = call(
         functools.partial(first_turn_kernel, count), "first_turn", [SMEM] + [VMEM] * 8,
         [whole, whole, smoothed, f32(1, columns), f32(6, STACKED, CELLS), edge, edge, row], 20_000_000,
-        [extended, sums, stacked, solved, lines],
+        [extended, sums, stacked, solved, lines, others],
     )(margin_rows, first, coarse_inverse, partner, other, held, rhs, viscosity, coupling)
     partner_rows, other_rows = swap(partner_rows, other_rows)
     second = from_everyone(second)

time: 46 us -> 46 us (level)
  transfers between devices with their start and end apart: 4 -> 4, of which waited for: 0 -> 0; matrix products, arithmetic and copies ran while one was open for 0% -> 0% of each run, Pallas kernels for 4% -> 3%
where the time goes in v22:
time: 46 us; the launch traced here: 45.8 us
  blocking collectives  31.6 us (69%)
  Pallas kernels  11.3 us (25%)
  starting transfers between devices  1.99 us (4%)
  between operations  0.74 us (2%)
    all_to_all x3, blocking collectives, from_everyone(): lax.all_to_all(rows, 'sub', 0, 0, tiled=True, axis_index_groups=order)  31.6 us
    pallas_call x1, Pallas kernels, on_device(): call(functools.partial(first_turn_kernel, count), 'first_turn', [SMEM] +...  3.82 us
    pallas_call x1, Pallas kernels, on_device(): call(functools.partial(second_turn_kernel, count), 'second_turn', [SMEM]...  2.54 us
    pallas_call x1, Pallas kernels, on_device(): call(pack_kernel, 'pack', [HBM] * 5, [packed, packed], 5000000, [pltpu.VM...  2.47 us
    pallas_call x1, Pallas kernels, on_device(): call(restrict_kernel, 'restrict', [VMEM] * 2, [row], 10000000, [sums, lin...  1.57 us
    ppermute x2, starting transfers between devices, swap(): lax.ppermute(other, 'sub', both(range(1, count - 1, 2)))  1.48 us
  transfers between devices with their start and end apart: 4, of which 0 were waited for; matrix products, arithmetic and copies ran while one was open for 0% of the time, Pallas kernels for 3%

profile of v22, /device:TPU:0, one launch (start us, length us, event | category | flops | bytes accessed | tf_op | source)
XLA Modules:
  0.0 45.8 jit_solution(8209011636666975472)
XLA Ops:
  0.6 0.0 copy-start.1
  0.6 0.0 copy-start.3
  0.7 0.0 copy-start.2
  0.7 0.0 copy-start.4
  0.7 0.0 copy-start
  0.7 0.0 copy-start.5
  0.7 2.5 %pack.1 = (f32[192,512]{1,0:T(8,128)S(1)}, f32[192,512]{1,0:T(8,128)S(1)}) custom-call(f32[2,64,512]{2,1,0:T(8,128)} %rhs_ref.7, f32[64,512]{1,0:T(8,128)} %visc_ref.5, f32[2,64,512]{2,1,0:T(8,128)} %coup_ref.5, f32[48,768]{1,0:T(8,128)} %inverse_ref.5, bf16[48,2,64,512]{3,2,1,0:T(8,128)(2,1)} %held.2), custom_call_target="tpu_custom_call" | custom-call | flops 5000000 | bytes 4000000 | tf_op jit(solution)/shard_map/pack/pallas_call | solution.py:704
  3.2 0.5 %collective-permute-start = (f32[192,512]{1,0:T(8,128)S(1)}, f32[192,512]{1,0:T(8,128)S(1)}, u32[]{:S(2)}, u32[]{:S(2)}) collective-permute-start(f32[192,512]{1,0:T(8,128)S(1)} %get-tuple-element.22), channel_id=1, source_target_pairs={{0,1},{1,0},{2,3},{3,2},{4,5},{5,4},{6,7},{7,6},{8,9},{9,8},{10,11... | collective-permute-start | bytes 1179656 | tf_op jit(solution)/shard_map/ppermute | solution.py:685
  3.7 0.8 %collective-permute-start.1 = (f32[192,512]{1,0:T(8,128)S(1)}, f32[192,512]{1,0:T(8,128)S(1)}, u32[]{:S(2)}, u32[]{:S(2)}) collective-permute-start(f32[192,512]{1,0:T(8,128)S(1)} %get-tuple-element.23), channel_id=1, source_target_pairs={{1,2},{2,1},{3,4},{4,3},{5,6},{6,5},{7,8},{8,7},{9,10},{10,9},{11,... | collective-permute-start | bytes 1179656 | tf_op jit(solution)/shard_map/ppermute | solution.py:686
  4.5 0.0 copy-done.1
  4.5 0.1 copy-done
  4.6 1.6 %restrict.1 = f32[16,128]{1,0:T(8,128)S(1)} custom-call(f32[2,64,512]{2,1,0:T(8,128)S(1)} %copy-done.1, bf16[48,2,64,512]{3,2,1,0:T(8,128)(2,1)S(1)} %copy-done), custom_call_target="tpu_custom_call" | custom-call | flops 10000000 | bytes 4000000 | tf_op jit(solution)/shard_map/restrict/pallas_call | solution.py:712
  6.2 11.8 %all_to_all.33 = f32[16,1,128]{2,1,0:T(1,128)S(1)} all-to-all(f32[16,1,128]{2,1,0:T(1,128)S(1)} %bitcast.19), channel_id=1, replica_groups={{15,14,13,12,11,10,9,8,7,6,5,4,3,2,1,0},{31,30,29,28,27,26,25,24,23,22,..., dimensions={0} | all-to-all | bytes 16384 | tf_op jit(solution)/shard_map/all_to_all | solution.py:678
  17.9 0.0 collective-permute-done.partner_ref
  18.0 0.0 collective-permute-done.1.other_ref
  18.0 0.0 copy-done.3
  18.0 0.0 copy-done.2
  18.0 0.0 copy-done.4
  18.0 0.0 copy-done.5
  18.0 3.8 %first_turn.1 = (f32[2,64,512]{2,1,0:T(8,128)S(1)}, f32[2,64,512]{2,1,0:T(8,128)S(1)}, f32[2,80,512]{2,1,0:T(8,128)S(1)}, f32[1,768]{1,0:T(1,128)S(1)}, f32[6,14...) custom-call(s32[16]{0:T(128)S(1)} %copy-done.5, ...), custom_call_target="tpu_custom_call" | custom-call | flops 20000000 | bytes 4000000 | tf_op jit(solution)/shard_map/first_turn/pallas_call | solution.py:716
  21.8 0.0 collective-permute-start.2
  21.8 0.7 %collective-permute-start.3 = (f32[8,512]{1,0:T(8,128)S(1)}, f32[8,512]{1,0:T(8,128)S(1)}, u32[]{:S(2)}, u32[]{:S(2)}) collective-permute-start(f32[8,512]{1,0:T(8,128)S(1)} %get-tuple-element.28), channel_id=1, source_target_pairs={{1,2},{2,1},{3,4},{4,3},{5,6},{6,5},{7,8},{8,7},{9,10},{10,9},{11,... | collective-permute-start | bytes 49160 | tf_op jit(solution)/shard_map/ppermute | solution.py:686
  22.5 11.4 %all_to_all.34 = f32[16,1,128]{2,1,0:T(1,128)S(1)} all-to-all(f32[16,1,128]{2,1,0:T(1,128)S(1)} %bitcast.20), channel_id=1, replica_groups={{15,14,13,12,11,10,9,8,7,6,5,4,3,2,1,0},{31,30,29,28,27,26,25,24,23,22,..., dimensions={0} | all-to-all | bytes 16384 | tf_op jit(solution)/shard_map/all_to_all | solution.py:678
  33.9 0.0 collective-permute-done.2.partner_rows_ref
  33.9 0.0 collective-permute-done.3.other_rows_ref
  34.0 2.5 %second_turn.1 = (f32[2,64,512]{2,1,0:T(8,128)S(1)}, f32[16,128]{1,0:T(8,128)S(1)}) custom-call(s32[16]{0:T(128)S(1)} %copy-done.5, f32[16,128]{1,0:T(8,128)S(1)} %bitcast.14, f32[16,128]{1,0:T(8,128)S(1)} %bitcast.16, f32[1,768]{1,0:T(1,128)S(1)} %get-tuple-element.25.residual_ref, f32[6,144,512]{2,1,0:T(8,128)S(1)} %get-tuple-element.26.factors_ref, ...), custom_call_target="tpu_custom_call" | custom-call | flops 20000000 | bytes 4000000 | tf_op jit(solution)/shard_map/second_turn/pallas_call | solution.py:723
  36.5 8.4 %all_to_all.35 = f32[16,1,128]{2,1,0:T(1,128)S(1)} all-to-all(f32[16,1,128]{2,1,0:T(1,128)S(1)} %bitcast.21), channel_id=1, replica_groups={{15,14,13,12,11,10,9,8,7,6,5,4,3,2,1,0},{31,30,29,28,27,26,25,24,23,22,..., dimensions={0} | all-to-all | bytes 16384 | tf_op jit(solution)/shard_map/all_to_all | solution.py:678
  44.9 0.9 %finish.1 = (f32[2,64,512]{2,1,0:T(8,128)}, f32[2,3]{1,0:T(2,128)}) custom-call(f32[16,128]{1,0:T(8,128)S(1)} %bitcast.15, f32[16,128]{1,0:T(8,128)S(1)} %bitcast.17, f32[16,128]{1,0:T(8,128)S(1)} %bitcast.18, f32[2,64,512]{2,1,0:T(8,128)S(1)} %get-tuple-element.32.first_direction_ref, f32[2,64,512]{2,1,0:T(8,128)S(1)} %get-tuple-element.33.second_direction_ref), custom_call_target="tpu_custom_call" | custom-call | flops 1000000 | bytes 4000000 | tf_op jit(solution)/shard_map/finish/pallas_call | solution.py:731
Async XLA Ops:
  0.6 3.9 %copy-start.1 = (f32[2,64,512]{2,1,0:T(8,128)S(1)}, f32[2,64,512]{2,1,0:T(8,128)}, u32[]{:S(2)}) copy-start(f32[2,64,512]{2,1,0:T(8,128)} %rhs_ref.7) | copy-start | bytes 786436
  0.6 17.3 %copy-start.3 = (f32[48,768]{1,0:T(8,128)S(1)}, f32[48,768]{1,0:T(8,128)}, u32[]{:S(2)}) copy-start(f32[48,768]{1,0:T(8,128)} %inverse_ref.5) | copy-start | bytes 442372
  0.7 17.3 %copy-start.2 = (f32[2,64,512]{2,1,0:T(8,128)S(1)}, f32[2,64,512]{2,1,0:T(8,128)}, u32[]{:S(2)}) copy-start(f32[2,64,512]{2,1,0:T(8,128)} %coup_ref.5) | copy-start | bytes 786436
  0.7 17.3 %copy-start.4 = (f32[64,512]{1,0:T(8,128)S(1)}, f32[64,512]{1,0:T(8,128)}, u32[]{:S(2)}) copy-start(f32[64,512]{1,0:T(8,128)} %visc_ref.5) | copy-start | bytes 393220
  0.7 3.9 %copy-start = (bf16[48,2,64,512]{3,2,1,0:T(8,128)(2,1)S(1)}, bf16[48,2,64,512]{3,2,1,0:T(8,128)(2,1)}, u32[]{:S(2)}) copy-start(bf16[48,2,64,512]{3,2,1,0:T(8,128)(2,1)} %held.2) | copy-start | bytes 18874372
  0.7 17.3 %copy-start.5 = (s32[16]{0:T(128)S(1)}, s32[16]{0:T(128)}, u32[]{:S(2)}) copy-start(s32[16]{0:T(128)} %margin_ref.3) | copy-start | bytes 196
  3.2 14.8 %collective-permute-start = (f32[192,512]{1,0:T(8,128)S(1)}, f32[192,512]{1,0:T(8,128)S(1)}, u32[]{:S(2)}, u32[]{:S(2)}) collective-permute-start(f32[192,512]{1,0:T(8,128)S(1)} %get-tuple-element.22), channel_id=1, source_target_pairs={{0,1},{1,0},{2,3},{3,2},{4,5},{5,4},{6,7},{7,6},{8,9},{9,8},{10,11... | collective-permute-start | bytes 1179656 | tf_op jit(solution)/shard_map/ppermute | solution.py:685
  3.7 14.3 %collective-permute-start.1 = (f32[192,512]{1,0:T(8,128)S(1)}, f32[192,512]{1,0:T(8,128)S(1)}, u32[]{:S(2)}, u32[]{:S(2)}) collective-permute-start(f32[192,512]{1,0:T(8,128)S(1)} %get-tuple-element.23), channel_id=1, source_target_pairs={{1,2},{2,1},{3,4},{4,3},{5,6},{6,5},{7,8},{8,7},{9,10},{10,9},{11,... | collective-permute-start | bytes 1179656 | tf_op jit(solution)/shard_map/ppermute | solution.py:686
  21.8 12.1 %collective-permute-start.2 = (f32[8,512]{1,0:T(8,128)S(1)}, f32[8,512]{1,0:T(8,128)S(1)}, u32[]{:S(2)}, u32[]{:S(2)}) collective-permute-start(f32[8,512]{1,0:T(8,128)S(1)} %get-tuple-element.27), channel_id=1, source_target_pairs={{0,1},{1,0},{2,3},{3,2},{4,5},{5,4},{6,7},{7,6},{8,9},{9,8},{10,11... | collective-permute-start | bytes 49160 | tf_op jit(solution)/shard_map/ppermute | solution.py:685
  21.8 12.1 %collective-permute-start.3 = (f32[8,512]{1,0:T(8,128)S(1)}, f32[8,512]{1,0:T(8,128)S(1)}, u32[]{:S(2)}, u32[]{:S(2)}) collective-permute-start(f32[8,512]{1,0:T(8,128)S(1)} %get-tuple-element.28), channel_id=1, source_target_pairs={{1,2},{2,1},{3,4},{4,3},{5,6},{6,5},{7,8},{8,7},{9,10},{10,9},{11,... | collective-permute-start | bytes 49160 | tf_op jit(solution)/shard_map/ppermute | solution.py:686

commit v23 on v20

--- a/solution.py
+++ b/solution.py
@@ -421,7 +421,7 @@
 
 
 def lift(inverse_ref, residual):
-    return rounded(jnp.sum(inverse_ref[...] * residual, 1, keepdims=True))
+    return jnp.sum(inverse_ref[...] * residual, 1, keepdims=True)
 
 
 def lift_packed(ref, residual):
@@ -443,7 +443,7 @@
             0,
         )
         total = term if total is None else total + term
-    return rounded(total)
+    return total
 
 
 def edge_values(ref, lifted):
@@ -475,7 +475,7 @@
             self.steps.append(functools.partial(self.edge, n))
 
     def lift_own(self):
-        self.own = lift(self.inverse, self.residual)
+        self.own = rounded(self.scaled(lift(self.inverse, self.residual), 2))
 
     def make_matrix(self):
         self.matrix = spread(self.own)
@@ -487,7 +487,7 @@
         )
 
     def lift_side(self, n):
-        self.lifted[n] = lift_packed(self.sides[n], self.residual)
+        self.lifted[n] = rounded(self.scaled(lift_packed(self.sides[n], self.residual), n))
 
     def edge(self, n):
         self.edges[n] = edge_values(self.sides[n], self.lifted[n])
@@ -529,7 +529,7 @@
 def first_turn_kernel(
     count, margin_ref, sums_ref, inverse_ref, partner_ref, other_ref, held, rhs_ref, visc_ref,
     coup_ref,
-    direction_ref, image_ref, smooth_ref, residual_ref, factors_ref, partner_rows_ref, other_rows_ref,
+    direction_ref, image_ref, smooth_ref, columns_ref, factors_ref, partner_rows_ref, other_rows_ref,
     next_ref,
     extended, sums, first_ref, solved, lines,
 ):
@@ -540,10 +540,15 @@
             coarse.over_beta = 1.0 / jnp.sqrt(lane_total(sums_ref[...], VECTORS))
 
         def line():
-            coarse.residual = line_up(sums_ref[...]) * coarse.over_beta
-            residual_ref[...] = coarse.residual
-
-        return [scale, line]
+            coarse.residual = line_up(sums_ref[...])
+
+        def scaled(column, n):
+            column = column * coarse.over_beta
+            columns_ref[n] = jnp.broadcast_to(column, (VECTORS, LANES))
+            return column
+
+        coarse.scaled = scaled
+        return [line, scale]
 
     coarse = Coarse(begin, inverse_ref, low, high, held, extended)
 
@@ -598,7 +603,7 @@
 
 
 def second_turn_kernel(
-    count, margin_ref, sums_ref, second_ref, residual_ref, factors_ref, inverse_ref, partner_ref, other_ref,
+    count, margin_ref, sums_ref, second_ref, columns_ref, factors_ref, inverse_ref, partner_ref, other_ref,
     partner_rows_ref, other_rows_ref, held, smooth_ref, rhs_ref, image_ref, visc_ref, coup_ref,
     direction_ref, next_ref,
     image_smooth, extended, sums, first_ref, solved,
@@ -611,10 +616,12 @@
             coarse.h_00, coarse.ratio, coarse.over = h_00, h_00 / beta, 1.0 / h_10
 
         def line():
-            lined = line_up(second_ref[...])
-            coarse.residual = (lined - coarse.h_00 * residual_ref[...]) * coarse.over
-
-        return [scale, line]
+            coarse.residual = line_up(second_ref[...])
+
+        coarse.scaled = lambda column, n: (
+            (column - coarse.h_00 * columns_ref[n][:, :1]) * coarse.over
+        )
+        return [line, scale]
 
     coarse = Coarse(begin, inverse_ref, low, high, held, extended)
     low_rows, high_rows = neighbours_of(partner_rows_ref, other_rows_ref)
@@ -727,9 +734,9 @@
         restrict_kernel, "restrict", [VMEM] * 2, [row], 10_000_000, [sums]
     )(rhs, held)
     first = from_everyone(first)
-    direction, image, smooth, residual, factors, partner_rows, other_rows, second = call(
+    direction, image, smooth, lifts, factors, partner_rows, other_rows, second = call(
         functools.partial(first_turn_kernel, count), "first_turn", [SMEM] + [VMEM] * 8,
-        [whole, whole, smoothed, f32(1, columns), f32(6, STACKED, CELLS), edge, edge, row], 20_000_000,
+        [whole, whole, smoothed, f32(3, VECTORS, LANES), f32(6, STACKED, CELLS), edge, edge, row], 20_000_000,
         [extended, sums, stacked, solved, lines],
     )(margin_rows, first, coarse_inverse, partner, other, held, rhs, viscosity, coupling)
     partner_rows, other_rows = swap(partner_rows, other_rows)
@@ -738,7 +745,7 @@
         functools.partial(second_turn_kernel, count), "second_turn", [SMEM] + [VMEM] * 15,
         [whole, row], 20_000_000, [extended, extended, sums, stacked, solved],
     )(
-        margin_rows, first, second, residual, factors, coarse_inverse, partner, other, partner_rows, other_rows,
+        margin_rows, first, second, lifts, factors, coarse_inverse, partner, other, partner_rows, other_rows,
         held, smooth, rhs, image, viscosity, coupling,
     )
     third = from_everyone(third)

time: 45.8 us -> 46.7 us (1.020)
  Pallas kernels: 11 us -> 11.9 us
    pallas_call x1, Pallas kernels: 3.64 us -> 4.13 us  [on_device(): call(functools.partial(first_turn_kernel, count), 'first_turn', [SMEM] +...]
where the time goes in v23:
time: 46.7 us; the launch traced here: 46.4 us
  blocking collectives  31.7 us (68%)
  Pallas kernels  11.9 us (25%)
  starting transfers between devices  1.99 us (4%)
  between operations  0.74 us (2%)
    all_to_all x3, blocking collectives, from_everyone(): lax.all_to_all(rows, 'sub', 0, 0, tiled=True, axis_index_groups=order)  31.7 us
    pallas_call x1, Pallas kernels, on_device(): call(functools.partial(first_turn_kernel, count), 'first_turn', [SMEM] +...  4.13 us
    pallas_call x1, Pallas kernels, on_device(): call(functools.partial(second_turn_kernel, count), 'second_turn', [SMEM]...  2.88 us
    pallas_call x1, Pallas kernels, on_device(): call(pack_kernel, 'pack', [HBM] * 5, [packed, packed], 5000000, [pltpu.VM...  2.47 us
    pallas_call x1, Pallas kernels, on_device(): call(restrict_kernel, 'restrict', [VMEM] * 2, [row], 10000000, [sums])  1.48 us
    ppermute x2, starting transfers between devices, swap(): lax.ppermute(other, 'sub', both(range(1, count - 1, 2)))  1.48 us
  transfers between devices with their start and end apart: 4, of which 0 were waited for; matrix products, arithmetic and copies ran while one was open for 0% of the time, Pallas kernels for 3%

profile of v23, /device:TPU:0, one launch (start us, length us, event | category | flops | bytes accessed | tf_op | source)
XLA Modules:
  0.0 46.4 jit_solution(6299664879744733256)
XLA Ops:
  0.6 0.0 copy-start.1
  0.6 0.0 copy-start.3
  0.7 0.0 copy-start.2
  0.7 0.0 copy-start.4
  0.7 0.0 copy-start
  0.7 0.0 copy-start.5
  0.7 2.5 %pack.1 = (f32[192,512]{1,0:T(8,128)S(1)}, f32[192,512]{1,0:T(8,128)S(1)}) custom-call(f32[2,64,512]{2,1,0:T(8,128)} %rhs_ref.7, f32[64,512]{1,0:T(8,128)} %visc_ref.5, f32[2,64,512]{2,1,0:T(8,128)} %coup_ref.5, f32[48,768]{1,0:T(8,128)} %inverse_ref.5, bf16[48,2,64,512]{3,2,1,0:T(8,128)(2,1)} %held.2), custom_call_target="tpu_custom_call" | custom-call | flops 5000000 | bytes 4000000 | tf_op jit(solution)/shard_map/pack/pallas_call | solution.py:725
  3.2 0.5 %collective-permute-start = (f32[192,512]{1,0:T(8,128)S(1)}, f32[192,512]{1,0:T(8,128)S(1)}, u32[]{:S(2)}, u32[]{:S(2)}) collective-permute-start(f32[192,512]{1,0:T(8,128)S(1)} %get-tuple-element.22), channel_id=1, source_target_pairs={{0,1},{1,0},{2,3},{3,2},{4,5},{5,4},{6,7},{7,6},{8,9},{9,8},{10,11... | collective-permute-start | bytes 1179656 | tf_op jit(solution)/shard_map/ppermute | solution.py:707
  3.7 0.8 %collective-permute-start.1 = (f32[192,512]{1,0:T(8,128)S(1)}, f32[192,512]{1,0:T(8,128)S(1)}, u32[]{:S(2)}, u32[]{:S(2)}) collective-permute-start(f32[192,512]{1,0:T(8,128)S(1)} %get-tuple-element.23), channel_id=1, source_target_pairs={{1,2},{2,1},{3,4},{4,3},{5,6},{6,5},{7,8},{8,7},{9,10},{10,9},{11,... | collective-permute-start | bytes 1179656 | tf_op jit(solution)/shard_map/ppermute | solution.py:708
  4.5 0.0 copy-done.1
  4.5 0.1 copy-done
  4.6 1.5 %restrict.1 = f32[16,128]{1,0:T(8,128)S(1)} custom-call(f32[2,64,512]{2,1,0:T(8,128)S(1)} %copy-done.1, bf16[48,2,64,512]{3,2,1,0:T(8,128)(2,1)S(1)} %copy-done), custom_call_target="tpu_custom_call" | custom-call | flops 10000000 | bytes 4000000 | tf_op jit(solution)/shard_map/restrict/pallas_call | solution.py:733
  6.1 11.7 %all_to_all.33 = f32[16,1,128]{2,1,0:T(1,128)S(1)} all-to-all(f32[16,1,128]{2,1,0:T(1,128)S(1)} %bitcast.19), channel_id=1, replica_groups={{15,14,13,12,11,10,9,8,7,6,5,4,3,2,1,0},{31,30,29,28,27,26,25,24,23,22,..., dimensions={0} | all-to-all | bytes 16384 | tf_op jit(solution)/shard_map/all_to_all | solution.py:700
  17.9 0.0 collective-permute-done.partner_ref
  17.9 0.0 collective-permute-done.1.other_ref
  17.9 0.0 copy-done.3
  17.9 0.0 copy-done.2
  17.9 0.0 copy-done.4
  17.9 0.0 copy-done.5
  17.9 4.1 %first_turn.1 = (f32[2,64,512]{2,1,0:T(8,128)S(1)}, f32[2,64,512]{2,1,0:T(8,128)S(1)}, f32[2,80,512]{2,1,0:T(8,128)S(1)}, f32[3,48,128]{2,1,0:T(8,128)S(1)}, f32...) custom-call(s32[16]{0:T(128)S(1)} %copy-done.5, ...), custom_call_target="tpu_custom_call" | custom-call | flops 20000000 | bytes 4000000 | tf_op jit(solution)/shard_map/first_turn/pallas_call | solution.py:737
  22.0 0.0 collective-permute-start.2
  22.0 0.7 %collective-permute-start.3 = (f32[8,512]{1,0:T(8,128)S(1)}, f32[8,512]{1,0:T(8,128)S(1)}, u32[]{:S(2)}, u32[]{:S(2)}) collective-permute-start(f32[8,512]{1,0:T(8,128)S(1)} %get-tuple-element.28), channel_id=1, source_target_pairs={{1,2},{2,1},{3,4},{4,3},{5,6},{6,5},{7,8},{8,7},{9,10},{10,9},{11,... | collective-permute-start | bytes 49160 | tf_op jit(solution)/shard_map/ppermute | solution.py:708
  22.7 11.5 %all_to_all.34 = f32[16,1,128]{2,1,0:T(1,128)S(1)} all-to-all(f32[16,1,128]{2,1,0:T(1,128)S(1)} %bitcast.20), channel_id=1, replica_groups={{15,14,13,12,11,10,9,8,7,6,5,4,3,2,1,0},{31,30,29,28,27,26,25,24,23,22,..., dimensions={0} | all-to-all | bytes 16384 | tf_op jit(solution)/shard_map/all_to_all | solution.py:700
  34.2 0.0 collective-permute-done.2.partner_rows_ref
  34.3 0.0 collective-permute-done.3.other_rows_ref
  34.3 2.9 %second_turn.1 = (f32[2,64,512]{2,1,0:T(8,128)S(1)}, f32[16,128]{1,0:T(8,128)S(1)}) custom-call(s32[16]{0:T(128)S(1)} %copy-done.5, f32[16,128]{1,0:T(8,128)S(1)} %bitcast.14, f32[16,128]{1,0:T(8,128)S(1)} %bitcast.16, f32[3,48,128]{2,1,0:T(8,128)S(1)} %get-tuple-element.25.columns_ref, f32[6,144,512]{2,1,0:T(8,128)S(1)} %get-tuple-element.26.factors_ref, ...), custom_call_target="tpu_custom_call" | custom-call | flops 20000000 | bytes 4000000 | tf_op jit(solution)/shard_map/second_turn/pallas_call | solution.py:744
  37.1 8.4 %all_to_all.35 = f32[16,1,128]{2,1,0:T(1,128)S(1)} all-to-all(f32[16,1,128]{2,1,0:T(1,128)S(1)} %bitcast.21), channel_id=1, replica_groups={{15,14,13,12,11,10,9,8,7,6,5,4,3,2,1,0},{31,30,29,28,27,26,25,24,23,22,..., dimensions={0} | all-to-all | bytes 16384 | tf_op jit(solution)/shard_map/all_to_all | solution.py:700
  45.5 0.9 %finish.1 = (f32[2,64,512]{2,1,0:T(8,128)}, f32[2,3]{1,0:T(2,128)}) custom-call(f32[16,128]{1,0:T(8,128)S(1)} %bitcast.15, f32[16,128]{1,0:T(8,128)S(1)} %bitcast.17, f32[16,128]{1,0:T(8,128)S(1)} %bitcast.18, f32[2,64,512]{2,1,0:T(8,128)S(1)} %get-tuple-element.32.first_direction_ref, f32[2,64,512]{2,1,0:T(8,128)S(1)} %get-tuple-element.33.second_direction_ref), custom_call_target="tpu_custom_call" | custom-call | flops 1000000 | bytes 4000000 | tf_op jit(solution)/shard_map/finish/pallas_call | solution.py:752
Async XLA Ops:
  0.6 3.9 %copy-start.1 = (f32[2,64,512]{2,1,0:T(8,128)S(1)}, f32[2,64,512]{2,1,0:T(8,128)}, u32[]{:S(2)}) copy-start(f32[2,64,512]{2,1,0:T(8,128)} %rhs_ref.7) | copy-start | bytes 786436
  0.6 17.2 %copy-start.3 = (f32[48,768]{1,0:T(8,128)S(1)}, f32[48,768]{1,0:T(8,128)}, u32[]{:S(2)}) copy-start(f32[48,768]{1,0:T(8,128)} %inverse_ref.5) | copy-start | bytes 442372
  0.7 17.2 %copy-start.2 = (f32[2,64,512]{2,1,0:T(8,128)S(1)}, f32[2,64,512]{2,1,0:T(8,128)}, u32[]{:S(2)}) copy-start(f32[2,64,512]{2,1,0:T(8,128)} %coup_ref.5) | copy-start | bytes 786436
  0.7 17.2 %copy-start.4 = (f32[64,512]{1,0:T(8,128)S(1)}, f32[64,512]{1,0:T(8,128)}, u32[]{:S(2)}) copy-start(f32[64,512]{1,0:T(8,128)} %visc_ref.5) | copy-start | bytes 393220
  0.7 3.9 %copy-start = (bf16[48,2,64,512]{3,2,1,0:T(8,128)(2,1)S(1)}, bf16[48,2,64,512]{3,2,1,0:T(8,128)(2,1)}, u32[]{:S(2)}) copy-start(bf16[48,2,64,512]{3,2,1,0:T(8,128)(2,1)} %held.2) | copy-start | bytes 18874372
  0.7 17.2 %copy-start.5 = (s32[16]{0:T(128)S(1)}, s32[16]{0:T(128)}, u32[]{:S(2)}) copy-start(s32[16]{0:T(128)} %margin_ref.3) | copy-start | bytes 196
  3.2 14.7 %collective-permute-start = (f32[192,512]{1,0:T(8,128)S(1)}, f32[192,512]{1,0:T(8,128)S(1)}, u32[]{:S(2)}, u32[]{:S(2)}) collective-permute-start(f32[192,512]{1,0:T(8,128)S(1)} %get-tuple-element.22), channel_id=1, source_target_pairs={{0,1},{1,0},{2,3},{3,2},{4,5},{5,4},{6,7},{7,6},{8,9},{9,8},{10,11... | collective-permute-start | bytes 1179656 | tf_op jit(solution)/shard_map/ppermute | solution.py:707
  3.7 14.2 %collective-permute-start.1 = (f32[192,512]{1,0:T(8,128)S(1)}, f32[192,512]{1,0:T(8,128)S(1)}, u32[]{:S(2)}, u32[]{:S(2)}) collective-permute-start(f32[192,512]{1,0:T(8,128)S(1)} %get-tuple-element.23), channel_id=1, source_target_pairs={{1,2},{2,1},{3,4},{4,3},{5,6},{6,5},{7,8},{8,7},{9,10},{10,9},{11,... | collective-permute-start | bytes 1179656 | tf_op jit(solution)/shard_map/ppermute | solution.py:708
  22.0 12.2 %collective-permute-start.2 = (f32[8,512]{1,0:T(8,128)S(1)}, f32[8,512]{1,0:T(8,128)S(1)}, u32[]{:S(2)}, u32[]{:S(2)}) collective-permute-start(f32[8,512]{1,0:T(8,128)S(1)} %get-tuple-element.27), channel_id=1, source_target_pairs={{0,1},{1,0},{2,3},{3,2},{4,5},{5,4},{6,7},{7,6},{8,9},{9,8},{10,11... | collective-permute-start | bytes 49160 | tf_op jit(solution)/shard_map/ppermute | solution.py:707
  22.0 12.2 %collective-permute-start.3 = (f32[8,512]{1,0:T(8,128)S(1)}, f32[8,512]{1,0:T(8,128)S(1)}, u32[]{:S(2)}, u32[]{:S(2)}) collective-permute-start(f32[8,512]{1,0:T(8,128)S(1)} %get-tuple-element.28), channel_id=1, source_target_pairs={{1,2},{2,1},{3,4},{4,3},{5,6},{6,5},{7,8},{8,7},{9,10},{10,9},{11,... | collective-permute-start | bytes 49160 | tf_op jit(solution)/shard_map/ppermute | solution.py:708

commit v24 on v20

--- a/solution.py
+++ b/solution.py
@@ -399,13 +399,19 @@
                         out_ref[a, tile_rows(e)] += weight_of(n, e) * value
 
 
+def gather_order(count):
+    return sorted(range(count), key=lambda rank: (abs(2 * rank - count + 1), -rank))
+
+
 def line_up(residuals):
     devices = residuals.shape[0]
+    order = gather_order(devices)
     lane = lax.broadcasted_iota(jnp.int32, (1, LANES), 1)
     tiles = [jnp.zeros((1, LANES), jnp.float32) for _ in range(devices * VECTORS // LANES)]
     for t in range(devices):
         tile, offset = divmod(VECTORS * t, LANES)
-        row = jnp.where(lane < VECTORS, residuals[devices - 1 - t : devices - t], 0.0)
+        at = order.index(t)
+        row = jnp.where(lane < VECTORS, residuals[at : at + 1], 0.0)
         if offset:
             row = pltpu.roll(row, offset, 1)
         if offset + VECTORS <= LANES:
@@ -689,7 +695,7 @@
 
 
 def from_everyone(rows):
-    order = [list(range(lax.axis_size("sub")))[::-1]]
+    order = [gather_order(lax.axis_size("sub"))]
     return lax.all_to_all(rows, "sub", 0, 0, tiled=True, axis_index_groups=order)
 
 

time: 45.8 us -> 47.2 us (1.031)
  blocking collectives: 31.7 us -> 33 us
    all_to_all x3, blocking collectives: 31.7 us -> 33 us  [from_everyone(): lax.all_to_all(rows, 'sub', 0, 0, tiled=True, axis_index_groups=order)]
where the time goes in v24:
time: 47.2 us; the launch traced here: 46.9 us
  blocking collectives  33 us (70%)
  Pallas kernels  11 us (23%)
  starting transfers between devices  1.99 us (4%)
  between operations  0.74 us (2%)
    all_to_all x3, blocking collectives, from_everyone(): lax.all_to_all(rows, 'sub', 0, 0, tiled=True, axis_index_groups=order)  33 us
    pallas_call x1, Pallas kernels, on_device(): call(functools.partial(first_turn_kernel, count), 'first_turn', [SMEM] +...  3.64 us
    pallas_call x1, Pallas kernels, on_device(): call(functools.partial(second_turn_kernel, count), 'second_turn', [SMEM]...  2.54 us
    pallas_call x1, Pallas kernels, on_device(): call(pack_kernel, 'pack', [HBM] * 5, [packed, packed], 5000000, [pltpu.VM...  2.47 us
    ppermute x2, starting transfers between devices, swap(): lax.ppermute(other, 'sub', both(range(1, count - 1, 2)))  1.48 us
    pallas_call x1, Pallas kernels, on_device(): call(restrict_kernel, 'restrict', [VMEM] * 2, [row], 10000000, [sums])  1.44 us
  transfers between devices with their start and end apart: 4, of which 0 were waited for; matrix products, arithmetic and copies ran while one was open for 0% of the time, Pallas kernels for 3%

profile of v24, /device:TPU:0, one launch (start us, length us, event | category | flops | bytes accessed | tf_op | source)
XLA Modules:
  0.0 46.9 jit_solution(7362832794895529671)
XLA Ops:
  0.6 0.0 copy-start.1
  0.6 0.0 copy-start.3
  0.7 0.0 copy-start.2
  0.7 0.0 copy-start.4
  0.7 0.0 copy-start
  0.7 0.0 copy-start.5
  0.7 2.5 %pack.1 = (f32[192,512]{1,0:T(8,128)S(1)}, f32[192,512]{1,0:T(8,128)S(1)}) custom-call(f32[2,64,512]{2,1,0:T(8,128)} %rhs_ref.7, f32[64,512]{1,0:T(8,128)} %visc_ref.5, f32[2,64,512]{2,1,0:T(8,128)} %coup_ref.5, f32[48,768]{1,0:T(8,128)} %inverse_ref.5, bf16[48,2,64,512]{3,2,1,0:T(8,128)(2,1)} %held.2), custom_call_target="tpu_custom_call" | custom-call | flops 5000000 | bytes 4000000 | tf_op jit(solution)/shard_map/pack/pallas_call | solution.py:724
  3.2 0.5 %collective-permute-start = (f32[192,512]{1,0:T(8,128)S(1)}, f32[192,512]{1,0:T(8,128)S(1)}, u32[]{:S(2)}, u32[]{:S(2)}) collective-permute-start(f32[192,512]{1,0:T(8,128)S(1)} %get-tuple-element.22), channel_id=1, source_target_pairs={{0,1},{1,0},{2,3},{3,2},{4,5},{5,4},{6,7},{7,6},{8,9},{9,8},{10,11... | collective-permute-start | bytes 1179656 | tf_op jit(solution)/shard_map/ppermute | solution.py:706
  3.7 0.8 %collective-permute-start.1 = (f32[192,512]{1,0:T(8,128)S(1)}, f32[192,512]{1,0:T(8,128)S(1)}, u32[]{:S(2)}, u32[]{:S(2)}) collective-permute-start(f32[192,512]{1,0:T(8,128)S(1)} %get-tuple-element.23), channel_id=1, source_target_pairs={{1,2},{2,1},{3,4},{4,3},{5,6},{6,5},{7,8},{8,7},{9,10},{10,9},{11,... | collective-permute-start | bytes 1179656 | tf_op jit(solution)/shard_map/ppermute | solution.py:707
  4.5 0.0 copy-done.1
  4.5 0.1 copy-done
  4.6 1.4 %restrict.1 = f32[16,128]{1,0:T(8,128)S(1)} custom-call(f32[2,64,512]{2,1,0:T(8,128)S(1)} %copy-done.1, bf16[48,2,64,512]{3,2,1,0:T(8,128)(2,1)S(1)} %copy-done), custom_call_target="tpu_custom_call" | custom-call | flops 10000000 | bytes 4000000 | tf_op jit(solution)/shard_map/restrict/pallas_call | solution.py:732
  6.1 12.9 %all_to_all.33 = f32[16,1,128]{2,1,0:T(1,128)S(1)} all-to-all(f32[16,1,128]{2,1,0:T(1,128)S(1)} %bitcast.19), channel_id=1, replica_groups={{8,7,9,6,10,5,11,4,12,3,13,2,14,1,15,0},{24,23,25,22,26,21,27,20,28,19,..., dimensions={0} | all-to-all | bytes 16384 | tf_op jit(solution)/shard_map/all_to_all | solution.py:699
  19.0 0.0 collective-permute-done.partner_ref
  19.0 0.0 collective-permute-done.1.other_ref
  19.0 0.0 copy-done.3
  19.0 0.0 copy-done.2
  19.0 0.0 copy-done.4
  19.0 0.0 copy-done.5
  19.0 3.6 %first_turn.1 = (f32[2,64,512]{2,1,0:T(8,128)S(1)}, f32[2,64,512]{2,1,0:T(8,128)S(1)}, f32[2,80,512]{2,1,0:T(8,128)S(1)}, f32[1,768]{1,0:T(1,128)S(1)}, f32[6,14...) custom-call(s32[16]{0:T(128)S(1)} %copy-done.5, ...), custom_call_target="tpu_custom_call" | custom-call | flops 20000000 | bytes 4000000 | tf_op jit(solution)/shard_map/first_turn/pallas_call | solution.py:736
  22.7 0.0 collective-permute-start.2
  22.7 0.7 %collective-permute-start.3 = (f32[8,512]{1,0:T(8,128)S(1)}, f32[8,512]{1,0:T(8,128)S(1)}, u32[]{:S(2)}, u32[]{:S(2)}) collective-permute-start(f32[8,512]{1,0:T(8,128)S(1)} %get-tuple-element.28), channel_id=1, source_target_pairs={{1,2},{2,1},{3,4},{4,3},{5,6},{6,5},{7,8},{8,7},{9,10},{10,9},{11,... | collective-permute-start | bytes 49160 | tf_op jit(solution)/shard_map/ppermute | solution.py:707
  23.3 11.9 %all_to_all.34 = f32[16,1,128]{2,1,0:T(1,128)S(1)} all-to-all(f32[16,1,128]{2,1,0:T(1,128)S(1)} %bitcast.20), channel_id=1, replica_groups={{8,7,9,6,10,5,11,4,12,3,13,2,14,1,15,0},{24,23,25,22,26,21,27,20,28,19,..., dimensions={0} | all-to-all | bytes 16384 | tf_op jit(solution)/shard_map/all_to_all | solution.py:699
  35.3 0.0 collective-permute-done.2.partner_rows_ref
  35.3 0.0 collective-permute-done.3.other_rows_ref
  35.3 2.5 %second_turn.1 = (f32[2,64,512]{2,1,0:T(8,128)S(1)}, f32[16,128]{1,0:T(8,128)S(1)}) custom-call(s32[16]{0:T(128)S(1)} %copy-done.5, f32[16,128]{1,0:T(8,128)S(1)} %bitcast.14, f32[16,128]{1,0:T(8,128)S(1)} %bitcast.16, f32[1,768]{1,0:T(1,128)S(1)} %get-tuple-element.25.residual_ref, f32[6,144,512]{2,1,0:T(8,128)S(1)} %get-tuple-element.26.factors_ref, ...), custom_call_target="tpu_custom_call" | custom-call | flops 20000000 | bytes 4000000 | tf_op jit(solution)/shard_map/second_turn/pallas_call | solution.py:743
  37.8 8.2 %all_to_all.35 = f32[16,1,128]{2,1,0:T(1,128)S(1)} all-to-all(f32[16,1,128]{2,1,0:T(1,128)S(1)} %bitcast.21), channel_id=1, replica_groups={{8,7,9,6,10,5,11,4,12,3,13,2,14,1,15,0},{24,23,25,22,26,21,27,20,28,19,..., dimensions={0} | all-to-all | bytes 16384 | tf_op jit(solution)/shard_map/all_to_all | solution.py:699
  46.0 0.9 %finish.1 = (f32[2,64,512]{2,1,0:T(8,128)}, f32[2,3]{1,0:T(2,128)}) custom-call(f32[16,128]{1,0:T(8,128)S(1)} %bitcast.15, f32[16,128]{1,0:T(8,128)S(1)} %bitcast.17, f32[16,128]{1,0:T(8,128)S(1)} %bitcast.18, f32[2,64,512]{2,1,0:T(8,128)S(1)} %get-tuple-element.32.first_direction_ref, f32[2,64,512]{2,1,0:T(8,128)S(1)} %get-tuple-element.33.second_direction_ref), custom_call_target="tpu_custom_call" | custom-call | flops 1000000 | bytes 4000000 | tf_op jit(solution)/shard_map/finish/pallas_call | solution.py:751
Async XLA Ops:
  0.6 3.9 %copy-start.1 = (f32[2,64,512]{2,1,0:T(8,128)S(1)}, f32[2,64,512]{2,1,0:T(8,128)}, u32[]{:S(2)}) copy-start(f32[2,64,512]{2,1,0:T(8,128)} %rhs_ref.7) | copy-start | bytes 786436
  0.6 18.3 %copy-start.3 = (f32[48,768]{1,0:T(8,128)S(1)}, f32[48,768]{1,0:T(8,128)}, u32[]{:S(2)}) copy-start(f32[48,768]{1,0:T(8,128)} %inverse_ref.5) | copy-start | bytes 442372
  0.7 18.3 %copy-start.2 = (f32[2,64,512]{2,1,0:T(8,128)S(1)}, f32[2,64,512]{2,1,0:T(8,128)}, u32[]{:S(2)}) copy-start(f32[2,64,512]{2,1,0:T(8,128)} %coup_ref.5) | copy-start | bytes 786436
  0.7 18.3 %copy-start.4 = (f32[64,512]{1,0:T(8,128)S(1)}, f32[64,512]{1,0:T(8,128)}, u32[]{:S(2)}) copy-start(f32[64,512]{1,0:T(8,128)} %visc_ref.5) | copy-start | bytes 393220
  0.7 3.9 %copy-start = (bf16[48,2,64,512]{3,2,1,0:T(8,128)(2,1)S(1)}, bf16[48,2,64,512]{3,2,1,0:T(8,128)(2,1)}, u32[]{:S(2)}) copy-start(bf16[48,2,64,512]{3,2,1,0:T(8,128)(2,1)} %held.2) | copy-start | bytes 18874372
  0.7 18.3 %copy-start.5 = (s32[16]{0:T(128)S(1)}, s32[16]{0:T(128)}, u32[]{:S(2)}) copy-start(s32[16]{0:T(128)} %margin_ref.3) | copy-start | bytes 196
  3.2 15.8 %collective-permute-start = (f32[192,512]{1,0:T(8,128)S(1)}, f32[192,512]{1,0:T(8,128)S(1)}, u32[]{:S(2)}, u32[]{:S(2)}) collective-permute-start(f32[192,512]{1,0:T(8,128)S(1)} %get-tuple-element.22), channel_id=1, source_target_pairs={{0,1},{1,0},{2,3},{3,2},{4,5},{5,4},{6,7},{7,6},{8,9},{9,8},{10,11... | collective-permute-start | bytes 1179656 | tf_op jit(solution)/shard_map/ppermute | solution.py:706
  3.7 15.3 %collective-permute-start.1 = (f32[192,512]{1,0:T(8,128)S(1)}, f32[192,512]{1,0:T(8,128)S(1)}, u32[]{:S(2)}, u32[]{:S(2)}) collective-permute-start(f32[192,512]{1,0:T(8,128)S(1)} %get-tuple-element.23), channel_id=1, source_target_pairs={{1,2},{2,1},{3,4},{4,3},{5,6},{6,5},{7,8},{8,7},{9,10},{10,9},{11,... | collective-permute-start | bytes 1179656 | tf_op jit(solution)/shard_map/ppermute | solution.py:707
  22.7 12.6 %collective-permute-start.2 = (f32[8,512]{1,0:T(8,128)S(1)}, f32[8,512]{1,0:T(8,128)S(1)}, u32[]{:S(2)}, u32[]{:S(2)}) collective-permute-start(f32[8,512]{1,0:T(8,128)S(1)} %get-tuple-element.27), channel_id=1, source_target_pairs={{0,1},{1,0},{2,3},{3,2},{4,5},{5,4},{6,7},{7,6},{8,9},{9,8},{10,11... | collective-permute-start | bytes 49160 | tf_op jit(solution)/shard_map/ppermute | solution.py:706
  22.7 12.6 %collective-permute-start.3 = (f32[8,512]{1,0:T(8,128)S(1)}, f32[8,512]{1,0:T(8,128)S(1)}, u32[]{:S(2)}, u32[]{:S(2)}) collective-permute-start(f32[8,512]{1,0:T(8,128)S(1)} %get-tuple-element.28), channel_id=1, source_target_pairs={{1,2},{2,1},{3,4},{4,3},{5,6},{6,5},{7,8},{8,7},{9,10},{10,9},{11,... | collective-permute-start | bytes 49160 | tf_op jit(solution)/shard_map/ppermute | solution.py:707

commit v25 on v20

--- a/solution.py
+++ b/solution.py
@@ -466,13 +466,16 @@
     def __init__(self, begin, inverse_ref, low, high, held, extended):
         self.inverse, self.sides, self.held, self.extended = inverse_ref, (low, high), held, extended
         self.lifted, self.edges = [None] * 2, [None] * 2
-        self.steps = begin(self) + [self.lift_own, self.make_matrix]
-        for a in range(2):
-            for r in range(0, ROWS, CHUNK):
-                self.steps.append(functools.partial(self.prolong, a, r))
+        for step in begin(self) + [self.lift_own, self.make_matrix]:
+            step()
+        self.steps = [
+            functools.partial(self.prolong, a, r) for a in range(2) for r in range(0, ROWS, CHUNK)
+        ]
+
+    def finish_sides(self):
         for n in range(2):
-            self.steps.insert(len(self.steps) - 6, functools.partial(self.lift_side, n))
-            self.steps.append(functools.partial(self.edge, n))
+            self.lift_side(n)
+            self.edge(n)
 
     def lift_own(self):
         self.own = lift(self.inverse, self.residual)
@@ -566,6 +569,7 @@
         count, margin_ref, factors_ref, make, field, smooth_ref, first_ref, solved, coarse.steps
     )
     smooth = lambda a, t: smooth_ref[a, tile_rows(t)] * coarse.over_beta
+    coarse.finish_sides()
     images = apply_operator(
         coarse.edges, smooth, extended, visc_ref, coup_ref, direction_ref
     )
@@ -633,6 +637,7 @@
         rows = tile_rows(t)
         return (image_smooth[a, rows] - coarse.ratio * smooth_ref[a, rows]) * coarse.over
 
+    coarse.finish_sides()
     images = apply_operator(
         coarse.edges, smooth, extended, visc_ref, coup_ref, direction_ref
     )

time: 45.8 us -> 45.8 us (level)
  no operation moved by 1% of the time
where the time goes in v25:
time: 45.8 us; the launch traced here: 45.5 us
  blocking collectives  31.7 us (69%)
  Pallas kernels  10.9 us (24%)
  starting transfers between devices  1.99 us (4%)
  between operations  0.74 us (2%)
    all_to_all x3, blocking collectives, from_everyone(): lax.all_to_all(rows, 'sub', 0, 0, tiled=True, axis_index_groups=order)  31.7 us
    pallas_call x1, Pallas kernels, on_device(): call(functools.partial(first_turn_kernel, count), 'first_turn', [SMEM] +...  3.64 us
    pallas_call x1, Pallas kernels, on_device(): call(functools.partial(second_turn_kernel, count), 'second_turn', [SMEM]...  2.48 us
    pallas_call x1, Pallas kernels, on_device(): call(pack_kernel, 'pack', [HBM] * 5, [packed, packed], 5000000, [pltpu.VM...  2.47 us
    ppermute x2, starting transfers between devices, swap(): lax.ppermute(other, 'sub', both(range(1, count - 1, 2)))  1.48 us
    pallas_call x1, Pallas kernels, on_device(): call(restrict_kernel, 'restrict', [VMEM] * 2, [row], 10000000, [sums])  1.44 us
  transfers between devices with their start and end apart: 4, of which 0 were waited for; matrix products, arithmetic and copies ran while one was open for 0% of the time, Pallas kernels for 3%

profile of v25, /device:TPU:0, one launch (start us, length us, event | category | flops | bytes accessed | tf_op | source)
XLA Modules:
  0.0 45.5 jit_solution(2790975889510503627)
XLA Ops:
  0.6 0.0 copy-start.1
  0.6 0.0 copy-start.3
  0.7 0.0 copy-start.2
  0.7 0.0 copy-start.4
  0.7 0.0 copy-start
  0.7 0.0 copy-start.5
  0.7 2.5 %pack.1 = (f32[192,512]{1,0:T(8,128)S(1)}, f32[192,512]{1,0:T(8,128)S(1)}) custom-call(f32[2,64,512]{2,1,0:T(8,128)} %rhs_ref.7, f32[64,512]{1,0:T(8,128)} %visc_ref.5, f32[2,64,512]{2,1,0:T(8,128)} %coup_ref.5, f32[48,768]{1,0:T(8,128)} %inverse_ref.5, bf16[48,2,64,512]{3,2,1,0:T(8,128)(2,1)} %held.2), custom_call_target="tpu_custom_call" | custom-call | flops 5000000 | bytes 4000000 | tf_op jit(solution)/shard_map/pack/pallas_call | solution.py:723
  3.2 0.5 %collective-permute-start = (f32[192,512]{1,0:T(8,128)S(1)}, f32[192,512]{1,0:T(8,128)S(1)}, u32[]{:S(2)}, u32[]{:S(2)}) collective-permute-start(f32[192,512]{1,0:T(8,128)S(1)} %get-tuple-element.22), channel_id=1, source_target_pairs={{0,1},{1,0},{2,3},{3,2},{4,5},{5,4},{6,7},{7,6},{8,9},{9,8},{10,11... | collective-permute-start | bytes 1179656 | tf_op jit(solution)/shard_map/ppermute | solution.py:705
  3.7 0.8 %collective-permute-start.1 = (f32[192,512]{1,0:T(8,128)S(1)}, f32[192,512]{1,0:T(8,128)S(1)}, u32[]{:S(2)}, u32[]{:S(2)}) collective-permute-start(f32[192,512]{1,0:T(8,128)S(1)} %get-tuple-element.23), channel_id=1, source_target_pairs={{1,2},{2,1},{3,4},{4,3},{5,6},{6,5},{7,8},{8,7},{9,10},{10,9},{11,... | collective-permute-start | bytes 1179656 | tf_op jit(solution)/shard_map/ppermute | solution.py:706
  4.5 0.0 copy-done.1
  4.5 0.1 copy-done
  4.6 1.4 %restrict.1 = f32[16,128]{1,0:T(8,128)S(1)} custom-call(f32[2,64,512]{2,1,0:T(8,128)S(1)} %copy-done.1, bf16[48,2,64,512]{3,2,1,0:T(8,128)(2,1)S(1)} %copy-done), custom_call_target="tpu_custom_call" | custom-call | flops 10000000 | bytes 4000000 | tf_op jit(solution)/shard_map/restrict/pallas_call | solution.py:731
  6.1 11.7 %all_to_all.33 = f32[16,1,128]{2,1,0:T(1,128)S(1)} all-to-all(f32[16,1,128]{2,1,0:T(1,128)S(1)} %bitcast.19), channel_id=1, replica_groups={{15,14,13,12,11,10,9,8,7,6,5,4,3,2,1,0},{31,30,29,28,27,26,25,24,23,22,..., dimensions={0} | all-to-all | bytes 16384 | tf_op jit(solution)/shard_map/all_to_all | solution.py:698
  17.8 0.0 collective-permute-done.partner_ref
  17.8 0.0 collective-permute-done.1.other_ref
  17.8 0.0 copy-done.3
  17.8 0.0 copy-done.2
  17.8 0.0 copy-done.4
  17.8 0.0 copy-done.5
  17.8 3.6 %first_turn.1 = (f32[2,64,512]{2,1,0:T(8,128)S(1)}, f32[2,64,512]{2,1,0:T(8,128)S(1)}, f32[2,80,512]{2,1,0:T(8,128)S(1)}, f32[1,768]{1,0:T(1,128)S(1)}, f32[6,14...) custom-call(s32[16]{0:T(128)S(1)} %copy-done.5, ...), custom_call_target="tpu_custom_call" | custom-call | flops 20000000 | bytes 4000000 | tf_op jit(solution)/shard_map/first_turn/pallas_call | solution.py:735
  21.5 0.0 collective-permute-start.2
  21.5 0.7 %collective-permute-start.3 = (f32[8,512]{1,0:T(8,128)S(1)}, f32[8,512]{1,0:T(8,128)S(1)}, u32[]{:S(2)}, u32[]{:S(2)}) collective-permute-start(f32[8,512]{1,0:T(8,128)S(1)} %get-tuple-element.28), channel_id=1, source_target_pairs={{1,2},{2,1},{3,4},{4,3},{5,6},{6,5},{7,8},{8,7},{9,10},{10,9},{11,... | collective-permute-start | bytes 49160 | tf_op jit(solution)/shard_map/ppermute | solution.py:706
  22.2 11.6 %all_to_all.34 = f32[16,1,128]{2,1,0:T(1,128)S(1)} all-to-all(f32[16,1,128]{2,1,0:T(1,128)S(1)} %bitcast.20), channel_id=1, replica_groups={{15,14,13,12,11,10,9,8,7,6,5,4,3,2,1,0},{31,30,29,28,27,26,25,24,23,22,..., dimensions={0} | all-to-all | bytes 16384 | tf_op jit(solution)/shard_map/all_to_all | solution.py:698
  33.8 0.0 collective-permute-done.2.partner_rows_ref
  33.8 0.0 collective-permute-done.3.other_rows_ref
  33.8 2.5 %second_turn.1 = (f32[2,64,512]{2,1,0:T(8,128)S(1)}, f32[16,128]{1,0:T(8,128)S(1)}) custom-call(s32[16]{0:T(128)S(1)} %copy-done.5, f32[16,128]{1,0:T(8,128)S(1)} %bitcast.14, f32[16,128]{1,0:T(8,128)S(1)} %bitcast.16, f32[1,768]{1,0:T(1,128)S(1)} %get-tuple-element.25.residual_ref, f32[6,144,512]{2,1,0:T(8,128)S(1)} %get-tuple-element.26.factors_ref, ...), custom_call_target="tpu_custom_call" | custom-call | flops 20000000 | bytes 4000000 | tf_op jit(solution)/shard_map/second_turn/pallas_call | solution.py:742
  36.2 8.4 %all_to_all.35 = f32[16,1,128]{2,1,0:T(1,128)S(1)} all-to-all(f32[16,1,128]{2,1,0:T(1,128)S(1)} %bitcast.21), channel_id=1, replica_groups={{15,14,13,12,11,10,9,8,7,6,5,4,3,2,1,0},{31,30,29,28,27,26,25,24,23,22,..., dimensions={0} | all-to-all | bytes 16384 | tf_op jit(solution)/shard_map/all_to_all | solution.py:698
  44.6 0.9 %finish.1 = (f32[2,64,512]{2,1,0:T(8,128)}, f32[2,3]{1,0:T(2,128)}) custom-call(f32[16,128]{1,0:T(8,128)S(1)} %bitcast.15, f32[16,128]{1,0:T(8,128)S(1)} %bitcast.17, f32[16,128]{1,0:T(8,128)S(1)} %bitcast.18, f32[2,64,512]{2,1,0:T(8,128)S(1)} %get-tuple-element.32.first_direction_ref, f32[2,64,512]{2,1,0:T(8,128)S(1)} %get-tuple-element.33.second_direction_ref), custom_call_target="tpu_custom_call" | custom-call | flops 1000000 | bytes 4000000 | tf_op jit(solution)/shard_map/finish/pallas_call | solution.py:750
Async XLA Ops:
  0.6 3.9 %copy-start.1 = (f32[2,64,512]{2,1,0:T(8,128)S(1)}, f32[2,64,512]{2,1,0:T(8,128)}, u32[]{:S(2)}) copy-start(f32[2,64,512]{2,1,0:T(8,128)} %rhs_ref.7) | copy-start | bytes 786436
  0.6 17.2 %copy-start.3 = (f32[48,768]{1,0:T(8,128)S(1)}, f32[48,768]{1,0:T(8,128)}, u32[]{:S(2)}) copy-start(f32[48,768]{1,0:T(8,128)} %inverse_ref.5) | copy-start | bytes 442372
  0.7 17.2 %copy-start.2 = (f32[2,64,512]{2,1,0:T(8,128)S(1)}, f32[2,64,512]{2,1,0:T(8,128)}, u32[]{:S(2)}) copy-start(f32[2,64,512]{2,1,0:T(8,128)} %coup_ref.5) | copy-start | bytes 786436
  0.7 17.2 %copy-start.4 = (f32[64,512]{1,0:T(8,128)S(1)}, f32[64,512]{1,0:T(8,128)}, u32[]{:S(2)}) copy-start(f32[64,512]{1,0:T(8,128)} %visc_ref.5) | copy-start | bytes 393220
  0.7 3.9 %copy-start = (bf16[48,2,64,512]{3,2,1,0:T(8,128)(2,1)S(1)}, bf16[48,2,64,512]{3,2,1,0:T(8,128)(2,1)}, u32[]{:S(2)}) copy-start(bf16[48,2,64,512]{3,2,1,0:T(8,128)(2,1)} %held.2) | copy-start | bytes 18874372
  0.7 17.2 %copy-start.5 = (s32[16]{0:T(128)S(1)}, s32[16]{0:T(128)}, u32[]{:S(2)}) copy-start(s32[16]{0:T(128)} %margin_ref.3) | copy-start | bytes 196
  3.2 14.6 %collective-permute-start = (f32[192,512]{1,0:T(8,128)S(1)}, f32[192,512]{1,0:T(8,128)S(1)}, u32[]{:S(2)}, u32[]{:S(2)}) collective-permute-start(f32[192,512]{1,0:T(8,128)S(1)} %get-tuple-element.22), channel_id=1, source_target_pairs={{0,1},{1,0},{2,3},{3,2},{4,5},{5,4},{6,7},{7,6},{8,9},{9,8},{10,11... | collective-permute-start | bytes 1179656 | tf_op jit(solution)/shard_map/ppermute | solution.py:705
  3.7 14.1 %collective-permute-start.1 = (f32[192,512]{1,0:T(8,128)S(1)}, f32[192,512]{1,0:T(8,128)S(1)}, u32[]{:S(2)}, u32[]{:S(2)}) collective-permute-start(f32[192,512]{1,0:T(8,128)S(1)} %get-tuple-element.23), channel_id=1, source_target_pairs={{1,2},{2,1},{3,4},{4,3},{5,6},{6,5},{7,8},{8,7},{9,10},{10,9},{11,... | collective-permute-start | bytes 1179656 | tf_op jit(solution)/shard_map/ppermute | solution.py:706
  21.5 12.3 %collective-permute-start.2 = (f32[8,512]{1,0:T(8,128)S(1)}, f32[8,512]{1,0:T(8,128)S(1)}, u32[]{:S(2)}, u32[]{:S(2)}) collective-permute-start(f32[8,512]{1,0:T(8,128)S(1)} %get-tuple-element.27), channel_id=1, source_target_pairs={{0,1},{1,0},{2,3},{3,2},{4,5},{5,4},{6,7},{7,6},{8,9},{9,8},{10,11... | collective-permute-start | bytes 49160 | tf_op jit(solution)/shard_map/ppermute | solution.py:705
  21.5 12.3 %collective-permute-start.3 = (f32[8,512]{1,0:T(8,128)S(1)}, f32[8,512]{1,0:T(8,128)S(1)}, u32[]{:S(2)}, u32[]{:S(2)}) collective-permute-start(f32[8,512]{1,0:T(8,128)S(1)} %get-tuple-element.28), channel_id=1, source_target_pairs={{1,2},{2,1},{3,4},{4,3},{5,6},{6,5},{7,8},{8,7},{9,10},{10,9},{11,... | collective-permute-start | bytes 49160 | tf_op jit(solution)/shard_map/ppermute | solution.py:706

commit v26 on v20

--- a/solution.py
+++ b/solution.py
@@ -463,7 +463,7 @@
 
 
 class Coarse:
-    def __init__(self, begin, inverse_ref, low, high, held, extended):
+    def __init__(self, begin, inverse_ref, low, high, held, extended, ahead=0):
         self.inverse, self.sides, self.held, self.extended = inverse_ref, (low, high), held, extended
         self.lifted, self.edges = [None] * 2, [None] * 2
         self.steps = begin(self) + [self.lift_own, self.make_matrix]
@@ -473,6 +473,8 @@
         for n in range(2):
             self.steps.insert(len(self.steps) - 6, functools.partial(self.lift_side, n))
             self.steps.append(functools.partial(self.edge, n))
+        for _ in range(ahead):
+            self.steps.pop(0)()
 
     def lift_own(self):
         self.own = lift(self.inverse, self.residual)
@@ -616,7 +618,7 @@
 
         return [scale, line]
 
-    coarse = Coarse(begin, inverse_ref, low, high, held, extended)
+    coarse = Coarse(begin, inverse_ref, low, high, held, extended, ahead=4)
     low_rows, high_rows = neighbours_of(partner_rows_ref, other_rows_ref)
 
     def field(a, t):

time: 45.8 us -> 45.8 us (level)
  no operation moved by 1% of the time
where the time goes in v26:
time: 45.8 us; the launch traced here: 45.6 us
  blocking collectives  31.7 us (69%)
  Pallas kernels  11 us (24%)
  starting transfers between devices  1.99 us (4%)
  between operations  0.74 us (2%)
    all_to_all x3, blocking collectives, from_everyone(): lax.all_to_all(rows, 'sub', 0, 0, tiled=True, axis_index_groups=order)  31.7 us
    pallas_call x1, Pallas kernels, on_device(): call(functools.partial(first_turn_kernel, count), 'first_turn', [SMEM] +...  3.64 us
    pallas_call x1, Pallas kernels, on_device(): call(functools.partial(second_turn_kernel, count), 'second_turn', [SMEM]...  2.54 us
    pallas_call x1, Pallas kernels, on_device(): call(pack_kernel, 'pack', [HBM] * 5, [packed, packed], 5000000, [pltpu.VM...  2.47 us
    ppermute x2, starting transfers between devices, swap(): lax.ppermute(other, 'sub', both(range(1, count - 1, 2)))  1.48 us
    pallas_call x1, Pallas kernels, on_device(): call(restrict_kernel, 'restrict', [VMEM] * 2, [row], 10000000, [sums])  1.44 us
  transfers between devices with their start and end apart: 4, of which 0 were waited for; matrix products, arithmetic and copies ran while one was open for 0% of the time, Pallas kernels for 3%

profile of v26, /device:TPU:0, one launch (start us, length us, event | category | flops | bytes accessed | tf_op | source)
XLA Modules:
  0.0 45.6 jit_solution(6937397069765354401)
XLA Ops:
  0.6 0.0 copy-start.1
  0.6 0.0 copy-start.3
  0.7 0.0 copy-start.2
  0.7 0.0 copy-start.4
  0.7 0.0 copy-start
  0.7 0.0 copy-start.5
  0.7 2.5 %pack.1 = (f32[192,512]{1,0:T(8,128)S(1)}, f32[192,512]{1,0:T(8,128)S(1)}) custom-call(f32[2,64,512]{2,1,0:T(8,128)} %rhs_ref.7, f32[64,512]{1,0:T(8,128)} %visc_ref.5, f32[2,64,512]{2,1,0:T(8,128)} %coup_ref.5, f32[48,768]{1,0:T(8,128)} %inverse_ref.5, bf16[48,2,64,512]{3,2,1,0:T(8,128)(2,1)} %held.2), custom_call_target="tpu_custom_call" | custom-call | flops 5000000 | bytes 4000000 | tf_op jit(solution)/shard_map/pack/pallas_call | solution.py:720
  3.2 0.5 %collective-permute-start = (f32[192,512]{1,0:T(8,128)S(1)}, f32[192,512]{1,0:T(8,128)S(1)}, u32[]{:S(2)}, u32[]{:S(2)}) collective-permute-start(f32[192,512]{1,0:T(8,128)S(1)} %get-tuple-element.22), channel_id=1, source_target_pairs={{0,1},{1,0},{2,3},{3,2},{4,5},{5,4},{6,7},{7,6},{8,9},{9,8},{10,11... | collective-permute-start | bytes 1179656 | tf_op jit(solution)/shard_map/ppermute | solution.py:702
  3.7 0.8 %collective-permute-start.1 = (f32[192,512]{1,0:T(8,128)S(1)}, f32[192,512]{1,0:T(8,128)S(1)}, u32[]{:S(2)}, u32[]{:S(2)}) collective-permute-start(f32[192,512]{1,0:T(8,128)S(1)} %get-tuple-element.23), channel_id=1, source_target_pairs={{1,2},{2,1},{3,4},{4,3},{5,6},{6,5},{7,8},{8,7},{9,10},{10,9},{11,... | collective-permute-start | bytes 1179656 | tf_op jit(solution)/shard_map/ppermute | solution.py:703
  4.5 0.0 copy-done.1
  4.5 0.1 copy-done
  4.6 1.4 %restrict.1 = f32[16,128]{1,0:T(8,128)S(1)} custom-call(f32[2,64,512]{2,1,0:T(8,128)S(1)} %copy-done.1, bf16[48,2,64,512]{3,2,1,0:T(8,128)(2,1)S(1)} %copy-done), custom_call_target="tpu_custom_call" | custom-call | flops 10000000 | bytes 4000000 | tf_op jit(solution)/shard_map/restrict/pallas_call | solution.py:728
  6.1 11.7 %all_to_all.33 = f32[16,1,128]{2,1,0:T(1,128)S(1)} all-to-all(f32[16,1,128]{2,1,0:T(1,128)S(1)} %bitcast.19), channel_id=1, replica_groups={{15,14,13,12,11,10,9,8,7,6,5,4,3,2,1,0},{31,30,29,28,27,26,25,24,23,22,..., dimensions={0} | all-to-all | bytes 16384 | tf_op jit(solution)/shard_map/all_to_all | solution.py:695
  17.8 0.0 collective-permute-done.partner_ref
  17.8 0.0 collective-permute-done.1.other_ref
  17.8 0.0 copy-done.3
  17.8 0.0 copy-done.2
  17.8 0.0 copy-done.4
  17.8 0.0 copy-done.5
  17.8 3.6 %first_turn.1 = (f32[2,64,512]{2,1,0:T(8,128)S(1)}, f32[2,64,512]{2,1,0:T(8,128)S(1)}, f32[2,80,512]{2,1,0:T(8,128)S(1)}, f32[1,768]{1,0:T(1,128)S(1)}, f32[6,14...) custom-call(s32[16]{0:T(128)S(1)} %copy-done.5, ...), custom_call_target="tpu_custom_call" | custom-call | flops 20000000 | bytes 4000000 | tf_op jit(solution)/shard_map/first_turn/pallas_call | solution.py:732
  21.5 0.0 collective-permute-start.2
  21.5 0.7 %collective-permute-start.3 = (f32[8,512]{1,0:T(8,128)S(1)}, f32[8,512]{1,0:T(8,128)S(1)}, u32[]{:S(2)}, u32[]{:S(2)}) collective-permute-start(f32[8,512]{1,0:T(8,128)S(1)} %get-tuple-element.28), channel_id=1, source_target_pairs={{1,2},{2,1},{3,4},{4,3},{5,6},{6,5},{7,8},{8,7},{9,10},{10,9},{11,... | collective-permute-start | bytes 49160 | tf_op jit(solution)/shard_map/ppermute | solution.py:703
  22.2 11.6 %all_to_all.34 = f32[16,1,128]{2,1,0:T(1,128)S(1)} all-to-all(f32[16,1,128]{2,1,0:T(1,128)S(1)} %bitcast.20), channel_id=1, replica_groups={{15,14,13,12,11,10,9,8,7,6,5,4,3,2,1,0},{31,30,29,28,27,26,25,24,23,22,..., dimensions={0} | all-to-all | bytes 16384 | tf_op jit(solution)/shard_map/all_to_all | solution.py:695
  33.8 0.0 collective-permute-done.2.partner_rows_ref
  33.8 0.0 collective-permute-done.3.other_rows_ref
  33.8 2.5 %second_turn.1 = (f32[2,64,512]{2,1,0:T(8,128)S(1)}, f32[16,128]{1,0:T(8,128)S(1)}) custom-call(s32[16]{0:T(128)S(1)} %copy-done.5, f32[16,128]{1,0:T(8,128)S(1)} %bitcast.14, f32[16,128]{1,0:T(8,128)S(1)} %bitcast.16, f32[1,768]{1,0:T(1,128)S(1)} %get-tuple-element.25.residual_ref, f32[6,144,512]{2,1,0:T(8,128)S(1)} %get-tuple-element.26.factors_ref, ...), custom_call_target="tpu_custom_call" | custom-call | flops 20000000 | bytes 4000000 | tf_op jit(solution)/shard_map/second_turn/pallas_call | solution.py:739
  36.3 8.4 %all_to_all.35 = f32[16,1,128]{2,1,0:T(1,128)S(1)} all-to-all(f32[16,1,128]{2,1,0:T(1,128)S(1)} %bitcast.21), channel_id=1, replica_groups={{15,14,13,12,11,10,9,8,7,6,5,4,3,2,1,0},{31,30,29,28,27,26,25,24,23,22,..., dimensions={0} | all-to-all | bytes 16384 | tf_op jit(solution)/shard_map/all_to_all | solution.py:695
  44.7 0.9 %finish.1 = (f32[2,64,512]{2,1,0:T(8,128)}, f32[2,3]{1,0:T(2,128)}) custom-call(f32[16,128]{1,0:T(8,128)S(1)} %bitcast.15, f32[16,128]{1,0:T(8,128)S(1)} %bitcast.17, f32[16,128]{1,0:T(8,128)S(1)} %bitcast.18, f32[2,64,512]{2,1,0:T(8,128)S(1)} %get-tuple-element.32.first_direction_ref, f32[2,64,512]{2,1,0:T(8,128)S(1)} %get-tuple-element.33.second_direction_ref), custom_call_target="tpu_custom_call" | custom-call | flops 1000000 | bytes 4000000 | tf_op jit(solution)/shard_map/finish/pallas_call | solution.py:747
Async XLA Ops:
  0.6 3.9 %copy-start.1 = (f32[2,64,512]{2,1,0:T(8,128)S(1)}, f32[2,64,512]{2,1,0:T(8,128)}, u32[]{:S(2)}) copy-start(f32[2,64,512]{2,1,0:T(8,128)} %rhs_ref.7) | copy-start | bytes 786436
  0.6 17.2 %copy-start.3 = (f32[48,768]{1,0:T(8,128)S(1)}, f32[48,768]{1,0:T(8,128)}, u32[]{:S(2)}) copy-start(f32[48,768]{1,0:T(8,128)} %inverse_ref.5) | copy-start | bytes 442372
  0.7 17.2 %copy-start.2 = (f32[2,64,512]{2,1,0:T(8,128)S(1)}, f32[2,64,512]{2,1,0:T(8,128)}, u32[]{:S(2)}) copy-start(f32[2,64,512]{2,1,0:T(8,128)} %coup_ref.5) | copy-start | bytes 786436
  0.7 17.2 %copy-start.4 = (f32[64,512]{1,0:T(8,128)S(1)}, f32[64,512]{1,0:T(8,128)}, u32[]{:S(2)}) copy-start(f32[64,512]{1,0:T(8,128)} %visc_ref.5) | copy-start | bytes 393220
  0.7 3.9 %copy-start = (bf16[48,2,64,512]{3,2,1,0:T(8,128)(2,1)S(1)}, bf16[48,2,64,512]{3,2,1,0:T(8,128)(2,1)}, u32[]{:S(2)}) copy-start(bf16[48,2,64,512]{3,2,1,0:T(8,128)(2,1)} %held.2) | copy-start | bytes 18874372
  0.7 17.2 %copy-start.5 = (s32[16]{0:T(128)S(1)}, s32[16]{0:T(128)}, u32[]{:S(2)}) copy-start(s32[16]{0:T(128)} %margin_ref.3) | copy-start | bytes 196
  3.2 14.6 %collective-permute-start = (f32[192,512]{1,0:T(8,128)S(1)}, f32[192,512]{1,0:T(8,128)S(1)}, u32[]{:S(2)}, u32[]{:S(2)}) collective-permute-start(f32[192,512]{1,0:T(8,128)S(1)} %get-tuple-element.22), channel_id=1, source_target_pairs={{0,1},{1,0},{2,3},{3,2},{4,5},{5,4},{6,7},{7,6},{8,9},{9,8},{10,11... | collective-permute-start | bytes 1179656 | tf_op jit(solution)/shard_map/ppermute | solution.py:702
  3.7 14.1 %collective-permute-start.1 = (f32[192,512]{1,0:T(8,128)S(1)}, f32[192,512]{1,0:T(8,128)S(1)}, u32[]{:S(2)}, u32[]{:S(2)}) collective-permute-start(f32[192,512]{1,0:T(8,128)S(1)} %get-tuple-element.23), channel_id=1, source_target_pairs={{1,2},{2,1},{3,4},{4,3},{5,6},{6,5},{7,8},{8,7},{9,10},{10,9},{11,... | collective-permute-start | bytes 1179656 | tf_op jit(solution)/shard_map/ppermute | solution.py:703
  21.5 12.3 %collective-permute-start.2 = (f32[8,512]{1,0:T(8,128)S(1)}, f32[8,512]{1,0:T(8,128)S(1)}, u32[]{:S(2)}, u32[]{:S(2)}) collective-permute-start(f32[8,512]{1,0:T(8,128)S(1)} %get-tuple-element.27), channel_id=1, source_target_pairs={{0,1},{1,0},{2,3},{3,2},{4,5},{5,4},{6,7},{7,6},{8,9},{9,8},{10,11... | collective-permute-start | bytes 49160 | tf_op jit(solution)/shard_map/ppermute | solution.py:702
  21.5 12.3 %collective-permute-start.3 = (f32[8,512]{1,0:T(8,128)S(1)}, f32[8,512]{1,0:T(8,128)S(1)}, u32[]{:S(2)}, u32[]{:S(2)}) collective-permute-start(f32[8,512]{1,0:T(8,128)S(1)} %get-tuple-element.28), channel_id=1, source_target_pairs={{1,2},{2,1},{3,4},{4,3},{5,6},{6,5},{7,8},{8,7},{9,10},{10,9},{11,... | collective-permute-start | bytes 49160 | tf_op jit(solution)/shard_map/ppermute | solution.py:703
